TPU v7x, 32 devices: a whole 2x2x4 slice. The times are simulated.
32 devices in a mesh: section: 2 (over x), head: 4 (over z), frame: 4 (over y, core).
Axes of the slice: x: 2, y: 2, z: 4, core: 2. Of those that a mesh axis runs over, the one named last changes fastest.
Arguments:
- inputs: bfloat16 [2, 2048, 1024], P(None, 'frame'), may hold values from -6 to 6
- lengths: int32 [2, 4], replicated, may hold values from 1 to 2045, as said below
- text: bfloat16 [2, 4, 64, 1024], P(None, None, 'frame'), may hold values from -6 to 6
- cotangent: float32 [2, 2048, 1024], P(None, 'frame'), may hold values from -6 to 6
- first_gain: float32 [2, 1024], P('section'), may hold values from 0.25 to 1.75
- first_shift: float32 [2, 1024], P('section'), may hold values from -2 to 2
- query_weight: bfloat16 [2, 1024, 1024], P('section', None, 'head'), may hold values from -0.1875 to 0.1875
- key_weight: bfloat16 [2, 1024, 1024], P('section', None, 'head'), may hold values from -0.1875 to 0.1875
- value_weight: bfloat16 [2, 1024, 1024], P('section', None, 'head'), may hold values from -0.1875 to 0.1875
- output_weight: bfloat16 [2, 1024, 1024], P('section', 'head'), may hold values from -4 to 4
- second_gain: float32 [2, 1024], P('section'), may hold values from 0.25 to 1.75
- second_shift: float32 [2, 1024], P('section'), may hold values from -2 to 2
- cross_query: bfloat16 [2, 1024, 1024], P('section', None, 'head'), may hold values from -0.1875 to 0.1875
- cross_key: bfloat16 [2, 1024, 1024], P('section', None, 'head'), may hold values from -0.1875 to 0.1875
- cross_value: bfloat16 [2, 1024, 1024], P('section', None, 'head'), may hold values from -0.1875 to 0.1875
- cross_output: bfloat16 [2, 1024, 1024], P('section', 'head'), may hold values from -0.75 to 0.75
- third_gain: float32 [2, 1024], P('section'), may hold values from 0.25 to 1.75
- third_shift: float32 [2, 1024], P('section'), may hold values from -2 to 2
- expand_weight: bfloat16 [2, 1024, 4096], P('section', None, 'head'), may hold values from -0.1875 to 0.1875
- reduce_weight: bfloat16 [2, 4096, 1024], P('section', 'head'), may hold values from -0.09375 to 0.09375
Outputs:
- layer_outputs: float32 [2, 2, 2048, 1024], P('section', None, 'frame')
- input_grads: float32 [2, 2, 2048, 1024], P('section', None, 'frame')
- text_grad: float32 [2, 4, 64, 1024], P(None, None, 'frame')
- first_gain_grad: float32 [2, 1024], P('section', 'frame')
- first_shift_grad: float32 [2, 1024], P('section', 'frame')
- query_weight_grad: float32 [2, 1024, 1024], P('section', 'frame', 'head')
- key_weight_grad: float32 [2, 1024, 1024], P('section', 'frame', 'head')
- value_weight_grad: float32 [2, 1024, 1024], P('section', 'frame', 'head')
- output_weight_grad: float32 [2, 1024, 1024], P('section', ('head', 'frame'))
- second_gain_grad: float32 [2, 1024], P('section', 'frame')
- second_shift_grad: float32 [2, 1024], P('section', 'frame')
- cross_query_grad: float32 [2, 1024, 1024], P('section', 'frame', 'head')
- cross_key_grad: float32 [2, 1024, 1024], P('section', 'frame', 'head')
- cross_value_grad: float32 [2, 1024, 1024], P('section', 'frame', 'head')
- cross_output_grad: float32 [2, 1024, 1024], P('section', ('head', 'frame'))
- third_gain_grad: float32 [2, 1024], P('section', 'frame')
- third_shift_grad: float32 [2, 1024], P('section', 'frame')
- expand_weight_grad: float32 [2, 1024, 4096], P('section', 'frame', 'head')
- reduce_weight_grad: float32 [2, 4096, 1024], P('section', ('head', 'frame'))
Inputs may be any that keep to these rules, and one draw needn't show every extreme that they name: Row m lists the lengths of the 4 items packed in order into micro-batch m; they sum to 2048. In every row one item, in a slot drawn from the seed, is longer than 1536; the other items together are shorter than 512. In one micro-batch, drawn from the seed, the other items have length 1 each.
All inputs are finite; a program needn't handle non-finite values.
Results may differ from a plain program's by a relative error of at most 0.025.
Values may be sent and summed in bfloat16 or wider, within the bound.
A program may use at most 320 MiB of HBM per device.

v0:
```python
import jax
import jax.numpy as jnp
from jax import lax
from jax.sharding import PartitionSpec as P

HEAD = 64
TEXT = 64
ITEMS = 4


masked_score = -1e30
inv_sqrt_two = 0.7071067811865476
inv_sqrt_tau = 0.3989422804014327


def passed_along(x, axis, by):
    length = lax.axis_size(axis)
    pairs = [(i, i + by) for i in range(length) if 0 <= i + by < length]
    return lax.ppermute(x, axis, pairs)


def as_sent(x):
    return jax.tree.map(lambda a: a.astype(jnp.bfloat16) if a.dtype == jnp.float32 else a, x)


def matmul(left_side, right_side):
    return jnp.dot(left_side, right_side, preferred_element_type=jnp.float32)


def matmul_tn(left_side, right_side):
    return lax.dot_general(
        left_side, right_side, (((0,), (0,)), ((), ())), preferred_element_type=jnp.float32
    )


def matmul_nt(left_side, right_side):
    return lax.dot_general(
        left_side, right_side, (((1,), (1,)), ((), ())), preferred_element_type=jnp.float32
    )


def layer_norm(signal, gain_vec, shift_vec):
    average = jnp.mean(signal, axis=-1, keepdims=True)
    centered = signal - average
    variance = jnp.mean(centered * centered, axis=-1, keepdims=True)
    return centered * lax.rsqrt(variance + 1e-05) * gain_vec + shift_vec


def norm_back(signal, gain_vec, upstream):
    average = jnp.mean(signal, axis=-1, keepdims=True)
    centered = signal - average
    inverse = lax.rsqrt(jnp.mean(centered * centered, axis=-1, keepdims=True) + 1e-05)
    standard = centered * inverse
    scaled = upstream * gain_vec
    through = inverse * (
        scaled
        - jnp.mean(scaled, axis=-1, keepdims=True)
        - standard * jnp.mean(scaled * standard, axis=-1, keepdims=True)
    )
    return (through, jnp.sum(upstream * standard, axis=0), jnp.sum(upstream, axis=0))


def head_total(partial_sum):
    return lax.psum(partial_sum.astype(jnp.bfloat16), "head").astype(jnp.float32)


def split_heads(matrix):
    return matrix.reshape(matrix.shape[0], matrix.shape[1] // HEAD, HEAD)


def softmax_rows(query, key_rows, allowed):
    logits = jnp.einsum(
        "qhd,khd->hqk",
        split_heads(query),
        split_heads(key_rows),
        preferred_element_type=jnp.float32,
    ) * HEAD ** (-0.5)
    logits = jnp.where(allowed[None], logits, masked_score)
    exponent = jnp.exp(logits - jnp.max(logits, axis=-1, keepdims=True))
    return exponent / jnp.sum(exponent, axis=-1, keepdims=True)


def attend(query, key_rows, value_rows, allowed):
    weights_low = softmax_rows(query, key_rows, allowed).astype(jnp.bfloat16)
    result = jnp.einsum(
        "hqk,khd->qhd", weights_low, split_heads(value_rows), preferred_element_type=jnp.float32
    )
    return result.reshape(query.shape).astype(jnp.bfloat16)


def attend_back(query, key_rows, value_rows, allowed, grad_out):
    probabilities = softmax_rows(query, key_rows, allowed)
    weights_low = probabilities.astype(jnp.bfloat16)
    grad_heads = split_heads(grad_out)
    grad_prob = jnp.einsum(
        "qhd,khd->hqk", grad_heads, split_heads(value_rows), preferred_element_type=jnp.float32
    )
    centre = jnp.sum(probabilities * grad_prob, axis=-1, keepdims=True)
    grad_logit = (probabilities * (grad_prob - centre)).astype(jnp.bfloat16)
    scale = HEAD ** (-0.5)
    grad_query = (
        jnp.einsum(
            "hqk,khd->qhd", grad_logit, split_heads(key_rows), preferred_element_type=jnp.float32
        )
        * scale
    )
    grad_keys = (
        jnp.einsum(
            "hqk,qhd->khd", grad_logit, split_heads(query), preferred_element_type=jnp.float32
        )
        * scale
    )
    grad_values = jnp.einsum(
        "hqk,qhd->khd", weights_low, grad_heads, preferred_element_type=jnp.float32
    )
    return (
        grad_query.reshape(query.shape),
        grad_keys.reshape(key_rows.shape),
        grad_values.reshape(value_rows.shape),
    )


def forward(entering, weights, text_full, self_allowed, cross_allowed):
    (
        first_gain,
        first_shift,
        query_weight,
        key_weight,
        value_weight,
        output_weight,
        second_gain,
        second_shift,
        cross_query,
        cross_key,
        cross_value,
        cross_output,
        third_gain,
        third_shift,
        expand_weight,
        reduce_weight,
    ) = weights
    signal = entering.astype(jnp.float32)
    first_normed = layer_norm(signal, first_gain, first_shift).astype(jnp.bfloat16)
    query = matmul(first_normed, query_weight).astype(jnp.bfloat16)
    key_rows = matmul(first_normed, key_weight).astype(jnp.bfloat16)
    value_rows = matmul(first_normed, value_weight).astype(jnp.bfloat16)
    all_keys, all_values = (
        lax.all_gather(key_rows, "frame", axis=0, tiled=True),
        lax.all_gather(value_rows, "frame", axis=0, tiled=True),
    )
    attended = attend(query, all_keys, all_values, self_allowed)
    middle = signal + head_total(matmul(attended, output_weight))
    second_normed = layer_norm(middle, second_gain, second_shift).astype(jnp.bfloat16)
    cross_queries = matmul(second_normed, cross_query).astype(jnp.bfloat16)
    cross_keys = matmul(text_full, cross_key).astype(jnp.bfloat16)
    cross_values = matmul(text_full, cross_value).astype(jnp.bfloat16)
    cross_att = attend(cross_queries, cross_keys, cross_values, cross_allowed)
    latter = middle + head_total(matmul(cross_att, cross_output))
    third_normed = layer_norm(latter, third_gain, third_shift).astype(jnp.bfloat16)
    hidden_pre = matmul(third_normed, expand_weight)
    hidden_act = jax.nn.gelu(hidden_pre, approximate=False).astype(jnp.bfloat16)
    result = latter + head_total(matmul(hidden_act, reduce_weight))
    saved = (
        signal,
        first_normed,
        query,
        all_keys,
        all_values,
        attended,
        middle,
        second_normed,
        cross_queries,
        cross_keys,
        cross_values,
        cross_att,
        latter,
        third_normed,
        hidden_pre,
        hidden_act,
    )
    return (result, saved)


def backward(saved, upstream, weights, text_local, self_allowed, cross_allowed):
    (
        first_gain,
        first_shift,
        query_weight,
        key_weight,
        value_weight,
        output_weight,
        second_gain,
        second_shift,
        cross_query,
        cross_key,
        cross_value,
        cross_output,
        third_gain,
        third_shift,
        expand_weight,
        reduce_weight,
    ) = weights
    (
        signal,
        first_normed,
        query,
        all_keys,
        all_values,
        attended,
        middle,
        second_normed,
        cross_queries,
        cross_keys,
        cross_values,
        cross_att,
        latter,
        third_normed,
        hidden_pre,
        hidden_act,
    ) = saved
    grad_out = upstream.astype(jnp.bfloat16)
    grad_reduce = matmul_tn(hidden_act, grad_out)
    grad_act = matmul_nt(grad_out, reduce_weight)
    slope = (
        0.5 * (1.0 + lax.erf(hidden_pre * inv_sqrt_two))
        + hidden_pre * jnp.exp(-0.5 * hidden_pre * hidden_pre) * inv_sqrt_tau
    )
    grad_pre = (grad_act * slope).astype(jnp.bfloat16)
    grad_expand = matmul_tn(third_normed, grad_pre)
    grad_third = head_total(matmul_nt(grad_pre, expand_weight))
    grad_latter, grad_third_gain, grad_third_shift = norm_back(latter, third_gain, grad_third)
    grad_latter = grad_latter + upstream
    grad_cross = grad_latter.astype(jnp.bfloat16)
    grad_cross_output = matmul_tn(cross_att, grad_cross)
    grad_cross_att = matmul_nt(grad_cross, cross_output).astype(jnp.bfloat16)
    grad_cq, grad_ck, grad_cv = attend_back(
        cross_queries, cross_keys, cross_values, cross_allowed, grad_cross_att
    )
    key_part, value_part = (
        lax.psum_scatter(
            grad_ck.reshape(ITEMS, TEXT, -1).astype(jnp.bfloat16),
            "frame",
            scatter_dimension=1,
            tiled=True,
        ).astype(jnp.float32),
        lax.psum_scatter(
            grad_cv.reshape(ITEMS, TEXT, -1).astype(jnp.bfloat16),
            "frame",
            scatter_dimension=1,
            tiled=True,
        ).astype(jnp.float32),
    )
    key_part = key_part.reshape(-1, key_part.shape[2]).astype(jnp.bfloat16)
    value_part = value_part.reshape(-1, value_part.shape[2]).astype(jnp.bfloat16)
    grad_cross_key = matmul_tn(text_local, key_part)
    grad_cross_value = matmul_tn(text_local, value_part)
    text_part = matmul_nt(key_part, cross_key) + matmul_nt(value_part, cross_value)
    grad_cquery = grad_cq.astype(jnp.bfloat16)
    grad_cross_query = matmul_tn(second_normed, grad_cquery)
    grad_second = head_total(matmul_nt(grad_cquery, cross_query))
    grad_middle, grad_second_gain, grad_second_shift = norm_back(middle, second_gain, grad_second)
    grad_middle = grad_middle + grad_latter
    grad_self = grad_middle.astype(jnp.bfloat16)
    grad_output = matmul_tn(attended, grad_self)
    grad_att = matmul_nt(grad_self, output_weight).astype(jnp.bfloat16)
    grad_q, grad_k_all, grad_v_all = attend_back(
        query, all_keys, all_values, self_allowed, grad_att
    )
    grad_k, grad_v = (
        lax.psum_scatter(
            grad_k_all.astype(jnp.bfloat16), "frame", scatter_dimension=0, tiled=True
        ).astype(jnp.float32),
        lax.psum_scatter(
            grad_v_all.astype(jnp.bfloat16), "frame", scatter_dimension=0, tiled=True
        ).astype(jnp.float32),
    )
    grad_query_low = grad_q.astype(jnp.bfloat16)
    grad_key_low = grad_k.astype(jnp.bfloat16)
    grad_value_low = grad_v.astype(jnp.bfloat16)
    grad_query = matmul_tn(first_normed, grad_query_low)
    grad_key = matmul_tn(first_normed, grad_key_low)
    grad_value = matmul_tn(first_normed, grad_value_low)
    grad_first = head_total(
        matmul_nt(grad_query_low, query_weight)
        + matmul_nt(grad_key_low, key_weight)
        + matmul_nt(grad_value_low, value_weight)
    )
    grad_signal, grad_first_gain, grad_first_shift = norm_back(signal, first_gain, grad_first)
    grad_signal = grad_signal + grad_middle
    grads = (
        grad_first_gain,
        grad_first_shift,
        grad_query,
        grad_key,
        grad_value,
        grad_output,
        grad_second_gain,
        grad_second_shift,
        grad_cross_query,
        grad_cross_key,
        grad_cross_value,
        grad_cross_output,
        grad_third_gain,
        grad_third_shift,
        grad_expand,
        grad_reduce,
    )
    return (grad_signal, grads, text_part)


def per_device(
    inputs,
    lengths,
    text,
    cotangent,
    first_gain,
    first_shift,
    query_weight,
    key_weight,
    value_weight,
    output_weight,
    second_gain,
    second_shift,
    cross_query,
    cross_key,
    cross_value,
    cross_output,
    third_gain,
    third_shift,
    expand_weight,
    reduce_weight,
):
    weight_args = (
        first_gain,
        first_shift,
        query_weight,
        key_weight,
        value_weight,
        output_weight,
        second_gain,
        second_shift,
        cross_query,
        cross_key,
        cross_value,
        cross_output,
        third_gain,
        third_shift,
        expand_weight,
        reduce_weight,
    )
    weights = tuple((array_in[0] for array_in in weight_args))
    section_count = lax.axis_size("section")
    section_index = lax.axis_index("section")
    frame_count = lax.axis_size("frame")
    frame_index = lax.axis_index("frame")
    micro_count, rows_dev, model_width = inputs.shape
    rows_all = rows_dev * frame_count
    text_rows_dev = text.shape[2]
    text_full = lax.all_gather(text, "frame", axis=2, tiled=True)
    own_start = frame_index * rows_dev
    own_positions = own_start + jnp.arange(rows_dev, dtype=jnp.int32)
    all_positions = jnp.arange(rows_all, dtype=jnp.int32)
    text_item = jnp.arange(ITEMS * TEXT, dtype=jnp.int32) // TEXT
    batch_ids = jnp.arange(micro_count, dtype=jnp.int32)

    def build_masks(which_batch):
        item_ends = jnp.cumsum(lengths[which_batch])
        seg_all = jnp.sum((all_positions[:, None] >= item_ends[None, :]).astype(jnp.int32), axis=1)
        seg_own = lax.dynamic_slice_in_dim(seg_all, own_start, rows_dev)
        self_allowed = (all_positions[None, :] <= own_positions[:, None]) & (
            seg_own[:, None] == seg_all[None, :]
        )
        keys_allowed = (own_positions[None, :] <= all_positions[:, None]) & (
            seg_all[:, None] == seg_own[None, :]
        )
        cross_allowed = seg_own[:, None] == text_item[None, :]
        return (self_allowed, cross_allowed, keys_allowed)

    def text_for(which_batch):
        return text_full[which_batch].reshape(ITEMS * TEXT, model_width)

    ticks = micro_count + section_count - 1
    carried = jnp.zeros((rows_dev, model_width), jnp.bfloat16)
    outputs = jnp.zeros((micro_count, rows_dev, model_width), jnp.float32)
    kept = []
    for moment in range(ticks):
        step_batch = moment - section_index
        active = (step_batch >= 0) & (step_batch < micro_count)
        which_batch = jnp.clip(step_batch, 0, micro_count - 1)
        entering = jnp.where(section_index == 0, inputs[which_batch], carried)
        self_allowed, cross_allowed, keys_allowed = build_masks(which_batch)
        result, saved = forward(
            entering, weights, text_for(which_batch), self_allowed, cross_allowed
        )
        selected = (batch_ids == which_batch) & active
        outputs = jnp.where(selected[:, None, None], result[None], outputs)
        kept.append(entering)
        if moment + 1 < ticks:
            carried = passed_along(result.astype(jnp.bfloat16), "section", 1)
    stacked = jax.tree.map(lambda *pieces: jnp.stack(pieces), *kept)
    totals = tuple((jnp.zeros(array_in.shape, jnp.float32) for array_in in weights))
    text_acc = jnp.zeros((micro_count, ITEMS, text_rows_dev, model_width), jnp.float32)
    in_grads = jnp.zeros((micro_count, rows_dev, model_width), jnp.float32)
    returning = jnp.zeros((rows_dev, model_width), jnp.bfloat16)
    last_section = section_count - 1
    for moment in range(ticks):
        step_batch = moment - (last_section - section_index)
        active = (step_batch >= 0) & (step_batch < micro_count)
        which_batch = jnp.clip(step_batch, 0, micro_count - 1)
        entry = lax.dynamic_index_in_dim(stacked, which_batch + section_index, 0, keepdims=False)
        self_allowed, cross_allowed, keys_allowed = build_masks(which_batch)
        unused_result, saved = forward(
            entry, weights, text_for(which_batch), self_allowed, cross_allowed
        )
        upstream = jnp.where(
            section_index == last_section, cotangent[which_batch], returning.astype(jnp.float32)
        )
        text_local = text[which_batch].reshape(ITEMS * text_rows_dev, model_width)
        grad_signal, grads, text_part = backward(
            saved, upstream, weights, text_local, self_allowed, cross_allowed
        )
        selected = (batch_ids == which_batch) & active
        in_grads = jnp.where(selected[:, None, None], grad_signal[None], in_grads)
        text_acc = text_acc + jnp.where(
            selected[:, None, None, None],
            text_part.reshape(ITEMS, text_rows_dev, model_width)[None],
            0.0,
        )
        masked = tuple((jnp.where(active, grad_piece, 0.0) for grad_piece in grads))
        totals = tuple(
            (total_piece + grad_piece for total_piece, grad_piece in zip(totals, masked))
        )
        if moment + 1 < ticks:
            returning = passed_along(grad_signal.astype(jnp.bfloat16), "section", -1)
    totals = jax.tree.map(
        lambda part: part.astype(jnp.float32),
        lax.psum_scatter(as_sent(totals), "frame", scatter_dimension=0, tiled=True),
    )
    text_grad = lax.psum(text_acc.astype(jnp.bfloat16), ("section", "head")).astype(jnp.float32)
    return (outputs[None], in_grads[None], text_grad) + tuple(
        (total_piece[None] for total_piece in totals)
    )


def solution(mesh):
    return jax.shard_map(
        per_device,
        mesh=mesh,
        in_specs=(
            P(None, "frame", None),
            P(),
            P(None, None, "frame", None),
            P(None, "frame", None),
            P("section", None),
            P("section", None),
            P("section", None, "head"),
            P("section", None, "head"),
            P("section", None, "head"),
            P("section", "head", None),
            P("section", None),
            P("section", None),
            P("section", None, "head"),
            P("section", None, "head"),
            P("section", None, "head"),
            P("section", "head", None),
            P("section", None),
            P("section", None),
            P("section", None, "head"),
            P("section", "head", None),
        ),
        out_specs=(
            P("section", None, "frame", None),
            P("section", None, "frame", None),
            P(None, None, "frame", None),
            P("section", "frame"),
            P("section", "frame"),
            P("section", "frame", "head"),
            P("section", "frame", "head"),
            P("section", "frame", "head"),
            P("section", ("head", "frame"), None),
            P("section", "frame"),
            P("section", "frame"),
            P("section", "frame", "head"),
            P("section", "frame", "head"),
            P("section", "frame", "head"),
            P("section", ("head", "frame"), None),
            P("section", "frame"),
            P("section", "frame"),
            P("section", "frame", "head"),
            P("section", ("head", "frame"), None),
        ),
        check_vma=False,
    )
```

profile of v0, /device:TPU:0, one launch (start us, length us, event | category | flops | bytes accessed | tf_op | source)
XLA Modules:
  0.0 2420.5 jit_solution(17014946790686993744)
XLA Ops:
  33.9 10.8 fusion.904
  52.8 9.0 fusion.400
  73.7 49.8 %all-reduce.32.cloned.1.call-done = bf16[512,1024]{1,0:T(8,128)(2,1)} async-done(((bf16[512,1024]{1,0:T(8,128)(2,1)}), bf16[512,1024]{1,0:T(8,128)(2,1)}) %all-reduce.32.cloned.1.call-update) | async-done | bytes 1048592 | tf_op jit(solution)/shard_map/psum | solution.py:64
  134.5 51.3 %all-reduce.34.cloned.1.call-done = bf16[512,1024]{1,0:T(8,128)(2,1)} async-done(((bf16[512,1024]{1,0:T(8,128)(2,1)}), bf16[512,1024]{1,0:T(8,128)(2,1)}) %all-reduce.34.cloned.1.call-update) | async-done | bytes 1048592 | tf_op jit(solution)/shard_map/psum | solution.py:64
  188.7 9.6 fusion.342
  198.9 50.8 %all-reduce.36.cloned.1.call-done = bf16[512,1024]{1,0:T(8,128)(2,1)} async-done(((bf16[512,1024]{1,0:T(8,128)(2,1)}), bf16[512,1024]{1,0:T(8,128)(2,1)}) %all-reduce.36.cloned.1.call-update) | async-done | bytes 1048592 | tf_op jit(solution)/shard_map/psum | solution.py:64
  257.5 22.5 collective-permute-done
  288.4 12.7 all-gather.22.cloned.1.call-done
  303.4 11.4 fusion.906
  322.4 8.8 fusion.399
  336.6 48.0 %all-reduce.38.cloned.1.call-done = bf16[512,1024]{1,0:T(8,128)(2,1)} async-done(((bf16[512,1024]{1,0:T(8,128)(2,1)}), bf16[512,1024]{1,0:T(8,128)(2,1)}) %all-reduce.38.cloned.1.call-update) | async-done | bytes 1048592 | tf_op jit(solution)/shard_map/psum | solution.py:64
  396.2 51.3 %all-reduce.40.cloned.1.call-done = bf16[512,1024]{1,0:T(8,128)(2,1)} async-done(((bf16[512,1024]{1,0:T(8,128)(2,1)}), bf16[512,1024]{1,0:T(8,128)(2,1)}) %all-reduce.40.cloned.1.call-update) | async-done | bytes 1048592 | tf_op jit(solution)/shard_map/psum | solution.py:64
  450.9 10.4 fusion.345
  461.4 51.3 %all-reduce.42.cloned.1.call-done = bf16[512,1024]{1,0:T(8,128)(2,1)} async-done(((bf16[512,1024]{1,0:T(8,128)(2,1)}), bf16[512,1024]{1,0:T(8,128)(2,1)}) %all-reduce.42.cloned.1.call-update) | async-done | bytes 1048592 | tf_op jit(solution)/shard_map/psum | solution.py:64
  521.9 21.9 collective-permute-done.1
  555.9 13.1 all-gather.36.cloned.1.call-done
  570.5 11.0 fusion.908
  590.3 8.5 fusion.389
  604.0 49.0 %all-reduce.46.cloned.1.call-done = bf16[512,1024]{1,0:T(8,128)(2,1)} async-done(((bf16[512,1024]{1,0:T(8,128)(2,1)}), bf16[512,1024]{1,0:T(8,128)(2,1)}) %all-reduce.46.cloned.1.call-update) | async-done | bytes 1048592 | tf_op jit(solution)/shard_map/psum | solution.py:64
  683.0 33.2 %all-reduce.48.cloned.1.call-done = bf16[512,1024]{1,0:T(8,128)(2,1)} async-done(((bf16[512,1024]{1,0:T(8,128)(2,1)}), bf16[512,1024]{1,0:T(8,128)(2,1)}) %all-reduce.48.cloned.1.call-update) | async-done | bytes 1048592 | tf_op jit(solution)/shard_map/psum | solution.py:64
  736.6 10.8 fusion.910
  755.4 8.9 fusion.386
  774.1 11.4 fusion.911
  793.2 9.0 fusion.383
  805.1 39.6 %all-reduce.50.cloned.1.call-done = bf16[512,1024]{1,0:T(8,128)(2,1)} async-done(((bf16[512,1024]{1,0:T(8,128)(2,1)}), bf16[512,1024]{1,0:T(8,128)(2,1)}) %all-reduce.50.cloned.1.call-update) | async-done | bytes 1048592 | tf_op jit(solution)/shard_map/psum | solution.py:64
  857.9 121.3 %all-reduce.68.cloned.1.call-done = (bf16[512,1024]{1,0:T(8,128)(2,1)}, bf16[512,1024]{1,0:T(8,128)(2,1)}, bf16[512,1024]{1,0:T(8,128)(2,1)}) async-done(((bf16[512,1024]{1,0:T(8,128)(2,1)}, bf16[512,1024]{1,0:T(8,128)(2,1)}, bf16[512,1024]{1,0:T(8,128)(2,1)}), (bf16[512,1024]{1,0:T(8,128)(2,1)}, bf16[512,1024]{1,0:T(8,128)(2,1)}, bf16[512,1024]{1,0:T(8,128)(2,1)})) %all-reduce.68.cloned.1.call-update) | async-done | bytes 3145744 | tf_op jit(solution)/shard_map/psum | solution.py:64
  988.8 14.6 multiply_reduce_fusion.2
  1014.5 8.1 fusion.101
  1041.3 24.7 %reduce-scatter.25.cloned.1.call-done = bf16[512,256]{0,1:T(8,128)(2,1)} async-done(((bf16[2048,256]{0,1:T(8,128)(2,1)}), bf16[512,256]{0,1:T(8,128)(2,1)}) %reduce-scatter.25.cloned.1.call-update) | async-done | bytes 262160 | tf_op jit(solution)/shard_map/reduce_scatter | solution.py:273
  1073.7 48.0 %all-reduce.52.cloned.1.call-done = bf16[512,1024]{1,0:T(8,128)(2,1)} async-done(((bf16[512,1024]{1,0:T(8,128)(2,1)}), bf16[512,1024]{1,0:T(8,128)(2,1)}) %all-reduce.52.cloned.1.call-update) | async-done | bytes 1048592 | tf_op jit(solution)/shard_map/psum | solution.py:64
  1136.3 51.3 %all-reduce.44.cloned.1.call-done = bf16[512,1024]{1,0:T(8,128)(2,1)} async-done(((bf16[512,1024]{1,0:T(8,128)(2,1)}), bf16[512,1024]{1,0:T(8,128)(2,1)}) %all-reduce.44.cloned.1.call-update) | async-done | bytes 1048592 | tf_op jit(solution)/shard_map/psum | solution.py:64
  1195.5 23.9 collective-permute-done.2
  1227.1 50.2 %all-reduce.54.cloned.1.call-done = bf16[512,1024]{1,0:T(8,128)(2,1)} async-done(((bf16[512,1024]{1,0:T(8,128)(2,1)}), bf16[512,1024]{1,0:T(8,128)(2,1)}) %all-reduce.54.cloned.1.call-update) | async-done | bytes 1048592 | tf_op jit(solution)/shard_map/psum | solution.py:64
  1294.2 47.9 %all-reduce.56.cloned.1.call-done = bf16[512,1024]{1,0:T(8,128)(2,1)} async-done(((bf16[512,1024]{1,0:T(8,128)(2,1)}), bf16[512,1024]{1,0:T(8,128)(2,1)}) %all-reduce.56.cloned.1.call-update) | async-done | bytes 1048592 | tf_op jit(solution)/shard_map/psum | solution.py:64
  1350.4 14.6 multiply_reduce_fusion.1
  1376.7 8.2 fusion.98
  1405.8 22.5 reduce-scatter.29.cloned.1.call-done
  1434.5 84.8 %all-reduce.66.cloned.1.call-done = (bf16[512,1024]{1,0:T(8,128)(2,1)}, bf16[512,1024]{1,0:T(8,128)(2,1)}) async-done(((bf16[512,1024]{1,0:T(8,128)(2,1)}, bf16[512,1024]{1,0:T(8,128)(2,1)}), (bf16[512,1024]{1,0:T(8,128)(2,1)}, bf16[512,1024]{1,0:T(8,128)(2,1)})) %all-reduce.66.cloned.1.call-update) | async-done | bytes 2097168 | tf_op jit(solution)/shard_map/psum | solution.py:64
  1542.2 16.0 collective-permute-done.3
  1567.7 11.5 fusion.914
  1581.4 8.8 fusion.398
  1622.2 55.0 %all-reduce.64.cloned.1.call-done = (bf16[512,1024]{1,0:T(8,128)(2,1)}, bf16[512,1024]{1,0:T(8,128)(2,1)}) async-done(((bf16[512,1024]{1,0:T(8,128)(2,1)}, bf16[512,1024]{1,0:T(8,128)(2,1)}), (bf16[512,1024]{1,0:T(8,128)(2,1)}, bf16[512,1024]{1,0:T(8,128)(2,1)})) %all-reduce.64.cloned.1.call-update) | async-done | bytes 2097168 | tf_op jit(solution)/shard_map/psum | solution.py:64
  1725.9 17.2 reduce-scatter.39.cloned.1.call-done
  1744.8 20.7 reduce-scatter.41.cloned.1.call-done
  1771.0 17.3 reduce-scatter.43.cloned.1.call-done
  1790.0 20.7 reduce-scatter.45.cloned.1.call-done
  1826.9 74.7 %all-reduce.62.cloned.1.call-done = (bf16[512,1024]{1,0:T(8,128)(2,1)}, bf16[512,1024]{1,0:T(8,128)(2,1)}) async-done(((bf16[512,1024]{1,0:T(8,128)(2,1)}, bf16[512,1024]{1,0:T(8,128)(2,1)}), (bf16[512,1024]{1,0:T(8,128)(2,1)}, bf16[512,1024]{1,0:T(8,128)(2,1)})) %all-reduce.62.cloned.1.call-update) | async-done | bytes 2097168 | tf_op jit(solution)/shard_map/psum | solution.py:64
  1909.2 14.8 multiply_reduce_fusion
  1935.4 7.9 fusion.95
  1958.3 7.7 fusion.419
  1971.6 8.3 add_convert_fusion
  2002.8 19.9 reduce-scatter.61.cloned.1.call-done
  2029.3 17.7 reduce-scatter.57.cloned.1.call-done
  2050.8 24.2 reduce-scatter.31.cloned.1.call-done
  2082.2 20.2 reduce-scatter.33.cloned.1.call-done
  2107.9 9.7 fusion.348
  2128.1 32.9 %reduce-scatter.63.cloned.1.call-done = bf16[256,1024]{1,0:T(8,128)(2,1)} async-done(((bf16[1024,1024]{1,0:T(8,128)(2,1)}), bf16[256,1024]{1,0:T(8,128)(2,1)}) %reduce-scatter.63.cloned.1.call-update) | async-done | bytes 524304 | tf_op jit(solution)/shard_map/reduce_scatter | solution.py:437
  2163.1 31.7 %reduce-scatter.65.cloned.1.call-done = bf16[256,1024]{1,0:T(8,128)(2,1)} async-done(((bf16[1024,1024]{1,0:T(8,128)(2,1)}), bf16[256,1024]{1,0:T(8,128)(2,1)}) %reduce-scatter.65.cloned.1.call-update) | async-done | bytes 524304 | tf_op jit(solution)/shard_map/reduce_scatter | solution.py:437
  2197.0 22.2 reduce-scatter.47.cloned.1.call-done
  2220.8 22.4 reduce-scatter.53.cloned.1.call-done
  2244.8 22.7 reduce-scatter.49.cloned.1.call-done
  2269.2 22.4 reduce-scatter.51.cloned.1.call-done
  2293.2 88.0 %all-reduce.60.cloned.1.call-done = (bf16[512,1024]{1,0:T(8,128)(2,1)}, bf16[512,1024]{1,0:T(8,128)(2,1)}) async-done(((bf16[512,1024]{1,0:T(8,128)(2,1)}, bf16[512,1024]{1,0:T(8,128)(2,1)}), (bf16[512,1024]{1,0:T(8,128)(2,1)}, bf16[512,1024]{1,0:T(8,128)(2,1)})) %all-reduce.60.cloned.1.call-update) | async-done | bytes 2097168 | tf_op jit(solution)/shard_map/psum | solution.py:64
  2387.8 11.5 all-reduce.6
  (1097 shorter events, 640.6 us)
Async XLA Ops:
  7.2 181.5 %copy-start = (bf16[1,1024,1024]{2,1,0:T(8,128)(2,1)S(1)}, bf16[1,1024,1024]{2,1,0:T(8,128)(2,1)}, u32[]{:S(2)}) copy-start(bf16[1,1024,1024]{2,1,0:T(8,128)(2,1)} %param.38) | copy-start | bytes 6291460
  7.2 24.4 %all-gather.16.cloned.1.call-start = ((), (), s32[]{:S(2)}) async-start(), calls=%async_computation.23 | async-start | bytes 1310720 | tf_op jit(solution)/shard_map/all_gather | solution.py:148
  12.0 38.5 %all-gather.14.cloned.1.call-start = ((), (), s32[]{:S(2)}) async-start(), calls=%async_computation.22 | async-start | bytes 1310720 | tf_op jit(solution)/shard_map/all_gather | solution.py:149
  14.6 54.2 %all-gather.18.cloned.1.call-start = ((), (), s32[]{:S(2)}) async-start(), calls=%async_computation.25 | async-start | bytes 1310720 | tf_op jit(solution)/shard_map/all_gather | solution.py:359
  15.3 108.1 %all-reduce.32.cloned.1.call-start = ((), (), s32[]{:S(2)}) async-start(), calls=%async_computation.24 | async-start | bytes 2097152 | tf_op jit(solution)/shard_map/psum | solution.py:64
  63.2 122.6 %all-reduce.34.cloned.1.call-start = ((), (), s32[]{:S(2)}) async-start(), calls=%async_computation.26 | async-start | bytes 2097152 | tf_op jit(solution)/shard_map/psum | solution.py:64
  134.5 115.3 %all-reduce.36.cloned.1.call-start = ((), (), s32[]{:S(2)}) async-start(), calls=%async_computation.27 | async-start | bytes 2097152 | tf_op jit(solution)/shard_map/psum | solution.py:64
  198.4 102.8 %all-gather.22.cloned.1.call-start = ((), (), s32[]{:S(2)}) async-start(), calls=%async_computation.29 | async-start | bytes 1310720 | tf_op jit(solution)/shard_map/all_gather | solution.py:148
  254.0 26.0 %collective-permute-start = (bf16[512,1024]{1,0:T(8,128)(2,1)S(1)}, bf16[512,1024]{1,0:T(8,128)(2,1)S(1)}, u32[]{:S(2)}, u32[]{:S(2)}) collective-permute-start(bf16[512,1024]{1,0:T(8,128)(2,1)S(1)} %get-tuple-element.98), channel_id=1, source_target_pairs={{0,16},{1,17},{2,18},{3,19},{4,20},{5,21},{6,22},{7,23},{8,24},{9,... | collective-permute-start | bytes 3145736 | tf_op jit(solution)/shard_map/ppermute | solution.py:19
  284.0 36.2 %all-gather.20.cloned.1.call-start = ((), (), s32[]{:S(2)}) async-start(), calls=%async_computation.28 | async-start | bytes 1310720 | tf_op jit(solution)/shard_map/all_gather | solution.py:149
  286.5 98.1 %all-reduce.38.cloned.1.call-start = ((), (), s32[]{:S(2)}) async-start(), calls=%async_computation.30 | async-start | bytes 2097152 | tf_op jit(solution)/shard_map/psum | solution.py:64
  332.7 114.8 %all-reduce.40.cloned.1.call-start = ((), (), s32[]{:S(2)}) async-start(), calls=%async_computation.31 | async-start | bytes 2097152 | tf_op jit(solution)/shard_map/psum | solution.py:64
  396.1 116.6 %all-reduce.42.cloned.1.call-start = ((), (), s32[]{:S(2)}) async-start(), calls=%async_computation.32 | async-start | bytes 2097152 | tf_op jit(solution)/shard_map/psum | solution.py:64
  461.4 107.6 %all-gather.36.cloned.1.call-start = ((), (), s32[]{:S(2)}) async-start(), calls=%async_computation.40 | async-start | bytes 1310720 | tf_op jit(solution)/shard_map/all_gather | solution.py:148
  517.5 26.3 %collective-permute-start.1 = (bf16[512,1024]{1,0:T(8,128)(2,1)}, bf16[512,1024]{1,0:T(8,128)(2,1)}, u32[]{:S(2)}, u32[]{:S(2)}) collective-permute-start(bf16[512,1024]{1,0:T(8,128)(2,1)} %get-tuple-element.94), channel_id=1, source_target_pairs={{0,16},{1,17},{2,18},{3,19},{4,20},{5,21},{6,22},{7,23},{8,24},{9,... | collective-permute-start | bytes 3145736 | tf_op jit(solution)/shard_map/ppermute | solution.py:19
  551.4 36.4 %all-gather.38.cloned.1.call-start = ((), (), s32[]{:S(2)}) async-start(), calls=%async_computation.41 | async-start | bytes 1310720 | tf_op jit(solution)/shard_map/all_gather | solution.py:149
  554.1 98.9 %all-reduce.46.cloned.1.call-start = ((), (), s32[]{:S(2)}) async-start(), calls=%async_computation.42 | async-start | bytes 2097152 | tf_op jit(solution)/shard_map/psum | solution.py:64
  601.1 115.1 %all-reduce.48.cloned.1.call-start = ((), (), s32[]{:S(2)}) async-start(), calls=%async_computation.43 | async-start | bytes 2097152 | tf_op jit(solution)/shard_map/psum | solution.py:64
  664.8 69.5 %all-gather.32.cloned.1.call-start = ((), (), s32[]{:S(2)}) async-start(), calls=%async_computation.37 | async-start | bytes 1310720 | tf_op jit(solution)/shard_map/all_gather | solution.py:148
  670.9 82.2 %all-gather.34.cloned.1.call-start = ((), (), s32[]{:S(2)}) async-start(), calls=%async_computation.38 | async-start | bytes 1310720 | tf_op jit(solution)/shard_map/all_gather | solution.py:149
  673.5 98.3 %all-gather.28.cloned.1.call-start = ((), (), s32[]{:S(2)}) async-start(), calls=%async_computation.35 | async-start | bytes 1310720 | tf_op jit(solution)/shard_map/all_gather | solution.py:148
  676.1 114.6 %all-gather.30.cloned.1.call-start = ((), (), s32[]{:S(2)}) async-start(), calls=%async_computation.36 | async-start | bytes 1310720 | tf_op jit(solution)/shard_map/all_gather | solution.py:149
  682.9 161.8 %all-reduce.50.cloned.1.call-start = ((), (), s32[]{:S(2)}) async-start(), calls=%async_computation.44 | async-start | bytes 2097152 | tf_op jit(solution)/shard_map/psum | solution.py:64
  718.6 129.8 %copy-start.208 = (f32[512]{0:T(512)}, f32[512]{0:T(512)S(1)}, u32[]{:S(2)}) copy-start(f32[512]{0:T(512)S(1)} %broadcast_multiply_fusion.18) | copy-start | bytes 6148
  729.3 249.9 %all-reduce.68.cloned.1.call-start = ((), (), s32[]{:S(2)}) async-start(), calls=%async_computation.75 | async-start | bytes 6291456 | tf_op jit(solution)/shard_map/psum | solution.py:64
  856.3 122.8 %copy-start.203 = (f32[512]{0:T(512)S(1)}, f32[512]{0:T(512)}, u32[]{:S(2)}) copy-start(f32[512]{0:T(512)} %copy-done.202) | copy-start | bytes 6148
  856.3 122.8 %copy-start.231 = (f32[512]{0:T(512)S(1)}, f32[512]{0:T(512)}, u32[]{:S(2)}) copy-start(f32[512]{0:T(512)} %copy-done.230) | copy-start | bytes 6148
  857.8 180.7 %reduce-scatter.23.cloned.1.call-start = ((), (), s32[]{:S(2)}) async-start(), calls=%async_computation.45 | async-start | bytes 1310720 | tf_op jit(solution)/shard_map/reduce_scatter | solution.py:270
  1014.5 51.5 %reduce-scatter.25.cloned.1.call-start = ((), (), s32[]{:S(2)}) async-start(), calls=%async_computation.46 | async-start | bytes 1310720 | tf_op jit(solution)/shard_map/reduce_scatter | solution.py:273
  1022.7 99.1 %all-reduce.52.cloned.1.call-start = ((), (), s32[]{:S(2)}) async-start(), calls=%async_computation.47 | async-start | bytes 2097152 | tf_op jit(solution)/shard_map/psum | solution.py:64
  1069.8 117.8 %all-reduce.44.cloned.1.call-start = ((), (), s32[]{:S(2)}) async-start(), calls=%async_computation.39 | async-start | bytes 2097152 | tf_op jit(solution)/shard_map/psum | solution.py:64
  1136.2 141.0 %all-reduce.54.cloned.1.call-start = ((), (), s32[]{:S(2)}) async-start(), calls=%async_computation.48 | async-start | bytes 2097152 | tf_op jit(solution)/shard_map/psum | solution.py:64
  1192.5 27.0 %collective-permute-start.2 = (bf16[512,1024]{1,0:T(8,128)(2,1)S(1)}, bf16[512,1024]{1,0:T(8,128)(2,1)S(1)}, u32[]{:S(2)}, u32[]{:S(2)}) collective-permute-start(bf16[512,1024]{1,0:T(8,128)(2,1)S(1)} %get-tuple-element.86), channel_id=1, source_target_pairs={{16,0},{17,1},{18,2},{19,3},{20,4},{21,5},{22,6},{23,7},{24,8},{25... | collective-permute-start | bytes 3145736 | tf_op jit(solution)/shard_map/ppermute | solution.py:19
  1226.8 115.2 %all-reduce.56.cloned.1.call-start = ((), (), s32[]{:S(2)}) async-start(), calls=%async_computation.49 | async-start | bytes 2097152 | tf_op jit(solution)/shard_map/psum | solution.py:64
  1290.7 112.3 %reduce-scatter.27.cloned.1.call-start = ((), (), s32[]{:S(2)}) async-start(), calls=%async_computation.50 | async-start | bytes 1310720 | tf_op jit(solution)/shard_map/reduce_scatter | solution.py:270
  1294.2 91.0 %copy-start.210 = (f32[512]{0:T(512)}, f32[512]{0:T(512)S(1)}, u32[]{:S(2)}) copy-start(f32[512]{0:T(512)S(1)} %broadcast_multiply_fusion.25) | copy-start | bytes 6148
  1376.1 52.2 %reduce-scatter.29.cloned.1.call-start = ((), (), s32[]{:S(2)}) async-start(), calls=%async_computation.51 | async-start | bytes 1310720 | tf_op jit(solution)/shard_map/reduce_scatter | solution.py:273
  1385.0 134.3 %all-reduce.66.cloned.1.call-start = ((), (), s32[]{:S(2)}) async-start(), calls=%async_computation.74 | async-start | bytes 4194304 | tf_op jit(solution)/shard_map/psum | solution.py:64
  1432.1 133.3 %all-gather.26.cloned.1.call-start = ((), (), s32[]{:S(2)}) async-start(), calls=%async_computation.34 | async-start | bytes 1310720 | tf_op jit(solution)/shard_map/all_gather | solution.py:148
  1531.0 48.1 %all-gather.24.cloned.1.call-start = ((), (), s32[]{:S(2)}) async-start(), calls=%async_computation.33 | async-start | bytes 1310720 | tf_op jit(solution)/shard_map/all_gather | solution.py:149
  1531.0 27.1 %collective-permute-start.3 = (bf16[512,1024]{1,0:T(8,128)(2,1)}, bf16[512,1024]{1,0:T(8,128)(2,1)}, u32[]{:S(2)}, u32[]{:S(2)}) collective-permute-start(bf16[512,1024]{1,0:T(8,128)(2,1)} %get-tuple-element.82), channel_id=1, source_target_pairs={{16,0},{17,1},{18,2},{19,3},{20,4},{21,5},{22,6},{23,7},{24,8},{25... | collective-permute-start | bytes 3145736 | tf_op jit(solution)/shard_map/ppermute | solution.py:19
  1534.9 142.4 %all-reduce.64.cloned.1.call-start = ((), (), s32[]{:S(2)}) async-start(), calls=%async_computation.73 | async-start | bytes 4194304 | tf_op jit(solution)/shard_map/psum | solution.py:64
  1537.5 143.3 %copy-start.225 = (f32[512]{0:T(512)}, f32[512]{0:T(512)S(1)}, u32[]{:S(2)}) copy-start(f32[512]{0:T(512)S(1)} %add_rsqrt_fusion.6) | copy-start | bytes 6148
  1591.6 120.9 %reduce-scatter.35.cloned.1.call-start = ((), (), s32[]{:S(2)}) async-start(), calls=%async_computation.54 | async-start | bytes 163840 | tf_op jit(solution)/shard_map/reduce_scatter | solution.py:240
  1601.1 119.3 %reduce-scatter.37.cloned.1.call-start = ((), (), s32[]{:S(2)}) async-start(), calls=%async_computation.55 | async-start | bytes 163840 | tf_op jit(solution)/shard_map/reduce_scatter | solution.py:246
  1607.4 135.6 %reduce-scatter.39.cloned.1.call-start = ((), (), s32[]{:S(2)}) async-start(), calls=%async_computation.56 | async-start | bytes 163840 | tf_op jit(solution)/shard_map/reduce_scatter | solution.py:240
  1615.7 149.9 %reduce-scatter.41.cloned.1.call-start = ((), (), s32[]{:S(2)}) async-start(), calls=%async_computation.57 | async-start | bytes 163840 | tf_op jit(solution)/shard_map/reduce_scatter | solution.py:246
  1622.2 166.1 %reduce-scatter.43.cloned.1.call-start = ((), (), s32[]{:S(2)}) async-start(), calls=%async_computation.58 | async-start | bytes 163840 | tf_op jit(solution)/shard_map/reduce_scatter | solution.py:240
  1698.4 112.3 %reduce-scatter.45.cloned.1.call-start = ((), (), s32[]{:S(2)}) async-start(), calls=%async_computation.59 | async-start | bytes 163840 | tf_op jit(solution)/shard_map/reduce_scatter | solution.py:246
  1709.7 191.8 %all-reduce.62.cloned.1.call-start = ((), (), s32[]{:S(2)}) async-start(), calls=%async_computation.72 | async-start | bytes 4194304 | tf_op jit(solution)/shard_map/psum | solution.py:64
  1712.5 277.7 %all-reduce.58.cloned.1.call-start = ((), (), s32[]{:S(2)}) async-start(), calls=%async_computation.60 | async-start | bytes 524288 | tf_op jit(solution)/shard_map/psum | solution.py:439
  1814.0 187.2 %reduce-scatter.55.cloned.1.call-start = ((), (), s32[]{:S(2)}) async-start(), calls=%async_computation.65 | async-start | bytes 655360 | tf_op jit(solution)/shard_map/reduce_scatter | solution.py:437
  1818.5 204.3 %reduce-scatter.61.cloned.1.call-start = ((), (), s32[]{:S(2)}) async-start(), calls=%async_computation.68 | async-start | bytes 655360 | tf_op jit(solution)/shard_map/reduce_scatter | solution.py:437
  1824.0 223.1 %reduce-scatter.57.cloned.1.call-start = ((), (), s32[]{:S(2)}) async-start(), calls=%async_computation.66 | async-start | bytes 655360 | tf_op jit(solution)/shard_map/reduce_scatter | solution.py:437
  1826.8 248.1 %reduce-scatter.31.cloned.1.call-start = ((), (), s32[]{:S(2)}) async-start(), calls=%async_computation.52 | async-start | bytes 1310720 | tf_op jit(solution)/shard_map/reduce_scatter | solution.py:270
  1935.4 167.0 %reduce-scatter.33.cloned.1.call-start = ((), (), s32[]{:S(2)}) async-start(), calls=%async_computation.53 | async-start | bytes 1310720 | tf_op jit(solution)/shard_map/reduce_scatter | solution.py:273
  1943.4 183.0 %reduce-scatter.59.cloned.1.call-start = ((), (), s32[]{:S(2)}) async-start(), calls=%async_computation.67 | async-start | bytes 655360 | tf_op jit(solution)/shard_map/reduce_scatter | solution.py:437
  1950.8 210.2 %reduce-scatter.63.cloned.1.call-start = ((), (), s32[]{:S(2)}) async-start(), calls=%async_computation.69 | async-start | bytes 2621440 | tf_op jit(solution)/shard_map/reduce_scatter | solution.py:437
  1958.2 236.6 %reduce-scatter.65.cloned.1.call-start = ((), (), s32[]{:S(2)}) async-start(), calls=%async_computation.70 | async-start | bytes 2621440 | tf_op jit(solution)/shard_map/reduce_scatter | solution.py:437
  1979.9 239.3 %reduce-scatter.47.cloned.1.call-start = ((), (), s32[]{:S(2)}) async-start(), calls=%async_computation.61 | async-start | bytes 655360 | tf_op jit(solution)/shard_map/reduce_scatter | solution.py:437
  2001.1 242.1 %reduce-scatter.53.cloned.1.call-start = ((), (), s32[]{:S(2)}) async-start(), calls=%async_computation.64 | async-start | bytes 655360 | tf_op jit(solution)/shard_map/reduce_scatter | solution.py:437
  2029.3 238.3 %reduce-scatter.49.cloned.1.call-start = ((), (), s32[]{:S(2)}) async-start(), calls=%async_computation.62 | async-start | bytes 655360 | tf_op jit(solution)/shard_map/reduce_scatter | solution.py:437
  2080.0 211.6 %reduce-scatter.51.cloned.1.call-start = ((), (), s32[]{:S(2)}) async-start(), calls=%async_computation.63 | async-start | bytes 655360 | tf_op jit(solution)/shard_map/reduce_scatter | solution.py:437
  2107.5 273.8 %all-reduce.60.cloned.1.call-start = ((), (), s32[]{:S(2)}) async-start(), calls=%async_computation.71 | async-start | bytes 4194304 | tf_op jit(solution)/shard_map/psum | solution.py:64
  (312 other events, 3413.6 us)
Sparse Core Ops, SparseCore 0:
  12.1 19.4 all-gather.15
  33.7 16.7 all-gather.13
  52.1 16.7 all-gather.17
  71.6 51.8 all-reduce.31
  134.6 51.1 all-reduce.33
  198.5 51.2 all-reduce.35
  284.1 17.0 all-gather.21
  303.4 16.7 all-gather.19
  332.8 51.7 all-reduce.37
  396.2 51.2 all-reduce.39
  461.5 51.1 all-reduce.41
  551.6 17.3 all-gather.35
  571.1 16.7 all-gather.37
  601.2 51.8 all-reduce.45
  664.9 51.2 all-reduce.47
  718.2 16.0 all-gather.31
  736.3 16.7 all-gather.33
  755.1 16.7 all-gather.27
  774.0 16.7 all-gather.29
  792.9 51.8 all-reduce.49
  857.9 121.1 all-reduce.67
  1014.6 23.8 reduce-scatter.22
  1041.0 24.8 reduce-scatter.24
  1069.9 51.7 all-reduce.51
  1136.3 51.2 all-reduce.43
  1227.0 50.2 all-reduce.53
  1290.8 51.1 all-reduce.55
  1376.2 24.5 reduce-scatter.26
  1403.3 24.9 reduce-scatter.28
  1432.2 87.0 all-reduce.65
  1531.1 15.7 all-gather.25
  1549.1 16.7 all-gather.23
  1591.7 85.4 all-reduce.63
  1679.8 18.5 reduce-scatter.34
  1700.8 19.5 reduce-scatter.36
  1723.4 19.5 reduce-scatter.38
  1745.9 19.5 reduce-scatter.40
  1768.7 19.5 reduce-scatter.42
  1791.1 19.5 reduce-scatter.44
  1814.5 87.0 all-reduce.61
  1905.5 69.5 all-reduce.57
  1977.7 20.9 reduce-scatter.54
  2001.1 21.6 reduce-scatter.60
  2025.4 21.6 reduce-scatter.56
  2050.0 24.8 reduce-scatter.30
  2077.5 24.8 reduce-scatter.32
  2104.8 21.6 reduce-scatter.58
  2129.6 31.3 reduce-scatter.62
  2163.4 31.4 reduce-scatter.64
  2197.5 21.6 reduce-scatter.46
  2221.5 21.6 reduce-scatter.52
  2245.9 21.6 reduce-scatter.48
  2269.9 21.6 reduce-scatter.50
  2294.1 87.0 all-reduce.59
where the time goes:
time: 2430 us; the launch traced here: 2420 us
  waiting for transfers between devices  1580 us (65%)
  matrix products  517 us (21%)
  other arithmetic  180 us (7%)
  local copies, waits for them, and re-layouts  90.8 us (4%)
    psum x18, waiting for transfers between devices, head_total(): lax.psum(partial_sum.astype(jnp.bfloat16), 'head').astype(jnp.float32)  1050 us
    reduce_scatter x10, waiting for transfers between devices, per_device(): lax.psum_scatter(as_sent(totals), 'frame', scatter_dimension=0, tiled=True)  197 us
    dot_general x54, matrix products, matmul(): return jnp.dot(left_side, right_side, preferred_element_type=jnp.float32)  117 us
    sub x12, matrix products, softmax_rows(): exponent = jnp.exp(logits - jnp.max(logits, axis=-1, keepdims=True))  87.1 us
    ppermute x4, waiting for transfers between devices, passed_along(): return lax.ppermute(x, axis, pairs)  84.4 us
    dot_general x30, matrix products, matmul_tn(): lax.dot_general(left_side, right_side, (((0,), (0,)), ((), ())), preferre...  77.5 us
    reduce_scatter x3, waiting for transfers between devices, backward(): lax.psum_scatter(grad_v_all.astype(jnp.bfloat16), 'frame', scatter_dimens...  67.4 us
    dot_general x12, matrix products, attend(): jnp.einsum('hqk,khd->qhd', weights_low, split_heads(value_rows), preferre...  64.8 us
  transfers between devices with their start and end apart: 58, of which 52 were waited for; matrix products, arithmetic and copies ran while one was open for 20% of the time, Pallas kernels for 0%

commit v1 on v0

v1 whole, which is shorter than its diff:
```python
import functools

import jax
import jax.numpy as jnp
from jax import lax
from jax.experimental import pallas as pl
from jax.experimental.pallas import tpu as pltpu
from jax.sharding import PartitionSpec as P

HEAD = 64
TEXT = 64
ITEMS = 4

masked_score = -1e30
inv_sqrt_two = 0.7071067811865476
inv_sqrt_tau = 0.3989422804014327
MESH_IDS = pl.DeviceIdType.MESH
LAG = 2
VMEM_BYTES = 56 * 1024 * 1024
EPS = 1e-05


def chunking(rows):
    return max(1, min(16, rows // 16))


def norm_parts(v):
    average = jnp.mean(v, axis=-1, keepdims=True)
    centered = v - average
    inverse = lax.rsqrt(jnp.mean(centered * centered, axis=-1, keepdims=True) + EPS)
    return centered * inverse, inverse


def line_sum(rows, pieces, send, recv, across, held, sems, partial_rows, finish_rows):
    send_in, recv_in, send_across, recv_across, send_out, recv_out = sems
    place = lax.axis_index("head")
    step = rows // pieces
    is_end = (place == 0) | (place == 3)
    in_middle = jnp.logical_not(is_end)
    inner = jnp.where(place == 0, 1, 2)
    outer = jnp.where(place == 1, 0, 3)
    peer = 3 - place

    def spot(piece):
        return pl.ds(pl.multiple_of(piece * step, step), step)

    def inwards(piece):
        return pltpu.make_async_remote_copy(
            src_ref=send.at[spot(piece)],
            dst_ref=recv.at[spot(piece)],
            send_sem=send_in.at[piece],
            recv_sem=recv_in.at[piece],
            device_id={"head": inner},
            device_id_type=MESH_IDS,
        )

    def crossing(piece):
        return pltpu.make_async_remote_copy(
            src_ref=send.at[spot(piece)],
            dst_ref=across.at[spot(piece)],
            send_sem=send_across.at[piece],
            recv_sem=recv_across.at[piece],
            device_id={"head": peer},
            device_id_type=MESH_IDS,
        )

    def outwards(piece):
        return pltpu.make_async_remote_copy(
            src_ref=held.at[spot(piece)],
            dst_ref=held.at[spot(piece)],
            send_sem=send_out.at[piece],
            recv_sem=recv_out.at[piece],
            device_id={"head": outer},
            device_id_type=MESH_IDS,
        )

    barrier = pltpu.get_barrier_semaphore()

    @pl.when(is_end)
    def _():
        pl.semaphore_signal(barrier, 1, device_id={"head": inner}, device_id_type=MESH_IDS)
        pl.semaphore_wait(barrier, 1)

    @pl.when(in_middle)
    def _():
        pl.semaphore_signal(barrier, 1, device_id={"head": outer}, device_id_type=MESH_IDS)
        pl.semaphore_signal(barrier, 1, device_id={"head": peer}, device_id_type=MESH_IDS)
        pl.semaphore_wait(barrier, 2)

    @pl.when(is_end)
    def _():
        def give(piece, carry):
            send[spot(piece), :] = partial_rows(spot(piece)).astype(jnp.bfloat16)
            inwards(piece).start()
            return carry

        lax.fori_loop(0, pieces, give, 0)

        def take(piece, carry):
            outwards(piece).wait_recv()
            finish_rows(spot(piece), piece)
            return carry

        lax.fori_loop(0, pieces, take, 0)

        def drain(piece, carry):
            inwards(piece).wait_send()
            return carry

        lax.fori_loop(0, pieces, drain, 0)

    @pl.when(in_middle)
    def _():
        def add(piece):
            part = partial_rows(spot(piece))
            inwards(piece).wait_recv()
            send[spot(piece), :] = (part + recv[spot(piece), :].astype(jnp.float32)).astype(jnp.bfloat16)
            crossing(piece).start()

        def settle(piece):
            crossing(piece).wait_recv()
            held[spot(piece), :] = (
                send[spot(piece), :].astype(jnp.float32) + across[spot(piece), :].astype(jnp.float32)
            ).astype(jnp.bfloat16)
            outwards(piece).start()
            finish_rows(spot(piece), piece)

        lag = min(LAG, pieces)

        def both(t, carry):
            @pl.when(t < pieces)
            def _():
                add(t)

            @pl.when(t >= lag)
            def _():
                settle(t - lag)

            return carry

        lax.fori_loop(0, pieces + lag, both, 0)

        def drain(piece, carry):
            crossing(piece).wait_send()
            outwards(piece).wait_send()
            return carry

        lax.fori_loop(0, pieces, drain, 0)


def product_rows(left, weight, transposed):
    def rows_of(where_rows):
        contract = ((1,), (1,)) if transposed else ((1,), (0,))
        return lax.dot_general(
            left[where_rows, :], weight[...], (contract, ((), ())), preferred_element_type=jnp.float32
        )

    return rows_of


def forward_sum_kernel(pieces, normed, flipped, rounded, left, weight, base, gain, shift, *rest):
    if normed:
        out, out_normed, *rest = rest
        if rounded:
            out_low, *rest = rest
    else:
        out, *rest = rest
    if flipped:
        turned, *rest = rest
        turned[...] = left[...].T
        left = turned
    send, recv, across, held, *sems = rest

    def finish_rows(where_rows, slot):
        value = base[where_rows, :].astype(jnp.float32) + held[where_rows, :].astype(jnp.float32)
        out[where_rows, :] = value
        if rounded:
            low = value.astype(jnp.bfloat16)
            out_low[where_rows, :] = low
            value = low.astype(jnp.float32)
        if normed:
            standard, _ = norm_parts(value)
            out_normed[where_rows, :] = (standard * gain[...] + shift[...]).astype(jnp.bfloat16)

    line_sum(left.shape[0], pieces, send, recv, across, held, sems, product_rows(left, weight, False), finish_rows)


def sum_scratch(rows, width, pieces):
    return [pltpu.VMEM((rows, width), jnp.bfloat16)] * 4 + [pltpu.SemaphoreType.DMA((pieces,))] * 6


def turned_scratch(left, flipped):
    return [pltpu.VMEM(left.shape[::-1], jnp.bfloat16)] if flipped else []


def forward_sum(left, weight, base, gain, shift, normed, flipped, rounded, collective_id):
    rows, width = base.shape
    pieces = chunking(rows)
    outs = [jax.ShapeDtypeStruct((rows, width), jnp.float32)]
    outs += [jax.ShapeDtypeStruct((rows, width), jnp.bfloat16)] * (normed + rounded)
    whole = pl.BlockSpec(memory_space=pltpu.VMEM)
    result = pl.pallas_call(
        functools.partial(forward_sum_kernel, pieces, normed, flipped, rounded),
        out_shape=outs,
        in_specs=[whole] * 5,
        out_specs=[whole] * len(outs),
        scratch_shapes=turned_scratch(left, flipped) + sum_scratch(rows, width, pieces),
        compiler_params=pltpu.CompilerParams(
            collective_id=collective_id, has_side_effects=True, vmem_limit_bytes=VMEM_BYTES
        ),
    )(left, weight, base, gain[None], shift[None])
    return result if normed else result[0]


def backward_sum_kernel(
    pieces, flipped, weight_flipped, left, weight, value, gain, upstream, out, out_low, gain_grad, shift_grad, *rest
):
    if flipped:
        turned, *rest = rest
        turned[...] = left[...].T
        left = turned
    send, recv, across, held, gain_parts, shift_parts, *sems = rest

    def finish_rows(where_rows, slot):
        grad = held[where_rows, :].astype(jnp.float32)
        standard, inverse = norm_parts(value[where_rows, :].astype(jnp.float32))
        scaled = grad * gain[...]
        through = inverse * (
            scaled
            - jnp.mean(scaled, axis=-1, keepdims=True)
            - standard * jnp.mean(scaled * standard, axis=-1, keepdims=True)
        )
        total = through + upstream[where_rows, :].astype(jnp.float32)
        out[where_rows, :] = total
        out_low[where_rows, :] = total.astype(jnp.bfloat16)
        gain_parts[slot] = jnp.sum(grad * standard, axis=0, keepdims=True)
        shift_parts[slot] = jnp.sum(grad, axis=0, keepdims=True)

    line_sum(left.shape[0], pieces, send, recv, across, held, sems, product_rows(left, weight, weight_flipped), finish_rows)
    gain_grad[...] = jnp.sum(gain_parts[...], axis=0)
    shift_grad[...] = jnp.sum(shift_parts[...], axis=0)


def backward_sum(left, weight, value, gain, upstream, flipped, weight_flipped, collective_id):
    rows, width = value.shape
    pieces = chunking(rows)
    whole = pl.BlockSpec(memory_space=pltpu.VMEM)
    vector = jax.ShapeDtypeStruct((1, width), jnp.float32)
    scratch = sum_scratch(rows, width, pieces)
    scratch[4:4] = [pltpu.VMEM((pieces, 1, width), jnp.float32)] * 2
    return pl.pallas_call(
        functools.partial(backward_sum_kernel, pieces, flipped, weight_flipped),
        out_shape=[
            jax.ShapeDtypeStruct((rows, width), jnp.float32),
            jax.ShapeDtypeStruct((rows, width), jnp.bfloat16),
            vector,
            vector,
        ],
        in_specs=[whole] * 5,
        out_specs=[whole] * 4,
        scratch_shapes=turned_scratch(left, flipped) + scratch,
        compiler_params=pltpu.CompilerParams(
            collective_id=collective_id, has_side_effects=True, vmem_limit_bytes=VMEM_BYTES
        ),
    )(left, weight, value, gain[None], upstream)


def block_of(rows):
    return 256 if rows % 256 == 0 else rows


def nt_product(left, right):
    return lax.dot_general(left, right, (((1,), (1,)), ((), ())), preferred_element_type=jnp.float32)


def plain_product(left, right):
    return jnp.dot(left, right, preferred_element_type=jnp.float32)


def greet_frames(frames):
    me = lax.axis_index("frame")
    barrier = pltpu.get_barrier_semaphore()
    for by in range(1, frames):
        pl.semaphore_signal(
            barrier, 1, device_id={"frame": lax.rem(me + by, frames)}, device_id_type=MESH_IDS
        )
    pl.semaphore_wait(barrier, frames - 1)


def masked_scores(keys, query_t, begins, start):
    reach, block = keys.shape[0], query_t.shape[1]
    scores = plain_product(keys, query_t)
    key_pos = lax.broadcasted_iota(jnp.int32, (reach, 1), 0)
    query_pos = start + lax.broadcasted_iota(jnp.int32, (1, block), 1)
    allowed = (key_pos <= query_pos) & (key_pos >= begins)
    return jnp.where(allowed, scores * HEAD ** (-0.5), masked_score)


def lane_span(index, width):
    return pl.ds(pl.multiple_of(index * width, width), width)


def exchange(frames, source, landing, send_sems, recv_sems):
    me = lax.axis_index("frame")

    def copy(by):
        other = lax.rem(me + by, frames)
        return pltpu.make_async_remote_copy(
            src_ref=source(other),
            dst_ref=landing(me),
            send_sem=send_sems.at[by - 1],
            recv_sem=recv_sems.at[by - 1],
            device_id={"frame": other},
            device_id_type=MESH_IDS,
        )

    return copy


def attention_kernel(frames, normed, weight, begins, heads_t, out, own, keys, mixed_t, *sems):
    send_heads, recv_heads, send_out, recv_out = sems
    me = lax.axis_index("frame")
    rows = normed.shape[0]
    total_rows = rows * frames
    block = block_of(rows)
    width = 3 * HEAD
    greet_frames(frames)
    to_heads = exchange(
        frames,
        lambda g: own.at[g],
        lambda f: heads_t.at[:, lane_span(f, rows)],
        send_heads,
        recv_heads,
    )
    for by in (2, 3, 1, 0):
        other = lax.rem(me + by, frames)
        piece = nt_product(weight[pl.ds(pl.multiple_of(other * width, width), width), :], normed[...])
        if by:
            own[other] = piece.astype(jnp.bfloat16)
            to_heads(by).start()
        else:
            heads_t[:, lane_span(me, rows)] = piece.astype(jnp.bfloat16)
    for by in (1, 2, 3):
        to_heads(by).wait()
    keys[...] = heads_t[HEAD : 2 * HEAD, :].T
    to_frames = exchange(
        frames,
        lambda g: mixed_t.at[g],
        lambda f: out.at[pl.ds(pl.multiple_of(f * HEAD, HEAD), HEAD), :],
        send_out,
        recv_out,
    )
    for target in range(frames):
        for start in range(target * rows, (target + 1) * rows, block):
            reach = start + block
            scores = masked_scores(keys[:reach, :], heads_t[:HEAD, start:reach], begins[:, start:reach], start)
            e = jnp.exp(scores - jnp.max(scores, axis=0, keepdims=True))
            total = jnp.sum(e, axis=0, keepdims=True)
            mixed = plain_product(heads_t[2 * HEAD :, :reach], e.astype(jnp.bfloat16))
            at = start - target * rows
            mixed_t[target, :, at : at + block] = (mixed * (1.0 / total)).astype(jnp.bfloat16)

        for by in range(1, frames):

            @pl.when(lax.rem(me + by, frames) == target)
            def _():
                to_frames(by).start()

    out[pl.ds(pl.multiple_of(me * HEAD, HEAD), HEAD), :] = mixed_t[me]
    for by in (1, 2, 3):
        to_frames(by).wait()


def attention(normed, weight, begins, collective_id):
    rows = normed.shape[0]
    frames = lax.axis_size("frame")
    whole = pl.BlockSpec(memory_space=pltpu.VMEM)
    dma = pltpu.SemaphoreType.DMA((frames - 1,))
    return pl.pallas_call(
        functools.partial(attention_kernel, frames),
        out_shape=[
            jax.ShapeDtypeStruct((3 * HEAD, rows * frames), jnp.bfloat16),
            jax.ShapeDtypeStruct((frames * HEAD, rows), jnp.bfloat16),
        ],
        in_specs=[whole] * 3,
        out_specs=[whole] * 2,
        scratch_shapes=[
            pltpu.VMEM((frames, 3 * HEAD, rows), jnp.bfloat16),
            pltpu.VMEM((rows * frames, HEAD), jnp.bfloat16),
            pltpu.VMEM((frames, HEAD, rows), jnp.bfloat16),
            dma,
            dma,
            dma,
            dma,
        ],
        compiler_params=pltpu.CompilerParams(
            collective_id=collective_id, has_side_effects=True, vmem_limit_bytes=VMEM_BYTES
        ),
    )(normed, weight, begins)


def attention_back_kernel(
    frames, heads_t, grad_low, weight, begins, out, own, grad_t, columns, key_sum, value_sum, grads_t, *sems
):
    send_heads, recv_heads, send_out, recv_out = sems
    me = lax.axis_index("frame")
    rows = grad_low.shape[0]
    block = block_of(rows)
    scale = HEAD ** (-0.5)
    width = 3 * HEAD
    greet_frames(frames)
    to_heads = exchange(
        frames,
        lambda g: own.at[g],
        lambda f: grad_t.at[:, lane_span(f, rows)],
        send_heads,
        recv_heads,
    )
    for by in (2, 3, 1, 0):
        other = lax.rem(me + by, frames)
        piece = nt_product(weight[pl.ds(pl.multiple_of(other * HEAD, HEAD), HEAD), :], grad_low[...])
        if by:
            own[other] = piece.astype(jnp.bfloat16)
            to_heads(by).start()
        else:
            grad_t[:, lane_span(me, rows)] = piece.astype(jnp.bfloat16)
    key_sum[...] = jnp.zeros_like(key_sum)
    value_sum[...] = jnp.zeros_like(value_sum)
    for part in range(3):
        columns[part] = heads_t[part * HEAD : (part + 1) * HEAD, :].T
    for by in (1, 2, 3):
        to_heads(by).wait()
    columns[3] = grad_t[...].T
    to_frames = exchange(
        frames,
        lambda g: grads_t.at[g],
        lambda f: out.at[pl.ds(pl.multiple_of(f * width, width), width), :],
        send_out,
        recv_out,
    )
    for target in reversed(range(frames)):
        for start in reversed(range(target * rows, (target + 1) * rows, block)):
            reach = start + block
            scores = masked_scores(
                columns[1, :reach, :], heads_t[:HEAD, start:reach], begins[:, start:reach], start
            )
            e = jnp.exp(scores - jnp.max(scores, axis=0, keepdims=True))
            p = e * (1.0 / jnp.sum(e, axis=0, keepdims=True))
            slope = plain_product(columns[2, :reach, :], grad_t[:, start:reach])
            weighted = p * slope
            ds = (weighted - p * jnp.sum(weighted, axis=0, keepdims=True)).astype(jnp.bfloat16)
            value_sum[:reach, :] += plain_product(p.astype(jnp.bfloat16), columns[3, start:reach, :])
            key_sum[:reach, :] += plain_product(ds, columns[0, start:reach, :])
            at = start - target * rows
            here = slice(at, at + block)
            grads_t[target, :HEAD, here] = (
                plain_product(heads_t[HEAD : 2 * HEAD, :reach], ds) * scale
            ).astype(jnp.bfloat16)
            grads_t[target, HEAD : 2 * HEAD, here] = (key_sum[start:reach, :] * scale).T.astype(jnp.bfloat16)
            grads_t[target, 2 * HEAD :, here] = value_sum[start:reach, :].T.astype(jnp.bfloat16)

        for by in range(1, frames):

            @pl.when(lax.rem(me + by, frames) == target)
            def _():
                to_frames(by).start()

    out[pl.ds(pl.multiple_of(me * width, width), width), :] = grads_t[me]
    for by in (1, 2, 3):
        to_frames(by).wait()


def attention_back(heads_t, grad_low, weight, begins, collective_id):
    rows = grad_low.shape[0]
    frames = lax.axis_size("frame")
    whole = pl.BlockSpec(memory_space=pltpu.VMEM)
    dma = pltpu.SemaphoreType.DMA((frames - 1,))
    total_rows = rows * frames
    return pl.pallas_call(
        functools.partial(attention_back_kernel, frames),
        out_shape=jax.ShapeDtypeStruct((frames * 3 * HEAD, rows), jnp.bfloat16),
        in_specs=[whole] * 4,
        out_specs=whole,
        scratch_shapes=[
            pltpu.VMEM((frames, HEAD, rows), jnp.bfloat16),
            pltpu.VMEM((HEAD, total_rows), jnp.bfloat16),
            pltpu.VMEM((4, total_rows, HEAD), jnp.bfloat16),
            pltpu.VMEM((total_rows, HEAD), jnp.float32),
            pltpu.VMEM((total_rows, HEAD), jnp.float32),
            pltpu.VMEM((frames, 3 * HEAD, rows), jnp.bfloat16),
            dma,
            dma,
            dma,
            dma,
        ],
        compiler_params=pltpu.CompilerParams(
            collective_id=collective_id, has_side_effects=True, vmem_limit_bytes=VMEM_BYTES
        ),
    )(heads_t, grad_low, weight, begins)


def matmul(left_side, right_side):
    return jnp.dot(left_side, right_side, preferred_element_type=jnp.float32)


def matmul_tn(left_side, right_side):
    return lax.dot_general(
        left_side, right_side, (((0,), (0,)), ((), ())), preferred_element_type=jnp.float32
    )


def matmul_nt(left_side, right_side):
    return lax.dot_general(
        left_side, right_side, (((1,), (1,)), ((), ())), preferred_element_type=jnp.float32
    )


def layer_norm(signal, gain_vec, shift_vec):
    average = jnp.mean(signal, axis=-1, keepdims=True)
    centered = signal - average
    variance = jnp.mean(centered * centered, axis=-1, keepdims=True)
    return centered * lax.rsqrt(variance + 1e-05) * gain_vec + shift_vec


def norm_back(signal, gain_vec, upstream):
    average = jnp.mean(signal, axis=-1, keepdims=True)
    centered = signal - average
    inverse = lax.rsqrt(jnp.mean(centered * centered, axis=-1, keepdims=True) + 1e-05)
    standard = centered * inverse
    scaled = upstream * gain_vec
    through = inverse * (
        scaled
        - jnp.mean(scaled, axis=-1, keepdims=True)
        - standard * jnp.mean(scaled * standard, axis=-1, keepdims=True)
    )
    return (through, jnp.sum(upstream * standard, axis=0), jnp.sum(upstream, axis=0))


def head_total(partial_sum):
    return lax.psum(partial_sum.astype(jnp.bfloat16), "head").astype(jnp.float32)


def swapped(x):
    return lax.ppermute(x, "section", [(0, 1), (1, 0)])


def across_frames(x, bit):
    return lax.ppermute(x, "frame", [(i, i ^ bit) for i in range(lax.axis_size("frame"))])


def split_heads(matrix):
    return matrix.reshape(matrix.shape[0], matrix.shape[1] // HEAD, HEAD)


def softmax_rows(query, key_rows, allowed):
    logits = jnp.einsum(
        "qhd,khd->hqk",
        split_heads(query),
        split_heads(key_rows),
        preferred_element_type=jnp.float32,
    ) * HEAD ** (-0.5)
    logits = jnp.where(allowed[None], logits, masked_score)
    exponent = jnp.exp(logits - jnp.max(logits, axis=-1, keepdims=True))
    return exponent / jnp.sum(exponent, axis=-1, keepdims=True)


def attend(query, key_rows, value_rows, allowed):
    weights_low = softmax_rows(query, key_rows, allowed).astype(jnp.bfloat16)
    result = jnp.einsum(
        "hqk,khd->qhd", weights_low, split_heads(value_rows), preferred_element_type=jnp.float32
    )
    return result.reshape(query.shape).astype(jnp.bfloat16)


def attend_back(query, key_rows, value_rows, allowed, grad_out):
    probabilities = softmax_rows(query, key_rows, allowed)
    weights_low = probabilities.astype(jnp.bfloat16)
    grad_heads = split_heads(grad_out)
    grad_prob = jnp.einsum(
        "qhd,khd->hqk", grad_heads, split_heads(value_rows), preferred_element_type=jnp.float32
    )
    centre = jnp.sum(probabilities * grad_prob, axis=-1, keepdims=True)
    grad_logit = (probabilities * (grad_prob - centre)).astype(jnp.bfloat16)
    scale = HEAD ** (-0.5)
    grad_query = (
        jnp.einsum(
            "hqk,khd->qhd", grad_logit, split_heads(key_rows), preferred_element_type=jnp.float32
        )
        * scale
    )
    grad_keys = (
        jnp.einsum(
            "hqk,qhd->khd", grad_logit, split_heads(query), preferred_element_type=jnp.float32
        )
        * scale
    )
    grad_values = jnp.einsum(
        "hqk,qhd->khd", weights_low, grad_heads, preferred_element_type=jnp.float32
    )
    return (
        grad_query.reshape(query.shape),
        grad_keys.reshape(key_rows.shape),
        grad_values.reshape(value_rows.shape),
    )


def add_and_norm(left, weight, base, gain, shift, normed, flipped, rounded, collective_id):
    if lax.axis_size("head") == 4:
        return forward_sum(left, weight, base, gain, shift, normed, flipped, rounded, collective_id)
    part = matmul_tn(left, weight) if flipped else matmul(left, weight)
    value = base.astype(jnp.float32) + head_total(part)
    if not normed:
        return value
    if not rounded:
        return value, layer_norm(value, gain, shift).astype(jnp.bfloat16)
    low = value.astype(jnp.bfloat16)
    return value, layer_norm(low.astype(jnp.float32), gain, shift).astype(jnp.bfloat16), low


def norm_and_back(left, weight, value, gain, upstream, flipped, weight_flipped, collective_id):
    if lax.axis_size("head") == 4:
        return backward_sum(
            left, weight, value, gain, upstream, flipped, weight_flipped, collective_id
        )
    left = left.T if flipped else left
    part = matmul_nt(left, weight) if weight_flipped else matmul(left, weight)
    through, gain_grad, shift_grad = norm_back(value.astype(jnp.float32), gain, head_total(part))
    through = through + upstream
    return through, through.astype(jnp.bfloat16), gain_grad[None], shift_grad[None]


def self_attention(normed, weight, masks):
    frames = lax.axis_size("frame")
    heads = weight.shape[0] // (3 * HEAD)
    if frames == heads:
        heads_t, attended_t = attention(normed, weight, masks["begins"], 1)
        return attended_t, heads_t
    rows = normed.shape[0]
    packed = matmul_nt(normed, weight).astype(jnp.bfloat16).reshape(rows, heads, 3, HEAD)
    query, keys, values = (packed[:, :, i].reshape(rows, heads * HEAD) for i in range(3))
    all_keys = lax.all_gather(keys, "frame", axis=0, tiled=True)
    all_values = lax.all_gather(values, "frame", axis=0, tiled=True)
    attended = attend(query, all_keys, all_values, masks["own"])
    return attended.T, (query, all_keys, all_values)


def self_attention_back(kept, grad_low, output_weight, masks):
    frames = lax.axis_size("frame")
    columns = output_weight.shape[0]
    heads = columns // HEAD
    if frames == heads:
        return attention_back(kept, grad_low, output_weight, masks["begins"], 2)
    query, keys, values = kept
    rows = query.shape[0]
    grad_out = matmul_nt(grad_low, output_weight).astype(jnp.bfloat16)
    grad_q, grad_k_all, grad_v_all = attend_back(query, keys, values, masks["own"], grad_out)
    grad_k, grad_v = (
        lax.psum_scatter(g.astype(jnp.bfloat16), "frame", scatter_dimension=0, tiled=True)
        for g in (grad_k_all, grad_v_all)
    )
    packed = jnp.stack(
        [g.reshape(rows, heads, HEAD) for g in (grad_q.astype(jnp.bfloat16), grad_k, grad_v)], axis=2
    )
    return packed.reshape(rows, heads * 3 * HEAD).T


def forward(entering, normed, vectors, next_vectors, weights, cross_keys, cross_values, masks):
    second_gain, second_shift, third_gain, third_shift = vectors[2:]
    heads_weight, output_weight, cross_query, cross_output, expand_weight, reduce_weight = weights
    attended_t, heads_kept = self_attention(normed, heads_weight, masks)
    middle, second_normed = add_and_norm(
        attended_t, output_weight, entering, second_gain, second_shift, True, True, False, 3
    )
    cross_queries = matmul(second_normed, cross_query).astype(jnp.bfloat16)
    cross_att = attend(cross_queries, cross_keys, cross_values, masks["cross"])
    latter, third_normed = add_and_norm(
        cross_att, cross_output, middle, third_gain, third_shift, True, False, False, 4
    )
    hidden_pre = matmul(third_normed, expand_weight)
    hidden_act = jax.nn.gelu(hidden_pre, approximate=False).astype(jnp.bfloat16)
    saved = (
        entering,
        normed,
        heads_kept,
        attended_t,
        middle,
        second_normed,
        cross_queries,
        cross_att,
        latter,
        third_normed,
        hidden_pre,
        hidden_act,
    )
    if next_vectors is None:
        result = add_and_norm(
            hidden_act, reduce_weight, latter, third_gain, third_shift, False, False, False, 5
        )
        return result, None, None, saved
    result, next_normed, result_low = add_and_norm(
        hidden_act, reduce_weight, latter, next_vectors[0], next_vectors[1], True, False, True, 6
    )
    return result, next_normed, result_low, saved


def frame_share(grad, axis):
    frames = lax.axis_size("frame")
    if frames != 4:
        return lax.psum_scatter(
            grad.astype(jnp.bfloat16), "frame", scatter_dimension=axis, tiled=True
        )
    me = lax.axis_index("frame")
    side, core = me // 2, me % 2
    share = grad.shape[axis] // 4

    def of_core(which):
        pieces = [
            lax.dynamic_slice_in_dim(grad, (2 * s + which) * share, share, axis) for s in range(2)
        ]
        return jnp.stack(pieces)

    mine = of_core(core).astype(jnp.float32)
    mine = mine + across_frames(of_core(1 - core).astype(jnp.bfloat16), 1).astype(jnp.float32)
    mine = mine.astype(jnp.bfloat16)
    kept = lax.dynamic_index_in_dim(mine, side, 0, keepdims=False).astype(jnp.float32)
    given = lax.dynamic_index_in_dim(mine, 1 - side, 0, keepdims=False)
    return (kept + across_frames(given, 2).astype(jnp.float32)).astype(jnp.bfloat16)


def backward(saved, upstream, grad_out, vectors, weights, cross_keys, cross_values, masks):
    first_gain, _, second_gain, _, third_gain, _ = vectors
    heads_weight, output_weight, cross_query, cross_output, expand_weight, reduce_weight = weights
    (
        entering,
        normed,
        heads_kept,
        attended_t,
        middle,
        second_normed,
        cross_queries,
        cross_att,
        latter,
        third_normed,
        hidden_pre,
        hidden_act,
    ) = saved
    grad_act = matmul_nt(grad_out, reduce_weight)
    slope = (
        0.5 * (1.0 + lax.erf(hidden_pre * inv_sqrt_two))
        + hidden_pre * jnp.exp(-0.5 * hidden_pre * hidden_pre) * inv_sqrt_tau
    )
    grad_pre = (grad_act * slope).astype(jnp.bfloat16)
    first_id = 7 if upstream.dtype == jnp.float32 else 10
    grad_latter, grad_cross, grad_third_gain, grad_third_shift = norm_and_back(
        grad_pre, expand_weight, latter, third_gain, upstream, False, True, first_id
    )
    grad_reduce = frame_share(matmul_tn(hidden_act, grad_out), 0)
    grad_expand = frame_share(matmul_tn(third_normed, grad_pre), 0)
    grad_cross_att = matmul_nt(grad_cross, cross_output).astype(jnp.bfloat16)
    grad_cq, grad_ck, grad_cv = attend_back(
        cross_queries, cross_keys, cross_values, masks["cross"], grad_cross_att
    )
    grad_text_rows = jnp.concatenate([grad_ck, grad_cv], axis=1)
    grad_text_rows = frame_share(grad_text_rows.reshape(ITEMS, TEXT, -1), 1)
    grad_cquery = grad_cq.astype(jnp.bfloat16)
    grad_middle, grad_self, grad_second_gain, grad_second_shift = norm_and_back(
        grad_cquery, cross_query, middle, second_gain, grad_latter, False, True, 8
    )
    grad_cross_output = frame_share(matmul_tn(cross_att, grad_cross), 0)
    grad_cross_query = frame_share(matmul_tn(second_normed, grad_cquery), 0)
    grad_heads_t = self_attention_back(heads_kept, grad_self, output_weight, masks)
    grad_output = frame_share(matmul(attended_t, grad_self), 0)
    grad_signal, grad_low, grad_first_gain, grad_first_shift = norm_and_back(
        grad_heads_t, heads_weight, entering, first_gain, grad_middle, True, False, 9
    )
    grad_heads = frame_share(matmul(grad_heads_t, normed), 1)
    vector_grads = jnp.concatenate(
        [
            grad_first_gain,
            grad_first_shift,
            grad_second_gain,
            grad_second_shift,
            grad_third_gain,
            grad_third_shift,
        ]
    )
    matrix_grads = (
        grad_heads,
        grad_output,
        grad_cross_query,
        grad_cross_output,
        grad_expand,
        grad_reduce,
    )
    return grad_signal, grad_low, vector_grads, matrix_grads, grad_text_rows


def per_device(
    inputs,
    lengths,
    text,
    cotangent,
    first_gain,
    first_shift,
    query_weight,
    key_weight,
    value_weight,
    output_weight,
    second_gain,
    second_shift,
    cross_query,
    cross_key,
    cross_value,
    cross_output,
    third_gain,
    third_shift,
    expand_weight,
    reduce_weight,
):
    section = lax.axis_index("section")
    at_zero = section == 0
    frame_count = lax.axis_size("frame")
    frame_index = lax.axis_index("frame")
    core = frame_index % 2
    micro_count, rows_dev, model_width = inputs.shape
    rows_all = rows_dev * frame_count
    text_rows_dev = text.shape[2]

    def keep(pair):
        return jnp.where(at_zero, pair[0], pair[1])

    def give(pair):
        return jnp.where(at_zero, pair[1], pair[0])

    def both_layers(weight):
        half = weight.shape[0] // 2
        mine = lax.dynamic_slice_in_dim(weight, core * half, half, 0)
        came = swapped(mine)
        sibling = across_frames(came, 1)
        other = jnp.concatenate(
            [jnp.where(core == 0, came, sibling), jnp.where(core == 0, sibling, came)], axis=0
        )
        return jnp.where(at_zero, weight, other), jnp.where(at_zero, other, weight)

    vector_args = jnp.concatenate(
        [first_gain, first_shift, second_gain, second_shift, third_gain, third_shift], axis=0
    )
    vectors = lax.all_gather(vector_args, "section")
    columns = query_weight.shape[2]
    heads_weight = jnp.stack(
        [
            w[0].T.reshape(columns // HEAD, HEAD, model_width)
            for w in (query_weight, key_weight, value_weight)
        ],
        axis=1,
    ).reshape(3 * columns, model_width)
    pairs = []
    previous = None
    for weight in (
        heads_weight,
        output_weight[0],
        cross_query[0],
        cross_output[0],
        expand_weight[0],
        reduce_weight[0],
    ):
        if previous is not None:
            weight, _ = lax.optimization_barrier((weight, previous))
        pairs.append(both_layers(weight))
        previous = pairs[-1][0][:8, :128]
    weights = list(zip(*pairs))

    text_full = lax.all_gather(text, "frame", axis=2, tiled=True)
    text_flat = text_full.reshape(micro_count * ITEMS * TEXT, model_width)
    text_heads = jnp.concatenate(
        [matmul(text_flat, cross_key[0]), matmul(text_flat, cross_value[0])], axis=1
    ).astype(jnp.bfloat16)
    text_heads = text_heads.reshape(micro_count, ITEMS * TEXT, -1)
    own_text = keep(text_heads)
    other_text = swapped(give(text_heads))
    cross_states = [
        jnp.where(at_zero, own_text, other_text),
        jnp.where(at_zero, other_text, own_text),
    ]
    cross_keys = [c[:, :columns] for c in cross_states]
    cross_values = [c[:, columns:] for c in cross_states]

    item_ends = jnp.cumsum(lax.dynamic_index_in_dim(lengths, section, 0, keepdims=False))
    all_positions = jnp.arange(rows_all, dtype=jnp.int32)
    passed = all_positions[:, None] >= item_ends[None, :]
    seg_all = jnp.sum(passed.astype(jnp.int32), axis=1)
    begins = jnp.max(jnp.where(passed, item_ends[None, :], 0), axis=1)
    own_start = frame_index * rows_dev
    own_positions = own_start + jnp.arange(rows_dev, dtype=jnp.int32)
    seg_own = lax.dynamic_slice_in_dim(seg_all, own_start, rows_dev)
    text_item = jnp.arange(ITEMS * TEXT, dtype=jnp.int32) // TEXT
    masks = {
        "own": (all_positions[None, :] <= own_positions[:, None])
        & (seg_own[:, None] == seg_all[None, :]),
        "begins": begins[None].astype(jnp.int32),
        "cross": seg_own[:, None] == text_item[None, :],
    }

    signal = lax.dynamic_index_in_dim(inputs, section, 0, keepdims=False)
    normed = layer_norm(signal.astype(jnp.float32), vectors[0][0], vectors[0][1])
    normed = normed.astype(jnp.bfloat16)
    results, saves = [], []
    for layer in range(2):
        result, normed, signal, saved = forward(
            signal,
            normed,
            vectors[layer],
            vectors[1] if layer == 0 else None,
            weights[layer],
            cross_keys[layer],
            cross_values[layer],
            masks,
        )
        results.append(result)
        saves.append(saved)

    upstream = lax.dynamic_index_in_dim(cotangent, section, 0, keepdims=False)
    grad_out = upstream.astype(jnp.bfloat16)
    in_grads, vector_grads, matrix_grads, text_grads = ([None] * 2 for _ in range(4))
    for layer in (1, 0):
        in_grads[layer], grad_low, vector_grads[layer], matrix_grads[layer], text_grads[layer] = (
            backward(
                saves[layer],
                upstream,
                grad_out,
                vectors[layer],
                weights[layer],
                cross_keys[layer],
                cross_values[layer],
                masks,
            )
        )
        grad_out = grad_low
        upstream = grad_low

    def both_micros(pair):
        own = keep(pair)
        other = swapped(give([p.astype(jnp.bfloat16) for p in pair])).astype(own.dtype)
        return jnp.stack([jnp.where(at_zero, own, other), jnp.where(at_zero, other, own)])

    layer_outputs = both_micros(results)
    input_grads = both_micros(in_grads)
    totals = [
        keep(pair).astype(jnp.float32) + swapped(give(pair)).astype(jnp.float32)
        for pair in zip(*matrix_grads)
    ]
    text_rows = both_micros(text_grads)
    text_rows = text_rows.reshape(micro_count * ITEMS * text_rows_dev, -1)
    key_part, value_part = text_rows[:, :columns], text_rows[:, columns:]
    text_local = text.reshape(-1, model_width)
    grad_cross_key, grad_cross_value = (
        frame_share(matmul_tn(text_local, part), 0).astype(jnp.float32)
        for part in (key_part, value_part)
    )
    text_part = matmul_nt(key_part, cross_key[0]) + matmul_nt(value_part, cross_value[0])
    text_grad = lax.psum(text_part.astype(jnp.bfloat16), ("section", "head")).astype(jnp.float32)
    text_grad = text_grad.reshape(text.shape)

    stacked = lax.psum_scatter(
        jnp.stack(vector_grads).astype(jnp.bfloat16), "frame", scatter_dimension=2, tiled=True
    )
    vector_total = keep(stacked).astype(jnp.float32) + swapped(give(stacked)).astype(jnp.float32)

    grad_heads, grad_o, grad_cq, grad_co, grad_e, grad_r = totals
    grad_heads = grad_heads.reshape(columns // HEAD, 3, HEAD, -1)
    grad_q, grad_k, grad_v = (grad_heads[:, i].reshape(columns, -1).T for i in range(3))
    ordered = (
        vector_total[0],
        vector_total[1],
        grad_q,
        grad_k,
        grad_v,
        grad_o,
        vector_total[2],
        vector_total[3],
        grad_cq,
        grad_cross_key,
        grad_cross_value,
        grad_co,
        vector_total[4],
        vector_total[5],
        grad_e,
        grad_r,
    )
    return (layer_outputs[None], input_grads[None], text_grad) + tuple(g[None] for g in ordered)


def solution(mesh):
    return jax.shard_map(
        per_device,
        mesh=mesh,
        in_specs=(
            P(None, "frame", None),
            P(),
            P(None, None, "frame", None),
            P(None, "frame", None),
            P("section", None),
            P("section", None),
            P("section", None, "head"),
            P("section", None, "head"),
            P("section", None, "head"),
            P("section", "head", None),
            P("section", None),
            P("section", None),
            P("section", None, "head"),
            P("section", None, "head"),
            P("section", None, "head"),
            P("section", "head", None),
            P("section", None),
            P("section", None),
            P("section", None, "head"),
            P("section", "head", None),
        ),
        out_specs=(
            P("section", None, "frame", None),
            P("section", None, "frame", None),
            P(None, None, "frame", None),
            P("section", "frame"),
            P("section", "frame"),
            P("section", "frame", "head"),
            P("section", "frame", "head"),
            P("section", "frame", "head"),
            P("section", ("head", "frame"), None),
            P("section", "frame"),
            P("section", "frame"),
            P("section", "frame", "head"),
            P("section", "frame", "head"),
            P("section", "frame", "head"),
            P("section", ("head", "frame"), None),
            P("section", "frame"),
            P("section", "frame"),
            P("section", "frame", "head"),
            P("section", ("head", "frame"), None),
        ),
        check_vma=False,
    )
```

time: 2430 us -> 1040 us (0.43)
  waiting for transfers between devices: 1580 us -> 124 us
  Pallas kernels: 0 us -> 562 us
  matrix products: 517 us -> 60.7 us
  other arithmetic: 180 us -> 98.8 us
  blocking collectives: 11.5 us -> 45.7 us
  starting transfers between devices: 17 us -> 41.5 us
    psum x19 -> x1, waiting for transfers between devices: 1050 us -> 32 us  [per_device(): lax.psum(text_part.astype(jnp.bfloat16), ('section', 'head'))]
    pallas_call x0 -> x16, Pallas kernels: none -> 562 us  [the longest x6 231 us: backward_sum(): pl.pallas_call(functools.partial(backward_sum_kernel, pieces, flipped, we...]
    reduce_scatter x22 -> x1, waiting for transfers between devices: 377 us -> 1.68 us  [per_device(): lax.psum_scatter(jnp.stack(vector_grads).astype(jnp.bfloat16), 'frame', s...]
    dot_general x54 -> x10, matrix products: 117 us -> 26.7 us  [matmul(): return jnp.dot(left_side, right_side, preferred_element_type=jnp.float32)]
    sub x12 -> x2, matrix products: 87.1 us -> 3.27 us  [softmax_rows(): exponent = jnp.exp(logits - jnp.max(logits, axis=-1, keepdims=True))]
    all_gather x12 -> x0, waiting for transfers between devices: 72.9 us -> none  [the longest x6 44.6 us: forward(): lax.all_gather(key_rows, 'frame', axis=0, tiled=True)]
    dot_general x30 -> x10, matrix products: 77.5 us -> 10.7 us  [matmul_tn(): lax.dot_general(left_side, right_side, (((0,), (0,)), ((), ())), preferre...]
    dot_general x12 -> x2, matrix products: 64.8 us -> 2.28 us  [attend(): jnp.einsum('hqk,khd->qhd', weights_low, split_heads(value_rows), preferre...]
  transfers between devices with their start and end apart: 58 -> 58, of which waited for: 52 -> 20; matrix products, arithmetic and copies ran while one was open for 20% -> 12% of each run, Pallas kernels for 0% -> 13%
where the time goes in v1:
time: 1040 us; the launch traced here: 1030 us
  Pallas kernels  562 us (54%)
  waiting for transfers between devices  124 us (12%)
  other arithmetic  98.8 us (10%)
  local copies, waits for them, and re-layouts  79 us (8%)
  matrix products  60.7 us (6%)
  blocking collectives  45.7 us (4%)
  starting transfers between devices  41.5 us (4%)
  between operations  16.5 us (2%)
    pallas_call x6, Pallas kernels, backward_sum(): pl.pallas_call(functools.partial(backward_sum_kernel, pieces, flipped, we...  231 us
    pallas_call x6, Pallas kernels, forward_sum(): pl.pallas_call(functools.partial(forward_sum_kernel, pieces, normed, flip...  223 us
    pallas_call x2, Pallas kernels, attention_back(): pl.pallas_call(functools.partial(attention_back_kernel, frames), out_shap...  61.3 us
    ppermute x38, waiting for transfers between devices, across_frames(): lax.ppermute(x, 'frame', [(i, i ^ bit) for i in range(lax.axis_size('fram...  49.1 us
    pallas_call x2, Pallas kernels, attention(): pl.pallas_call(functools.partial(attention_kernel, frames), out_shape=[ja...  46.4 us
    all_gather x1, blocking collectives, per_device(): vectors = lax.all_gather(vector_args, 'section')  45.7 us
    ppermute x17, waiting for transfers between devices, swapped(): return lax.ppermute(x, 'section', [(0, 1), (1, 0)])  40.8 us
    psum x1, waiting for transfers between devices, per_device(): lax.psum(text_part.astype(jnp.bfloat16), ('section', 'head'))  32 us
  transfers between devices with their start and end apart: 58, of which 20 were waited for; matrix products, arithmetic and copies ran while one was open for 12% of the time, Pallas kernels for 13%

profile of v1, /device:TPU:0, one launch (start us, length us, event | category | flops | bytes accessed | tf_op | source)
XLA Modules:
  0.0 1028.8 jit_solution(2802006401660835674)
XLA Ops:
  9.7 3.0 collective-permute-start.5
  15.3 2.1 collective-permute-start.3
  19.5 2.3 constant_dynamic-slice_fusion
  21.8 2.0 collective-permute-start.11
  24.8 45.7 %all-gather.1 = f32[2,6,1024]{2,1,0:T(8,128)S(1)} all-gather(f32[1,6,1024]{2,1,0:T(8,128)S(1)} %bitcast.555), channel_id=2, replica_groups=mesh['section'=2,'head'=4,'frame'=4] {'section'}, dimensions={0}, use_global_device_ids=true | all-gather | bytes 73728 | tf_op jit(solution)/shard_map/all_gather | solution.py:848
  75.3 3.3 dynamic-slice_bitcast_fusion.upstream
  88.9 16.6 %collective-permute-done.9 = bf16[512,1024]{1,0:T(8,128)(2,1)} collective-permute-done((bf16[512,1024]{1,0:T(8,128)(2,1)}, bf16[512,1024]{1,0:T(8,128)(2,1)}, u32[]{:S(2)}, u32[]{:S(2)}) %collective-permute-start.9) | collective-permute-done | bytes 1048608 | tf_op jit(solution)/shard_map/ppermute | solution.py:544
  109.1 1.8 collective-permute-start
  112.4 2.7 broadcast_select_fusion.4
  115.1 23.1 %shard_map.339 = (bf16[192,2048]{1,0:T(8,128)(2,1)}, bf16[256,512]{1,0:T(8,128)(2,1)}) custom-call(bf16[512,1024]{1,0:T(8,128)(2,1)} %fusion.7.normed, bf16[768,1024]{1,0:T(8,128)(2,1)} %get-tuple-element.211.weight, s32[1,2048]{1,0:T(1,128)} %bitcast.551), custom_call_target="tpu_custom_call" | custom-call | tf_op jit(solution)/shard_map/pallas_call | solution.py:379
  138.4 38.1 %shard_map.340 = (f32[512,1024]{1,0:T(8,128)}, bf16[512,1024]{1,0:T(8,128)(2,1)}) custom-call(bf16[256,512]{1,0:T(8,128)(2,1)} %get-tuple-element.57.left, bf16[256,1024]{1,0:T(8,128)(2,1)} %get-tuple-element.255.weight, bf16[512,1024]{1,0:T(8,128)(2,1)} %copy-done.1, f32[1,1024]{1,0:T(1,128)} %get-tuple-element.290.gain, f32[1,1024]{1,0:T(1,128)} %get-tuple-element.289.shift), custom_call_target="tpu_custom_call" | custom-call | tf_op jit(solution)/shard_map/pallas_call | solution.py:202
  182.3 36.9 %shard_map.341 = (f32[512,1024]{1,0:T(8,128)}, bf16[512,1024]{1,0:T(8,128)(2,1)}) custom-call(bf16[512,256]{1,0:T(8,128)(2,1)} %copy.120.left, bf16[256,1024]{1,0:T(8,128)(2,1)} %get-tuple-element.251.weight, f32[512,1024]{1,0:T(8,128)} %get-tuple-element.59.base.value, f32[1,1024]{1,0:T(1,128)} %get-tuple-element.288.gain, f32[1,1024]{1,0:T(1,128)} %get-tuple-element.287.shift), custom_call_target="tpu_custom_call" | custom-call | tf_op jit(solution)/shard_map/pallas_call | solution.py:202
  219.3 1.8 broadcast_select_fusion.9
  222.7 3.2 broadcast_select_fusion.7
  226.4 3.2 broadcast_select_fusion
  229.7 6.7 fusion.14
  236.4 39.0 %shard_map.342 = (f32[512,1024]{1,0:T(8,128)}, bf16[512,1024]{1,0:T(8,128)(2,1)}, bf16[512,1024]{1,0:T(8,128)(2,1)}) custom-call(bf16[512,1024]{1,0:T(8,128)(2,1)} %get-tuple-element.302.left, bf16[1024,1024]{1,0:T(8,128)(2,1)} %get-tuple-element.199.weight, f32[512,1024]{1,0:T(8,128)} %get-tuple-element.61.base.value, f32[1,1024]{1,0:T(1,128)} %get-tuple-element.286.gain, ...), custom_call_target="tpu_custom_call" | custom-call | tf_op jit(solution)/shard_map/pallas_call | solution.py:202
  275.4 23.3 %shard_map.343 = (bf16[192,2048]{1,0:T(8,128)(2,1)}, bf16[256,512]{1,0:T(8,128)(2,1)}) custom-call(bf16[512,1024]{1,0:T(8,128)(2,1)} %get-tuple-element.63.normed, bf16[768,1024]{1,0:T(8,128)(2,1)} %get-tuple-element.210.weight, s32[1,2048]{1,0:T(1,128)} %bitcast.552), custom_call_target="tpu_custom_call" | custom-call | tf_op jit(solution)/shard_map/pallas_call | solution.py:379
  298.7 36.6 %shard_map.344 = (f32[512,1024]{1,0:T(8,128)}, bf16[512,1024]{1,0:T(8,128)(2,1)}) custom-call(bf16[256,512]{1,0:T(8,128)(2,1)} %get-tuple-element.64.left, bf16[256,1024]{1,0:T(8,128)(2,1)} %get-tuple-element.254.weight, bf16[512,1024]{1,0:T(8,128)(2,1)} %get-tuple-element.65.base.value, f32[1,1024]{1,0:T(1,128)} %get-tuple-element.284.gain, ...), custom_call_target="tpu_custom_call" | custom-call | tf_op jit(solution)/shard_map/pallas_call | solution.py:202
  337.0 2.3 fusion.176
  339.4 2.0 convolution_convert_fusion.2
  342.2 36.7 %shard_map.345 = (f32[512,1024]{1,0:T(8,128)}, bf16[512,1024]{1,0:T(8,128)(2,1)}) custom-call(bf16[512,256]{1,0:T(8,128)(2,1)} %copy.122.left, bf16[256,1024]{1,0:T(8,128)(2,1)} %get-tuple-element.250.weight, f32[512,1024]{1,0:T(8,128)} %get-tuple-element.67.base.value, f32[1,1024]{1,0:T(1,128)} %get-tuple-element.282.gain, f32[1,1024]{1,0:T(1,128)} %get-tuple-element.293.shift), custom_call_target="tpu_custom_call" | custom-call | tf_op jit(solution)/shard_map/pallas_call | solution.py:202
  379.0 7.9 fusion.17
  386.9 2.8 fusion.23.left
  389.6 41.5 %shard_map.347 = (f32[512,1024]{1,0:T(8,128)}, bf16[512,1024]{1,0:T(8,128)(2,1)}, f32[1,1024]{1,0:T(1,128)}, f32[1,1024]{1,0:T(1,128)}) custom-call(bf16[512,1024]{1,0:T(8,128)(2,1)} %fusion.23.left, bf16[1024,1024]{1,0:T(8,128)(2,1)} %copy-done.13, f32[512,1024]{1,0:T(8,128)} %get-tuple-element.69.base.value, f32[1,1024]{1,0:T(1,128)} %get-tuple-element.282.gain, ...), custom_call_target="tpu_custom_call" | custom-call | tf_op jit(solution)/shard_map/pallas_call | solution.py:251
  431.2 1.8 convolution_convert_fusion.1
  433.4 35.9 %shard_map.346 = f32[512,1024]{1,0:T(8,128)} custom-call(bf16[512,1024]{1,0:T(8,128)(2,1)} %get-tuple-element.306.left, bf16[1024,1024]{1,0:T(8,128)(2,1)} %get-tuple-element.198.weight, f32[512,1024]{1,0:T(8,128)} %get-tuple-element.69.base.value, f32[1,1024]{1,0:T(1,128)} %get-tuple-element.282.gain, f32[1,1024]{1,0:T(1,128)} %get-tuple-element.293.shift), custom_call_target="tpu_custom_call" | custom-call | tf_op jit(solution)/shard_map/pallas_call | solution.py:202
  469.4 3.3 fusion.90
  477.8 2.7 fusion.75
  481.1 3.1 dynamic-slice_bitcast_fusion.2
  485.1 35.4 %shard_map.348 = (f32[512,1024]{1,0:T(8,128)}, bf16[512,1024]{1,0:T(8,128)(2,1)}, f32[1,1024]{1,0:T(1,128)}, f32[1,1024]{1,0:T(1,128)}) custom-call(bf16[512,256]{1,0:T(8,128)(2,1)} %copy.124.left, bf16[1024,256]{1,0:T(8,128)(2,1)} %get-tuple-element.252.weight, f32[512,1024]{1,0:T(8,128)} %get-tuple-element.67.base.value, ...), custom_call_target="tpu_custom_call" | custom-call | tf_op jit(solution)/shard_map/pallas_call | solution.py:251
  520.4 31.2 %shard_map.349.left = bf16[768,512]{1,0:T(8,128)(2,1)} custom-call(bf16[192,2048]{1,0:T(8,128)(2,1)} %get-tuple-element.71.heads_t, bf16[512,1024]{1,0:T(8,128)(2,1)} %get-tuple-element.74.grad_low, bf16[256,1024]{1,0:T(8,128)(2,1)} %get-tuple-element.254.weight, s32[1,2048]{1,0:T(1,128)} %bitcast.553), custom_call_target="tpu_custom_call" | custom-call | tf_op jit(solution)/shard_map/pallas_call | solution.py:479
  551.7 39.0 %shard_map.350 = (f32[512,1024]{1,0:T(8,128)}, bf16[512,1024]{1,0:T(8,128)(2,1)}, f32[1,1024]{1,0:T(1,128)}, f32[1,1024]{1,0:T(1,128)}) custom-call(bf16[768,512]{1,0:T(8,128)(2,1)} %shard_map.349.left, bf16[768,1024]{1,0:T(8,128)(2,1)} %get-tuple-element.210.weight, bf16[512,1024]{1,0:T(8,128)(2,1)} %get-tuple-element.65.base.value, ...), custom_call_target="tpu_custom_call" | custom-call | tf_op jit(solution)/shard_map/pallas_call | solution.py:251
  590.8 4.0 fusion.29.left
  594.7 40.8 %shard_map.351 = (f32[512,1024]{1,0:T(8,128)}, bf16[512,1024]{1,0:T(8,128)(2,1)}, f32[1,1024]{1,0:T(1,128)}, f32[1,1024]{1,0:T(1,128)}) custom-call(bf16[512,1024]{1,0:T(8,128)(2,1)} %fusion.29.left, bf16[1024,1024]{1,0:T(8,128)(2,1)} %copy-done.14, f32[512,1024]{1,0:T(8,128)} %get-tuple-element.61.base.value, f32[1,1024]{1,0:T(1,128)} %get-tuple-element.288.gain, ...), custom_call_target="tpu_custom_call" | custom-call | tf_op jit(solution)/shard_map/pallas_call | solution.py:251
  651.9 2.0 reshape.300
  663.5 35.3 %shard_map.352 = (f32[512,1024]{1,0:T(8,128)}, bf16[512,1024]{1,0:T(8,128)(2,1)}, f32[1,1024]{1,0:T(1,128)}, f32[1,1024]{1,0:T(1,128)}) custom-call(bf16[512,256]{1,0:T(8,128)(2,1)} %copy.126.left, bf16[1024,256]{1,0:T(8,128)(2,1)} %copy-done.28, f32[512,1024]{1,0:T(8,128)} %get-tuple-element.59.base.value, f32[1,1024]{1,0:T(1,128)} %get-tuple-element.290.gain, ...), custom_call_target="tpu_custom_call" | custom-call | tf_op jit(solution)/shard_map/pallas_call | solution.py:251
  702.0 30.1 %shard_map.353.left = bf16[768,512]{1,0:T(8,128)(2,1)} custom-call(bf16[192,2048]{1,0:T(8,128)(2,1)} %get-tuple-element.70.heads_t, bf16[512,1024]{1,0:T(8,128)(2,1)} %get-tuple-element.79.grad_low, bf16[256,1024]{1,0:T(8,128)(2,1)} %get-tuple-element.255.weight, s32[1,2048]{1,0:T(1,128)} %bitcast.554), custom_call_target="tpu_custom_call" | custom-call | tf_op jit(solution)/shard_map/pallas_call | solution.py:479
  732.1 2.1 fusion.177
  759.5 39.3 %shard_map.354 = (f32[512,1024]{1,0:T(8,128)}, bf16[512,1024]{1,0:T(8,128)(2,1)}, f32[1,1024]{1,0:T(1,128)}, f32[1,1024]{1,0:T(1,128)}) custom-call(bf16[768,512]{1,0:T(8,128)(2,1)} %shard_map.353.left, bf16[768,1024]{1,0:T(8,128)(2,1)} %get-tuple-element.211.weight, bf16[512,1024]{1,0:T(8,128)(2,1)} %copy-done.1, f32[1,1024]{1,0:T(1,128)} %get-tuple-element.281.gain, ...), custom_call_target="tpu_custom_call" | custom-call | tf_op jit(solution)/shard_map/pallas_call | solution.py:251
  806.3 1.8 pad_maximum_fusion.17
  811.5 2.1 pad_maximum_fusion.9
  814.4 3.0 convert_select_fusion.4
  831.6 1.9 collective-permute-start.16
  858.4 3.4 collective-permute-done.34
  867.1 2.5 collective-permute-done.27
  870.2 4.9 collective-permute-done.44
  877.4 2.7 collective-permute-done.35
  882.2 4.6 collective-permute-done.30
  890.5 32.0 %all-reduce.2.cloned.1.call-done = bf16[2,4,16,1024]{3,2,1,0:T(8,128)(2,1)} async-done(((bf16[2,4,16,1024]{3,2,1,0:T(8,128)(2,1)}), bf16[2,4,16,1024]{3,2,1,0:T(8,128)(2,1)}) %all-reduce.2.cloned.1.call-update) | async-done | bytes 262160 | tf_op jit(solution)/shard_map/psum | solution.py:961
  922.5 1.8 reshape.273
  927.4 1.8 copy.141
  932.0 1.8 copy.142
  945.8 2.3 fusion.8
  948.1 4.3 collective-permute-done.14
  953.4 2.2 fusion.10
  957.1 2.6 maximum_bitcast_fusion
  960.8 2.6 maximum_bitcast_fusion.1
  964.3 18.5 %collective-permute-done.46 = bf16[256,1024]{1,0:T(8,128)(2,1)S(1)} collective-permute-done((bf16[256,1024]{1,0:T(8,128)(2,1)S(1)}, bf16[256,1024]{1,0:T(8,128)(2,1)S(1)}, u32[]{:S(2)}, u32[]{:S(2)}) %collective-permute-start.46) | collective-permute-done | bytes 524320 | tf_op jit(solution)/shard_map/ppermute | solution.py:548
  982.9 11.2 %collective-permute-done.48 = bf16[256,1024]{1,0:T(8,128)(2,1)S(1)} collective-permute-done((bf16[256,1024]{1,0:T(8,128)(2,1)S(1)}, bf16[256,1024]{1,0:T(8,128)(2,1)S(1)}, u32[]{:S(2)}, u32[]{:S(2)}) %collective-permute-start.48) | collective-permute-done | bytes 524320 | tf_op jit(solution)/shard_map/ppermute | solution.py:548
  996.6 8.0 collective-permute-done.51
  1009.9 3.0 add_bitcast_fusion.1
  1012.9 6.4 collective-permute-done.54
  1019.3 2.5 add_bitcast_fusion
  (602 shorter events, 193.6 us)
Async XLA Ops:
  7.2 100.1 %copy-start = (bf16[1,1024,256]{2,1,0:T(8,128)(2,1)S(1)}, bf16[1,1024,256]{2,1,0:T(8,128)(2,1)}, u32[]{:S(2)}) copy-start(bf16[1,1024,256]{2,1,0:T(8,128)(2,1)} %param.33) | copy-start | bytes 1572868
  7.2 98.3 %all-gather.4.cloned.1.call-start = ((), (), s32[]{:S(2)}) async-start(), calls=%async_computation.1 | async-start | bytes 1310720 | tf_op jit(solution)/shard_map/all_gather | solution.py:873
  8.0 816.1 %reduce-scatter.2.cloned.1.call-start = ((), (), s32[]{:S(2)}) async-start(), calls=%async_computation.3 | async-start | bytes 40960 | tf_op jit(solution)/shard_map/reduce_scatter | solution.py:964
  9.7 65.5 %collective-permute-start.5 = (bf16[512,256]{1,0:T(8,128)(2,1)}, bf16[512,256]{1,0:T(8,128)(2,1)}, u32[]{:S(2)}, u32[]{:S(2)}) collective-permute-start(bf16[512,256]{1,0:T(8,128)(2,1)} %constant_dynamic-slice_fusion.3), channel_id=1, source_target_pairs={{0,16},{16,0},{1,17},{17,1},{2,18},{18,2},{3,19},{19,3},{4,20},{20... | collective-permute-start | bytes 786440 | tf_op jit(solution)/shard_map/ppermute | solution.py:544
  14.3 64.3 %collective-permute-start.7 = (bf16[128,1024]{1,0:T(8,128)(2,1)}, bf16[128,1024]{1,0:T(8,128)(2,1)}, u32[]{:S(2)}, u32[]{:S(2)}) collective-permute-start(bf16[128,1024]{1,0:T(8,128)(2,1)} %constant_dynamic-slice_fusion.2), channel_id=1, source_target_pairs={{0,16},{16,0},{1,17},{17,1},{2,18},{18,2},{3,19},{19,3},{4,20},{20... | collective-permute-start | bytes 786440 | tf_op jit(solution)/shard_map/ppermute | solution.py:544
  15.3 64.7 %collective-permute-start.3 = (bf16[128,1024]{1,0:T(8,128)(2,1)S(1)}, bf16[128,1024]{1,0:T(8,128)(2,1)}, u32[]{:S(2)}, u32[]{:S(2)}) collective-permute-start(bf16[128,1024]{1,0:T(8,128)(2,1)S(1)} %constant_dynamic-slice_fusion.4), channel_id=1, source_target_pairs={{0,16},{16,0},{1,17},{17,1},{2,18},{18,2},{3,19},{19,3},{4,20},{20... | collective-permute-start | bytes 786440 | tf_op jit(solution)/shard_map/ppermute | solution.py:544
  19.5 68.0 %collective-permute-start.1 = (bf16[384,1024]{1,0:T(8,128)(2,1)}, bf16[384,1024]{1,0:T(8,128)(2,1)}, u32[]{:S(2)}, u32[]{:S(2)}) collective-permute-start(bf16[384,1024]{1,0:T(8,128)(2,1)} %constant_dynamic-slice_fusion.5), channel_id=1, source_target_pairs={{0,16},{16,0},{1,17},{17,1},{2,18},{18,2},{3,19},{19,3},{4,20},{20... | collective-permute-start | bytes 2359304 | tf_op jit(solution)/shard_map/ppermute | solution.py:544
  21.8 67.1 %collective-permute-start.11 = (bf16[512,1024]{1,0:T(8,128)(2,1)}, bf16[512,1024]{1,0:T(8,128)(2,1)}, u32[]{:S(2)}, u32[]{:S(2)}) collective-permute-start(bf16[512,1024]{1,0:T(8,128)(2,1)} %constant_dynamic-slice_fusion), channel_id=1, source_target_pairs={{0,16},{16,0},{1,17},{17,1},{2,18},{18,2},{3,19},{19,3},{4,20},{20... | collective-permute-start | bytes 3145736 | tf_op jit(solution)/shard_map/ppermute | solution.py:544
  75.3 6.5 collective-permute-start.6
  78.6 4.2 collective-permute-start.8
  80.0 25.5 %collective-permute-start.9 = (bf16[512,1024]{1,0:T(8,128)(2,1)}, bf16[512,1024]{1,0:T(8,128)(2,1)}, u32[]{:S(2)}, u32[]{:S(2)}) collective-permute-start(bf16[512,1024]{1,0:T(8,128)(2,1)} %constant_dynamic-slice_fusion.1), channel_id=1, source_target_pairs={{0,16},{16,0},{1,17},{17,1},{2,18},{18,2},{3,19},{19,3},{4,20},{20... | collective-permute-start | bytes 3145736 | tf_op jit(solution)/shard_map/ppermute | solution.py:544
  81.8 2.1 collective-permute-start.4
  87.4 23.5 %collective-permute-start.2 = (bf16[384,1024]{1,0:T(8,128)(2,1)}, bf16[384,1024]{1,0:T(8,128)(2,1)}, u32[]{:S(2)}, u32[]{:S(2)}) collective-permute-start(bf16[384,1024]{1,0:T(8,128)(2,1)} %collective-permute-done.1), channel_id=1, source_target_pairs={{0,1},{1,0},{2,3},{3,2},{4,5},{5,4},{6,7},{7,6},{8,9},{9,8},{10,11... | collective-permute-start | bytes 2359304 | tf_op jit(solution)/shard_map/ppermute | solution.py:548
  88.9 87.7 %copy-start.28 = (bf16[1024,256]{1,0:T(8,128)(2,1)}, bf16[1024,256]{1,0:T(8,128)(2,1)S(1)}, u32[]{:S(2)}) copy-start(bf16[1024,256]{1,0:T(8,128)(2,1)S(1)} %get-tuple-element.253.weight) | copy-start | bytes 1572868
  88.9 133.8 %collective-permute-start.12 = (bf16[512,1024]{1,0:T(8,128)(2,1)}, bf16[512,1024]{1,0:T(8,128)(2,1)}, u32[]{:S(2)}, u32[]{:S(2)}) collective-permute-start(bf16[512,1024]{1,0:T(8,128)(2,1)} %collective-permute-done.11), channel_id=1, source_target_pairs={{0,1},{1,0},{2,3},{3,2},{4,5},{5,4},{6,7},{7,6},{8,9},{9,8},{10,11... | collective-permute-start | bytes 3145736 | tf_op jit(solution)/shard_map/ppermute | solution.py:548
  105.6 113.7 %collective-permute-start.10 = (bf16[512,1024]{1,0:T(8,128)(2,1)}, bf16[512,1024]{1,0:T(8,128)(2,1)}, u32[]{:S(2)}, u32[]{:S(2)}) collective-permute-start(bf16[512,1024]{1,0:T(8,128)(2,1)} %collective-permute-done.9), channel_id=1, source_target_pairs={{0,1},{1,0},{2,3},{3,2},{4,5},{5,4},{6,7},{7,6},{8,9},{9,8},{10,11... | collective-permute-start | bytes 3145736 | tf_op jit(solution)/shard_map/ppermute | solution.py:548
  109.1 69.3 %collective-permute-start = (bf16[256,512]{0,1:T(8,128)(2,1)S(1)}, bf16[256,512]{0,1:T(8,128)(2,1)S(1)}, u32[]{:S(2)}, u32[]{:S(2)}) collective-permute-start(bf16[256,512]{0,1:T(8,128)(2,1)S(1)} %broadcast_select_fusion.31), channel_id=1, source_target_pairs={{0,16},{16,0},{1,17},{17,1},{2,18},{18,2},{3,19},{19,3},{4,20},{20... | collective-permute-start | bytes 786440 | tf_op jit(solution)/shard_map/ppermute | solution.py:544
  222.7 156.3 %copy-start.13 = (bf16[1024,1024]{1,0:T(8,128)(2,1)}, bf16[1024,1024]{1,0:T(8,128)(2,1)S(1)}, u32[]{:S(2)}) copy-start(bf16[1024,1024]{1,0:T(8,128)(2,1)S(1)} %get-tuple-element.200.weight) | copy-start | bytes 6291460
  275.4 59.9 %copy-start.29 = (bf16[1024,256]{1,0:T(8,128)(2,1)S(1)}, bf16[1024,256]{1,0:T(8,128)(2,1)}, u32[]{:S(2)}) copy-start(bf16[1024,256]{1,0:T(8,128)(2,1)} %get-tuple-element.252.weight) | copy-start | bytes 1572868
  751.9 84.4 %collective-permute-start.42 = (bf16[2,64,1024]{2,1,0:T(8,128)(2,1)}, bf16[2,64,1024]{2,1,0:T(8,128)(2,1)}, u32[]{:S(2)}, u32[]{:S(2)}) collective-permute-start(bf16[2,64,1024]{2,1,0:T(8,128)(2,1)} %pad_maximum_fusion.21), channel_id=1, source_target_pairs={{0,1},{1,0},{2,3},{3,2},{4,5},{5,4},{6,7},{7,6},{8,9},{9,8},{10,11... | collective-permute-start | bytes 786440 | tf_op jit(solution)/shard_map/ppermute | solution.py:548
  753.0 184.7 %collective-permute-start.52 = (bf16[2,256,1024]{2,1,0:T(8,128)(2,1)}, bf16[2,256,1024]{2,1,0:T(8,128)(2,1)}, u32[]{:S(2)}, u32[]{:S(2)}) collective-permute-start(bf16[2,256,1024]{2,1,0:T(8,128)(2,1)} %pad_maximum_fusion.7), channel_id=1, source_target_pairs={{0,1},{1,0},{2,3},{3,2},{4,5},{5,4},{6,7},{7,6},{8,9},{9,8},{10,11... | collective-permute-start | bytes 3145736 | tf_op jit(solution)/shard_map/ppermute | solution.py:548
  754.8 189.4 %collective-permute-start.13 = (bf16[512,1024]{1,0:T(8,128)(2,1)}, bf16[512,1024]{1,0:T(8,128)(2,1)}, u32[]{:S(2)}, u32[]{:S(2)}) collective-permute-start(bf16[512,1024]{1,0:T(8,128)(2,1)} %convert_select_fusion.5), channel_id=1, source_target_pairs={{0,16},{16,0},{1,17},{17,1},{2,18},{18,2},{3,19},{19,3},{4,20},{20... | collective-permute-start | bytes 3145736 | tf_op jit(solution)/shard_map/ppermute | solution.py:544
  759.5 69.8 %collective-permute-start.17 = (bf16[2,4,16,512]{3,2,1,0:T(8,128)(2,1)}, bf16[2,4,16,512]{3,2,1,0:T(8,128)(2,1)}, u32[]{:S(2)}, u32[]{:S(2)}) collective-permute-start(bf16[2,4,16,512]{3,2,1,0:T(8,128)(2,1)} %pad_maximum_fusion.23), channel_id=1, source_target_pairs={{0,1},{1,0},{2,3},{3,2},{4,5},{5,4},{6,7},{7,6},{8,9},{9,8},{10,11... | collective-permute-start | bytes 393224 | tf_op jit(solution)/shard_map/ppermute | solution.py:548
  806.0 116.5 %all-reduce.2.cloned.1.call-start = ((), (), s32[]{:S(2)}) async-start(), calls=%async_computation.2 | async-start | bytes 524288 | tf_op jit(solution)/shard_map/psum | solution.py:961
  825.0 3.6 collective-permute-start.20
  828.6 2.0 collective-permute-start.15
  830.4 4.9 collective-permute-start.18
  831.6 4.7 collective-permute-start.16
  835.3 2.7 collective-permute-start.33
  836.3 1.9 collective-permute-start.40
  836.4 3.8 collective-permute-start.28
  838.0 95.8 %collective-permute-start.23 = (bf16[2,768,256]{2,1,0:T(8,128)(2,1)}, bf16[2,768,256]{2,1,0:T(8,128)(2,1)}, u32[]{:S(2)}, u32[]{:S(2)}) collective-permute-start(bf16[2,768,256]{2,1,0:T(8,128)(2,1)} %pad_maximum_fusion.9), channel_id=1, source_target_pairs={{0,1},{1,0},{2,3},{3,2},{4,5},{5,4},{6,7},{7,6},{8,9},{9,8},{10,11... | collective-permute-start | bytes 2359304 | tf_op jit(solution)/shard_map/ppermute | solution.py:548
  838.2 2.5 collective-permute-start.31
  840.2 4.2 collective-permute-start.26
  840.8 5.9 collective-permute-start.19
  844.4 10.9 %collective-permute-start.43 = (bf16[64,1024]{1,0:T(8,128)(2,1)}, bf16[64,1024]{1,0:T(8,128)(2,1)S(1)}, u32[]{:S(2)}, u32[]{:S(2)}) collective-permute-start(bf16[64,1024]{1,0:T(8,128)(2,1)} %dynamic-slice_bitcast_fusion.36), channel_id=1, source_target_pairs={{0,2},{1,3},{2,0},{3,1},{4,6},{5,7},{6,4},{7,5},{8,10},{9,11},{10,... | collective-permute-start | bytes 393224 | tf_op jit(solution)/shard_map/ppermute | solution.py:548
  846.6 10.2 collective-permute-start.41
  855.3 6.5 collective-permute-start.34
  856.8 7.8 collective-permute-start.32
  861.8 5.3 collective-permute-start.29
  864.6 5.0 collective-permute-start.27
  867.1 13.8 %collective-permute-start.36 = (bf16[2,256,256]{1,2,0:T(8,128)(2,1)S(1)}, bf16[2,256,256]{1,2,0:T(8,128)(2,1)S(1)}, u32[]{:S(2)}, u32[]{:S(2)}) collective-permute-start(bf16[2,256,256]{1,2,0:T(8,128)(2,1)S(1)} %pad_maximum_fusion.18), channel_id=1, source_target_pairs={{0,1},{1,0},{2,3},{3,2},{4,5},{5,4},{6,7},{7,6},{8,9},{9,8},{10,11... | collective-permute-start | bytes 786440 | tf_op jit(solution)/shard_map/ppermute | solution.py:548
  869.6 5.5 collective-permute-start.44
  875.1 5.0 collective-permute-start.35
  880.1 7.5 collective-permute-start.38
  880.9 5.9 collective-permute-start.30
  886.8 48.8 %collective-permute-start.21 = (bf16[2,768,256]{2,1,0:T(8,128)(2,1)}, bf16[2,768,256]{2,1,0:T(8,128)(2,1)}, u32[]{:S(2)}, u32[]{:S(2)}) collective-permute-start(bf16[2,768,256]{2,1,0:T(8,128)(2,1)} %pad_maximum_fusion.8), channel_id=1, source_target_pairs={{0,1},{1,0},{2,3},{3,2},{4,5},{5,4},{6,7},{7,6},{8,9},{9,8},{10,11... | collective-permute-start | bytes 2359304 | tf_op jit(solution)/shard_map/ppermute | solution.py:548
  887.6 36.7 %collective-permute-start.37 = (bf16[256,256]{0,1:T(8,128)(2,1)}, bf16[256,256]{0,1:T(8,128)(2,1)S(1)}, u32[]{:S(2)}, u32[]{:S(2)}) collective-permute-start(bf16[256,256]{0,1:T(8,128)(2,1)} %dynamic-slice_bitcast_fusion.39), channel_id=1, source_target_pairs={{0,2},{1,3},{2,0},{3,1},{4,6},{5,7},{6,4},{7,5},{8,10},{9,11},{10,... | collective-permute-start | bytes 393224 | tf_op jit(solution)/shard_map/ppermute | solution.py:548
  924.3 5.3 collective-permute-start.39
  929.6 22.8 %collective-permute-start.14 = (bf16[512,1024]{1,0:T(8,128)(2,1)}, bf16[512,1024]{1,0:T(8,128)(2,1)}, u32[]{:S(2)}, u32[]{:S(2)}) collective-permute-start(bf16[512,1024]{1,0:T(8,128)(2,1)} %convert_select_fusion.4), channel_id=1, source_target_pairs={{0,16},{16,0},{1,17},{17,1},{2,18},{18,2},{3,19},{19,3},{4,20},{20... | collective-permute-start | bytes 3145736 | tf_op jit(solution)/shard_map/ppermute | solution.py:544
  933.8 6.1 collective-permute-start.45
  935.6 6.4 collective-permute-start.47
  937.7 17.9 %collective-permute-start.50 = (bf16[2,256,1024]{2,1,0:T(8,128)(2,1)S(1)}, bf16[2,256,1024]{2,1,0:T(8,128)(2,1)S(1)}, u32[]{:S(2)}, u32[]{:S(2)}) collective-permute-start(bf16[2,256,1024]{2,1,0:T(8,128)(2,1)S(1)} %copy-done.89), channel_id=1, source_target_pairs={{0,1},{1,0},{2,3},{3,2},{4,5},{5,4},{6,7},{7,6},{8,9},{9,8},{10,11... | collective-permute-start | bytes 3145736 | tf_op jit(solution)/shard_map/ppermute | solution.py:548
  939.9 64.6 %copy-start.17 = (bf16[2,256,1024]{2,1,0:T(8,128)(2,1)}, bf16[2,256,1024]{2,1,0:T(8,128)(2,1)S(1)}, u32[]{:S(2)}) copy-start(bf16[2,256,1024]{2,1,0:T(8,128)(2,1)S(1)} %fusion.33) | copy-start | bytes 3145732
  940.0 19.8 %collective-permute-start.24 = (bf16[768,256]{1,0:T(8,128)(2,1)S(1)}, bf16[768,256]{1,0:T(8,128)(2,1)S(1)}, u32[]{:S(2)}, u32[]{:S(2)}) collective-permute-start(bf16[768,256]{1,0:T(8,128)(2,1)S(1)} %dynamic-slice_bitcast_fusion.18), channel_id=1, source_target_pairs={{0,2},{1,3},{2,0},{3,1},{4,6},{5,7},{6,4},{7,5},{8,10},{9,11},{10,... | collective-permute-start | bytes 1179656 | tf_op jit(solution)/shard_map/ppermute | solution.py:548
  941.9 52.2 %copy-start.19 = (bf16[2,256,1024]{2,1,0:T(8,128)(2,1)}, bf16[2,256,1024]{2,1,0:T(8,128)(2,1)S(1)}, u32[]{:S(2)}) copy-start(bf16[2,256,1024]{2,1,0:T(8,128)(2,1)S(1)} %fusion.30) | copy-start | bytes 3145732
  942.0 21.4 %collective-permute-start.22 = (bf16[768,256]{1,0:T(8,128)(2,1)S(1)}, bf16[768,256]{1,0:T(8,128)(2,1)S(1)}, u32[]{:S(2)}, u32[]{:S(2)}) collective-permute-start(bf16[768,256]{1,0:T(8,128)(2,1)S(1)} %dynamic-slice_bitcast_fusion.19), channel_id=1, source_target_pairs={{0,2},{1,3},{2,0},{3,1},{4,6},{5,7},{6,4},{7,5},{8,10},{9,11},{10,... | collective-permute-start | bytes 1179656 | tf_op jit(solution)/shard_map/ppermute | solution.py:548
  944.3 52.3 %collective-permute-start.53 = (bf16[256,1024]{1,0:T(8,128)(2,1)S(1)}, bf16[256,1024]{1,0:T(8,128)(2,1)S(1)}, u32[]{:S(2)}, u32[]{:S(2)}) collective-permute-start(bf16[256,1024]{1,0:T(8,128)(2,1)S(1)} %dynamic-slice_bitcast_fusion.14), channel_id=1, source_target_pairs={{0,2},{1,3},{2,0},{3,1},{4,6},{5,7},{6,4},{7,5},{8,10},{9,11},{10,... | collective-permute-start | bytes 1572872 | tf_op jit(solution)/shard_map/ppermute | solution.py:548
  952.4 30.5 %collective-permute-start.46 = (bf16[256,1024]{1,0:T(8,128)(2,1)S(1)}, bf16[256,1024]{1,0:T(8,128)(2,1)S(1)}, u32[]{:S(2)}, u32[]{:S(2)}) collective-permute-start(bf16[256,1024]{1,0:T(8,128)(2,1)S(1)} %dynamic-slice_bitcast_fusion.17), channel_id=1, source_target_pairs={{0,2},{1,3},{2,0},{3,1},{4,6},{5,7},{6,4},{7,5},{8,10},{9,11},{10,... | collective-permute-start | bytes 1572872 | tf_op jit(solution)/shard_map/ppermute | solution.py:548
  955.6 38.5 %collective-permute-start.48 = (bf16[256,1024]{1,0:T(8,128)(2,1)S(1)}, bf16[256,1024]{1,0:T(8,128)(2,1)S(1)}, u32[]{:S(2)}, u32[]{:S(2)}) collective-permute-start(bf16[256,1024]{1,0:T(8,128)(2,1)S(1)} %dynamic-slice_bitcast_fusion.16), channel_id=1, source_target_pairs={{0,2},{1,3},{2,0},{3,1},{4,6},{5,7},{6,4},{7,5},{8,10},{9,11},{10,... | collective-permute-start | bytes 1572872 | tf_op jit(solution)/shard_map/ppermute | solution.py:548
  959.7 44.8 %collective-permute-start.51 = (bf16[256,1024]{1,0:T(8,128)(2,1)S(1)}, bf16[256,1024]{1,0:T(8,128)(2,1)S(1)}, u32[]{:S(2)}, u32[]{:S(2)}) collective-permute-start(bf16[256,1024]{1,0:T(8,128)(2,1)S(1)} %dynamic-slice_bitcast_fusion.15), channel_id=1, source_target_pairs={{0,2},{1,3},{2,0},{3,1},{4,6},{5,7},{6,4},{7,5},{8,10},{9,11},{10,... | collective-permute-start | bytes 1572872 | tf_op jit(solution)/shard_map/ppermute | solution.py:548
  963.6 43.4 %collective-permute-start.25 = (bf16[768,256]{1,0:T(8,128)(2,1)S(1)}, bf16[768,256]{1,0:T(8,128)(2,1)S(1)}, u32[]{:S(2)}, u32[]{:S(2)}) collective-permute-start(bf16[768,256]{1,0:T(8,128)(2,1)S(1)} %broadcast_select_fusion.22), channel_id=1, source_target_pairs={{0,16},{16,0},{1,17},{17,1},{2,18},{18,2},{3,19},{19,3},{4,20},{20... | collective-permute-start | bytes 1179656 | tf_op jit(solution)/shard_map/ppermute | solution.py:544
  995.3 14.6 %collective-permute-start.49 = (bf16[256,1024]{1,0:T(8,128)(2,1)}, bf16[256,1024]{1,0:T(8,128)(2,1)}, u32[]{:S(2)}, u32[]{:S(2)}) collective-permute-start(bf16[256,1024]{1,0:T(8,128)(2,1)} %broadcast_select_fusion.17), channel_id=1, source_target_pairs={{0,16},{16,0},{1,17},{17,1},{2,18},{18,2},{3,19},{19,3},{4,20},{20... | collective-permute-start | bytes 1572872 | tf_op jit(solution)/shard_map/ppermute | solution.py:544
  1005.7 13.6 %collective-permute-start.54 = (bf16[256,1024]{1,0:T(8,128)(2,1)}, bf16[256,1024]{1,0:T(8,128)(2,1)}, u32[]{:S(2)}, u32[]{:S(2)}) collective-permute-start(bf16[256,1024]{1,0:T(8,128)(2,1)} %broadcast_select_fusion.16), channel_id=1, source_target_pairs={{0,16},{16,0},{1,17},{17,1},{2,18},{18,2},{3,19},{19,3},{4,20},{20... | collective-permute-start | bytes 1572872 | tf_op jit(solution)/shard_map/ppermute | solution.py:544
  (149 other events, 1307.7 us)
Sparse Core Ops, SparseCore 0:
  9.6 19.4 all-gather.3
  806.1 17.9 reduce-scatter.1
  852.0 70.5 all-reduce.1

commit v2 on v0

v2 whole, which is shorter than its diff:
```python
import jax
import jax.numpy as jnp
from jax import lax
from jax.experimental import pallas as pl
from jax.experimental.pallas import tpu as pltpu
from jax.sharding import PartitionSpec as P

HEAD = 64
TEXT = 64
ITEMS = 4

masked_score = -1e30
inv_sqrt_two = 0.7071067811865476
inv_sqrt_tau = 0.3989422804014327

MESH_IDS = pl.DeviceIdType.MESH
BUSY = pl.CostEstimate(flops=30_000_000_000, bytes_accessed=8_000_000, transcendentals=0)
LAG = 2
BLOCK = 128
VMEM_BYTES = 56 * 1024 * 1024
EPS = 1e-05


class Task:
    operands = ()
    outs = ()
    out_in_vmem = True
    scratch = ()
    greets = ()

    def bind(self, ins, outs, scratch):
        self.ins, self.out, self.room = ins, outs, scratch


def remote(source, landing, send_sem, recv_sem, target):
    return pltpu.make_async_remote_copy(
        src_ref=source,
        dst_ref=landing,
        send_sem=send_sem,
        recv_sem=recv_sem,
        device_id=target,
        device_id_type=MESH_IDS,
    )


def frame_partners():
    me = lax.axis_index("frame")
    return (me + 1 - 2 * lax.rem(me, 2), lax.rem(me + 2, 4), 3 - me)


def span(index, size):
    return pl.ds(pl.multiple_of(index * size, size), size)


class WeightTask(Task):
    out_in_vmem = False
    greets = ("section", "frame")

    def __init__(self, weight):
        self.operands = (weight,)
        self.outs = (jax.ShapeDtypeStruct(weight.shape, weight.dtype),)
        self.scratch = (pltpu.SemaphoreType.DMA((4,)),)
        self.half = weight.shape[0] // 2

    def copies(self):
        (sems,) = self.room
        core = lax.rem(lax.axis_index("frame"), 2)
        rows = span(core, self.half)
        other_section = {"section": 1 - lax.axis_index("section")}
        other_core = {"frame": frame_partners()[0]}
        over = remote(self.ins[0].at[rows], self.out[0].at[rows], sems.at[0], sems.at[1], other_section)
        on = remote(self.out[0].at[rows], self.out[0].at[rows], sems.at[2], sems.at[3], other_core)
        return over, on

    def begin(self):
        self.copies()[0].start()

    def steps(self):
        over, on = self.copies()

        def pass_on():
            over.wait_recv()
            on.start()

        def end():
            over.wait_send()
            on.wait()

        return [pass_on, end]


class ShareTask(Task):
    greets = ("frame",)

    def __init__(self, grad):
        rows, width = grad.shape
        self.share = rows // lax.axis_size("frame")
        self.operands = (grad,)
        self.outs = (jax.ShapeDtypeStruct((self.share, width), jnp.bfloat16),)
        self.scratch = (
            pltpu.VMEM((3, self.share, width), jnp.bfloat16),
            pltpu.VMEM((self.share, width), jnp.bfloat16),
            pltpu.SemaphoreType.DMA((3,)),
            pltpu.SemaphoreType.DMA((3,)),
            pltpu.SemaphoreType.DMA,
        )

    def copies(self):
        landing, own, send_sems, recv_sems, here = self.room
        me = lax.axis_index("frame")
        away = [
            remote(
                self.ins[0].at[span(partner, self.share)],
                landing.at[k],
                send_sems.at[k],
                recv_sems.at[k],
                {"frame": partner},
            )
            for k, partner in enumerate(frame_partners())
        ]
        return away, pltpu.make_async_copy(self.ins[0].at[span(me, self.share)], own, here)

    def begin(self):
        away, stay = self.copies()
        for copy in away[::-1]:
            copy.start()
        stay.start()

    def steps(self):
        away, stay = self.copies()

        def end():
            stay.wait()
            for copy in away:
                copy.wait()
            landing, own = self.room[:2]
            total = own[...].astype(jnp.float32)
            for k in range(3):
                total = total + landing[k].astype(jnp.float32)
            self.out[0][...] = total.astype(jnp.bfloat16)

        return [end]


class CrossTask(Task):
    greets = ("section",)

    def __init__(self, first, second, added):
        self.operands = (first, second)
        self.added = added
        self.out_in_vmem = added
        shape = first.shape
        if added:
            self.outs = (jax.ShapeDtypeStruct(shape, jnp.float32),)
            self.scratch = (pltpu.VMEM(shape, jnp.bfloat16),) * 2 + (pltpu.SemaphoreType.DMA((3,)),)
        else:
            self.outs = (jax.ShapeDtypeStruct(shape, first.dtype),)
            self.scratch = (pltpu.SemaphoreType.DMA((2,)),)

    def copies(self, given, kept):
        sems = self.room[-1]
        landing = self.room[0] if self.added else self.out[0]
        target = {"section": 1 - lax.axis_index("section")}
        copies = [remote(self.ins[given], landing, sems.at[0], sems.at[1], target)]
        if self.added:
            copies.append(pltpu.make_async_copy(self.ins[kept], self.room[1], sems.at[2]))
        return copies

    def begin(self):
        section = lax.axis_index("section")
        for which in (0, 1):

            @pl.when(section == which)
            def _():
                for copy in self.copies(1 - which, which):
                    copy.start()

    def steps(self):
        def end():
            for copy in self.copies(0, 1):
                copy.wait()
            if self.added:
                self.out[0][...] = self.room[0][...].astype(jnp.float32) + self.room[1][...].astype(
                    jnp.float32
                )

        return [end]


class TextTask(Task):
    out_in_vmem = False
    greets = ("section", "frame", "both")

    def __init__(self, states):
        micros, rows, width = states.shape
        self.operands = (states,)
        self.outs = (jax.ShapeDtypeStruct((2, 4, rows, width), states.dtype),)
        self.scratch = (pltpu.SemaphoreType.DMA((8,)), pltpu.SemaphoreType.DMA((8,)))

    def copies(self):
        send_sems, recv_sems = self.room
        section, me = lax.axis_index("section"), lax.axis_index("frame")
        landing = self.out[0].at[section, me]
        copies = []
        for far in (0, 1):
            micro = section if far == 0 else 1 - section
            for k, frame in enumerate((me,) + frame_partners()):
                slot = far * 4 + k
                source = self.ins[0].at[micro]
                if slot == 0:
                    copies.append(pltpu.make_async_copy(source, landing, send_sems.at[0]))
                    continue
                target = {"section": micro, "frame": frame}
                copies.append(remote(source, landing, send_sems.at[slot], recv_sems.at[slot], target))
        return copies

    def begin(self):
        for copy in self.copies():
            copy.start()

    def steps(self):
        def end():
            for copy in self.copies():
                copy.wait()

        return [end]


class TotalTask(Task):
    greets = ("section", "head")

    def __init__(self, part):
        rows, width = part.shape
        self.share = rows // 4
        self.operands = (part,)
        self.outs = (jax.ShapeDtypeStruct((rows, width), jnp.bfloat16),)
        piece = (self.share, width)
        self.scratch = (
            pltpu.VMEM((4,) + piece, jnp.bfloat16),
            pltpu.VMEM((2,) + piece, jnp.bfloat16),
            pltpu.SemaphoreType.DMA((4,)),
            pltpu.SemaphoreType.DMA((4,)),
            pltpu.SemaphoreType.DMA((2,)),
            pltpu.SemaphoreType.DMA((4,)),
            pltpu.SemaphoreType.DMA((4,)),
        )

    def partners(self):
        me = lax.axis_index("head")
        return [lax.rem(me + by, 4) for by in (1, 2, 3)]

    def spread(self):
        landing, _, send_sems, recv_sems = self.room[:4]
        me = lax.axis_index("head")
        away = [
            remote(
                self.ins[0].at[span(partner, self.share)],
                landing.at[by],
                send_sems.at[by],
                recv_sems.at[by],
                {"head": partner},
            )
            for by, partner in enumerate(self.partners(), 1)
        ]
        stay = pltpu.make_async_copy(self.ins[0].at[span(me, self.share)], landing.at[0], send_sems.at[0])
        return away + [stay]

    def over(self):
        sums, sems = self.room[1], self.room[4]
        target = {"section": 1 - lax.axis_index("section")}
        return remote(sums.at[0], sums.at[1], sems.at[0], sems.at[1], target)

    def gather(self):
        send_sems, recv_sems = self.room[5:]
        mine = self.out[0].at[span(lax.axis_index("head"), self.share)]
        return [
            remote(mine, mine, send_sems.at[by], recv_sems.at[by], {"head": partner})
            for by, partner in enumerate(self.partners(), 1)
        ]

    def begin(self):
        for copy in self.spread():
            copy.start()

    def steps(self):
        landing, sums = self.room[:2]

        def first():
            for copy in self.spread():
                copy.wait()
            total = landing[0].astype(jnp.float32)
            for by in (1, 2, 3):
                total = total + landing[by].astype(jnp.float32)
            sums[0] = total.astype(jnp.bfloat16)
            self.over().start()

        def second():
            self.over().wait()
            total = sums[0].astype(jnp.float32) + sums[1].astype(jnp.float32)
            self.out[0][span(lax.axis_index("head"), self.share), :] = total.astype(jnp.bfloat16)
            for copy in self.gather():
                copy.start()

        def third():
            for copy in self.gather():
                copy.wait()

        return [first, second, third]


class VectorTask(Task):
    greets = ("section", "frame")

    def __init__(self, grads):
        self.operands = (grads,)
        shape = grads.shape[1:]
        self.outs = (jax.ShapeDtypeStruct(shape, jnp.float32),)
        self.scratch = (
            pltpu.VMEM((4,) + grads.shape, jnp.float32),
            pltpu.VMEM((3,) + shape, jnp.float32),
            pltpu.SemaphoreType.DMA((4,)),
            pltpu.SemaphoreType.DMA((4,)),
            pltpu.SemaphoreType.DMA((2,)),
        )

    def spread(self):
        landing, _, send_sems, recv_sems, _ = self.room
        away = [
            remote(self.ins[0], landing.at[k], send_sems.at[k], recv_sems.at[k], {"frame": partner})
            for k, partner in enumerate(frame_partners(), 1)
        ]
        return away + [pltpu.make_async_copy(self.ins[0], landing.at[0], send_sems.at[0])]

    def over(self):
        sums, sems = self.room[1], self.room[4]
        target = {"section": 1 - lax.axis_index("section")}
        return remote(sums.at[0], sums.at[1], sems.at[0], sems.at[1], target)

    def begin(self):
        for copy in self.spread():
            copy.start()

    def steps(self):
        landing, sums = self.room[:2]
        section = lax.axis_index("section")

        def first():
            for copy in self.spread():
                copy.wait()
            total = [
                (landing[0, layer] + landing[1, layer]) + (landing[2, layer] + landing[3, layer])
                for layer in (0, 1)
            ]
            for which in (0, 1):

                @pl.when(section == which)
                def _():
                    sums[0] = total[1 - which]
                    sums[2] = total[which]

            self.over().start()

        def second():
            self.over().wait()
            self.out[0][...] = sums[2] + sums[1]

        return [first, second]


def greet(kinds):
    barrier = pltpu.get_barrier_semaphore()
    section, head, frame = (lax.axis_index(a) for a in ("section", "head", "frame"))
    targets = []
    if "frame" in kinds:
        targets += [{"frame": other} for other in frame_partners()]
    if "section" in kinds:
        targets.append({"section": 1 - section})
    if "both" in kinds:
        targets += [{"section": 1 - section, "frame": other} for other in frame_partners()]
    if "head" in kinds:
        targets += [{"head": lax.rem(head + by, 4)} for by in (1, 2, 3)]
    for target in targets:
        pl.semaphore_signal(barrier, 1, device_id=target, device_id_type=MESH_IDS)
    if "line" not in kinds or "head" in kinds:
        pl.semaphore_wait(barrier, len(targets))
        return

    for way in (-1, 1):
        other = head + way

        @pl.when((other >= 0) & (other < 4))
        def _():
            pl.semaphore_signal(barrier, 1, device_id={"head": other}, device_id_type=MESH_IDS)

    is_end = (head == 0) | (head == 3)

    @pl.when(is_end)
    def _():
        pl.semaphore_wait(barrier, len(targets) + 1)

    @pl.when(jnp.logical_not(is_end))
    def _():
        pl.semaphore_wait(barrier, len(targets) + 2)


def call(body, operands, outs, scratch, kinds, collective_id, tasks=(), picked=()):
    whole, anywhere = pl.BlockSpec(memory_space=pltpu.VMEM), pl.BlockSpec(memory_space=pl.ANY)
    in_specs, out_specs = [whole] * len(operands), [whole] * len(outs)
    operands, all_outs, scratch = list(operands), list(outs), list(scratch)
    n_plain, n_scratch = len(operands), len(scratch)
    for own, other, _ in picked:
        operands += [own, other]
        in_specs += [anywhere] * 2
        scratch.append(pltpu.VMEM(own.shape, own.dtype))
    if picked:
        scratch.append(pltpu.SemaphoreType.DMA((len(picked),)))
    counts = [(len(operands), len(outs), len(scratch))]
    kinds = set(kinds)
    for task in tasks:
        kinds |= set(task.greets)
        in_specs += [anywhere] * len(task.operands)
        out_specs += [whole if task.out_in_vmem else anywhere] * len(task.outs)
        operands += task.operands
        all_outs += task.outs
        scratch += task.scratch
        counts.append((len(task.operands), len(task.outs), len(task.scratch)))
    n_in, n_out = len(operands), len(all_outs)

    def kernel(*refs):
        groups = [list(refs[:n_in]), list(refs[n_in : n_in + n_out]), list(refs[n_in + n_out :])]
        bound = []
        for sizes in counts:
            bound.append([])
            for group, size in zip(groups, sizes):
                bound[-1].append(group[:size])
                del group[:size]
        for task, parts in zip(tasks, bound[1:]):
            task.bind(*parts)
        ins, main_outs, room = bound[0]
        section = lax.axis_index("section")

        def fetch(index, from_other):
            source = ins[n_plain + 2 * index + from_other]
            return pltpu.make_async_copy(source, room[n_scratch + index], room[-1].at[index])

        for index, (_, _, layer) in enumerate(picked):

            @pl.when(section == layer)
            def _():
                fetch(index, 0).start()

            @pl.when(section != layer)
            def _():
                fetch(index, 1).start()

        greet(kinds)
        for task in tasks:
            task.begin()
        for index in range(len(picked)):
            fetch(index, 0).wait()
        if body is not None:
            body(ins[:n_plain] + room[n_scratch : n_scratch + len(picked)], main_outs, room[:n_scratch])
        queues = [task.steps() for task in tasks]
        while any(queues):
            for queue in queues:
                if queue:
                    queue.pop(0)()

    results = pl.pallas_call(
        kernel,
        out_shape=all_outs,
        in_specs=in_specs,
        out_specs=out_specs,
        scratch_shapes=scratch,
        cost_estimate=BUSY,
        compiler_params=pltpu.CompilerParams(
            collective_id=collective_id, has_side_effects=True, vmem_limit_bytes=VMEM_BYTES
        ),
    )(*operands)
    results = list(results)
    main, results = results[: len(outs)], results[len(outs) :]
    carried = []
    for task in tasks:
        carried.append(results[: len(task.outs)])
        results = results[len(task.outs) :]
    return main, [c[0] for c in carried]


def chunking(rows):
    return max(1, min(16, rows // 16))


def nt_product(left, right):
    return lax.dot_general(left, right, (((1,), (1,)), ((), ())), preferred_element_type=jnp.float32)


def plain_product(left, right):
    return jnp.dot(left, right, preferred_element_type=jnp.float32)


def norm_parts(v):
    average = jnp.mean(v, axis=-1, keepdims=True)
    centered = v - average
    inverse = lax.rsqrt(jnp.mean(centered * centered, axis=-1, keepdims=True) + EPS)
    return centered * inverse, inverse


def line_scratch(rows, width):
    pieces = chunking(rows)
    return [pltpu.VMEM((rows, width), jnp.bfloat16)] * 4 + [pltpu.SemaphoreType.DMA((pieces,))] * 6


def line_sum(rows, room, partial_rows, finish_rows, prepare=None):
    send, recv, across, held, send_in, recv_in, send_across, recv_across, send_out, recv_out = room
    pieces = chunking(rows)
    place = lax.axis_index("head")
    step = rows // pieces
    per_block = max(1, BLOCK // step)
    is_end = (place == 0) | (place == 3)
    inner = {"head": jnp.where(place == 0, 1, 2)}
    outer = {"head": jnp.where(place == 1, 0, 3)}
    peer = {"head": 3 - place}

    def inwards(piece):
        at = span(piece, step)
        return remote(send.at[at], recv.at[at], send_in.at[piece], recv_in.at[piece], inner)

    def crossing(piece):
        at = span(piece, step)
        return remote(send.at[at], across.at[at], send_across.at[piece], recv_across.at[piece], peer)

    def outwards(piece):
        at = span(piece, step)
        return remote(held.at[at], held.at[at], send_out.at[piece], recv_out.at[piece], outer)

    def part_of(piece):
        if prepare is not None:

            @pl.when(lax.rem(piece, per_block) == 0)
            def _():
                prepare(lax.div(piece, per_block))

        return partial_rows(span(piece, step))

    @pl.when(is_end)
    def _():
        def give(piece, carry):
            send[span(piece, step), :] = part_of(piece).astype(jnp.bfloat16)
            inwards(piece).start()
            return carry

        lax.fori_loop(0, pieces, give, 0)

        def take(piece, carry):
            outwards(piece).wait_recv()
            finish_rows(span(piece, step), piece)
            return carry

        lax.fori_loop(0, pieces, take, 0)

        def drain(piece, carry):
            inwards(piece).wait_send()
            return carry

        lax.fori_loop(0, pieces, drain, 0)

    @pl.when(jnp.logical_not(is_end))
    def _():
        def add(piece):
            at = span(piece, step)
            part = part_of(piece)
            inwards(piece).wait_recv()
            send[at, :] = (part + recv[at, :].astype(jnp.float32)).astype(jnp.bfloat16)
            crossing(piece).start()

        def settle(piece):
            at = span(piece, step)
            crossing(piece).wait_recv()
            total = send[at, :].astype(jnp.float32) + across[at, :].astype(jnp.float32)
            held[at, :] = total.astype(jnp.bfloat16)
            outwards(piece).start()
            finish_rows(at, piece)

        lag = min(LAG, pieces)

        def both(t, carry):
            @pl.when(t < pieces)
            def _():
                add(t)

            @pl.when(t >= lag)
            def _():
                settle(t - lag)

            return carry

        lax.fori_loop(0, pieces + lag, both, 0)

        def drain(piece, carry):
            crossing(piece).wait_send()
            outwards(piece).wait_send()
            return carry

        lax.fori_loop(0, pieces, drain, 0)


def sum_forward(kind, layer, operands, weights, base, gain, shift, mode, collective_id, tasks):
    rows, width = base.shape
    wide = [jax.ShapeDtypeStruct((rows, width), jnp.float32)]
    low = jax.ShapeDtypeStruct((rows, width), jnp.bfloat16)
    outs = wide + [low] * {"norm": 1, "next": 2, "end": 0}[mode]
    n_main = len(outs)
    block = min(BLOCK, rows)
    scratch = line_scratch(rows, width)
    if kind == "self":
        columns = operands[0].shape[0]
        scratch.append(pltpu.VMEM((rows, columns), jnp.bfloat16))
    elif kind == "cross":
        columns = weights[0][0].shape[1]
        states = operands[1].shape[0]
        outs += [jax.ShapeDtypeStruct((rows, columns), jnp.bfloat16)] * 2
        scratch.append(pltpu.VMEM((columns, states), jnp.bfloat16))
    else:
        hidden = weights[0][0].shape[1]
        outs += [
            jax.ShapeDtypeStruct((rows, hidden), jnp.float32),
            jax.ShapeDtypeStruct((rows, hidden), jnp.bfloat16),
        ]

    def body(ins, outs, scratch):
        *parts, base, gain, shift = ins[: len(operands) + 3]
        matrices = ins[len(operands) + 3 :]
        room, extra = scratch[:10], scratch[10:]
        result = outs[0]
        prepare = None
        if kind == "self":
            (left,) = extra
            left[...] = parts[0][...].T
        elif kind == "cross":
            queries, left = outs[n_main:]
            normed, keys, values, seg = parts
            (values_t,) = extra
            values_t[...] = values[...].T

            def prepare(index):
                at = span(index, block)
                query = plain_product(normed[at, :], matrices[0][...]).astype(jnp.bfloat16)
                queries[at, :] = query
                query_t = query.T
                allowed = text_mask(states, seg[:, at])
                mixed = []
                for head in range(columns // HEAD):
                    cols = slice(head * HEAD, (head + 1) * HEAD)
                    scores = plain_product(keys[:, cols], query_t[cols, :]) * HEAD ** (-0.5)
                    scores = jnp.where(allowed, scores, masked_score)
                    e = jnp.exp(scores - jnp.max(scores, axis=0, keepdims=True))
                    total = jnp.sum(e, axis=0, keepdims=True)
                    value = plain_product(values_t[cols, :], e.astype(jnp.bfloat16))
                    mixed.append((value * (1.0 / total)).astype(jnp.bfloat16))
                left[at, :] = jnp.concatenate(mixed, axis=0).T

        else:
            before, left = outs[n_main:]
            (normed,) = parts

            def prepare(index):
                at = span(index, block)
                u = plain_product(normed[at, :], matrices[0][...])
                before[at, :] = u
                left[at, :] = (0.5 * u * (1.0 + lax.erf(u * inv_sqrt_two))).astype(jnp.bfloat16)

        def partial_rows(at):
            return plain_product(left[at, :], matrices[-1][...])

        def finish_rows(at, piece):
            value = base[at, :].astype(jnp.float32) + room[3][at, :].astype(jnp.float32)
            result[at, :] = value
            if mode == "next":
                rounded = value.astype(jnp.bfloat16)
                outs[2][at, :] = rounded
                value = rounded.astype(jnp.float32)
            if mode != "end":
                standard, _ = norm_parts(value)
                outs[1][at, :] = (standard * gain[...] + shift[...]).astype(jnp.bfloat16)

        line_sum(rows, room, partial_rows, finish_rows, prepare)

    return call(
        body, [*operands, base, gain[None], shift[None]], outs, scratch, ("line",), collective_id, tasks,
        [(*pair, layer) for pair in weights],
    )


def text_mask(states, seg):
    item = lax.rem(lax.div(lax.broadcasted_iota(jnp.int32, (states, 1), 0), TEXT // 4), ITEMS)
    return item == seg


def sum_backward(kind, layer, operands, weights, value, gain, upstream, collective_id, tasks, spare=None):
    rows, width = value.shape
    vector = jax.ShapeDtypeStruct((1, width), jnp.float32)
    low = jax.ShapeDtypeStruct((rows, width), jnp.bfloat16)
    outs = [jax.ShapeDtypeStruct((rows, width), jnp.float32), low, vector, vector]
    if spare is not None:
        outs.append(low)
    n_main = len(outs)
    block = min(BLOCK, rows)
    pieces = chunking(rows)
    scratch = line_scratch(rows, width)
    scratch += [pltpu.VMEM((pieces, 1, width), jnp.float32)] * 2
    scratch += [pltpu.SemaphoreType.DMA((pieces,))] * 2
    if kind == "self":
        columns = operands[0].shape[0]
        scratch.append(pltpu.VMEM((rows, columns), jnp.bfloat16))
    elif kind == "cross":
        columns = weights[0][0].shape[0]
        states = operands[2].shape[0]
        outs += [
            jax.ShapeDtypeStruct((rows, columns), jnp.bfloat16),
            jax.ShapeDtypeStruct((states, 2 * columns), jnp.bfloat16),
        ]
        scratch += [pltpu.VMEM((columns, states), jnp.bfloat16), pltpu.VMEM((states, 2 * columns), jnp.float32)]
    else:
        hidden = weights[0][0].shape[0]
        outs.append(jax.ShapeDtypeStruct((rows, hidden), jnp.bfloat16))

    def body(ins, outs, scratch):
        n_fixed = len(operands) + 3 + (spare is not None)
        *parts, value, gain, upstream = ins[: len(operands) + 3]
        matrices = ins[n_fixed:]
        room, (gain_parts, shift_parts, send_cross, recv_cross, *extra) = scratch[:10], scratch[10:]
        result, result_low, gain_grad, shift_grad = outs[:4]
        section = lax.axis_index("section")
        prepare = None
        if kind == "self":
            (left,) = extra
            left[...] = parts[0][...].T
        elif kind == "cross":
            left, state_grads = outs[n_main:]
            keys_t, sums = extra
            grad_low, queries, keys, values, seg = parts
            keys_t[...] = keys[...].T
            sums[...] = jnp.zeros_like(sums)

            def prepare(index):
                at = span(index, block)
                grad = nt_product(grad_low[at, :], matrices[0][...]).astype(jnp.bfloat16)
                query = queries[at, :]
                grad_t, query_t = grad.T, query.T
                allowed = text_mask(states, seg[:, at])
                query_grads = []
                for head in range(columns // HEAD):
                    cols = slice(head * HEAD, (head + 1) * HEAD)
                    more = slice(columns + head * HEAD, columns + (head + 1) * HEAD)
                    scores = plain_product(keys[:, cols], query_t[cols, :]) * HEAD ** (-0.5)
                    scores = jnp.where(allowed, scores, masked_score)
                    e = jnp.exp(scores - jnp.max(scores, axis=0, keepdims=True))
                    p = e * (1.0 / jnp.sum(e, axis=0, keepdims=True))
                    slope = plain_product(values[:, cols], grad_t[cols, :])
                    weighted = p * slope
                    ds = weighted - p * jnp.sum(weighted, axis=0, keepdims=True)
                    ds = ds.astype(jnp.bfloat16)
                    query_grads.append(
                        (plain_product(keys_t[cols, :], ds) * HEAD ** (-0.5)).astype(jnp.bfloat16)
                    )
                    sums[:, cols] += plain_product(ds, query[:, cols]) * HEAD ** (-0.5)
                    sums[:, more] += plain_product(p.astype(jnp.bfloat16), grad[:, cols])
                left[at, :] = jnp.concatenate(query_grads, axis=0).T

        else:
            (left,) = outs[n_main:]
            grad_out, before = parts

            def prepare(index):
                at = span(index, block)
                grad = nt_product(grad_out[at, :], matrices[0][...])
                u = before[at, :]
                slope = 0.5 * (1.0 + lax.erf(u * inv_sqrt_two)) + u * jnp.exp(-0.5 * u * u) * inv_sqrt_tau
                left[at, :] = (grad * slope).astype(jnp.bfloat16)

        def partial_rows(at):
            if kind == "self":
                return plain_product(left[at, :], matrices[-1][...])
            return nt_product(left[at, :], matrices[-1][...])

        def over(at, piece, source):
            target = {"section": 1 - section}
            return remote(source.at[at], outs[4].at[at], send_cross.at[piece], recv_cross.at[piece], target)

        def finish_rows(at, piece):
            grad = room[3][at, :].astype(jnp.float32)
            standard, inverse = norm_parts(value[at, :].astype(jnp.float32))
            scaled = grad * gain[...]
            through = inverse * (
                scaled
                - jnp.mean(scaled, axis=-1, keepdims=True)
                - standard * jnp.mean(scaled * standard, axis=-1, keepdims=True)
            )
            total = through + upstream[at, :].astype(jnp.float32)
            result[at, :] = total
            result_low[at, :] = total.astype(jnp.bfloat16)
            gain_parts[piece] = jnp.sum(grad * standard, axis=0, keepdims=True)
            shift_parts[piece] = jnp.sum(grad, axis=0, keepdims=True)
            if spare is not None:

                @pl.when(section == 0)
                def _():
                    over(at, piece, ins[len(operands) + 3]).start()

                @pl.when(section == 1)
                def _():
                    over(at, piece, result_low).start()

        line_sum(rows, room, partial_rows, finish_rows, prepare)
        gain_grad[...] = jnp.sum(gain_parts[...], axis=0)
        shift_grad[...] = jnp.sum(shift_parts[...], axis=0)
        if kind == "cross":
            state_grads[...] = sums[...].astype(jnp.bfloat16)
        if spare is not None:

            def drain(piece, carry):
                over(span(piece, rows // pieces), piece, result_low).wait()
                return carry

            lax.fori_loop(0, pieces, drain, 0)

    fixed = [*operands, value, gain[None], upstream]
    kinds = ("line",)
    if spare is not None:
        fixed.append(spare)
        kinds = ("line", "section")
    return call(
        body, fixed, outs, scratch, kinds, collective_id, tasks, [(*pair, layer) for pair in weights]
    )


def masked_scores(keys, query_t, begins, start):
    reach, block = keys.shape[0], query_t.shape[1]
    scores = plain_product(keys, query_t)
    key_pos = lax.broadcasted_iota(jnp.int32, (reach, 1), 0)
    query_pos = start + lax.broadcasted_iota(jnp.int32, (1, block), 1)
    allowed = (key_pos <= query_pos) & (key_pos >= begins)
    return jnp.where(allowed, scores * HEAD ** (-0.5), masked_score)


def to_frames(source, landing, sems):
    me = lax.axis_index("frame")
    send_sems, recv_sems = sems
    return [
        remote(source(other), landing(me), send_sems.at[k], recv_sems.at[k], {"frame": other})
        for k, other in enumerate(frame_partners())
    ]


def self_forward(normed, weight, begins, layer, collective_id, tasks):
    rows, frames, width = normed.shape[0], 4, 3 * HEAD
    dma = pltpu.SemaphoreType.DMA((frames - 1,))
    outs = [
        jax.ShapeDtypeStruct((width, rows * frames), jnp.bfloat16),
        jax.ShapeDtypeStruct((frames * HEAD, rows), jnp.bfloat16),
    ]
    scratch = [
        pltpu.VMEM((frames, width, rows), jnp.bfloat16),
        pltpu.VMEM((rows * frames, HEAD), jnp.bfloat16),
        pltpu.VMEM((frames, HEAD, rows), jnp.bfloat16),
        dma,
        dma,
        dma,
        dma,
    ]

    def body(ins, outs, scratch):
        normed, begins, weight = ins
        heads_t, out = outs
        own, keys, mixed_t, *sems = scratch
        me = lax.axis_index("frame")
        partners = frame_partners()
        block = min(2 * BLOCK, rows)
        arriving = to_frames(lambda g: own.at[g], lambda f: heads_t.at[:, span(f, rows)], sems[:2])
        leaving = to_frames(lambda g: mixed_t.at[g], lambda f: out.at[span(f, HEAD), :], sems[2:])

        def project(other):
            return nt_product(weight[span(other, width), :], normed[...]).astype(jnp.bfloat16)

        for k in (2, 1, 0):
            own[partners[k]] = project(partners[k])
            arriving[k].start()
        heads_t[:, span(me, rows)] = project(me)
        for copy in arriving:
            copy.wait()
        keys[...] = heads_t[HEAD : 2 * HEAD, :].T
        for target in range(frames):
            for start in range(target * rows, (target + 1) * rows, block):
                reach = start + block
                scores = masked_scores(
                    keys[:reach, :], heads_t[:HEAD, start:reach], begins[:, start:reach], start
                )
                e = jnp.exp(scores - jnp.max(scores, axis=0, keepdims=True))
                total = jnp.sum(e, axis=0, keepdims=True)
                mixed = plain_product(heads_t[2 * HEAD :, :reach], e.astype(jnp.bfloat16))
                at = start - target * rows
                mixed_t[target, :, at : at + block] = (mixed * (1.0 / total)).astype(jnp.bfloat16)

            for copy, other in zip(leaving, partners):

                @pl.when(other == target)
                def _():
                    copy.start()

        out[span(me, HEAD), :] = mixed_t[me]
        for copy in leaving:
            copy.wait()

    return call(
        body, [normed, begins], outs, scratch, ("frame",), collective_id, tasks, [(*weight, layer)]
    )


def self_backward(heads_t, grad_low, weight, begins, layer, collective_id, tasks):
    rows, frames, width = grad_low.shape[0], 4, 3 * HEAD
    all_rows = rows * frames
    dma = pltpu.SemaphoreType.DMA((frames - 1,))
    outs = [jax.ShapeDtypeStruct((frames * width, rows), jnp.bfloat16)]
    scratch = [
        pltpu.VMEM((frames, HEAD, rows), jnp.bfloat16),
        pltpu.VMEM((HEAD, all_rows), jnp.bfloat16),
        pltpu.VMEM((4, all_rows, HEAD), jnp.bfloat16),
        pltpu.VMEM((all_rows, HEAD), jnp.float32),
        pltpu.VMEM((all_rows, HEAD), jnp.float32),
        pltpu.VMEM((frames, width, rows), jnp.bfloat16),
        dma,
        dma,
        dma,
        dma,
    ]

    def body(ins, outs, scratch):
        heads_t, grad_low, begins, weight = ins
        (out,) = outs
        own, grad_t, columns, key_sum, value_sum, grads_t, *sems = scratch
        me = lax.axis_index("frame")
        partners = frame_partners()
        block = min(2 * BLOCK, rows)
        scale = HEAD ** (-0.5)
        arriving = to_frames(lambda g: own.at[g], lambda f: grad_t.at[:, span(f, rows)], sems[:2])
        leaving = to_frames(lambda g: grads_t.at[g], lambda f: out.at[span(f, width), :], sems[2:])

        def project(other):
            return nt_product(weight[span(other, HEAD), :], grad_low[...]).astype(jnp.bfloat16)

        for k in (2, 1, 0):
            own[partners[k]] = project(partners[k])
            arriving[k].start()
        grad_t[:, span(me, rows)] = project(me)
        key_sum[...] = jnp.zeros_like(key_sum)
        value_sum[...] = jnp.zeros_like(value_sum)
        for part in range(3):
            columns[part] = heads_t[part * HEAD : (part + 1) * HEAD, :].T
        for copy in arriving:
            copy.wait()
        columns[3] = grad_t[...].T
        for target in reversed(range(frames)):
            for start in reversed(range(target * rows, (target + 1) * rows, block)):
                reach = start + block
                scores = masked_scores(
                    columns[1, :reach, :], heads_t[:HEAD, start:reach], begins[:, start:reach], start
                )
                e = jnp.exp(scores - jnp.max(scores, axis=0, keepdims=True))
                p = e * (1.0 / jnp.sum(e, axis=0, keepdims=True))
                slope = plain_product(columns[2, :reach, :], grad_t[:, start:reach])
                weighted = p * slope
                ds = (weighted - p * jnp.sum(weighted, axis=0, keepdims=True)).astype(jnp.bfloat16)
                value_sum[:reach, :] += plain_product(p.astype(jnp.bfloat16), columns[3, start:reach, :])
                key_sum[:reach, :] += plain_product(ds, columns[0, start:reach, :])
                here = slice(start - target * rows, reach - target * rows)
                grads_t[target, :HEAD, here] = (
                    plain_product(heads_t[HEAD : 2 * HEAD, :reach], ds) * scale
                ).astype(jnp.bfloat16)
                grads_t[target, HEAD : 2 * HEAD, here] = (
                    (key_sum[start:reach, :] * scale).T.astype(jnp.bfloat16)
                )
                grads_t[target, 2 * HEAD :, here] = value_sum[start:reach, :].T.astype(jnp.bfloat16)

            for copy, other in zip(leaving, partners):

                @pl.when(other == target)
                def _():
                    copy.start()

        out[span(me, width), :] = grads_t[me]
        for copy in leaving:
            copy.wait()

    return call(
        body,
        [heads_t, grad_low, begins],
        outs,
        scratch,
        ("frame",),
        collective_id,
        tasks,
        [(*weight, layer)],
    )


def matmul(left_side, right_side):
    return jnp.dot(left_side, right_side, preferred_element_type=jnp.float32)


def matmul_tn(left_side, right_side):
    return lax.dot_general(
        left_side, right_side, (((0,), (0,)), ((), ())), preferred_element_type=jnp.float32
    )


def matmul_nt(left_side, right_side):
    return lax.dot_general(
        left_side, right_side, (((1,), (1,)), ((), ())), preferred_element_type=jnp.float32
    )


def layer_norm(signal, gain_vec, shift_vec):
    average = jnp.mean(signal, axis=-1, keepdims=True)
    centered = signal - average
    variance = jnp.mean(centered * centered, axis=-1, keepdims=True)
    return centered * lax.rsqrt(variance + 1e-05) * gain_vec + shift_vec


def norm_back(signal, gain_vec, upstream):
    average = jnp.mean(signal, axis=-1, keepdims=True)
    centered = signal - average
    inverse = lax.rsqrt(jnp.mean(centered * centered, axis=-1, keepdims=True) + 1e-05)
    standard = centered * inverse
    scaled = upstream * gain_vec
    through = inverse * (
        scaled
        - jnp.mean(scaled, axis=-1, keepdims=True)
        - standard * jnp.mean(scaled * standard, axis=-1, keepdims=True)
    )
    return (through, jnp.sum(upstream * standard, axis=0), jnp.sum(upstream, axis=0))


def head_total(partial_sum):
    return lax.psum(partial_sum.astype(jnp.bfloat16), "head").astype(jnp.float32)


def swapped(x):
    return lax.ppermute(x, "section", [(0, 1), (1, 0)])


def split_heads(matrix):
    return matrix.reshape(matrix.shape[0], matrix.shape[1] // HEAD, HEAD)


def softmax_rows(query, key_rows, allowed):
    logits = jnp.einsum(
        "qhd,khd->hqk",
        split_heads(query),
        split_heads(key_rows),
        preferred_element_type=jnp.float32,
    ) * HEAD ** (-0.5)
    logits = jnp.where(allowed[None], logits, masked_score)
    exponent = jnp.exp(logits - jnp.max(logits, axis=-1, keepdims=True))
    return exponent / jnp.sum(exponent, axis=-1, keepdims=True)


def attend(query, key_rows, value_rows, allowed):
    weights_low = softmax_rows(query, key_rows, allowed).astype(jnp.bfloat16)
    result = jnp.einsum(
        "hqk,khd->qhd", weights_low, split_heads(value_rows), preferred_element_type=jnp.float32
    )
    return result.reshape(query.shape).astype(jnp.bfloat16)


def attend_back(query, key_rows, value_rows, allowed, grad_out):
    probabilities = softmax_rows(query, key_rows, allowed)
    weights_low = probabilities.astype(jnp.bfloat16)
    grad_heads = split_heads(grad_out)
    grad_prob = jnp.einsum(
        "qhd,khd->hqk", grad_heads, split_heads(value_rows), preferred_element_type=jnp.float32
    )
    centre = jnp.sum(probabilities * grad_prob, axis=-1, keepdims=True)
    grad_logit = (probabilities * (grad_prob - centre)).astype(jnp.bfloat16)
    scale = HEAD ** (-0.5)
    grad_query = (
        jnp.einsum(
            "hqk,khd->qhd", grad_logit, split_heads(key_rows), preferred_element_type=jnp.float32
        )
        * scale
    )
    grad_keys = (
        jnp.einsum(
            "hqk,qhd->khd", grad_logit, split_heads(query), preferred_element_type=jnp.float32
        )
        * scale
    )
    grad_values = jnp.einsum(
        "hqk,qhd->khd", weights_low, grad_heads, preferred_element_type=jnp.float32
    )
    return (
        grad_query.reshape(query.shape),
        grad_keys.reshape(key_rows.shape),
        grad_values.reshape(value_rows.shape),
    )


def sum_rows(rows):
    return jnp.concatenate(rows, axis=0)


def on_four_frames(inputs, lengths, text, cotangent, vector_args, matrix_args):
    section = lax.axis_index("section")
    at_zero = section == 0
    frame_index = lax.axis_index("frame")
    micro_count, rows_dev, model_width = inputs.shape
    rows_all = rows_dev * 4
    (
        query_weight,
        key_weight,
        value_weight,
        output_weight,
        cross_query,
        cross_key,
        cross_value,
        cross_output,
        expand_weight,
        reduce_weight,
    ) = (w[0] for w in matrix_args)
    columns = query_weight.shape[1]
    heads = columns // HEAD

    def by_section(first, second):
        return jnp.where(at_zero, first, second)

    own_vectors = jnp.pad(jnp.concatenate(vector_args, axis=0), ((0, 2), (0, 0)))
    heads_weight = jnp.stack(
        [w.T.reshape(heads, HEAD, model_width) for w in (query_weight, key_weight, value_weight)], axis=1
    ).reshape(3 * columns, model_width)
    _, (other_heads, other_vectors) = call(
        None, [], [], [], (), 1, [WeightTask(heads_weight), CrossTask(own_vectors, own_vectors, False)]
    )
    vectors = [by_section(own_vectors, other_vectors), by_section(other_vectors, own_vectors)]
    heads_pair = (heads_weight, other_heads)
    text_local = text.reshape(-1, model_width)
    text_states = jnp.concatenate(
        [matmul(text_local, cross_key), matmul(text_local, cross_value)], axis=1
    ).astype(jnp.bfloat16)
    text_states = text_states.reshape(micro_count, -1, 2 * columns)

    item_ends = jnp.cumsum(lax.dynamic_index_in_dim(lengths, section, 0, keepdims=False))
    passed = jnp.arange(rows_all, dtype=jnp.int32)[None, :] >= item_ends[:, None]
    begins = jnp.max(jnp.where(passed, item_ends[:, None], 0), axis=0, keepdims=True).astype(jnp.int32)
    seg = jnp.sum(passed.astype(jnp.int32), axis=0, keepdims=True)
    seg = lax.dynamic_slice_in_dim(seg, frame_index * rows_dev, rows_dev, 1)

    entering = lax.dynamic_index_in_dim(inputs, section, 0, keepdims=False)
    normed = layer_norm(entering.astype(jnp.float32), vectors[0][0], vectors[0][1]).astype(jnp.bfloat16)
    saved, results = [], []
    for layer in range(2):
        gains = vectors[layer]
        first = layer == 0
        (heads_t, attended_t), carried = self_forward(
            normed,
            heads_pair,
            begins,
            layer,
            2 + layer,
            [
                WeightTask(output_weight),
                WeightTask(cross_query),
                WeightTask(cross_output),
                TextTask(text_states),
            ]
            if first
            else [],
        )
        if first:
            output_pair, query_pair, cross_pair = (
                (own, other) for own, other in zip((output_weight, cross_query, cross_output), carried)
            )
            states = carried[3].reshape(2, -1, 2 * columns)
        keys, values = states[layer, :, :columns], states[layer, :, columns:]
        (middle, second_normed), carried = sum_forward(
            "self",
            layer,
            [attended_t],
            [output_pair],
            entering,
            gains[2],
            gains[3],
            "norm",
            4 + layer,
            [WeightTask(expand_weight)] if first else [],
        )
        if first:
            expand_pair = (expand_weight, carried[0])
        (latter, third_normed, queries, cross_att), carried = sum_forward(
            "cross",
            layer,
            [second_normed, keys, values, seg],
            [query_pair, cross_pair],
            middle,
            gains[4],
            gains[5],
            "norm",
            6 + layer,
            [WeightTask(reduce_weight)] if first else [],
        )
        if first:
            reduce_pair = (reduce_weight, carried[0])
        after = vectors[1]
        (result, *lows, before, hidden), _ = sum_forward(
            "feed",
            layer,
            [third_normed],
            [expand_pair, reduce_pair],
            latter,
            after[0],
            after[1],
            "next" if first else "end",
            8 + layer,
            [],
        )
        saved.append(
            (
                entering,
                normed,
                heads_t,
                attended_t,
                middle,
                second_normed,
                queries,
                keys,
                values,
                cross_att,
                latter,
                third_normed,
                before,
                hidden,
            )
        )
        results.append(result)
        if first:
            normed, entering = lows

    upstream = lax.dynamic_index_in_dim(cotangent, section, 0, keepdims=False)
    grad_out = upstream.astype(jnp.bfloat16)
    in_grads, in_lows, vector_grads, shares = [None] * 2, [None] * 2, [None] * 2, [{}, {}]
    totals = {}

    def low_product(left, right):
        return matmul_tn(left, right).astype(jnp.bfloat16)

    for layer in (1, 0):
        last = layer == 0
        gains = vectors[layer]
        (
            entering,
            normed,
            heads_t,
            attended_t,
            middle,
            second_normed,
            queries,
            keys,
            values,
            cross_att,
            latter,
            third_normed,
            before,
            hidden,
        ) = saved[layer]
        mine, later = shares[layer], shares[1]

        def crossing(*names):
            return [CrossTask(mine[name], later[name], True) for name in names] if last else []

        tasks = [ShareTask(low_product(hidden, grad_out))]
        if not last:
            lows = (saved[1][0], results[1].astype(jnp.bfloat16))
            tasks.append(CrossTask(*lows, False))
        (grad_latter, grad_cross, third_gain_grad, third_shift_grad, grad_pre), carried = sum_backward(
            "feed",
            layer,
            [grad_out, before],
            [reduce_pair, expand_pair],
            latter,
            gains[4],
            upstream,
            10 + layer,
            tasks,
        )
        mine["reduce"] = carried[0]
        if not last:
            other_result = carried[1]

        tasks = [
            ShareTask(low_product(third_normed, grad_pre)),
            ShareTask(low_product(cross_att, grad_cross)),
        ]
        (grad_middle, grad_self, second_gain_grad, second_shift_grad, grad_queries, grad_states), carried = (
            sum_backward(
                "cross",
                layer,
                [grad_cross, queries, keys, values, seg],
                [cross_pair, query_pair],
                middle,
                gains[2],
                grad_latter,
                12 + layer,
                tasks + crossing("reduce"),
            )
        )
        mine["expand"], mine["cross_output"] = carried[:2]
        if last:
            totals["reduce"] = carried[2]

        tasks = [
            ShareTask(low_product(second_normed, grad_queries)),
            ShareTask(grad_states),
            ShareTask(matmul(attended_t, grad_self).astype(jnp.bfloat16)),
        ]
        (grad_heads_t,), carried = self_backward(
            heads_t,
            grad_self,
            output_pair,
            begins,
            layer,
            14 + layer,
            tasks + crossing("expand", "cross_output"),
        )
        mine["cross_query"], mine["states"], mine["output"] = carried[:3]
        if last:
            totals["expand"], totals["cross_output"] = carried[3:]

        grad_heads = lax.dot_general(
            normed, grad_heads_t, (((0,), (1,)), ((), ())), preferred_element_type=jnp.float32
        ).astype(jnp.bfloat16)
        tasks = [ShareTask(grad_heads)] + crossing("cross_query", "output")
        if last:
            tasks.append(CrossTask(mine["states"], later["states"], False))
        (in_grads[layer], in_lows[layer], first_gain_grad, first_shift_grad, *other_grad), carried = (
            sum_backward(
                "self",
                layer,
                [grad_heads_t],
                [heads_pair],
                entering,
                gains[0],
                grad_middle,
                16 + layer,
                tasks,
                in_lows[1] if last else None,
            )
        )
        mine["heads"] = carried[0]
        if last:
            totals["cross_query"], totals["output"], other_states = carried[1:]
        vector_grads[layer] = sum_rows(
            [
                first_gain_grad,
                first_shift_grad,
                second_gain_grad,
                second_shift_grad,
                third_gain_grad,
                third_shift_grad,
                jnp.zeros((2, model_width), jnp.float32),
            ]
        )
        grad_out = upstream = in_lows[layer]

    own_states = by_section(shares[0]["states"], shares[1]["states"])
    text_rows = sum_rows([by_section(own_states, other_states), by_section(other_states, own_states)])
    key_part, value_part = text_rows[:, :columns], text_rows[:, columns:]
    text_part = matmul_nt(key_part, cross_key) + matmul_nt(value_part, cross_value)
    _, (heads_total, text_grad, vector_total, cross_grads) = call(
        None,
        [],
        [],
        [],
        (),
        18,
        [
            CrossTask(shares[0]["heads"], shares[1]["heads"], True),
            TotalTask(text_part.astype(jnp.bfloat16)),
            VectorTask(jnp.stack(vector_grads)),
            ShareTask(low_product(text_local, text_rows)),
        ],
    )
    text_grad = text_grad.astype(jnp.float32).reshape(text.shape)
    vector_total = lax.dynamic_slice_in_dim(
        vector_total, frame_index * (model_width // 4), model_width // 4, 1
    )
    grad_query, grad_key, grad_value = (
        heads_total.reshape(-1, heads, 3, HEAD)[:, :, i].reshape(-1, columns) for i in range(3)
    )
    cross_grads = cross_grads.astype(jnp.float32)

    def both_micros(pair, other):
        own = by_section(*pair)
        other = other.astype(own.dtype)
        return jnp.where(at_zero, jnp.stack([own, other]), jnp.stack([other, own]))

    ordered = (
        vector_total[0],
        vector_total[1],
        grad_query,
        grad_key,
        grad_value,
        totals["output"],
        vector_total[2],
        vector_total[3],
        totals["cross_query"],
        cross_grads[:, :columns],
        cross_grads[:, columns:],
        totals["cross_output"],
        vector_total[4],
        vector_total[5],
        totals["expand"],
        totals["reduce"],
    )
    layer_outputs = both_micros(results, other_result)
    input_grads = both_micros(in_grads, other_grad[0])
    return (layer_outputs[None], input_grads[None], text_grad) + tuple(g[None] for g in ordered)


def self_attention(query, key_rows, value_rows, masks):
    all_keys = lax.all_gather(key_rows, "frame", axis=0, tiled=True)
    all_values = lax.all_gather(value_rows, "frame", axis=0, tiled=True)
    return attend(query, all_keys, all_values, masks["own"]), (query, all_keys, all_values)


def self_attention_back(kept, grad_out, masks):
    query, keys, values = kept
    grad_q, grad_k_all, grad_v_all = attend_back(query, keys, values, masks["own"], grad_out)
    grad_k, grad_v = (
        lax.psum_scatter(g.astype(jnp.bfloat16), "frame", scatter_dimension=0, tiled=True)
        for g in (grad_k_all, grad_v_all)
    )
    return grad_q.astype(jnp.bfloat16), grad_k, grad_v


def forward(entering, vectors, weights, cross_keys, cross_values, masks):
    first_gain, first_shift, second_gain, second_shift, third_gain, third_shift = vectors
    (
        query_weight,
        key_weight,
        value_weight,
        output_weight,
        cross_query,
        cross_output,
        expand_weight,
        reduce_weight,
    ) = weights
    signal = entering.astype(jnp.float32)
    first_normed = layer_norm(signal, first_gain, first_shift).astype(jnp.bfloat16)
    query = matmul(first_normed, query_weight).astype(jnp.bfloat16)
    key_rows = matmul(first_normed, key_weight).astype(jnp.bfloat16)
    value_rows = matmul(first_normed, value_weight).astype(jnp.bfloat16)
    attended, heads_kept = self_attention(query, key_rows, value_rows, masks)
    middle = signal + head_total(matmul(attended, output_weight))
    second_normed = layer_norm(middle, second_gain, second_shift).astype(jnp.bfloat16)
    cross_queries = matmul(second_normed, cross_query).astype(jnp.bfloat16)
    cross_att = attend(cross_queries, cross_keys, cross_values, masks["cross"])
    latter = middle + head_total(matmul(cross_att, cross_output))
    third_normed = layer_norm(latter, third_gain, third_shift).astype(jnp.bfloat16)
    hidden_pre = matmul(third_normed, expand_weight)
    hidden_act = jax.nn.gelu(hidden_pre, approximate=False).astype(jnp.bfloat16)
    result = latter + head_total(matmul(hidden_act, reduce_weight))
    saved = (
        signal,
        first_normed,
        heads_kept,
        attended,
        middle,
        second_normed,
        cross_queries,
        cross_att,
        latter,
        third_normed,
        hidden_pre,
        hidden_act,
    )
    return (result, saved)


def backward(saved, upstream, vectors, weights, cross_keys, cross_values, masks):
    first_gain, first_shift, second_gain, second_shift, third_gain, third_shift = vectors
    (
        query_weight,
        key_weight,
        value_weight,
        output_weight,
        cross_query,
        cross_output,
        expand_weight,
        reduce_weight,
    ) = weights
    (
        signal,
        first_normed,
        heads_kept,
        attended,
        middle,
        second_normed,
        cross_queries,
        cross_att,
        latter,
        third_normed,
        hidden_pre,
        hidden_act,
    ) = saved
    grad_out = upstream.astype(jnp.bfloat16)
    grad_reduce = matmul_tn(hidden_act, grad_out)
    grad_act = matmul_nt(grad_out, reduce_weight)
    slope = (
        0.5 * (1.0 + lax.erf(hidden_pre * inv_sqrt_two))
        + hidden_pre * jnp.exp(-0.5 * hidden_pre * hidden_pre) * inv_sqrt_tau
    )
    grad_pre = (grad_act * slope).astype(jnp.bfloat16)
    grad_expand = matmul_tn(third_normed, grad_pre)
    grad_third = head_total(matmul_nt(grad_pre, expand_weight))
    grad_latter, grad_third_gain, grad_third_shift = norm_back(latter, third_gain, grad_third)
    grad_latter = grad_latter + upstream
    grad_cross = grad_latter.astype(jnp.bfloat16)
    grad_cross_output = matmul_tn(cross_att, grad_cross)
    grad_cross_att = matmul_nt(grad_cross, cross_output).astype(jnp.bfloat16)
    grad_cq, grad_ck, grad_cv = attend_back(
        cross_queries, cross_keys, cross_values, masks["cross"], grad_cross_att
    )
    grad_text_rows = jnp.concatenate([grad_ck, grad_cv], axis=1).astype(jnp.bfloat16)
    grad_text_rows = lax.psum_scatter(
        grad_text_rows.reshape(ITEMS, TEXT, -1), "frame", scatter_dimension=1, tiled=True
    )
    grad_cquery = grad_cq.astype(jnp.bfloat16)
    grad_cross_query = matmul_tn(second_normed, grad_cquery)
    grad_second = head_total(matmul_nt(grad_cquery, cross_query))
    grad_middle, grad_second_gain, grad_second_shift = norm_back(middle, second_gain, grad_second)
    grad_middle = grad_middle + grad_latter
    grad_self = grad_middle.astype(jnp.bfloat16)
    grad_output = matmul_tn(attended, grad_self)
    grad_att = matmul_nt(grad_self, output_weight).astype(jnp.bfloat16)
    grad_query_low, grad_key_low, grad_value_low = self_attention_back(heads_kept, grad_att, masks)
    grad_query = matmul_tn(first_normed, grad_query_low)
    grad_key = matmul_tn(first_normed, grad_key_low)
    grad_value = matmul_tn(first_normed, grad_value_low)
    grad_first = head_total(
        matmul_nt(grad_query_low, query_weight)
        + matmul_nt(grad_key_low, key_weight)
        + matmul_nt(grad_value_low, value_weight)
    )
    grad_signal, grad_first_gain, grad_first_shift = norm_back(signal, first_gain, grad_first)
    grad_signal = grad_signal + grad_middle
    vector_grads = (
        grad_first_gain,
        grad_first_shift,
        grad_second_gain,
        grad_second_shift,
        grad_third_gain,
        grad_third_shift,
    )
    matrix_grads = (
        grad_query,
        grad_key,
        grad_value,
        grad_output,
        grad_cross_query,
        grad_cross_output,
        grad_expand,
        grad_reduce,
    )
    matrix_grads = tuple(
        lax.psum_scatter(g.astype(jnp.bfloat16), "frame", scatter_dimension=0, tiled=True)
        for g in matrix_grads
    )
    return grad_signal, vector_grads, matrix_grads, grad_text_rows


def per_device(
    inputs,
    lengths,
    text,
    cotangent,
    first_gain,
    first_shift,
    query_weight,
    key_weight,
    value_weight,
    output_weight,
    second_gain,
    second_shift,
    cross_query,
    cross_key,
    cross_value,
    cross_output,
    third_gain,
    third_shift,
    expand_weight,
    reduce_weight,
):
    head_count, frame_count = lax.axis_size("head"), lax.axis_size("frame")
    local_heads = query_weight.shape[2] // HEAD
    if head_count == 4 and frame_count == 4 and local_heads == 4:
        return on_four_frames(
            inputs,
            lengths,
            text,
            cotangent,
            (first_gain, first_shift, second_gain, second_shift, third_gain, third_shift),
            (
                query_weight,
                key_weight,
                value_weight,
                output_weight,
                cross_query,
                cross_key,
                cross_value,
                cross_output,
                expand_weight,
                reduce_weight,
            ),
        )
    section = lax.axis_index("section")
    at_zero = section == 0
    frame_index = lax.axis_index("frame")
    micro_count, rows_dev, model_width = inputs.shape
    rows_all = rows_dev * frame_count
    text_rows_dev = text.shape[2]

    def keep(pair):
        return jnp.where(at_zero, pair[0], pair[1])

    def give(pair):
        return jnp.where(at_zero, pair[1], pair[0])

    vector_args = jnp.concatenate(
        [first_gain, first_shift, second_gain, second_shift, third_gain, third_shift], axis=0
    )
    vectors = lax.all_gather(vector_args, "section")
    matrix_args = (
        query_weight,
        key_weight,
        value_weight,
        output_weight,
        cross_query,
        cross_output,
        expand_weight,
        reduce_weight,
    )
    matrices = [lax.all_gather(w[0], "section") for w in matrix_args]
    weights = [tuple(w[layer] for w in matrices) for layer in range(2)]

    text_full = lax.all_gather(text, "frame", axis=2, tiled=True)
    text_flat = text_full.reshape(micro_count * ITEMS * TEXT, model_width)
    text_heads = jnp.concatenate(
        [matmul(text_flat, cross_key[0]), matmul(text_flat, cross_value[0])], axis=1
    ).astype(jnp.bfloat16)
    text_heads = text_heads.reshape(micro_count, ITEMS * TEXT, -1)
    own_text = keep(text_heads)
    other_text = swapped(give(text_heads))
    columns = cross_key.shape[2]
    cross_states = [
        jnp.where(at_zero, own_text, other_text),
        jnp.where(at_zero, other_text, own_text),
    ]
    cross_keys = [c[:, :columns] for c in cross_states]
    cross_values = [c[:, columns:] for c in cross_states]

    item_ends = jnp.cumsum(lax.dynamic_index_in_dim(lengths, section, 0, keepdims=False))
    all_positions = jnp.arange(rows_all, dtype=jnp.int32)
    seg_all = jnp.sum((all_positions[:, None] >= item_ends[None, :]).astype(jnp.int32), axis=1)
    own_start = frame_index * rows_dev
    own_positions = own_start + jnp.arange(rows_dev, dtype=jnp.int32)
    seg_own = lax.dynamic_slice_in_dim(seg_all, own_start, rows_dev)
    text_item = jnp.arange(ITEMS * TEXT, dtype=jnp.int32) // TEXT
    masks = {
        "own": (all_positions[None, :] <= own_positions[:, None])
        & (seg_own[:, None] == seg_all[None, :]),
        "cross": seg_own[:, None] == text_item[None, :],
    }

    signal = lax.dynamic_index_in_dim(inputs, section, 0, keepdims=False)
    results, saves = [], []
    for layer in range(2):
        result, saved = forward(
            signal, vectors[layer], weights[layer], cross_keys[layer], cross_values[layer], masks
        )
        results.append(result)
        saves.append(saved)
        signal = result.astype(jnp.bfloat16)

    upstream = lax.dynamic_index_in_dim(cotangent, section, 0, keepdims=False)
    in_grads, vector_grads, matrix_grads, text_grads = [None] * 2, [None] * 2, [None] * 2, [None] * 2
    for layer in (1, 0):
        grad_signal, vector_grads[layer], matrix_grads[layer], text_grads[layer] = backward(
            saves[layer],
            upstream,
            vectors[layer],
            weights[layer],
            cross_keys[layer],
            cross_values[layer],
            masks,
        )
        in_grads[layer] = grad_signal
        upstream = grad_signal.astype(jnp.bfloat16).astype(jnp.float32)

    def both_micros(pair):
        own = keep(pair)
        other = swapped(give([p.astype(jnp.bfloat16) for p in pair])).astype(own.dtype)
        return jnp.stack([jnp.where(at_zero, own, other), jnp.where(at_zero, other, own)])

    layer_outputs = both_micros(results)
    input_grads = both_micros(in_grads)
    totals = [
        keep(pair).astype(jnp.float32) + swapped(give(pair)).astype(jnp.float32)
        for pair in zip(*matrix_grads)
    ]
    text_rows = both_micros(text_grads)
    text_rows = text_rows.reshape(micro_count * ITEMS * text_rows_dev, -1)
    key_part, value_part = text_rows[:, :columns], text_rows[:, columns:]
    text_local = text.reshape(-1, model_width)
    grad_cross_key, grad_cross_value = (
        lax.psum_scatter(
            matmul_tn(text_local, part).astype(jnp.bfloat16),
            "frame",
            scatter_dimension=0,
            tiled=True,
        ).astype(jnp.float32)
        for part in (key_part, value_part)
    )
    text_part = matmul_nt(key_part, cross_key[0]) + matmul_nt(value_part, cross_value[0])
    text_grad = lax.psum(text_part.astype(jnp.bfloat16), ("section", "head")).astype(jnp.float32)
    text_grad = text_grad.reshape(text.shape)

    stacked = jnp.stack([jnp.stack(v) for v in vector_grads])
    stacked = lax.psum_scatter(
        stacked.astype(jnp.bfloat16), "frame", scatter_dimension=2, tiled=True
    )
    vector_total = keep(stacked).astype(jnp.float32) + swapped(give(stacked)).astype(jnp.float32)

    grad_q, grad_k, grad_v, grad_o, grad_cq, grad_co, grad_e, grad_r = totals
    ordered = (
        vector_total[0],
        vector_total[1],
        grad_q,
        grad_k,
        grad_v,
        grad_o,
        vector_total[2],
        vector_total[3],
        grad_cq,
        grad_cross_key,
        grad_cross_value,
        grad_co,
        vector_total[4],
        vector_total[5],
        grad_e,
        grad_r,
    )
    return (layer_outputs[None], input_grads[None], text_grad) + tuple(g[None] for g in ordered)


def solution(mesh):
    return jax.shard_map(
        per_device,
        mesh=mesh,
        in_specs=(
            P(None, "frame", None),
            P(),
            P(None, None, "frame", None),
            P(None, "frame", None),
            P("section", None),
            P("section", None),
            P("section", None, "head"),
            P("section", None, "head"),
            P("section", None, "head"),
            P("section", "head", None),
            P("section", None),
            P("section", None),
            P("section", None, "head"),
            P("section", None, "head"),
            P("section", None, "head"),
            P("section", "head", None),
            P("section", None),
            P("section", None),
            P("section", None, "head"),
            P("section", "head", None),
        ),
        out_specs=(
            P("section", None, "frame", None),
            P("section", None, "frame", None),
            P(None, None, "frame", None),
            P("section", "frame"),
            P("section", "frame"),
            P("section", "frame", "head"),
            P("section", "frame", "head"),
            P("section", "frame", "head"),
            P("section", ("head", "frame"), None),
            P("section", "frame"),
            P("section", "frame"),
            P("section", "frame", "head"),
            P("section", "frame", "head"),
            P("section", "frame", "head"),
            P("section", ("head", "frame"), None),
            P("section", "frame"),
            P("section", "frame"),
            P("section", "frame", "head"),
            P("section", ("head", "frame"), None),
        ),
        check_vma=False,
    )
```

time: 2430 us -> 809 us (0.33)
  waiting for transfers between devices: 1580 us -> 0 us
  Pallas kernels: 0 us -> 718 us
  matrix products: 517 us -> 38.3 us
  other arithmetic: 180 us -> 22.4 us
  local copies, waits for them, and re-layouts: 90.8 us -> 19.2 us
    psum x19 -> x0, waiting for transfers between devices: 1050 us -> none  [the longest x18 1050 us: head_total(): lax.psum(partial_sum.astype(jnp.bfloat16), 'head').astype(jnp.float32)]
    pallas_call x0 -> x18, Pallas kernels: none -> 718 us  [call(): pl.pallas_call(kernel, out_shape=all_outs, in_specs=in_specs, out_specs=o...]
    reduce_scatter x22 -> x0, waiting for transfers between devices: 377 us -> none  [the longest x10 197 us: per_device(): lax.psum_scatter(as_sent(totals), 'frame', scatter_dimension=0, tiled=True)]
    dot_general x36 -> x2, matrix products: 177 us -> 6.61 us  [on_four_frames(): lax.dot_general(normed, grad_heads_t, (((0,), (1,)), ((), ())), preferred...]
    dot_general x54 -> x4, matrix products: 117 us -> 5.39 us  [matmul(): return jnp.dot(left_side, right_side, preferred_element_type=jnp.float32)]
    sub x12 -> x0, matrix products: 87.1 us -> none  [softmax_rows(): exponent = jnp.exp(logits - jnp.max(logits, axis=-1, keepdims=True))]
    ppermute x4 -> x0, waiting for transfers between devices: 84.4 us -> none  [passed_along(): return lax.ppermute(x, axis, pairs)]
    all_gather x13 -> x0, waiting for transfers between devices: 76.2 us -> none  [the longest x6 44.6 us: forward(): lax.all_gather(key_rows, 'frame', axis=0, tiled=True)]
  transfers between devices with their start and end apart: 58 -> 0, of which waited for: 52 -> 0; matrix products, arithmetic and copies ran while one was open for 20% -> 0% of each run, Pallas kernels for 0% -> 0%
where the time goes in v2:
time: 809 us; the launch traced here: 799 us
  Pallas kernels  718 us (89%)
  matrix products  38.3 us (5%)
  other arithmetic  22.4 us (3%)
  local copies, waits for them, and re-layouts  19.2 us (2%)
    pallas_call x18, Pallas kernels, call(): pl.pallas_call(kernel, out_shape=all_outs, in_specs=in_specs, out_specs=o...  718 us
    dot_general x9, matrix products, matmul_tn(): lax.dot_general(left_side, right_side, (((0,), (0,)), ((), ())), preferre...  25 us

profile of v2, /device:TPU:0, one launch (start us, length us, event | category | flops | bytes accessed | tf_op | source)
XLA Modules:
  0.0 799.2 jit_solution(17144547376889008737)
XLA Ops:
  0.7 1.6 convert_reduce_fusion
  3.1 1.2 copy.54
  4.7 1.3 copy.55
  6.1 0.6 pad.4.refs_1_.refs_2_
  6.7 25.3 %shard_map.339 = (bf16[768,1024]{1,0:T(8,128)(2,1)}, f32[8,1024]{1,0:T(8,128)}) custom-call(bf16[768,1024]{1,0:T(8,128)(2,1)} %bitcast.120, f32[8,1024]{1,0:T(8,128)} %pad.4.refs_1_.refs_2_, f32[8,1024]{1,0:T(8,128)} %pad.4.refs_1_.refs_2_), custom_call_target="tpu_custom_call" | custom-call | flops 30000001024 | bytes 8000000 | tf_op jit(solution)/shard_map/pallas_call | solution.py:469
  32.0 0.8 broadcast_select_fusion.3
  33.5 1.4 fusion.5.refs_0_
  35.1 0.7 convert_reduce_fusion.1
  36.3 0.7 pad_maximum_fusion.3.refs_7_
  37.0 30.3 %shard_map.340 = (bf16[192,2048]{1,0:T(8,128)(2,1)}, bf16[256,512]{1,0:T(8,128)(2,1)}, bf16[256,1024]{1,0:T(8,128)(2,1)}, bf16[1024,256]{1,0:T(8,128)(2,1)}, bf1...) custom-call(bf16[512,1024]{1,0:T(8,128)(2,1)} %fusion.5.refs_0_, s32[1,2048]{1,0:T(1,128)} %bitcast.139, ...), custom_call_target="tpu_custom_call" | custom-call | flops 30000001024 | bytes 8000000 | tf_op jit(solution)/shard_map/pallas_call | solution.py:469
  67.3 42.9 %shard_map.341 = (f32[512,1024]{1,0:T(8,128)}, bf16[512,1024]{1,0:T(8,128)(2,1)}, bf16[1024,1024]{1,0:T(8,128)(2,1)}) custom-call(bf16[256,512]{1,0:T(8,128)(2,1)} %get-tuple-element.110.refs_0_, bf16[512,1024]{1,0:T(8,128)(2,1)} %copy-done.1, f32[1,1024]{1,0:T(1,128)} %get-tuple-element.271.refs_2_.refs_6_, f32[1,1024]{1,0:T(1,128)} %get-tuple-element.270.refs_3_, ...), custom_call_target="tpu_custom_call" | custom-call | flops 30000001024 | bytes 8000000 | tf_op jit(solution)/shard_map/pallas_call | solution.py:469
  110.3 0.8 slice_bitcast_fusion.2
  111.1 0.7 dynamic-slice.3
  111.7 45.4 %shard_map.342 = (f32[512,1024]{1,0:T(8,128)}, bf16[512,1024]{1,0:T(8,128)(2,1)}, bf16[512,256]{1,0:T(8,128)(2,1)}, bf16[512,256]{1,0:T(8,128)(2,1)}, bf16[1024,1024]{1,0:T(8,128)(2,1)}) custom-call(bf16[512,1024]{1,0:T(8,128)(2,1)} %get-tuple-element.112.refs_0_, bf16[256,256]{1,0:T(8,128)(2,1)} %get-tuple-element.251.refs_1_.refs_2_, ...), custom_call_target="tpu_custom_call" | custom-call | flops 30000001024 | bytes 8000000 | tf_op jit(solution)/shard_map/pallas_call | solution.py:469
  157.1 0.6 fusion.24
  157.8 43.4 %shard_map.343 = (f32[512,1024]{1,0:T(8,128)}, bf16[512,1024]{1,0:T(8,128)(2,1)}, bf16[512,1024]{1,0:T(8,128)(2,1)}, f32[512,1024]{1,0:T(8,128)}, bf16[512,1024]{1,0:T(8,128)(2,1)}) custom-call(bf16[512,1024]{1,0:T(8,128)(2,1)} %get-tuple-element.117.refs_0_, f32[512,1024]{1,0:T(8,128)} %get-tuple-element.118.refs_1_.refs_2_, ...), custom_call_target="tpu_custom_call" | custom-call | flops 30000001024 | bytes 8000000 | tf_op jit(solution)/shard_map/pallas_call | solution.py:469
  201.2 22.9 %shard_map.344 = (bf16[192,2048]{1,0:T(8,128)(2,1)}, bf16[256,512]{1,0:T(8,128)(2,1)}) custom-call(bf16[512,1024]{1,0:T(8,128)(2,1)} %get-tuple-element.122.refs_0_, s32[1,2048]{1,0:T(1,128)} %bitcast.140, bf16[768,1024]{1,0:T(8,128)(2,1)} %bitcast.122, bf16[768,1024]{1,0:T(8,128)(2,1)} %get-tuple-element.109.refs_3_.refs_5_.refs_6_), custom_call_target="tpu_custom_call" | custom-call | flops 30000001024 | bytes 8000000 | tf_op jit(solution)/shard_map/pallas_call | solution.py:469
  224.1 37.1 %shard_map.345 = (f32[512,1024]{1,0:T(8,128)}, bf16[512,1024]{1,0:T(8,128)(2,1)}) custom-call(bf16[256,512]{1,0:T(8,128)(2,1)} %get-tuple-element.123.refs_0_, bf16[512,1024]{1,0:T(8,128)(2,1)} %get-tuple-element.124.refs_1_.refs_10_, f32[1,1024]{1,0:T(1,128)} %get-tuple-element.265.refs_2_.refs_6_, f32[1,1024]{1,0:T(1,128)} %get-tuple-element.264.refs_3_, ...), custom_call_target="tpu_custom_call" | custom-call | flops 30000001024 | bytes 8000000 | tf_op jit(solution)/shard_map/pallas_call | solution.py:469
  261.2 41.5 %shard_map.346 = (f32[512,1024]{1,0:T(8,128)}, bf16[512,1024]{1,0:T(8,128)(2,1)}, bf16[512,256]{1,0:T(8,128)(2,1)}, bf16[512,256]{1,0:T(8,128)(2,1)}) custom-call(bf16[512,1024]{1,0:T(8,128)(2,1)} %get-tuple-element.125.refs_0_, bf16[256,256]{1,0:T(8,128)(2,1)} %get-tuple-element.249.refs_1_.refs_2_, bf16[256,256]{1,0:T(8,128)(2,1)} %get-tuple-element.248.refs_2_.refs_3_, ...), custom_call_target="tpu_custom_call" | custom-call | flops 30000001024 | bytes 8000000 | tf_op jit(solution)/shard_map/pallas_call | solution.py:469
  302.7 40.0 %shard_map.347 = (f32[512,1024]{1,0:T(8,128)}, f32[512,1024]{1,0:T(8,128)}, bf16[512,1024]{1,0:T(8,128)(2,1)}) custom-call(bf16[512,1024]{1,0:T(8,128)(2,1)} %get-tuple-element.127.refs_0_, f32[512,1024]{1,0:T(8,128)} %get-tuple-element.128.refs_1_.refs_2_, f32[1,1024]{1,0:T(1,128)} %get-tuple-element.267.refs_2_, f32[1,1024]{1,0:T(1,128)} %get-tuple-element.266.refs_3_, ...), custom_call_target="tpu_custom_call" | custom-call | flops 30000001024 | bytes 8000000 | tf_op jit(solution)/shard_map/pallas_call | solution.py:469
  342.8 4.8 select_bitcast_fusion.1
  347.6 1.6 fusion.21
  349.2 2.6 convolution_convert_fusion.3.refs_9_
  351.9 49.5 %shard_map.348 = (f32[512,1024]{1,0:T(8,128)}, bf16[512,1024]{1,0:T(8,128)(2,1)}, f32[1,1024]{1,0:T(1,128)}, f32[1,1024]{1,0:T(1,128)}, bf16[512,1024]{1,0:T(8,1...) custom-call(bf16[512,1024]{1,0:T(8,128)(2,1)} %copy-done.14, f32[512,1024]{1,0:T(8,128)} %get-tuple-element.130.refs_1_, ...), custom_call_target="tpu_custom_call" | custom-call | flops 30000001024 | bytes 8000000 | tf_op jit(solution)/shard_map/pallas_call | solution.py:469
  401.4 2.5 convolution_convert_fusion.12.refs_13_
  403.8 3.8 convolution_convert_fusion.2.refs_12_
  407.7 48.1 %shard_map.349 = (f32[512,1024]{1,0:T(8,128)}, bf16[512,1024]{1,0:T(8,128)(2,1)}, f32[1,1024]{1,0:T(1,128)}, f32[1,1024]{1,0:T(1,128)}, bf16[512,256]{1,0:T(8,12...) custom-call(bf16[512,1024]{1,0:T(8,128)(2,1)} %get-tuple-element.135.refs_0_, ...), custom_call_target="tpu_custom_call" | custom-call | flops 30000001024 | bytes 8000000 | tf_op jit(solution)/shard_map/pallas_call | solution.py:469
  455.8 2.5 convolution_convert_fusion.10.refs_7_
  458.3 2.2 convolution_convert_fusion.11.refs_5_
  460.5 43.5 %shard_map.350 = (bf16[768,512]{1,0:T(8,128)(2,1)}, bf16[256,256]{1,0:T(8,128)(2,1)}, bf16[64,512]{1,0:T(8,128)(2,1)}, bf16[64,1024]{1,0:T(8,128)(2,1)}) custom-call(bf16[192,2048]{1,0:T(8,128)(2,1)} %get-tuple-element.134.refs_0_, bf16[512,1024]{1,0:T(8,128)(2,1)} %get-tuple-element.140.refs_1_, s32[1,2048]{1,0:T(1,128)} %bitcast.141, ...), custom_call_target="tpu_custom_call" | custom-call | flops 30000001024 | bytes 8000000 | tf_op jit(solution)/shard_map/pallas_call | solution.py:469
  504.0 3.3 convolution_convert_fusion.5.refs_6_
  507.3 40.7 %shard_map.351 = (f32[512,1024]{1,0:T(8,128)}, bf16[512,1024]{1,0:T(8,128)(2,1)}, f32[1,1024]{1,0:T(1,128)}, f32[1,1024]{1,0:T(1,128)}, bf16[256,768]{1,0:T(8,128)(2,1)}) custom-call(bf16[768,512]{1,0:T(8,128)(2,1)} %get-tuple-element.143.refs_0_, bf16[512,1024]{1,0:T(8,128)(2,1)} %get-tuple-element.124.refs_1_.refs_10_, ...), custom_call_target="tpu_custom_call" | custom-call | flops 30000001024 | bytes 8000000 | tf_op jit(solution)/shard_map/pallas_call | solution.py:469
  548.0 3.8 convolution_convert_fusion.1.refs_9_
  551.8 46.4 %shard_map.352 = (f32[512,1024]{1,0:T(8,128)}, bf16[512,1024]{1,0:T(8,128)(2,1)}, f32[1,1024]{1,0:T(1,128)}, f32[1,1024]{1,0:T(1,128)}, bf16[512,1024]{1,0:T(8,128)(2,1)}, /*index=5*/bf16[256,1024]{1,0:T(8,128)(2,1)}) custom-call(bf16[512,1024]{1,0:T(8,128)(2,1)} %get-tuple-element.145.refs_0_.refs_4_, f32[512,1024]{1,0:T(8,128)} %get-tuple-element.146.refs_1_, ...), custom_call_target="tpu_custom_call" | custom-call | flops 30000001024 | bytes 8000000 | tf_op jit(solution)/shard_map/pallas_call | solution.py:469
  598.2 2.5 convolution_convert_fusion.9.refs_13_
  600.7 3.8 convolution_convert_fusion.refs_12_
  604.5 48.5 %shard_map.353 = (f32[512,1024]{1,0:T(8,128)}, bf16[512,1024]{1,0:T(8,128)(2,1)}, f32[1,1024]{1,0:T(1,128)}, f32[1,1024]{1,0:T(1,128)}, bf16[512,256]{1,0:T(8,12...) custom-call(bf16[512,1024]{1,0:T(8,128)(2,1)} %get-tuple-element.148, ...), custom_call_target="tpu_custom_call" | custom-call | flops 30000001024 | bytes 8000000 | tf_op jit(solution)/shard_map/pallas_call | solution.py:469
  653.1 2.5 convolution_convert_fusion.7.refs_7_
  655.5 2.2 convolution_convert_fusion.8.refs_5_
  657.8 43.4 %shard_map.354 = (bf16[768,512]{1,0:T(8,128)(2,1)}, bf16[256,256]{1,0:T(8,128)(2,1)}, bf16[64,512]{1,0:T(8,128)(2,1)}, bf16[64,1024]{1,0:T(8,128)(2,1)}, f32[256,1024]{1,0:T(8,128)}, /*index=5*/f32[64,1024]{1,0:T(8,128)}) custom-call(bf16[192,2048]{1,0:T(8,128)(2,1)} %get-tuple-element.133.refs_0_, bf16[512,1024]{1,0:T(8,128)(2,1)} %get-tuple-element.155.refs_1_, ...), custom_call_target="tpu_custom_call" | custom-call | flops 30000001024 | bytes 8000000 | tf_op jit(solution)/shard_map/pallas_call | solution.py:469
  701.2 3.3 convolution_convert_fusion.4.refs_7_
  704.6 44.8 %shard_map.355 = (f32[512,1024]{1,0:T(8,128)}, bf16[512,1024]{1,0:T(8,128)(2,1)}, f32[1,1024]{1,0:T(1,128)}, f32[1,1024]{1,0:T(1,128)}, bf16[512,1024]{1,0:T(8,1...) custom-call(bf16[768,512]{1,0:T(8,128)(2,1)} %get-tuple-element.162.refs, ...), custom_call_target="tpu_custom_call" | custom-call | flops 30000001024 | bytes 8000000 | tf_op jit(solution)/shard_map/pallas_call | solution.py:469
  749.5 0.9 broadcast_select_fusion
  750.4 1.5 fusion.6.refs_4_
  751.9 0.7 concatenate.48
  752.8 0.6 pad_maximum_fusion.4.refs_3_
  753.7 1.0 fusion.7.refs_2_
  754.7 23.9 %shard_map.356 = (f32[256,768]{1,0:T(8,128)}, bf16[128,1024]{1,0:T(8,128)(2,1)}, f32[8,1024]{1,0:T(8,128)}, bf16[256,512]{1,0:T(8,128)(2,1)}) custom-call(bf16[256,768]{1,0:T(8,128)(2,1)} %get-tuple-element.173.refs_0_, bf16[256,768]{1,0:T(8,128)(2,1)} %get-tuple-element.174.refs_1_, bf16[128,1024]{1,0:T(8,128)(2,1)} %fusion.7.refs_2_, ...), custom_call_target="tpu_custom_call" | custom-call | flops 30000001024 | bytes 8000000 | tf_op jit(solution)/shard_map/pallas_call | solution.py:469
  778.6 1.4 copy.57
  780.2 0.8 copy.58
  781.0 0.8 copy.59
  781.8 0.8 copy.60
  782.7 0.8 slice_bitcast_fusion
  783.6 0.8 convert.13
  784.4 1.6 fusion.23
  786.0 1.5 bitcast_convert_fusion
  787.5 2.1 select_bitcast_fusion
  789.8 1.3 copy-done.2
  791.1 3.8 maximum_select_fusion
  795.0 0.7 copy.67
  795.7 0.7 copy.68
  796.4 0.7 copy.69
  797.1 1.0 copy.70
  798.0 1.0 copy.71
  (125 shorter events, 3.3 us)
Async XLA Ops:
  0.7 35.4 %copy-start = (bf16[1,1024,256]{2,1,0:T(8,128)(2,1)S(1)}, bf16[1,1024,256]{2,1,0:T(8,128)(2,1)}, u32[]{:S(2)}) copy-start(bf16[1,1024,256]{2,1,0:T(8,128)(2,1)} %param.33) | copy-start | bytes 1572868
  0.7 2.0 copy-start.15
  0.7 2.2 copy-start.16
  2.3 31.2 %copy-start.1 = (bf16[512,1024]{1,0:T(8,128)(2,1)}, bf16[512,1024]{1,0:T(8,128)(2,1)S(1)}, u32[]{:S(2)}) copy-start(bf16[512,1024]{1,0:T(8,128)(2,1)S(1)} %get-tuple-element.238.refs_1_) | copy-start | bytes 3145732
  4.6 1.4 copy-start.30
  4.6 1.4 copy-start.31
  4.6 1.4 copy-start.32
  4.6 1.4 copy-start.33
  4.6 1.4 copy-start.34
  4.6 1.4 copy-start.35
  32.0 2.9 copy-start.46
  32.0 3.8 copy-start.3
  32.0 3.8 copy-start.7
  33.5 2.3 copy-start.29
  67.3 43.0 %copy-start.17 = (bf16[2,4,64,512]{3,2,1,0:T(8,128)(2,1)S(1)}, bf16[2,4,64,512]{3,2,1,0:T(8,128)(2,1)}, u32[]{:S(2)}) copy-start(bf16[2,4,64,512]{3,2,1,0:T(8,128)(2,1)} %get-tuple-element.113) | copy-start | bytes 1572868
  302.7 40.1 %copy-start.6 = (f32[512,1024]{1,0:T(8,128)S(1)}, f32[512,1024]{1,0:T(8,128)}, u32[]{:S(2)}) copy-start(f32[512,1024]{1,0:T(8,128)} %get-tuple-element.121) | copy-start | bytes 6291460
  342.8 4.8 copy-start.10
  347.6 1.6 copy-start.53
  349.2 2.6 copy-start.14
  351.9 49.5 %copy-start.21 = (bf16[512,256]{1,0:T(8,128)(2,1)S(1)}, bf16[512,256]{1,0:T(8,128)(2,1)}, u32[]{:S(2)}) copy-start(bf16[512,256]{1,0:T(8,128)(2,1)} %get-tuple-element.139) | copy-start | bytes 786436
  351.9 52.0 %copy-start.52 = (bf16[512,1024]{1,0:T(8,128)(2,1)S(1)}, bf16[512,1024]{1,0:T(8,128)(2,1)}, u32[]{:S(2)}) copy-start(bf16[512,1024]{1,0:T(8,128)(2,1)} %get-tuple-element.127.refs_0_) | copy-start | bytes 3145732
  407.7 48.1 %copy-start.20 = (bf16[256,512]{1,0:T(8,128)(2,1)S(1)}, bf16[256,512]{1,0:T(8,128)(2,1)}, u32[]{:S(2)}) copy-start(bf16[256,512]{1,0:T(8,128)(2,1)} %get-tuple-element.123.refs_0_) | copy-start | bytes 786436
  407.7 50.6 %copy-start.48 = (bf16[512,1024]{1,0:T(8,128)(2,1)S(1)}, bf16[512,1024]{1,0:T(8,128)(2,1)}, u32[]{:S(2)}) copy-start(bf16[512,1024]{1,0:T(8,128)(2,1)} %get-tuple-element.125.refs_0_) | copy-start | bytes 3145732
  460.5 43.5 %copy-start.49 = (bf16[512,1024]{1,0:T(8,128)(2,1)S(1)}, bf16[512,1024]{1,0:T(8,128)(2,1)}, u32[]{:S(2)}) copy-start(bf16[512,1024]{1,0:T(8,128)(2,1)} %get-tuple-element.122.refs_0_) | copy-start | bytes 3145732
  507.3 40.7 %copy-start.51 = (bf16[512,1024]{1,0:T(8,128)(2,1)S(1)}, bf16[512,1024]{1,0:T(8,128)(2,1)}, u32[]{:S(2)}) copy-start(bf16[512,1024]{1,0:T(8,128)(2,1)} %get-tuple-element.147) | copy-start | bytes 3145732
  551.8 46.4 %copy-start.19 = (bf16[512,256]{1,0:T(8,128)(2,1)S(1)}, bf16[512,256]{1,0:T(8,128)(2,1)}, u32[]{:S(2)}) copy-start(bf16[512,256]{1,0:T(8,128)(2,1)} %get-tuple-element.152) | copy-start | bytes 786436
  551.8 48.9 %copy-start.50 = (bf16[512,1024]{1,0:T(8,128)(2,1)S(1)}, bf16[512,1024]{1,0:T(8,128)(2,1)}, u32[]{:S(2)}) copy-start(bf16[512,1024]{1,0:T(8,128)(2,1)} %get-tuple-element.117.refs_0_) | copy-start | bytes 3145732
  604.5 48.5 %copy-start.18 = (bf16[256,512]{1,0:T(8,128)(2,1)S(1)}, bf16[256,512]{1,0:T(8,128)(2,1)}, u32[]{:S(2)}) copy-start(bf16[256,512]{1,0:T(8,128)(2,1)} %get-tuple-element.110.refs_0_) | copy-start | bytes 786436
  604.5 51.0 %copy-start.47 = (bf16[512,1024]{1,0:T(8,128)(2,1)S(1)}, bf16[512,1024]{1,0:T(8,128)(2,1)}, u32[]{:S(2)}) copy-start(bf16[512,1024]{1,0:T(8,128)(2,1)} %get-tuple-element.112.refs_0_) | copy-start | bytes 3145732
  657.8 43.5 %copy-start.11 = (bf16[512,1024]{1,0:T(8,128)(2,1)S(1)}, bf16[512,1024]{1,0:T(8,128)(2,1)}, u32[]{:S(2)}) copy-start(bf16[512,1024]{1,0:T(8,128)(2,1)} %fusion.5.refs_0_) | copy-start | bytes 3145732
  704.5 45.0 %copy-start.27 = (bf16[64,512]{1,0:T(8,128)(2,1)S(1)}, bf16[64,512]{1,0:T(8,128)(2,1)}, u32[]{:S(2)}) copy-start(bf16[64,512]{1,0:T(8,128)(2,1)} %get-tuple-element.169.refs_13_) | copy-start | bytes 196612
  704.5 45.0 %copy-start.28 = (bf16[64,512]{1,0:T(8,128)(2,1)S(1)}, bf16[64,512]{1,0:T(8,128)(2,1)}, u32[]{:S(2)}) copy-start(bf16[64,512]{1,0:T(8,128)(2,1)} %get-tuple-element.168.refs_12_) | copy-start | bytes 196612
  704.5 45.9 %copy-start.4 = (bf16[2,4,16,1024]{3,2,1,0:T(8,128)(2,1)S(1)}, bf16[2,4,16,1024]{3,2,1,0:T(8,128)(2,1)}, u32[]{:S(2)}) copy-start(bf16[2,4,16,1024]{3,2,1,0:T(8,128)(2,1)} %param.22) | copy-start | bytes 786436
  704.5 47.3 %copy-start.42 = (f32[1,1024]{1,0:T(1,128)S(1)}, f32[1,1024]{1,0:T(1,128)}, u32[]{:S(2)}) copy-start(f32[1,1024]{1,0:T(1,128)} %get-tuple-element.180) | copy-start | bytes 12292
  704.6 47.3 %copy-start.43 = (f32[1,1024]{1,0:T(1,128)S(1)}, f32[1,1024]{1,0:T(1,128)}, u32[]{:S(2)}) copy-start(f32[1,1024]{1,0:T(1,128)} %get-tuple-element.181) | copy-start | bytes 12292
  704.6 47.3 %copy-start.44 = (f32[1,1024]{1,0:T(1,128)S(1)}, f32[1,1024]{1,0:T(1,128)}, u32[]{:S(2)}) copy-start(f32[1,1024]{1,0:T(1,128)} %get-tuple-element.178) | copy-start | bytes 12292
  704.6 47.3 %copy-start.45 = (f32[1,1024]{1,0:T(1,128)S(1)}, f32[1,1024]{1,0:T(1,128)}, u32[]{:S(2)}) copy-start(f32[1,1024]{1,0:T(1,128)} %get-tuple-element.179) | copy-start | bytes 12292
  704.6 48.1 %copy-start.36 = (f32[1,1024]{1,0:T(1,128)S(1)}, f32[1,1024]{1,0:T(1,128)}, u32[]{:S(2)}) copy-start(f32[1,1024]{1,0:T(1,128)} %get-tuple-element.186) | copy-start | bytes 12292
  704.6 48.1 %copy-start.37 = (f32[1,1024]{1,0:T(1,128)S(1)}, f32[1,1024]{1,0:T(1,128)}, u32[]{:S(2)}) copy-start(f32[1,1024]{1,0:T(1,128)} %get-tuple-element.187) | copy-start | bytes 12292
  704.6 48.1 %copy-start.38 = (f32[1,1024]{1,0:T(1,128)S(1)}, f32[1,1024]{1,0:T(1,128)}, u32[]{:S(2)}) copy-start(f32[1,1024]{1,0:T(1,128)} %get-tuple-element.184) | copy-start | bytes 12292
  704.6 48.1 %copy-start.39 = (f32[1,1024]{1,0:T(1,128)S(1)}, f32[1,1024]{1,0:T(1,128)}, u32[]{:S(2)}) copy-start(f32[1,1024]{1,0:T(1,128)} %get-tuple-element.185) | copy-start | bytes 12292
  704.6 48.1 %copy-start.40 = (f32[1,1024]{1,0:T(1,128)S(1)}, f32[1,1024]{1,0:T(1,128)}, u32[]{:S(2)}) copy-start(f32[1,1024]{1,0:T(1,128)} %get-tuple-element.182) | copy-start | bytes 12292
  704.6 48.1 %copy-start.41 = (f32[1,1024]{1,0:T(1,128)S(1)}, f32[1,1024]{1,0:T(1,128)}, u32[]{:S(2)}) copy-start(f32[1,1024]{1,0:T(1,128)} %get-tuple-element.183) | copy-start | bytes 12292
  749.5 4.2 copy-start.8
  778.6 4.0 copy-start.23
  780.1 3.4 copy-start.22
  783.6 3.9 copy-start.5
  787.5 2.1 copy-start.9
  789.5 1.6 copy-start.2
  791.1 3.8 copy-start.26
  791.1 4.5 copy-start.25
  791.1 5.2 copy-start.24
  791.1 5.9 copy-start.13
  795.0 3.1 copy-start.12

commit v3 on v2

v3 whole, which is shorter than its diff:
```python
import jax
import jax.numpy as jnp
from jax import lax
from jax.experimental import pallas as pl
from jax.experimental.pallas import tpu as pltpu
from jax.sharding import PartitionSpec as P

HEAD = 64
TEXT = 64
ITEMS = 4

masked_score = -1e30
inv_sqrt_two = 0.7071067811865476
inv_sqrt_tau = 0.3989422804014327

MESH_IDS = pl.DeviceIdType.MESH
BUSY = pl.CostEstimate(flops=30_000_000_000, bytes_accessed=8_000_000, transcendentals=0)
LAG = 2
BLOCK = 128
VMEM_BYTES = 56 * 1024 * 1024
EPS = 1e-05
SECTION, LINE, FRAME = "section", "head", "frame"
BOTH, LINE_ONLY, BY_SECTION = "both", "line", "one"
NORM, NEXT, END = range(3)


class Task:
    operands = ()
    outs = ()
    out_in_vmem = True
    scratch = ()
    greets = ()

    def bind(self, ins, outs, scratch):
        self.ins, self.out, self.room = ins, outs, scratch


def remote(source, landing, send_sem, recv_sem, target):
    return pltpu.make_async_remote_copy(
        src_ref=source,
        dst_ref=landing,
        send_sem=send_sem,
        recv_sem=recv_sem,
        device_id=target,
        device_id_type=MESH_IDS,
    )


def frame_partners():
    me = lax.axis_index(FRAME)
    return (me + 1 - 2 * lax.rem(me, 2), lax.rem(me + 2, 4), 3 - me)


def span(index, size):
    return pl.ds(pl.multiple_of(index * size, size), size)


class WeightTask(Task):
    out_in_vmem = False
    greets = (SECTION, FRAME)

    def __init__(self, weight):
        self.operands = (weight,)
        self.outs = (jax.ShapeDtypeStruct(weight.shape, weight.dtype),)
        self.scratch = (pltpu.SemaphoreType.DMA((4,)),)
        self.half = weight.shape[0] // 2

    def copies(self):
        (sems,) = self.room
        core = lax.rem(lax.axis_index(FRAME), 2)
        rows = span(core, self.half)
        other_section = {SECTION: 1 - lax.axis_index(SECTION)}
        other_core = {FRAME: frame_partners()[0]}
        over = remote(self.ins[0].at[rows], self.out[0].at[rows], sems.at[0], sems.at[1], other_section)
        on = remote(self.out[0].at[rows], self.out[0].at[rows], sems.at[2], sems.at[3], other_core)
        return over, on

    def begin(self):
        self.copies()[0].start()

    def steps(self):
        over, on = self.copies()

        def pass_on():
            over.wait_recv()
            on.start()

        def end():
            over.wait_send()
            on.wait()

        return [pass_on, end]


class ShareTask(Task):
    greets = (FRAME,)

    def __init__(self, grad):
        rows, width = grad.shape
        self.share = rows // lax.axis_size(FRAME)
        self.operands = (grad,)
        self.outs = (jax.ShapeDtypeStruct((self.share, width), jnp.bfloat16),)
        self.scratch = (
            pltpu.VMEM((3, self.share, width), jnp.bfloat16),
            pltpu.VMEM((self.share, width), jnp.bfloat16),
            pltpu.SemaphoreType.DMA((3,)),
            pltpu.SemaphoreType.DMA((3,)),
            pltpu.SemaphoreType.DMA,
        )

    def copies(self):
        landing, own, send_sems, recv_sems, here = self.room
        me = lax.axis_index(FRAME)
        away = [
            remote(
                self.ins[0].at[span(partner, self.share)],
                landing.at[k],
                send_sems.at[k],
                recv_sems.at[k],
                {FRAME: partner},
            )
            for k, partner in enumerate(frame_partners())
        ]
        return away, pltpu.make_async_copy(self.ins[0].at[span(me, self.share)], own, here)

    def begin(self):
        away, stay = self.copies()
        for copy in away[::-1]:
            copy.start()
        stay.start()

    def steps(self):
        away, stay = self.copies()

        def end():
            stay.wait()
            for copy in away:
                copy.wait()
            landing, own = self.room[:2]
            total = own[...].astype(jnp.float32)
            for k in range(3):
                total = total + landing[k].astype(jnp.float32)
            self.out[0][...] = total.astype(jnp.bfloat16)

        return [end]


class CrossTask(Task):
    greets = (SECTION,)

    def __init__(self, first, second, added):
        self.operands = (first, second)
        self.added = added
        self.out_in_vmem = added
        shape = first.shape
        if added:
            self.outs = (jax.ShapeDtypeStruct(shape, jnp.float32),)
            self.scratch = (pltpu.VMEM(shape, jnp.bfloat16),) * 2 + (pltpu.SemaphoreType.DMA((3,)),)
        else:
            self.outs = (jax.ShapeDtypeStruct(shape, first.dtype),)
            self.scratch = (pltpu.SemaphoreType.DMA((2,)),)

    def copies(self, given, kept):
        sems = self.room[-1]
        landing = self.room[0] if self.added else self.out[0]
        target = {SECTION: 1 - lax.axis_index(SECTION)}
        copies = [remote(self.ins[given], landing, sems.at[0], sems.at[1], target)]
        if self.added:
            copies.append(pltpu.make_async_copy(self.ins[kept], self.room[1], sems.at[2]))
        return copies

    def begin(self):
        section = lax.axis_index(SECTION)
        for which in (0, 1):

            @pl.when(section == which)
            def _():
                for copy in self.copies(1 - which, which):
                    copy.start()

    def steps(self):
        def end():
            for copy in self.copies(0, 1):
                copy.wait()
            if self.added:
                self.out[0][...] = self.room[0][...].astype(jnp.float32) + self.room[1][...].astype(
                    jnp.float32
                )

        return [end]


class TextTask(Task):
    out_in_vmem = False
    greets = (SECTION, FRAME, BOTH)

    def __init__(self, states):
        micros, rows, width = states.shape
        self.operands = (states,)
        self.outs = (jax.ShapeDtypeStruct((2, 4, rows, width), states.dtype),)
        self.scratch = (pltpu.SemaphoreType.DMA((8,)), pltpu.SemaphoreType.DMA((8,)))

    def copies(self):
        send_sems, recv_sems = self.room
        section, me = lax.axis_index(SECTION), lax.axis_index(FRAME)
        landing = self.out[0].at[section, me]
        copies = []
        for far in (0, 1):
            micro = section if far == 0 else 1 - section
            for k, frame in enumerate((me,) + frame_partners()):
                slot = far * 4 + k
                source = self.ins[0].at[micro]
                if slot == 0:
                    copies.append(pltpu.make_async_copy(source, landing, send_sems.at[0]))
                    continue
                target = {SECTION: micro, FRAME: frame}
                copies.append(remote(source, landing, send_sems.at[slot], recv_sems.at[slot], target))
        return copies

    def begin(self):
        for copy in self.copies():
            copy.start()

    def steps(self):
        def end():
            for copy in self.copies():
                copy.wait()

        return [end]


class TotalTask(Task):
    greets = (SECTION, LINE)

    def __init__(self, part):
        rows, width = part.shape
        self.share = rows // 4
        self.operands = (part,)
        self.outs = (jax.ShapeDtypeStruct((rows, width), jnp.bfloat16),)
        piece = (self.share, width)
        self.scratch = (
            pltpu.VMEM((4,) + piece, jnp.bfloat16),
            pltpu.VMEM((2,) + piece, jnp.bfloat16),
            pltpu.SemaphoreType.DMA((4,)),
            pltpu.SemaphoreType.DMA((4,)),
            pltpu.SemaphoreType.DMA((2,)),
            pltpu.SemaphoreType.DMA((4,)),
            pltpu.SemaphoreType.DMA((4,)),
        )

    def partners(self):
        me = lax.axis_index(LINE)
        return [lax.rem(me + by, 4) for by in (1, 2, 3)]

    def spread(self):
        landing, _, send_sems, recv_sems = self.room[:4]
        me = lax.axis_index(LINE)
        away = [
            remote(
                self.ins[0].at[span(partner, self.share)],
                landing.at[by],
                send_sems.at[by],
                recv_sems.at[by],
                {LINE: partner},
            )
            for by, partner in enumerate(self.partners(), 1)
        ]
        stay = pltpu.make_async_copy(self.ins[0].at[span(me, self.share)], landing.at[0], send_sems.at[0])
        return away + [stay]

    def over(self):
        sums, sems = self.room[1], self.room[4]
        target = {SECTION: 1 - lax.axis_index(SECTION)}
        return remote(sums.at[0], sums.at[1], sems.at[0], sems.at[1], target)

    def gather(self):
        send_sems, recv_sems = self.room[5:]
        mine = self.out[0].at[span(lax.axis_index(LINE), self.share)]
        return [
            remote(mine, mine, send_sems.at[by], recv_sems.at[by], {LINE: partner})
            for by, partner in enumerate(self.partners(), 1)
        ]

    def begin(self):
        for copy in self.spread():
            copy.start()

    def steps(self):
        landing, sums = self.room[:2]

        def first():
            for copy in self.spread():
                copy.wait()
            total = landing[0].astype(jnp.float32)
            for by in (1, 2, 3):
                total = total + landing[by].astype(jnp.float32)
            sums[0] = total.astype(jnp.bfloat16)
            self.over().start()

        def second():
            self.over().wait()
            total = sums[0].astype(jnp.float32) + sums[1].astype(jnp.float32)
            self.out[0][span(lax.axis_index(LINE), self.share), :] = total.astype(jnp.bfloat16)
            for copy in self.gather():
                copy.start()

        def third():
            for copy in self.gather():
                copy.wait()

        return [first, second, third]


class VectorTask(Task):
    greets = (SECTION, FRAME)

    def __init__(self, grads):
        self.operands = (grads,)
        shape = grads.shape[1:]
        self.outs = (jax.ShapeDtypeStruct(shape, jnp.float32),)
        self.scratch = (
            pltpu.VMEM((4,) + grads.shape, jnp.float32),
            pltpu.VMEM((3,) + shape, jnp.float32),
            pltpu.SemaphoreType.DMA((4,)),
            pltpu.SemaphoreType.DMA((4,)),
            pltpu.SemaphoreType.DMA((2,)),
        )

    def spread(self):
        landing, _, send_sems, recv_sems, _ = self.room
        away = [
            remote(self.ins[0], landing.at[k], send_sems.at[k], recv_sems.at[k], {FRAME: partner})
            for k, partner in enumerate(frame_partners(), 1)
        ]
        return away + [pltpu.make_async_copy(self.ins[0], landing.at[0], send_sems.at[0])]

    def over(self):
        sums, sems = self.room[1], self.room[4]
        target = {SECTION: 1 - lax.axis_index(SECTION)}
        return remote(sums.at[0], sums.at[1], sems.at[0], sems.at[1], target)

    def begin(self):
        for copy in self.spread():
            copy.start()

    def steps(self):
        landing, sums = self.room[:2]
        section = lax.axis_index(SECTION)

        def first():
            for copy in self.spread():
                copy.wait()
            total = [
                (landing[0, layer] + landing[1, layer]) + (landing[2, layer] + landing[3, layer])
                for layer in (0, 1)
            ]
            for which in (0, 1):

                @pl.when(section == which)
                def _():
                    sums[0] = total[1 - which]
                    sums[2] = total[which]

            self.over().start()

        def second():
            self.over().wait()
            self.out[0][...] = sums[2] + sums[1]

        return [first, second]


def greet(kinds):
    barrier = pltpu.get_barrier_semaphore()
    section, head, frame = (lax.axis_index(a) for a in (SECTION, LINE, FRAME))
    targets = []
    if FRAME in kinds:
        targets += [{FRAME: other} for other in frame_partners()]
    if SECTION in kinds:
        targets.append({SECTION: 1 - section})
    if BOTH in kinds:
        targets += [{SECTION: 1 - section, FRAME: other} for other in frame_partners()]
    if LINE in kinds:
        targets += [{LINE: lax.rem(head + by, 4)} for by in (1, 2, 3)]
    for target in targets:
        pl.semaphore_signal(barrier, 1, device_id=target, device_id_type=MESH_IDS)
    if LINE_ONLY not in kinds or LINE in kinds:
        pl.semaphore_wait(barrier, len(targets))
        return

    for way in (-1, 1):
        other = head + way

        @pl.when((other >= 0) & (other < 4))
        def _():
            pl.semaphore_signal(barrier, 1, device_id={LINE: other}, device_id_type=MESH_IDS)

    is_end = (head == 0) | (head == 3)

    @pl.when(is_end)
    def _():
        pl.semaphore_wait(barrier, len(targets) + 1)

    @pl.when(jnp.logical_not(is_end))
    def _():
        pl.semaphore_wait(barrier, len(targets) + 2)


def call(body, operands, outs, scratch, kinds, collective_id, tasks=(), in_vmem=True, end=None):
    whole, anywhere = pl.BlockSpec(memory_space=pltpu.VMEM), pl.BlockSpec(memory_space=pl.ANY)
    place = whole if in_vmem else anywhere
    in_specs, out_specs = [place] * len(operands), [place] * len(outs)
    operands, all_outs, scratch = list(operands), list(outs), list(scratch)
    counts = [(len(operands), len(outs), len(scratch))]
    kinds = set(kinds)
    for task in tasks:
        kinds |= set(task.greets)
        in_specs += [anywhere] * len(task.operands)
        out_specs += [whole if task.out_in_vmem else anywhere] * len(task.outs)
        operands += task.operands
        all_outs += task.outs
        scratch += task.scratch
        counts.append((len(task.operands), len(task.outs), len(task.scratch)))
    n_in, n_out = len(operands), len(all_outs)

    def kernel(*refs):
        groups = [list(refs[:n_in]), list(refs[n_in : n_in + n_out]), list(refs[n_in + n_out :])]
        bound = []
        for sizes in counts:
            bound.append([])
            for group, size in zip(groups, sizes):
                bound[-1].append(group[:size])
                del group[:size]
        for task, parts in zip(tasks, bound[1:]):
            task.bind(*parts)

        def meet():
            greet(kinds)

        def ride():
            for task in tasks:
                task.begin()

        if body is None:
            meet()
            ride()
        else:
            body(*bound[0], meet, ride)
        queues = [task.steps() for task in tasks]
        while any(queues):
            for queue in queues:
                if queue:
                    queue.pop(0)()
        if end is not None:
            end()

    results = pl.pallas_call(
        kernel,
        out_shape=all_outs,
        in_specs=in_specs,
        out_specs=out_specs,
        scratch_shapes=scratch,
        compiler_params=pltpu.CompilerParams(
            collective_id=collective_id, has_side_effects=True, vmem_limit_bytes=VMEM_BYTES
        ),
    )(*operands)
    results = list(results)
    main, results = results[: len(outs)], results[len(outs) :]
    return main, results


def chunking(rows):
    return max(1, min(16, rows // 16))


def nt_product(left, right):
    return lax.dot_general(left, right, (((1,), (1,)), ((), ())), preferred_element_type=jnp.float32)


def plain_product(left, right):
    return jnp.dot(left, right, preferred_element_type=jnp.float32)


def norm_parts(v):
    average = jnp.mean(v, axis=-1, keepdims=True)
    centered = v - average
    inverse = lax.rsqrt(jnp.mean(centered * centered, axis=-1, keepdims=True) + EPS)
    return centered * inverse, inverse


class Held:
    def __init__(self, shape, dtype, sources=(), choose=None, stage=0, kept=False):
        self.shape, self.dtype = tuple(shape), dtype
        self.sources, self.choose, self.stage, self.kept = sources, choose, stage, kept
        self.ref = self.far = self.sem = None

    def copy_in(self, index=0):
        source = self.far[index]
        if self.choose == BY_SECTION:
            source = source.at[lax.axis_index(SECTION)]
        return pltpu.make_async_copy(source, self.ref, self.sem)

    def start_in(self):
        if not isinstance(self.choose, int):
            self.copy_in().start()
            return
        section = lax.axis_index(SECTION)

        @pl.when(section == self.choose)
        def _():
            self.copy_in(0).start()

        @pl.when(section != self.choose)
        def _():
            self.copy_in(1).start()

    def write(self, at, value):
        self.ref[at, :] = value
        if self.kept:
            pltpu.make_async_copy(self.ref.at[at], self.far[0].at[at], self.sem).start()

    def drain(self):
        pltpu.make_async_copy(self.ref, self.far[0], self.sem).wait()


class Build:
    def __init__(self):
        self.helds, self.rooms, self.extras = [], [], []

    def add(self, held):
        self.helds.append(held)
        return held

    def arg(self, array, stage, choose=None):
        shape = array.shape[1:] if choose == BY_SECTION else array.shape
        return self.add(Held(shape, array.dtype, (array,), choose, stage))

    def pick(self, pair, layer, stage):
        return self.add(Held(pair[0].shape, pair[0].dtype, tuple(pair), layer, stage))

    def out(self, shape, dtype):
        return self.add(Held(shape, dtype, kept=True))

    def temp(self, shape, dtype):
        return self.add(Held(shape, dtype))

    def extra(self, scratch):
        self.extras.append(scratch)
        return len(self.extras) - 1


class Stage:
    def __init__(self, rows, width):
        self.rows, self.width = rows, width
        self.begin = self.prepare = self.partial = self.finish = None
        self.ends = []


def line_chain(stages, need):
    place = lax.axis_index(LINE)
    rows = stages[0].rows
    pieces = chunking(rows)
    step = rows // pieces
    per_block = max(1, min(BLOCK, rows) // step)
    lag = max(0, min(LAG, pieces - per_block))
    is_end = (place == 0) | (place == 3)
    inner = {LINE: jnp.where(place == 0, 1, 2)}
    outer = {LINE: jnp.where(place == 1, 0, 3)}
    peer = {LINE: 3 - place}

    def inwards(stage, piece):
        send, recv, _, _, send_sems, recv_sems = stage.room[:6]
        at = span(piece, step)
        return remote(send.at[at], recv.at[at], send_sems.at[piece], recv_sems.at[piece], inner)

    def crossing(stage, piece):
        send, _, across = stage.room[:3]
        send_sems, recv_sems = stage.room[6:8]
        at = span(piece, step)
        return remote(send.at[at], across.at[at], send_sems.at[piece], recv_sems.at[piece], peer)

    def outwards(stage, piece):
        held = stage.room[3]
        send_sems, recv_sems = stage.room[8:]
        at = span(piece, step)
        return remote(held.at[at], held.at[at], send_sems.at[piece], recv_sems.at[piece], outer)

    def open_stage(index):
        need(index)
        if stages[index].begin is not None:
            stages[index].begin()

    def loop(first, last, step_of):
        def one(piece, carry):
            step_of(piece)
            return carry

        lax.fori_loop(first, last, one, 0)

    @pl.when(is_end)
    def _():
        def give(stage, piece):
            at = span(piece, step)
            stage.room[0][at, :] = stage.partial(at).astype(jnp.bfloat16)
            inwards(stage, piece).start()

        def take(stage, piece):
            outwards(stage, piece).wait_recv()
            stage.finish(span(piece, step), piece)

        for index, stage in enumerate(stages):
            open_stage(index)

            def block_step(block):
                low, high = block * per_block, (block + 1) * per_block
                if index:
                    loop(low, high, lambda piece: take(stages[index - 1], piece))
                if stage.prepare is not None:
                    stage.prepare(block)
                loop(low, high, lambda piece: give(stage, piece))

            loop(0, pieces // per_block, block_step)
        loop(0, pieces, lambda piece: take(stages[-1], piece))
        for stage in stages:
            loop(0, pieces, lambda piece: inwards(stage, piece).wait_send())

    @pl.when(jnp.logical_not(is_end))
    def _():
        def add(stage, piece):
            if stage.prepare is not None:

                @pl.when(lax.rem(piece, per_block) == 0)
                def _():
                    stage.prepare(lax.div(piece, per_block))

            at = span(piece, step)
            send, recv = stage.room[:2]
            part = stage.partial(at)
            inwards(stage, piece).wait_recv()
            send[at, :] = (part + recv[at, :].astype(jnp.float32)).astype(jnp.bfloat16)
            crossing(stage, piece).start()

        def settle(stage, piece):
            at = span(piece, step)
            send, _, across, held = stage.room[:4]
            crossing(stage, piece).wait_recv()
            total = send[at, :].astype(jnp.float32) + across[at, :].astype(jnp.float32)
            held[at, :] = total.astype(jnp.bfloat16)
            outwards(stage, piece).start()
            stage.finish(at, piece)

        for index, stage in enumerate(stages):
            open_stage(index)

            def both(piece):
                add(stage, piece)

                @pl.when(piece >= lag)
                def _():
                    settle(stage, piece - lag)

                if index and lag:

                    @pl.when(piece < lag)
                    def _():
                        settle(stages[index - 1], pieces - lag + piece)

            loop(0, pieces, both)
        loop(pieces - lag, pieces, lambda piece: settle(stages[-1], piece))

        def drain(stage, piece):
            crossing(stage, piece).wait_send()
            outwards(stage, piece).wait_send()

        for stage in stages:
            loop(0, pieces, lambda piece: drain(stage, piece))

    for stage in stages:
        for end in stage.ends:
            end()


def run_build(build, body, kinds, collective_id, tasks):
    operands, outs, scratch = [], [], []
    for held in build.helds:
        operands += held.sources
        if held.kept:
            outs.append(jax.ShapeDtypeStruct(held.shape, held.dtype))
        scratch.append(pltpu.VMEM(held.shape, held.dtype))
    n_held = len(scratch)
    scratch += build.extras
    scratch.append(pltpu.SemaphoreType.DMA((n_held,)))
    reads = sorted((held for held in build.helds if held.sources), key=lambda held: held.stage)

    def need(stage):
        for held in reads:
            if held.stage == stage:
                held.copy_in().wait()

    def run(ins, outs, scratch, meet, ride):
        ins, outs = list(ins), list(outs)
        sems = scratch[-1]
        for index, held in enumerate(build.helds):
            held.ref, held.sem = scratch[index], sems.at[index]
            held.far = [ins.pop(0) for _ in held.sources]
            if held.kept:
                held.far = [outs.pop(0)]
        build.bound = scratch[n_held:-1]
        for held in reads:
            held.start_in()
        body(need, meet, ride)

    def end():
        for held in build.helds:
            if held.kept:
                held.drain()

    return call(run, operands, outs, scratch, kinds, collective_id, tasks, in_vmem=False, end=end)


def run_chain(build, stages, collective_id, tasks, kinds=(LINE_ONLY,)):
    slots = []
    for stage in stages:
        pieces = chunking(stage.rows)
        room = [pltpu.VMEM((stage.rows, stage.width), jnp.bfloat16)] * 4
        room += [pltpu.SemaphoreType.DMA((pieces,))] * 6
        slots.append([build.extra(scratch) for scratch in room])

    def body(need, meet, ride):
        for stage, places in zip(stages, slots):
            stage.room = [build.bound[place] for place in places]
        meet()
        ride()
        line_chain(stages, need)

    return run_build(build, body, kinds, collective_id, tasks)


def residual_norm(build, index, stage, base, gain, shift, mode):
    shape = (stage.rows, stage.width)
    result = build.out(shape, jnp.float32)
    normed = build.out(shape, jnp.bfloat16) if mode != END else None
    low = build.out(shape, jnp.bfloat16) if mode != NORM else None
    if mode != END:
        gain, shift = build.arg(gain[None], index), build.arg(shift[None], index)

    def finish(at, piece):
        value = base.ref[at, :].astype(jnp.float32) + stage.room[3][at, :].astype(jnp.float32)
        result.write(at, value)
        if low is not None:
            rounded = value.astype(jnp.bfloat16)
            low.write(at, rounded)
            value = rounded.astype(jnp.float32)
        if normed is not None:
            standard, _ = norm_parts(value)
            normed.write(at, (standard * gain.ref[...] + shift.ref[...]).astype(jnp.bfloat16))

    stage.finish = finish
    return result, normed, low


def self_out_stage(build, index, layer, attended_t, weight, base):
    rows, width = base.shape
    stage = Stage(rows, width)
    flipped, matrix = build.arg(attended_t, index), build.pick(weight, layer, index)
    left = build.temp(attended_t.shape[::-1], jnp.bfloat16)

    def begin():
        left.ref[...] = flipped.ref[...].T

    stage.begin = begin
    stage.partial = lambda at: plain_product(left.ref[at, :], matrix.ref[...])
    return stage


def text_mask(states, seg):
    item = lax.rem(lax.div(lax.broadcasted_iota(jnp.int32, (states, 1), 0), TEXT // 4), ITEMS)
    return item == seg


def cross_stage(build, index, layer, normed, states, seg, into, out_of):
    rows, width = normed.shape
    stage = Stage(rows, width)
    columns, block = into[0].shape[1], min(BLOCK, rows)
    states, seg = build.arg(states, index), build.arg(seg, index)
    into, out_of = build.pick(into, layer, index), build.pick(out_of, layer, index)
    queries = build.out((rows, columns), jnp.bfloat16)
    left = build.out((rows, columns), jnp.bfloat16)
    values_t = build.temp((columns, states.shape[0]), jnp.bfloat16)

    def begin():
        values_t.ref[...] = states.ref[:, columns:].T

    def prepare(number):
        at = span(number, block)
        query = plain_product(normed.ref[at, :], into.ref[...]).astype(jnp.bfloat16)
        queries.write(at, query)
        query_t = query.T
        allowed = text_mask(states.shape[0], seg.ref[:, at])
        mixed = []
        for head in range(columns // HEAD):
            cols = slice(head * HEAD, (head + 1) * HEAD)
            scores = plain_product(states.ref[:, cols], query_t[cols, :]) * HEAD ** (-0.5)
            scores = jnp.where(allowed, scores, masked_score)
            e = jnp.exp(scores - jnp.max(scores, axis=0, keepdims=True))
            total = jnp.sum(e, axis=0, keepdims=True)
            value = plain_product(values_t.ref[cols, :], e.astype(jnp.bfloat16))
            mixed.append((value * (1.0 / total)).astype(jnp.bfloat16))
        left.write(at, jnp.concatenate(mixed, axis=0).T)

    stage.begin, stage.prepare = begin, prepare
    stage.partial = lambda at: plain_product(left.ref[at, :], out_of.ref[...])
    return stage


def feed_stage(build, index, layer, normed, into, out_of):
    rows, width = normed.shape
    stage = Stage(rows, width)
    hidden, block = into[0].shape[1], min(BLOCK, rows)
    into, out_of = build.pick(into, layer, index), build.pick(out_of, layer, index)
    before = build.out((rows, hidden), jnp.float32)
    left = build.out((rows, hidden), jnp.bfloat16)

    def prepare(number):
        at = span(number, block)
        u = plain_product(normed.ref[at, :], into.ref[...])
        before.write(at, u)
        left.write(at, (0.5 * u * (1.0 + lax.erf(u * inv_sqrt_two))).astype(jnp.bfloat16))

    stage.prepare = prepare
    stage.partial = lambda at: plain_product(left.ref[at, :], out_of.ref[...])
    return stage


def norm_backward(build, index, stage, value, gain, upstream, kept, spare=None):
    shape = (stage.rows, stage.width)
    pieces = chunking(stage.rows)
    vector = (1, stage.width)
    by_section = BY_SECTION if value.ndim == 3 else None
    value, gain = build.arg(value, index, by_section), build.arg(gain[None], index)
    result = (build.out if kept else build.temp)(shape, jnp.float32)
    low = build.out(shape, jnp.bfloat16)
    gain_grad, shift_grad = build.out(vector, jnp.float32), build.out(vector, jnp.float32)
    parts = build.extra(pltpu.VMEM((2, pieces, 1, stage.width), jnp.float32))
    if spare is not None:
        spare = build.arg(spare, index)
        other = build.out(shape, jnp.bfloat16)
        sems = build.extra(pltpu.SemaphoreType.DMA((2, pieces)))

    def over(at, piece, source):
        target = {SECTION: 1 - lax.axis_index(SECTION)}
        pair = build.bound[sems]
        return remote(source.ref.at[at], other.ref.at[at], pair.at[0, piece], pair.at[1, piece], target)

    def finish(at, piece):
        grad = stage.room[3][at, :].astype(jnp.float32)
        standard, inverse = norm_parts(value.ref[at, :].astype(jnp.float32))
        scaled = grad * gain.ref[...]
        through = inverse * (
            scaled
            - jnp.mean(scaled, axis=-1, keepdims=True)
            - standard * jnp.mean(scaled * standard, axis=-1, keepdims=True)
        )
        total = through + upstream.ref[at, :].astype(jnp.float32)
        result.write(at, total)
        low.write(at, total.astype(jnp.bfloat16))
        build.bound[parts][0, piece] = jnp.sum(grad * standard, axis=0, keepdims=True)
        build.bound[parts][1, piece] = jnp.sum(grad, axis=0, keepdims=True)
        if spare is not None:
            section = lax.axis_index(SECTION)

            @pl.when(section == 0)
            def _():
                over(at, piece, spare).start()

            @pl.when(section == 1)
            def _():
                over(at, piece, low).start()

    def end():
        whole = slice(0, 1)
        gain_grad.write(whole, jnp.sum(build.bound[parts][0], axis=0))
        shift_grad.write(whole, jnp.sum(build.bound[parts][1], axis=0))
        if spare is not None:
            step = stage.rows // pieces

            def one(piece, carry):
                at = span(piece, step)
                over(at, piece, low).wait()
                pltpu.make_async_copy(other.ref.at[at], other.far[0].at[at], other.sem).start()
                return carry

            lax.fori_loop(0, pieces, one, 0)

    stage.finish = finish
    stage.ends.append(end)
    return result, low


def feed_back_stage(build, index, layer, grad_out, before, out_of, into):
    rows, width = grad_out.shape
    stage = Stage(rows, width)
    hidden, block = out_of[0].shape[0], min(BLOCK, rows)
    before = build.arg(before, index)
    out_of, into = build.pick(out_of, layer, index), build.pick(into, layer, index)
    left = build.out((rows, hidden), jnp.bfloat16)

    def prepare(number):
        at = span(number, block)
        grad = nt_product(grad_out.ref[at, :].astype(jnp.bfloat16), out_of.ref[...])
        u = before.ref[at, :]
        slope = 0.5 * (1.0 + lax.erf(u * inv_sqrt_two)) + u * jnp.exp(-0.5 * u * u) * inv_sqrt_tau
        left.write(at, (grad * slope).astype(jnp.bfloat16))

    stage.prepare = prepare
    stage.partial = lambda at: nt_product(left.ref[at, :], into.ref[...])
    return stage


def cross_back_stage(build, index, layer, grad_low, queries, states, seg, out_of, into):
    rows, width = grad_low.shape
    stage = Stage(rows, width)
    columns, block = out_of[0].shape[0], min(BLOCK, rows)
    queries, states, seg = (build.arg(array, index) for array in (queries, states, seg))
    out_of, into = build.pick(out_of, layer, index), build.pick(into, layer, index)
    left = build.out((rows, columns), jnp.bfloat16)
    state_grads = build.out(states.shape, jnp.bfloat16)
    keys_t = build.temp((columns, states.shape[0]), jnp.bfloat16)
    sums = build.temp(states.shape, jnp.float32)
    scale = HEAD ** (-0.5)

    def begin():
        keys_t.ref[...] = states.ref[:, :columns].T
        sums.ref[...] = jnp.zeros(sums.shape, jnp.float32)

    def prepare(number):
        at = span(number, block)
        grad = nt_product(grad_low.ref[at, :], out_of.ref[...]).astype(jnp.bfloat16)
        query = queries.ref[at, :]
        grad_t, query_t = grad.T, query.T
        allowed = text_mask(states.shape[0], seg.ref[:, at])
        query_grads = []
        for head in range(columns // HEAD):
            cols = slice(head * HEAD, (head + 1) * HEAD)
            more = slice(columns + head * HEAD, columns + (head + 1) * HEAD)
            scores = plain_product(states.ref[:, cols], query_t[cols, :]) * scale
            scores = jnp.where(allowed, scores, masked_score)
            e = jnp.exp(scores - jnp.max(scores, axis=0, keepdims=True))
            p = e * (1.0 / jnp.sum(e, axis=0, keepdims=True))
            slope = plain_product(states.ref[:, more], grad_t[cols, :])
            weighted = p * slope
            ds = (weighted - p * jnp.sum(weighted, axis=0, keepdims=True)).astype(jnp.bfloat16)
            query_grads.append((plain_product(keys_t.ref[cols, :], ds) * scale).astype(jnp.bfloat16))
            sums.ref[:, cols] += plain_product(ds, query[:, cols]) * scale
            sums.ref[:, more] += plain_product(p.astype(jnp.bfloat16), grad[:, cols])
        left.write(at, jnp.concatenate(query_grads, axis=0).T)

    def end():
        state_grads.write(slice(0, states.shape[0]), sums.ref[...].astype(jnp.bfloat16))

    stage.begin, stage.prepare = begin, prepare
    stage.partial = lambda at: nt_product(left.ref[at, :], into.ref[...])
    stage.ends.append(end)
    return stage


def self_in_stage(build, index, layer, grads_t, weight, width):
    columns, rows = grads_t.shape
    stage = Stage(rows, width)
    flipped, matrix = build.arg(grads_t, index), build.pick(weight, layer, index)
    left = build.temp((rows, columns), jnp.bfloat16)

    def begin():
        left.ref[...] = flipped.ref[...].T

    stage.begin = begin
    stage.partial = lambda at: plain_product(left.ref[at, :], matrix.ref[...])
    return stage


def forward_chain(
    layer, attended_t, entering, states, seg, gains, weights, collective_id, tasks
):
    output, query, cross, *more = weights
    build = Build()
    base = build.arg(entering, 0, BY_SECTION if entering.ndim == 3 else None)
    first = self_out_stage(build, 0, layer, attended_t, output, base)
    middle, second_normed, _ = residual_norm(build, 0, first, base, gains[2], gains[3], NORM)
    second = cross_stage(build, 1, layer, second_normed, states, seg, query, cross)
    latter, third_normed, _ = residual_norm(build, 1, second, middle, gains[4], gains[5], NORM)
    stages = [first, second]
    if more:
        stages.append(feed_stage(build, 2, layer, third_normed, *more))
        residual_norm(build, 2, stages[2], latter, None, None, END)
    return run_chain(build, stages, collective_id, tasks)


def feed_chain(layer, normed, latter, weights, after, collective_id):
    build = Build()
    normed, latter = build.arg(normed, 0), build.arg(latter, 0)
    stage = feed_stage(build, 0, layer, normed, *weights[3:])
    residual_norm(build, 0, stage, latter, after[0], after[1], NEXT)
    return run_chain(build, [stage], collective_id, [])


def backward_chain(
    layer, upstream, before, latter, queries, states, seg, middle, gains, weights, collective_id, tasks
):
    _, query, cross, expand, reduce = weights
    build = Build()
    arriving = build.arg(upstream, 0, BY_SECTION if upstream.ndim == 3 else None)
    first = feed_back_stage(build, 0, layer, arriving, before, reduce, expand)
    grad_latter, grad_cross = norm_backward(build, 0, first, latter, gains[4], arriving, False)
    second = cross_back_stage(build, 1, layer, grad_cross, queries, states, seg, cross, query)
    norm_backward(build, 1, second, middle, gains[2], grad_latter, True)
    return run_chain(build, [first, second], collective_id, tasks)


def last_chain(layer, grads_t, entering, gain, upstream, weight, spare, collective_id, tasks):
    build = Build()
    upstream = build.arg(upstream, 0)
    stage = self_in_stage(build, 0, layer, grads_t, weight, upstream.shape[1])
    norm_backward(build, 0, stage, entering, gain, upstream, True, spare)
    kinds = (LINE_ONLY,) if spare is None else (LINE_ONLY, SECTION)
    return run_chain(build, [stage], collective_id, tasks, kinds)


def masked_scores(keys, query_t, begins, start):
    reach, block = keys.shape[0], query_t.shape[1]
    scores = plain_product(keys, query_t)
    key_pos = lax.broadcasted_iota(jnp.int32, (reach, 1), 0)
    query_pos = start + lax.broadcasted_iota(jnp.int32, (1, block), 1)
    allowed = (key_pos <= query_pos) & (key_pos >= begins)
    return jnp.where(allowed, scores * HEAD ** (-0.5), masked_score)


def to_frames(source, landing, sems):
    me = lax.axis_index(FRAME)
    return [
        remote(source(other), landing(me), sems.at[0, k], sems.at[1, k], {FRAME: other})
        for k, other in enumerate(frame_partners())
    ]


def self_forward(normed, weight, begins, layer, collective_id, tasks):
    rows, frames, width = normed.shape[0], 4, 3 * HEAD
    all_rows = rows * frames
    build = Build()
    normed, begins, weight = build.arg(normed, 0), build.arg(begins, 1), build.pick(weight, layer, 0)
    heads_t = build.out((width, all_rows), jnp.bfloat16)
    out = build.out((frames * HEAD, rows), jnp.bfloat16)
    own = build.temp((frames, width, rows), jnp.bfloat16)
    keys = build.temp((all_rows, HEAD), jnp.bfloat16)
    mixed_t = build.temp((frames, HEAD, rows), jnp.bfloat16)
    sems = [build.extra(pltpu.SemaphoreType.DMA((2, frames - 1))) for _ in range(2)]

    def body(need, meet, ride):
        me = lax.axis_index(FRAME)
        partners = frame_partners()
        block = min(2 * BLOCK, rows)
        arriving = to_frames(
            lambda g: own.ref.at[g], lambda f: heads_t.ref.at[:, span(f, rows)], build.bound[sems[0]]
        )
        leaving = to_frames(
            lambda g: mixed_t.ref.at[g], lambda f: out.ref.at[span(f, HEAD), :], build.bound[sems[1]]
        )

        def project(other):
            return nt_product(weight.ref[span(other, width), :], normed.ref[...]).astype(jnp.bfloat16)

        meet()
        need(0)
        for k in (2, 1, 0):
            own.ref[partners[k]] = project(partners[k])
            arriving[k].start()
        ride()
        heads_t.ref[:, span(me, rows)] = project(me)
        need(1)
        for copy in arriving:
            copy.wait()
        pltpu.make_async_copy(heads_t.ref, heads_t.far[0], heads_t.sem).start()
        keys.ref[...] = heads_t.ref[HEAD : 2 * HEAD, :].T
        for target in range(frames):
            for start in range(target * rows, (target + 1) * rows, block):
                reach = start + block
                scores = masked_scores(
                    keys.ref[:reach, :], heads_t.ref[:HEAD, start:reach], begins.ref[:, start:reach], start
                )
                e = jnp.exp(scores - jnp.max(scores, axis=0, keepdims=True))
                total = jnp.sum(e, axis=0, keepdims=True)
                mixed = plain_product(heads_t.ref[2 * HEAD :, :reach], e.astype(jnp.bfloat16))
                at = start - target * rows
                mixed_t.ref[target, :, at : at + block] = (mixed * (1.0 / total)).astype(jnp.bfloat16)

            for copy, other in zip(leaving, partners):

                @pl.when(other == target)
                def _():
                    copy.start()

        out.ref[span(me, HEAD), :] = mixed_t.ref[me]
        for copy in leaving:
            copy.wait()
        pltpu.make_async_copy(out.ref, out.far[0], out.sem).start()

    return run_build(build, body, (FRAME,), collective_id, tasks)


def self_backward(heads_t, grad_low, weight, begins, layer, collective_id, tasks):
    rows, frames, width = grad_low.shape[0], 4, 3 * HEAD
    all_rows = rows * frames
    build = Build()
    heads_t, begins = build.arg(heads_t, 1), build.arg(begins, 1)
    grad_low, weight = build.arg(grad_low, 0), build.pick(weight, layer, 0)
    out = build.out((frames * width, rows), jnp.bfloat16)
    own = build.temp((frames, HEAD, rows), jnp.bfloat16)
    grad_t = build.temp((HEAD, all_rows), jnp.bfloat16)
    columns = build.temp((4, all_rows, HEAD), jnp.bfloat16)
    key_sum, value_sum = (build.temp((all_rows, HEAD), jnp.float32) for _ in range(2))
    grads_t = build.temp((frames, width, rows), jnp.bfloat16)
    sems = [build.extra(pltpu.SemaphoreType.DMA((2, frames - 1))) for _ in range(2)]

    def body(need, meet, ride):
        me = lax.axis_index(FRAME)
        partners = frame_partners()
        block = min(2 * BLOCK, rows)
        scale = HEAD ** (-0.5)
        arriving = to_frames(
            lambda g: own.ref.at[g], lambda f: grad_t.ref.at[:, span(f, rows)], build.bound[sems[0]]
        )
        leaving = to_frames(
            lambda g: grads_t.ref.at[g], lambda f: out.ref.at[span(f, width), :], build.bound[sems[1]]
        )

        def project(other):
            return nt_product(weight.ref[span(other, HEAD), :], grad_low.ref[...]).astype(jnp.bfloat16)

        meet()
        need(0)
        for k in (2, 1, 0):
            own.ref[partners[k]] = project(partners[k])
            arriving[k].start()
        ride()
        grad_t.ref[:, span(me, rows)] = project(me)
        key_sum.ref[...] = jnp.zeros(key_sum.shape, jnp.float32)
        value_sum.ref[...] = jnp.zeros(key_sum.shape, jnp.float32)
        need(1)
        for part in range(3):
            columns.ref[part] = heads_t.ref[part * HEAD : (part + 1) * HEAD, :].T
        for copy in arriving:
            copy.wait()
        columns.ref[3] = grad_t.ref[...].T
        for target in reversed(range(frames)):
            for start in reversed(range(target * rows, (target + 1) * rows, block)):
                reach = start + block
                scores = masked_scores(
                    columns.ref[1, :reach, :],
                    heads_t.ref[:HEAD, start:reach],
                    begins.ref[:, start:reach],
                    start,
                )
                e = jnp.exp(scores - jnp.max(scores, axis=0, keepdims=True))
                p = e * (1.0 / jnp.sum(e, axis=0, keepdims=True))
                slope = plain_product(columns.ref[2, :reach, :], grad_t.ref[:, start:reach])
                weighted = p * slope
                ds = (weighted - p * jnp.sum(weighted, axis=0, keepdims=True)).astype(jnp.bfloat16)
                value_sum.ref[:reach, :] += plain_product(
                    p.astype(jnp.bfloat16), columns.ref[3, start:reach, :]
                )
                key_sum.ref[:reach, :] += plain_product(ds, columns.ref[0, start:reach, :])
                here = slice(start - target * rows, reach - target * rows)
                query_grad = plain_product(heads_t.ref[HEAD : 2 * HEAD, :reach], ds) * scale
                grads_t.ref[target, :HEAD, here] = query_grad.astype(jnp.bfloat16)
                key_grad = key_sum.ref[start:reach, :] * scale
                grads_t.ref[target, HEAD : 2 * HEAD, here] = key_grad.T.astype(jnp.bfloat16)
                grads_t.ref[target, 2 * HEAD :, here] = value_sum.ref[start:reach, :].T.astype(jnp.bfloat16)

            for copy, other in zip(leaving, partners):

                @pl.when(other == target)
                def _():
                    copy.start()

        out.ref[span(me, width), :] = grads_t.ref[me]
        for copy in leaving:
            copy.wait()
        pltpu.make_async_copy(out.ref, out.far[0], out.sem).start()

    return run_build(build, body, (FRAME,), collective_id, tasks)


def matmul(left_side, right_side):
    return jnp.dot(left_side, right_side, preferred_element_type=jnp.float32)


def matmul_tn(left_side, right_side):
    return lax.dot_general(
        left_side, right_side, (((0,), (0,)), ((), ())), preferred_element_type=jnp.float32
    )


def matmul_nt(left_side, right_side):
    return lax.dot_general(
        left_side, right_side, (((1,), (1,)), ((), ())), preferred_element_type=jnp.float32
    )


def layer_norm(signal, gain_vec, shift_vec):
    average = jnp.mean(signal, axis=-1, keepdims=True)
    centered = signal - average
    variance = jnp.mean(centered * centered, axis=-1, keepdims=True)
    return centered * lax.rsqrt(variance + 1e-05) * gain_vec + shift_vec


def norm_back(signal, gain_vec, upstream):
    average = jnp.mean(signal, axis=-1, keepdims=True)
    centered = signal - average
    inverse = lax.rsqrt(jnp.mean(centered * centered, axis=-1, keepdims=True) + 1e-05)
    standard = centered * inverse
    scaled = upstream * gain_vec
    through = inverse * (
        scaled
        - jnp.mean(scaled, axis=-1, keepdims=True)
        - standard * jnp.mean(scaled * standard, axis=-1, keepdims=True)
    )
    return (through, jnp.sum(upstream * standard, axis=0), jnp.sum(upstream, axis=0))


def head_total(partial_sum):
    return lax.psum(partial_sum.astype(jnp.bfloat16), LINE).astype(jnp.float32)


def swapped(x):
    return lax.ppermute(x, SECTION, [(0, 1), (1, 0)])


def split_heads(matrix):
    return matrix.reshape(matrix.shape[0], matrix.shape[1] // HEAD, HEAD)


def softmax_rows(query, key_rows, allowed):
    logits = jnp.einsum(
        "qhd,khd->hqk",
        split_heads(query),
        split_heads(key_rows),
        preferred_element_type=jnp.float32,
    ) * HEAD ** (-0.5)
    logits = jnp.where(allowed[None], logits, masked_score)
    exponent = jnp.exp(logits - jnp.max(logits, axis=-1, keepdims=True))
    return exponent / jnp.sum(exponent, axis=-1, keepdims=True)


def attend(query, key_rows, value_rows, allowed):
    weights_low = softmax_rows(query, key_rows, allowed).astype(jnp.bfloat16)
    result = jnp.einsum(
        "hqk,khd->qhd", weights_low, split_heads(value_rows), preferred_element_type=jnp.float32
    )
    return result.reshape(query.shape).astype(jnp.bfloat16)


def attend_back(query, key_rows, value_rows, allowed, grad_out):
    probabilities = softmax_rows(query, key_rows, allowed)
    weights_low = probabilities.astype(jnp.bfloat16)
    grad_heads = split_heads(grad_out)
    grad_prob = jnp.einsum(
        "qhd,khd->hqk", grad_heads, split_heads(value_rows), preferred_element_type=jnp.float32
    )
    centre = jnp.sum(probabilities * grad_prob, axis=-1, keepdims=True)
    grad_logit = (probabilities * (grad_prob - centre)).astype(jnp.bfloat16)
    scale = HEAD ** (-0.5)
    grad_query = (
        jnp.einsum(
            "hqk,khd->qhd", grad_logit, split_heads(key_rows), preferred_element_type=jnp.float32
        )
        * scale
    )
    grad_keys = (
        jnp.einsum(
            "hqk,qhd->khd", grad_logit, split_heads(query), preferred_element_type=jnp.float32
        )
        * scale
    )
    grad_values = jnp.einsum(
        "hqk,qhd->khd", weights_low, grad_heads, preferred_element_type=jnp.float32
    )
    return (
        grad_query.reshape(query.shape),
        grad_keys.reshape(key_rows.shape),
        grad_values.reshape(value_rows.shape),
    )


def sum_rows(rows):
    return jnp.concatenate(rows, axis=0)


def on_four_frames(inputs, lengths, text, cotangent, vector_args, matrix_args):
    section = lax.axis_index(SECTION)
    at_zero = section == 0
    frame_index = lax.axis_index(FRAME)
    micro_count, rows_dev, model_width = inputs.shape
    rows_all = rows_dev * 4
    (
        query_weight,
        key_weight,
        value_weight,
        output_weight,
        cross_query,
        cross_key,
        cross_value,
        cross_output,
        expand_weight,
        reduce_weight,
    ) = (w[0] for w in matrix_args)
    columns = query_weight.shape[1]
    heads = columns // HEAD

    def by_section(first, second):
        return jnp.where(at_zero, first, second)

    own_vectors = jnp.pad(jnp.concatenate(vector_args, axis=0), ((0, 2), (0, 0)))
    heads_weight = jnp.stack(
        [w.T.reshape(heads, HEAD, model_width) for w in (query_weight, key_weight, value_weight)], axis=1
    ).reshape(3 * columns, model_width)
    _, (other_heads, other_vectors) = call(
        None, [], [], [], (), 1, [WeightTask(heads_weight), CrossTask(own_vectors, own_vectors, False)]
    )
    vectors = [by_section(own_vectors, other_vectors), by_section(other_vectors, own_vectors)]
    heads_pair = (heads_weight, other_heads)
    text_local = text.reshape(-1, model_width)
    text_states = jnp.concatenate(
        [matmul(text_local, cross_key), matmul(text_local, cross_value)], axis=1
    ).astype(jnp.bfloat16)
    text_states = text_states.reshape(micro_count, -1, 2 * columns)

    item_ends = jnp.cumsum(lax.dynamic_index_in_dim(lengths, section, 0, keepdims=False))
    passed = jnp.arange(rows_all, dtype=jnp.int32)[None, :] >= item_ends[:, None]
    begins = jnp.max(jnp.where(passed, item_ends[:, None], 0), axis=0, keepdims=True).astype(jnp.int32)
    seg = jnp.sum(passed.astype(jnp.int32), axis=0, keepdims=True)
    seg = lax.dynamic_slice_in_dim(seg, frame_index * rows_dev, rows_dev, 1)

    entering = inputs
    normed = layer_norm(
        lax.dynamic_index_in_dim(inputs, section, 0, keepdims=False).astype(jnp.float32),
        vectors[0][0],
        vectors[0][1],
    ).astype(jnp.bfloat16)
    saved, results = [], []
    for layer in range(2):
        gains, first = vectors[layer], layer == 0
        tasks = []
        if first:
            tasks = [WeightTask(w) for w in (output_weight, cross_query, cross_output)]
            tasks.append(TextTask(text_states))
        (heads_t, attended_t), carried = self_forward(
            normed, heads_pair, begins, layer, 2 + layer, tasks
        )
        tasks = []
        if first:
            weights = list(zip((output_weight, cross_query, cross_output), carried))
            states = carried[3].reshape(2, -1, 2 * columns)
            (middle, second_normed, queries, cross_att, latter, third_normed), carried = forward_chain(
                layer,
                attended_t,
                entering,
                states[layer],
                seg,
                gains,
                weights,
                4,
                [WeightTask(expand_weight), WeightTask(reduce_weight)],
            )
            weights += list(zip((expand_weight, reduce_weight), carried))
            (before, hidden, result, next_normed, result_low), _ = feed_chain(
                layer, third_normed, latter, weights, vectors[1], 5
            )
        else:
            outs, _ = forward_chain(
                layer, attended_t, entering, states[layer], seg, gains, weights, 6, []
            )
            (middle, second_normed, queries, cross_att, latter, third_normed) = outs[:6]
            before, hidden, result, result_low = outs[6:]
        saved.append(
            (
                entering,
                normed,
                heads_t,
                attended_t,
                middle,
                second_normed,
                latter,
                third_normed,
                queries,
                cross_att,
                before,
                hidden,
            )
        )
        results.append(result)
        if first:
            normed, entering = next_normed, result_low

    upstream = cotangent
    in_grads, in_lows, vector_grads, shares = [None] * 2, [None] * 2, [None] * 2, [{}, {}]
    totals = {}

    def low_product(left, right):
        return matmul_tn(left, right).astype(jnp.bfloat16)

    def crossing(*names):
        return [CrossTask(shares[0][name], shares[1][name], True) for name in names]

    def shared(layer, names, arrays):
        for name, array in zip(names, arrays):
            shares[layer][name] = array

    held_back = {}
    for layer in (1, 0):
        last = layer == 0
        gains = vectors[layer]
        (
            entering,
            normed,
            heads_t,
            attended_t,
            middle,
            second_normed,
            latter,
            third_normed,
            queries,
            cross_att,
            before,
            hidden,
        ) = saved[layer]
        if last:
            grad_out = in_lows[1]
        else:
            grad_out = lax.dynamic_index_in_dim(cotangent, section, 0, keepdims=False)
            grad_out = grad_out.astype(jnp.bfloat16)
        tasks = [ShareTask(low_product(hidden, grad_out))]
        if last:
            tasks += [ShareTask(grad) for grad in held_back.values()]
        else:
            tasks.append(CrossTask(saved[1][0], result_low, False))
        (
            grad_pre,
            grad_cross,
            third_gain_grad,
            third_shift_grad,
            grad_queries,
            grad_states,
            grad_middle,
            grad_self,
            second_gain_grad,
            second_shift_grad,
        ), carried = backward_chain(
            layer,
            upstream,
            before,
            latter,
            queries,
            states[layer],
            seg,
            middle,
            gains,
            weights,
            8 + layer,
            tasks,
        )
        shares[layer]["reduce"] = carried[0]
        if last:
            shared(1, held_back, carried[1:])
        else:
            other_result = carried[1]

        expand_grad = low_product(third_normed, grad_pre)
        tasks = [ShareTask(grad_states)]
        if last:
            tasks += [ShareTask(expand_grad)] + crossing("reduce")
        (grad_heads_t,), carried = self_backward(
            heads_t, grad_self, weights[0], begins, layer, 10 + layer, tasks
        )
        shares[layer]["states"] = carried[0]
        if last:
            shares[0]["expand"], totals["reduce"] = carried[1:]

        grads = {
            "cross_output": low_product(cross_att, grad_cross),
            "cross_query": low_product(second_normed, grad_queries),
            "output": matmul(attended_t, grad_self).astype(jnp.bfloat16),
            "heads": lax.dot_general(
                normed, grad_heads_t, (((0,), (1,)), ((), ())), preferred_element_type=jnp.float32
            ).astype(jnp.bfloat16),
        }
        if last:
            tasks = [ShareTask(grad) for grad in grads.values()] + crossing("expand")
            tasks.append(CrossTask(shares[0]["states"], shares[1]["states"], False))
        else:
            held_back = grads
            tasks = [ShareTask(expand_grad)]
        (in_grads[layer], in_lows[layer], first_gain_grad, first_shift_grad, *other_grad), carried = (
            last_chain(
                layer,
                grad_heads_t,
                entering,
                gains[0],
                grad_middle,
                heads_pair,
                in_lows[1] if last else None,
                12 + layer,
                tasks,
            )
        )
        if last:
            shared(0, grads, carried)
            totals["expand"], other_states = carried[len(grads) :]
        else:
            shares[1]["expand"] = carried[0]
        vector_grads[layer] = sum_rows(
            [
                first_gain_grad,
                first_shift_grad,
                second_gain_grad,
                second_shift_grad,
                third_gain_grad,
                third_shift_grad,
                jnp.zeros((2, model_width), jnp.float32),
            ]
        )
        upstream = in_lows[layer]

    own_states = by_section(shares[0]["states"], shares[1]["states"])
    text_rows = sum_rows([by_section(own_states, other_states), by_section(other_states, own_states)])
    key_part, value_part = text_rows[:, :columns], text_rows[:, columns:]
    text_part = matmul_nt(key_part, cross_key) + matmul_nt(value_part, cross_value)
    names = ("heads", "output", "cross_query", "cross_output")
    _, (text_grad, vector_total, cross_grads, *carried) = call(
        None,
        [],
        [],
        [],
        (),
        18,
        [
            TotalTask(text_part.astype(jnp.bfloat16)),
            VectorTask(jnp.stack(vector_grads)),
            ShareTask(low_product(text_local, text_rows)),
        ]
        + crossing(*names),
    )
    totals.update(zip(names, carried))
    text_grad = text_grad.astype(jnp.float32).reshape(text.shape)
    vector_total = lax.dynamic_slice_in_dim(
        vector_total, frame_index * (model_width // 4), model_width // 4, 1
    )
    grad_query, grad_key, grad_value = (
        totals["heads"].reshape(-1, heads, 3, HEAD)[:, :, i].reshape(-1, columns) for i in range(3)
    )
    cross_grads = cross_grads.astype(jnp.float32)

    def both_micros(pair, other):
        own = by_section(*pair)
        other = other.astype(own.dtype)
        return jnp.where(at_zero, jnp.stack([own, other]), jnp.stack([other, own]))

    ordered = (
        vector_total[0],
        vector_total[1],
        grad_query,
        grad_key,
        grad_value,
        totals["output"],
        vector_total[2],
        vector_total[3],
        totals["cross_query"],
        cross_grads[:, :columns],
        cross_grads[:, columns:],
        totals["cross_output"],
        vector_total[4],
        vector_total[5],
        totals["expand"],
        totals["reduce"],
    )
    layer_outputs = both_micros(results, other_result)
    input_grads = both_micros(in_grads, other_grad[0])
    return (layer_outputs[None], input_grads[None], text_grad) + tuple(g[None] for g in ordered)


def self_attention(query, key_rows, value_rows, masks):
    all_keys = lax.all_gather(key_rows, FRAME, axis=0, tiled=True)
    all_values = lax.all_gather(value_rows, FRAME, axis=0, tiled=True)
    return attend(query, all_keys, all_values, masks["own"]), (query, all_keys, all_values)


def self_attention_back(kept, grad_out, masks):
    query, keys, values = kept
    grad_q, grad_k_all, grad_v_all = attend_back(query, keys, values, masks["own"], grad_out)
    grad_k, grad_v = (
        lax.psum_scatter(g.astype(jnp.bfloat16), FRAME, scatter_dimension=0, tiled=True)
        for g in (grad_k_all, grad_v_all)
    )
    return grad_q.astype(jnp.bfloat16), grad_k, grad_v


def forward(entering, vectors, weights, cross_keys, cross_values, masks):
    first_gain, first_shift, second_gain, second_shift, third_gain, third_shift = vectors
    (
        query_weight,
        key_weight,
        value_weight,
        output_weight,
        cross_query,
        cross_output,
        expand_weight,
        reduce_weight,
    ) = weights
    signal = entering.astype(jnp.float32)
    first_normed = layer_norm(signal, first_gain, first_shift).astype(jnp.bfloat16)
    query = matmul(first_normed, query_weight).astype(jnp.bfloat16)
    key_rows = matmul(first_normed, key_weight).astype(jnp.bfloat16)
    value_rows = matmul(first_normed, value_weight).astype(jnp.bfloat16)
    attended, heads_kept = self_attention(query, key_rows, value_rows, masks)
    middle = signal + head_total(matmul(attended, output_weight))
    second_normed = layer_norm(middle, second_gain, second_shift).astype(jnp.bfloat16)
    cross_queries = matmul(second_normed, cross_query).astype(jnp.bfloat16)
    cross_att = attend(cross_queries, cross_keys, cross_values, masks["cross"])
    latter = middle + head_total(matmul(cross_att, cross_output))
    third_normed = layer_norm(latter, third_gain, third_shift).astype(jnp.bfloat16)
    hidden_pre = matmul(third_normed, expand_weight)
    hidden_act = jax.nn.gelu(hidden_pre, approximate=False).astype(jnp.bfloat16)
    result = latter + head_total(matmul(hidden_act, reduce_weight))
    saved = (
        signal,
        first_normed,
        heads_kept,
        attended,
        middle,
        second_normed,
        cross_queries,
        cross_att,
        latter,
        third_normed,
        hidden_pre,
        hidden_act,
    )
    return (result, saved)


def backward(saved, upstream, vectors, weights, cross_keys, cross_values, masks):
    first_gain, first_shift, second_gain, second_shift, third_gain, third_shift = vectors
    (
        query_weight,
        key_weight,
        value_weight,
        output_weight,
        cross_query,
        cross_output,
        expand_weight,
        reduce_weight,
    ) = weights
    (
        signal,
        first_normed,
        heads_kept,
        attended,
        middle,
        second_normed,
        cross_queries,
        cross_att,
        latter,
        third_normed,
        hidden_pre,
        hidden_act,
    ) = saved
    grad_out = upstream.astype(jnp.bfloat16)
    grad_reduce = matmul_tn(hidden_act, grad_out)
    grad_act = matmul_nt(grad_out, reduce_weight)
    slope = (
        0.5 * (1.0 + lax.erf(hidden_pre * inv_sqrt_two))
        + hidden_pre * jnp.exp(-0.5 * hidden_pre * hidden_pre) * inv_sqrt_tau
    )
    grad_pre = (grad_act * slope).astype(jnp.bfloat16)
    grad_expand = matmul_tn(third_normed, grad_pre)
    grad_third = head_total(matmul_nt(grad_pre, expand_weight))
    grad_latter, grad_third_gain, grad_third_shift = norm_back(latter, third_gain, grad_third)
    grad_latter = grad_latter + upstream
    grad_cross = grad_latter.astype(jnp.bfloat16)
    grad_cross_output = matmul_tn(cross_att, grad_cross)
    grad_cross_att = matmul_nt(grad_cross, cross_output).astype(jnp.bfloat16)
    grad_cq, grad_ck, grad_cv = attend_back(
        cross_queries, cross_keys, cross_values, masks["cross"], grad_cross_att
    )
    grad_text_rows = jnp.concatenate([grad_ck, grad_cv], axis=1).astype(jnp.bfloat16)
    grad_text_rows = lax.psum_scatter(
        grad_text_rows.reshape(ITEMS, TEXT, -1), FRAME, scatter_dimension=1, tiled=True
    )
    grad_cquery = grad_cq.astype(jnp.bfloat16)
    grad_cross_query = matmul_tn(second_normed, grad_cquery)
    grad_second = head_total(matmul_nt(grad_cquery, cross_query))
    grad_middle, grad_second_gain, grad_second_shift = norm_back(middle, second_gain, grad_second)
    grad_middle = grad_middle + grad_latter
    grad_self = grad_middle.astype(jnp.bfloat16)
    grad_output = matmul_tn(attended, grad_self)
    grad_att = matmul_nt(grad_self, output_weight).astype(jnp.bfloat16)
    grad_query_low, grad_key_low, grad_value_low = self_attention_back(heads_kept, grad_att, masks)
    grad_query = matmul_tn(first_normed, grad_query_low)
    grad_key = matmul_tn(first_normed, grad_key_low)
    grad_value = matmul_tn(first_normed, grad_value_low)
    grad_first = head_total(
        matmul_nt(grad_query_low, query_weight)
        + matmul_nt(grad_key_low, key_weight)
        + matmul_nt(grad_value_low, value_weight)
    )
    grad_signal, grad_first_gain, grad_first_shift = norm_back(signal, first_gain, grad_first)
    grad_signal = grad_signal + grad_middle
    vector_grads = (
        grad_first_gain,
        grad_first_shift,
        grad_second_gain,
        grad_second_shift,
        grad_third_gain,
        grad_third_shift,
    )
    matrix_grads = (
        grad_query,
        grad_key,
        grad_value,
        grad_output,
        grad_cross_query,
        grad_cross_output,
        grad_expand,
        grad_reduce,
    )
    matrix_grads = tuple(
        lax.psum_scatter(g.astype(jnp.bfloat16), FRAME, scatter_dimension=0, tiled=True)
        for g in matrix_grads
    )
    return grad_signal, vector_grads, matrix_grads, grad_text_rows


def per_device(
    inputs,
    lengths,
    text,
    cotangent,
    first_gain,
    first_shift,
    query_weight,
    key_weight,
    value_weight,
    output_weight,
    second_gain,
    second_shift,
    cross_query,
    cross_key,
    cross_value,
    cross_output,
    third_gain,
    third_shift,
    expand_weight,
    reduce_weight,
):
    head_count, frame_count = lax.axis_size(LINE), lax.axis_size(FRAME)
    local_heads = query_weight.shape[2] // HEAD
    if head_count == 4 and frame_count == 4 and local_heads == 4:
        return on_four_frames(
            inputs,
            lengths,
            text,
            cotangent,
            (first_gain, first_shift, second_gain, second_shift, third_gain, third_shift),
            (
                query_weight,
                key_weight,
                value_weight,
                output_weight,
                cross_query,
                cross_key,
                cross_value,
                cross_output,
                expand_weight,
                reduce_weight,
            ),
        )
    section = lax.axis_index(SECTION)
    at_zero = section == 0
    frame_index = lax.axis_index(FRAME)
    micro_count, rows_dev, model_width = inputs.shape
    rows_all = rows_dev * frame_count
    text_rows_dev = text.shape[2]

    def keep(pair):
        return jnp.where(at_zero, pair[0], pair[1])

    def give(pair):
        return jnp.where(at_zero, pair[1], pair[0])

    vector_args = jnp.concatenate(
        [first_gain, first_shift, second_gain, second_shift, third_gain, third_shift], axis=0
    )
    vectors = lax.all_gather(vector_args, SECTION)
    matrix_args = (
        query_weight,
        key_weight,
        value_weight,
        output_weight,
        cross_query,
        cross_output,
        expand_weight,
        reduce_weight,
    )
    matrices = [lax.all_gather(w[0], SECTION) for w in matrix_args]
    weights = [tuple(w[layer] for w in matrices) for layer in range(2)]

    text_full = lax.all_gather(text, FRAME, axis=2, tiled=True)
    text_flat = text_full.reshape(micro_count * ITEMS * TEXT, model_width)
    text_heads = jnp.concatenate(
        [matmul(text_flat, cross_key[0]), matmul(text_flat, cross_value[0])], axis=1
    ).astype(jnp.bfloat16)
    text_heads = text_heads.reshape(micro_count, ITEMS * TEXT, -1)
    own_text = keep(text_heads)
    other_text = swapped(give(text_heads))
    columns = cross_key.shape[2]
    cross_states = [
        jnp.where(at_zero, own_text, other_text),
        jnp.where(at_zero, other_text, own_text),
    ]
    cross_keys = [c[:, :columns] for c in cross_states]
    cross_values = [c[:, columns:] for c in cross_states]

    item_ends = jnp.cumsum(lax.dynamic_index_in_dim(lengths, section, 0, keepdims=False))
    all_positions = jnp.arange(rows_all, dtype=jnp.int32)
    seg_all = jnp.sum((all_positions[:, None] >= item_ends[None, :]).astype(jnp.int32), axis=1)
    own_start = frame_index * rows_dev
    own_positions = own_start + jnp.arange(rows_dev, dtype=jnp.int32)
    seg_own = lax.dynamic_slice_in_dim(seg_all, own_start, rows_dev)
    text_item = jnp.arange(ITEMS * TEXT, dtype=jnp.int32) // TEXT
    masks = {
        "own": (all_positions[None, :] <= own_positions[:, None])
        & (seg_own[:, None] == seg_all[None, :]),
        "cross": seg_own[:, None] == text_item[None, :],
    }

    signal = lax.dynamic_index_in_dim(inputs, section, 0, keepdims=False)
    results, saves = [], []
    for layer in range(2):
        result, saved = forward(
            signal, vectors[layer], weights[layer], cross_keys[layer], cross_values[layer], masks
        )
        results.append(result)
        saves.append(saved)
        signal = result.astype(jnp.bfloat16)

    upstream = lax.dynamic_index_in_dim(cotangent, section, 0, keepdims=False)
    in_grads, vector_grads, matrix_grads, text_grads = [None] * 2, [None] * 2, [None] * 2, [None] * 2
    for layer in (1, 0):
        grad_signal, vector_grads[layer], matrix_grads[layer], text_grads[layer] = backward(
            saves[layer],
            upstream,
            vectors[layer],
            weights[layer],
            cross_keys[layer],
            cross_values[layer],
            masks,
        )
        in_grads[layer] = grad_signal
        upstream = grad_signal.astype(jnp.bfloat16).astype(jnp.float32)

    def both_micros(pair):
        own = keep(pair)
        other = swapped(give([p.astype(jnp.bfloat16) for p in pair])).astype(own.dtype)
        return jnp.stack([jnp.where(at_zero, own, other), jnp.where(at_zero, other, own)])

    layer_outputs = both_micros(results)
    input_grads = both_micros(in_grads)
    totals = [
        keep(pair).astype(jnp.float32) + swapped(give(pair)).astype(jnp.float32)
        for pair in zip(*matrix_grads)
    ]
    text_rows = both_micros(text_grads)
    text_rows = text_rows.reshape(micro_count * ITEMS * text_rows_dev, -1)
    key_part, value_part = text_rows[:, :columns], text_rows[:, columns:]
    text_local = text.reshape(-1, model_width)
    grad_cross_key, grad_cross_value = (
        lax.psum_scatter(
            matmul_tn(text_local, part).astype(jnp.bfloat16),
            FRAME,
            scatter_dimension=0,
            tiled=True,
        ).astype(jnp.float32)
        for part in (key_part, value_part)
    )
    text_part = matmul_nt(key_part, cross_key[0]) + matmul_nt(value_part, cross_value[0])
    text_grad = lax.psum(text_part.astype(jnp.bfloat16), (SECTION, LINE)).astype(jnp.float32)
    text_grad = text_grad.reshape(text.shape)

    stacked = jnp.stack([jnp.stack(v) for v in vector_grads])
    stacked = lax.psum_scatter(
        stacked.astype(jnp.bfloat16), FRAME, scatter_dimension=2, tiled=True
    )
    vector_total = keep(stacked).astype(jnp.float32) + swapped(give(stacked)).astype(jnp.float32)

    grad_q, grad_k, grad_v, grad_o, grad_cq, grad_co, grad_e, grad_r = totals
    ordered = (
        vector_total[0],
        vector_total[1],
        grad_q,
        grad_k,
        grad_v,
        grad_o,
        vector_total[2],
        vector_total[3],
        grad_cq,
        grad_cross_key,
        grad_cross_value,
        grad_co,
        vector_total[4],
        vector_total[5],
        grad_e,
        grad_r,
    )
    return (layer_outputs[None], input_grads[None], text_grad) + tuple(g[None] for g in ordered)


def solution(mesh):
    return jax.shard_map(
        per_device,
        mesh=mesh,
        in_specs=(
            P(None, FRAME, None),
            P(),
            P(None, None, FRAME, None),
            P(None, FRAME, None),
            P(SECTION, None),
            P(SECTION, None),
            P(SECTION, None, LINE),
            P(SECTION, None, LINE),
            P(SECTION, None, LINE),
            P(SECTION, LINE, None),
            P(SECTION, None),
            P(SECTION, None),
            P(SECTION, None, LINE),
            P(SECTION, None, LINE),
            P(SECTION, None, LINE),
            P(SECTION, LINE, None),
            P(SECTION, None),
            P(SECTION, None),
            P(SECTION, None, LINE),
            P(SECTION, LINE, None),
        ),
        out_specs=(
            P(SECTION, None, FRAME, None),
            P(SECTION, None, FRAME, None),
            P(None, None, FRAME, None),
            P(SECTION, FRAME),
            P(SECTION, FRAME),
            P(SECTION, FRAME, LINE),
            P(SECTION, FRAME, LINE),
            P(SECTION, FRAME, LINE),
            P(SECTION, (LINE, FRAME), None),
            P(SECTION, FRAME),
            P(SECTION, FRAME),
            P(SECTION, FRAME, LINE),
            P(SECTION, FRAME, LINE),
            P(SECTION, FRAME, LINE),
            P(SECTION, (LINE, FRAME), None),
            P(SECTION, FRAME),
            P(SECTION, FRAME),
            P(SECTION, FRAME, LINE),
            P(SECTION, (LINE, FRAME), None),
        ),
        check_vma=False,
    )
```

time: 809 us -> 699 us (0.86)
  Pallas kernels: 718 us -> 604 us
    pallas_call x18 -> x13, Pallas kernels: 718 us -> 604 us  [call(): pl.pallas_call(kernel, out_shape=all_outs, in_specs=in_specs, out_specs=o...]
where the time goes in v3:
time: 699 us; the launch traced here: 690 us
  Pallas kernels  604 us (86%)
  matrix products  33.3 us (5%)
  local copies, waits for them, and re-layouts  25.9 us (4%)
  other arithmetic  24.7 us (4%)
    pallas_call x13, Pallas kernels, call(): pl.pallas_call(kernel, out_shape=all_outs, in_specs=in_specs, out_specs=o...  604 us
    dot_general x9, matrix products, matmul_tn(): lax.dot_general(left_side, right_side, (((0,), (0,)), ((), ())), preferre...  23.5 us

profile of v3, /device:TPU:0, one launch (start us, length us, event | category | flops | bytes accessed | tf_op | source)
XLA Modules:
  0.0 689.6 jit_solution(936971003321074133)
XLA Ops:
  0.8 0.8 fusion.21
  1.8 1.5 convert_reduce_fusion
  3.3 1.7 fusion.3
  5.0 0.7 convert_reduce_fusion.1
  5.7 0.7 dynamic-slice.3
  6.5 0.6 pad.4.refs_1_.refs_2_
  7.6 0.7 pad_maximum_fusion.3.refs_7_
  9.1 1.3 copy.55
  10.4 25.3 %shard_map.339 = (bf16[768,1024]{1,0:T(8,128)(2,1)}, f32[8,1024]{1,0:T(8,128)}) custom-call(bf16[768,1024]{1,0:T(8,128)(2,1)} %bitcast.118, f32[8,1024]{1,0:T(8,128)} %pad.4.refs_1_.refs_2_, f32[8,1024]{1,0:T(8,128)} %pad.4.refs_1_.refs_2_), custom_call_target="tpu_custom_call" | custom-call | tf_op jit(solution)/shard_map/pallas_call | solution.py:457
  35.6 0.8 broadcast_select_fusion.3
  36.4 0.6 fusion.28
  37.0 0.6 fusion.29
  37.7 1.4 fusion.6.refs_0_
  39.1 28.3 %shard_map.340 = (bf16[192,2048]{1,0:T(8,128)(2,1)}, bf16[256,512]{1,0:T(8,128)(2,1)}, bf16[256,1024]{1,0:T(8,128)(2,1)}, bf16[1024,256]{1,0:T(8,128)(2,1)}, bf1...) custom-call(bf16[512,1024]{1,0:T(8,128)(2,1)} %fusion.6.refs_0_, s32[1,2048]{1,0:T(1,128)} %bitcast.168, ...), custom_call_target="tpu_custom_call" | custom-call | tf_op jit(solution)/shard_map/pallas_call | solution.py:457
  67.3 1.9 fusion.26
  69.2 67.9 %shard_map.341 = (f32[512,1024]{1,0:T(8,128)}, bf16[512,1024]{1,0:T(8,128)(2,1)}, bf16[512,256]{1,0:T(8,128)(2,1)}, bf16[512,256]{1,0:T(8,128)(2,1)}, f32[512,10...) custom-call(bf16[2,512,1024]{2,1,0:T(8,128)(2,1)} %refs_4_.1, ...), custom_call_target="tpu_custom_call" | custom-call | tf_op jit(solution)/shard_map/pallas_call | solution.py:457
  137.1 40.8 %shard_map.342 = (f32[512,1024]{1,0:T(8,128)}, bf16[512,1024]{1,0:T(8,128)(2,1)}, f32[512,1024]{1,0:T(8,128)}, bf16[512,1024]{1,0:T(8,128)(2,1)}, bf16[512,1024]{1,0:T(8,128)(2,1)}) custom-call(bf16[512,1024]{1,0:T(8,128)(2,1)} %get-tuple-element.114.refs_0_, f32[512,1024]{1,0:T(8,128)} %get-tuple-element.115.refs_1_.refs_6_, bf16[1024,1024]{1,0:T(8,128)(2,1)} %bitcast.124, ...), custom_call_target="tpu_custom_call" | custom-call | tf_op jit(solution)/shard_map/pallas_call | solution.py:457
  177.9 21.7 %shard_map.343 = (bf16[192,2048]{1,0:T(8,128)(2,1)}, bf16[256,512]{1,0:T(8,128)(2,1)}) custom-call(bf16[512,1024]{1,0:T(8,128)(2,1)} %get-tuple-element.120.refs_0_, s32[1,2048]{1,0:T(1,128)} %bitcast.169, bf16[768,1024]{1,0:T(8,128)(2,1)} %bitcast.120, bf16[768,1024]{1,0:T(8,128)(2,1)} %get-tuple-element.108.refs_3_), custom_call_target="tpu_custom_call" | custom-call | tf_op jit(solution)/shard_map/pallas_call | solution.py:457
  199.6 86.5 %shard_map.344 = (f32[512,1024]{1,0:T(8,128)}, bf16[512,1024]{1,0:T(8,128)(2,1)}, bf16[512,256]{1,0:T(8,128)(2,1)}, bf16[512,256]{1,0:T(8,128)(2,1)}, f32[512,10...) custom-call(bf16[512,1024]{1,0:T(8,128)(2,1)} %get-tuple-element.119, ...), custom_call_target="tpu_custom_call" | custom-call | tf_op jit(solution)/shard_map/pallas_call | solution.py:457
  286.1 0.4 select_bitcast_fusion.1
  286.6 0.8 copy-done.48
  287.4 4.2 convolution_convert_fusion.3.refs_17_
  291.6 74.9 %shard_map.345 = (bf16[512,1024]{1,0:T(8,128)(2,1)}, bf16[512,1024]{1,0:T(8,128)(2,1)}, f32[1,1024]{1,0:T(1,128)}, f32[1,1024]{1,0:T(1,128)}, bf16[512,256]{1,0:...) custom-call(f32[2,512,1024]{2,1,0:T(8,128)} %refs_0_.3, ...), custom_call_target="tpu_custom_call" | custom-call | tf_op jit(solution)/shard_map/pallas_call | solution.py:457
  366.5 2.2 convolution_convert_fusion.11.refs_19_
  368.7 28.3 %shard_map.346 = (bf16[768,512]{1,0:T(8,128)(2,1)}, bf16[64,512]{1,0:T(8,128)(2,1)}) custom-call(bf16[192,2048]{1,0:T(8,128)(2,1)} %get-tuple-element.131.refs_0_, s32[1,2048]{1,0:T(1,128)} %bitcast.170, bf16[512,1024]{1,0:T(8,128)(2,1)} %get-tuple-element.132.refs_2_, bf16[256,1024]{1,0:T(8,128)(2,1)} %bitcast.146, ...), custom_call_target="tpu_custom_call" | custom-call | tf_op jit(solution)/shard_map/pallas_call | solution.py:457
  397.1 1.3 convolution_convert_fusion.10.refs_20_
  398.4 1.3 convolution_convert_fusion.12.refs_18_
  399.7 2.2 convolution_convert_fusion.5.refs_21_
  401.9 1.6 bitcast_convert_fusion.1
  403.5 0.7 copy-done.46
  404.2 2.6 convolution_convert_fusion.2.refs_6_
  406.8 39.9 %shard_map.347 = (f32[512,1024]{1,0:T(8,128)}, bf16[512,1024]{1,0:T(8,128)(2,1)}, f32[1,1024]{1,0:T(1,128)}, f32[1,1024]{1,0:T(1,128)}, bf16[256,1024]{1,0:T(8,128)(2,1)}) custom-call(f32[512,1024]{1,0:T(8,128)} %get-tuple-element.130.refs_0_, bf16[768,512]{1,0:T(8,128)(2,1)} %get-tuple-element.134.refs_1_, bf16[768,1024]{1,0:T(8,128)(2,1)} %bitcast.121, ...), custom_call_target="tpu_custom_call" | custom-call | tf_op jit(solution)/shard_map/pallas_call | solution.py:457
  446.8 1.3 concatenate.49
  448.1 4.2 convolution_convert_fusion.1.refs_17_
  452.3 75.1 %shard_map.348 = (bf16[512,1024]{1,0:T(8,128)(2,1)}, bf16[512,1024]{1,0:T(8,128)(2,1)}, f32[1,1024]{1,0:T(1,128)}, f32[1,1024]{1,0:T(1,128)}, bf16[512,256]{1,0:...) custom-call(bf16[512,1024]{1,0:T(8,128)(2,1)} %get-tuple-element.137, ...), custom_call_target="tpu_custom_call" | custom-call | tf_op jit(solution)/shard_map/pallas_call | solution.py:457
  527.4 2.3 convolution_convert_fusion.8.refs_8_
  529.8 2.6 convolution_convert_fusion.9.refs_7_
  532.4 1.2 convolution_convert_fusion.7.refs_9_
  533.6 2.6 convolution_convert_fusion.refs_6_
  536.3 42.5 %shard_map.349 = (bf16[768,512]{1,0:T(8,128)(2,1)}, bf16[64,512]{1,0:T(8,128)(2,1)}, bf16[256,1024]{1,0:T(8,128)(2,1)}, f32[256,1024]{1,0:T(8,128)}) custom-call(bf16[192,2048]{1,0:T(8,128)(2,1)} %get-tuple-element.147.refs_0_, s32[1,2048]{1,0:T(1,128)} %bitcast.171, bf16[512,1024]{1,0:T(8,128)(2,1)} %get-tuple-element.148.refs_2_, ...), custom_call_target="tpu_custom_call" | custom-call | tf_op jit(solution)/shard_map/pallas_call | solution.py:457
  578.7 3.3 convolution_convert_fusion.4.refs_10_
  582.0 47.7 %shard_map.350 = (f32[512,1024]{1,0:T(8,128)}, bf16[512,1024]{1,0:T(8,128)(2,1)}, f32[1,1024]{1,0:T(1,128)}, f32[1,1024]{1,0:T(1,128)}, bf16[512,1024]{1,0:T(8,1...) custom-call(f32[512,1024]{1,0:T(8,128)} %get-tuple-element.146.refs_, ...), custom_call_target="tpu_custom_call" | custom-call | tf_op jit(solution)/shard_map/pallas_call | solution.py:457
  629.8 3.5 select_bitcast_fusion
  633.4 1.4 concatenate.48
  634.8 1.4 pad_maximum_fusion.4.refs_1_
  636.5 1.0 fusion.8.refs_0_
  637.5 1.4 fusion.7.refs_2_
  638.9 25.4 %shard_map.351 = (bf16[128,1024]{1,0:T(8,128)(2,1)}, f32[8,1024]{1,0:T(8,128)}, bf16[256,512]{1,0:T(8,128)(2,1)}, f32[256,768]{1,0:T(8,128)}, f32[64,1024]{1,0:T...) custom-call(bf16[128,1024]{1,0:T(8,128)(2,1)} %fusion.8.refs_0_, f32[2,8,1024]{2,1,0:T(8,128)} %pad_maximum_fusion.4.refs_1_, ...), custom_call_target="tpu_custom_call" | custom-call | tf_op jit(solution)/shard_map/pallas_call | solution.py:457
  664.4 1.6 fusion.27
  665.9 1.8 convert.13
  667.7 1.0 convert_element_type.93
  668.7 0.8 slice_bitcast_fusion
  669.6 1.4 copy.57
  671.0 0.9 fusion.25
  671.9 1.8 copy.60
  673.7 1.8 copy.59
  675.4 1.8 copy.58
  677.2 1.6 bitcast_convert_fusion
  679.1 6.2 maximum_select_fusion
  685.3 0.7 copy.67
  686.0 0.7 copy.68
  686.7 0.7 copy.69
  687.4 1.0 copy.70
  688.4 1.0 copy.71
  (109 shorter events, 2.3 us)
Async XLA Ops:
  0.7 6.7 copy-start
  0.7 6.4 copy-start.9
  0.7 6.4 copy-start.6
  0.7 5.7 copy-start.36
  0.7 5.7 copy-start.35
  0.7 5.7 copy-start.34
  0.7 5.6 copy-start.33
  0.7 5.6 copy-start.32
  0.7 5.6 copy-start.31
  1.8 6.5 copy-start.19
  3.3 5.2 copy-start.20
  6.4 2.3 copy-start.21
  9.1 28.6 %copy-start.1 = (bf16[2,512,1024]{2,1,0:T(8,128)(2,1)S(1)}, bf16[2,512,1024]{2,1,0:T(8,128)(2,1)}, u32[]{:S(2)}) copy-start(bf16[2,512,1024]{2,1,0:T(8,128)(2,1)} %refs_4_.1) | copy-start | bytes 6291460
  37.6 29.7 %copy-start.30 = (f32[1,1024]{1,0:T(1,128)}, f32[1,1024]{1,0:T(1,128)S(1)}, u32[]{:S(2)}) copy-start(f32[1,1024]{1,0:T(1,128)S(1)} %get-tuple-element.263.refs_5_) | copy-start | bytes 12292
  199.6 86.5 %copy-start.8 = (f32[512,1024]{1,0:T(8,128)S(1)}, f32[512,1024]{1,0:T(8,128)}, u32[]{:S(2)}) copy-start(f32[512,1024]{1,0:T(8,128)} %get-tuple-element.118) | copy-start | bytes 6291460
  286.1 1.2 copy-start.48
  291.6 74.9 %copy-start.47 = (bf16[512,1024]{1,0:T(8,128)(2,1)S(1)}, bf16[512,1024]{1,0:T(8,128)(2,1)}, u32[]{:S(2)}) copy-start(bf16[512,1024]{1,0:T(8,128)(2,1)} %get-tuple-element.144) | copy-start | bytes 3145732
  368.7 28.4 %copy-start.3 = (bf16[512,1024]{1,0:T(8,128)(2,1)S(1)}, bf16[512,1024]{1,0:T(8,128)(2,1)}, u32[]{:S(2)}) copy-start(bf16[512,1024]{1,0:T(8,128)(2,1)} %get-tuple-element.132.refs_2_) | copy-start | bytes 3145732
  368.7 28.4 %copy-start.13 = (bf16[256,512]{1,0:T(8,128)(2,1)S(1)}, bf16[256,512]{1,0:T(8,128)(2,1)}, u32[]{:S(2)}) copy-start(bf16[256,512]{1,0:T(8,128)(2,1)} %get-tuple-element.121.refs_1_) | copy-start | bytes 786436
  368.7 29.7 %copy-start.14 = (bf16[512,1024]{1,0:T(8,128)(2,1)S(1)}, bf16[512,1024]{1,0:T(8,128)(2,1)}, u32[]{:S(2)}) copy-start(bf16[512,1024]{1,0:T(8,128)(2,1)} %get-tuple-element.143) | copy-start | bytes 3145732
  368.7 29.7 %copy-start.25 = (bf16[512,256]{1,0:T(8,128)(2,1)S(1)}, bf16[512,256]{1,0:T(8,128)(2,1)}, u32[]{:S(2)}) copy-start(bf16[512,256]{1,0:T(8,128)(2,1)} %get-tuple-element.142) | copy-start | bytes 786436
  397.1 2.6 copy-start.17
  397.1 2.6 copy-start.18
  399.7 2.2 copy-start.11
  401.9 1.6 copy-start.44
  401.9 2.3 copy-start.46
  406.8 40.0 %copy-start.39 = (f32[1,1024]{1,0:T(1,128)S(1)}, f32[1,1024]{1,0:T(1,128)}, u32[]{:S(2)}) copy-start(f32[1,1024]{1,0:T(1,128)} %get-tuple-element.176) | copy-start | bytes 12292
  406.8 40.0 %copy-start.40 = (f32[1,1024]{1,0:T(1,128)S(1)}, f32[1,1024]{1,0:T(1,128)}, u32[]{:S(2)}) copy-start(f32[1,1024]{1,0:T(1,128)} %get-tuple-element.177) | copy-start | bytes 12292
  406.8 40.0 %copy-start.41 = (f32[1,1024]{1,0:T(1,128)S(1)}, f32[1,1024]{1,0:T(1,128)}, u32[]{:S(2)}) copy-start(f32[1,1024]{1,0:T(1,128)} %get-tuple-element.174) | copy-start | bytes 12292
  406.8 40.0 %copy-start.42 = (f32[1,1024]{1,0:T(1,128)S(1)}, f32[1,1024]{1,0:T(1,128)}, u32[]{:S(2)}) copy-start(f32[1,1024]{1,0:T(1,128)} %get-tuple-element.175) | copy-start | bytes 12292
  452.3 75.1 %copy-start.43 = (bf16[512,1024]{1,0:T(8,128)(2,1)S(1)}, bf16[512,1024]{1,0:T(8,128)(2,1)}, u32[]{:S(2)}) copy-start(bf16[512,1024]{1,0:T(8,128)(2,1)} %get-tuple-element.156) | copy-start | bytes 3145732
  527.4 2.4 copy-start.24
  527.4 5.0 copy-start.5
  527.4 5.0 copy-start.12
  529.7 3.9 copy-start.10
  529.7 3.9 copy-start.45
  536.3 42.5 %copy-start.4 = (bf16[512,1024]{1,0:T(8,128)(2,1)S(1)}, bf16[512,1024]{1,0:T(8,128)(2,1)}, u32[]{:S(2)}) copy-start(bf16[512,1024]{1,0:T(8,128)(2,1)} %fusion.6.refs_0_) | copy-start | bytes 3145732
  582.0 47.7 %copy-start.7 = (f32[512,1024]{1,0:T(8,128)S(1)}, f32[512,1024]{1,0:T(8,128)}, u32[]{:S(2)}) copy-start(f32[512,1024]{1,0:T(8,128)} %get-tuple-element.163) | copy-start | bytes 6291460
  629.8 3.6 copy-start.22
  629.8 3.6 copy-start.23
  629.8 3.6 copy-start.29
  629.8 3.6 copy-start.37
  629.8 3.6 copy-start.38
  677.2 1.9 copy-start.2
  679.1 6.2 copy-start.28
  679.1 6.9 %copy-start.27 = (f32[256,256]{1,0:T(8,128)S(1)}, f32[256,256]{1,0:T(8,128)}, u32[]{:S(2)}) copy-start(f32[256,256]{1,0:T(8,128)} %get-tuple-element.190) | copy-start | bytes 786436
  679.1 7.6 %copy-start.26 = (f32[64,1024]{1,0:T(8,128)S(1)}, f32[64,1024]{1,0:T(8,128)}, u32[]{:S(2)}) copy-start(f32[64,1024]{1,0:T(8,128)} %get-tuple-element.192) | copy-start | bytes 786436
  679.1 8.3 %copy-start.16 = (f32[256,1024]{1,0:T(8,128)S(1)}, f32[256,1024]{1,0:T(8,128)}, u32[]{:S(2)}) copy-start(f32[256,1024]{1,0:T(8,128)} %get-tuple-element.193) | copy-start | bytes 3145732
  685.3 3.1 copy-start.15

commit v4 on v3

--- a/solution.py
+++ b/solution.py
@@ -15,7 +15,7 @@
 
 MESH_IDS = pl.DeviceIdType.MESH
 BUSY = pl.CostEstimate(flops=30_000_000_000, bytes_accessed=8_000_000, transcendentals=0)
-LAG = 2
+LAG = 3
 BLOCK = 128
 VMEM_BYTES = 56 * 1024 * 1024
 EPS = 1e-05
@@ -30,6 +30,10 @@
     out_in_vmem = True
     scratch = ()
     greets = ()
+    late = False
+
+    def middle(self):
+        pass
 
     def bind(self, ins, outs, scratch):
         self.ins, self.out, self.room = ins, outs, scratch
@@ -97,50 +101,99 @@
 
     def __init__(self, grad):
         rows, width = grad.shape
-        self.share = rows // lax.axis_size(FRAME)
-        self.operands = (grad,)
-        self.outs = (jax.ShapeDtypeStruct((self.share, width), jnp.bfloat16),)
+        self.share = rows // 4
+        self.operands = (grad,) if isinstance(grad, jax.Array) else ()
+        piece = (self.share, width)
+        self.outs = (jax.ShapeDtypeStruct(piece, jnp.bfloat16),)
         self.scratch = (
-            pltpu.VMEM((3, self.share, width), jnp.bfloat16),
-            pltpu.VMEM((self.share, width), jnp.bfloat16),
+            pltpu.VMEM((2,) + piece, jnp.bfloat16),
+            pltpu.VMEM((2,) + piece, jnp.bfloat16),
+            pltpu.VMEM((2,) + piece, jnp.bfloat16),
             pltpu.SemaphoreType.DMA((3,)),
             pltpu.SemaphoreType.DMA((3,)),
-            pltpu.SemaphoreType.DMA,
+            pltpu.SemaphoreType.DMA((2,)),
         )
 
-    def copies(self):
-        landing, own, send_sems, recv_sems, here = self.room
+    def within(self):
+        own, landing, _, send_sems, recv_sems, here = self.room
         me = lax.axis_index(FRAME)
-        away = [
-            remote(
-                self.ins[0].at[span(partner, self.share)],
-                landing.at[k],
-                send_sems.at[k],
-                recv_sems.at[k],
-                {FRAME: partner},
+        other = frame_partners()[0]
+        side = lax.div(me, 2)
+        copies = []
+        for k, to_side in enumerate((1 - side, side)):
+            given = 2 * to_side + lax.rem(other, 2)
+            kept = 2 * to_side + lax.rem(me, 2)
+            copies.append(
+                remote(
+                    self.ins[0].at[span(given, self.share)],
+                    landing.at[k],
+                    send_sems.at[k],
+                    recv_sems.at[k],
+                    {FRAME: other},
+                )
             )
-            for k, partner in enumerate(frame_partners())
-        ]
-        return away, pltpu.make_async_copy(self.ins[0].at[span(me, self.share)], own, here)
+            copies.append(
+                pltpu.make_async_copy(self.ins[0].at[span(kept, self.share)], own.at[k], here.at[k])
+            )
+        return copies
+
+    def over(self):
+        crossing, send_sems, recv_sems = self.room[2:5]
+        target = {FRAME: frame_partners()[1]}
+        return remote(crossing.at[0], crossing.at[1], send_sems.at[2], recv_sems.at[2], target)
+
+    def chip_sum(self, k):
+        own, landing = self.room[:2]
+        return own[k].astype(jnp.float32) + landing[k].astype(jnp.float32)
 
     def begin(self):
-        away, stay = self.copies()
-        for copy in away[::-1]:
+        for copy in self.within():
             copy.start()
-        stay.start()
+
+    def middle(self):
+        for copy in self.within():
+            copy.wait()
+        self.room[2][0] = self.chip_sum(0).astype(jnp.bfloat16)
+        self.over().start()
 
     def steps(self):
-        away, stay = self.copies()
-
         def end():
-            stay.wait()
-            for copy in away:
+            self.over().wait()
+            total = self.chip_sum(1) + self.room[2][1].astype(jnp.float32)
+            self.out[0][...] = total.astype(jnp.bfloat16)
+
+        return [end]
+
+
+class BothTask(Task):
+    out_in_vmem = False
+    greets = (SECTION,)
+
+    def __init__(self, first, second):
+        self.operands = (first, second)
+        self.outs = (jax.ShapeDtypeStruct((2,) + first.shape, first.dtype),)
+        self.scratch = (pltpu.SemaphoreType.DMA((3,)),)
+
+    def copies(self, given, kept):
+        (sems,) = self.room
+        section = lax.axis_index(SECTION)
+        place = self.out[0].at[section]
+        over = remote(self.ins[given], place, sems.at[0], sems.at[1], {SECTION: 1 - section})
+        return over, pltpu.make_async_copy(self.ins[kept], place, sems.at[2])
+
+    def begin(self):
+        section = lax.axis_index(SECTION)
+        for which in (0, 1):
+
+            @pl.when(section == which)
+            def _():
+                for copy in self.copies(1 - which, which):
+                    copy.start()
+
+    def steps(self):
+        def end():
+            for copy in self.copies(0, 1):
                 copy.wait()
-            landing, own = self.room[:2]
-            total = own[...].astype(jnp.float32)
-            for k in range(3):
-                total = total + landing[k].astype(jnp.float32)
-            self.out[0][...] = total.astype(jnp.bfloat16)
 
         return [end]
 
@@ -439,13 +492,20 @@
 
         def ride():
             for task in tasks:
-                task.begin()
+                if not task.late:
+                    task.begin()
+
+        def middle():
+            for task in tasks:
+                if not task.late:
+                    task.middle()
 
         if body is None:
             meet()
             ride()
+            middle()
         else:
-            body(*bound[0], meet, ride)
+            body(*bound[0], meet, ride, middle)
         queues = [task.steps() for task in tasks]
         while any(queues):
             for queue in queues:
@@ -519,6 +579,9 @@
         if self.kept:
             pltpu.make_async_copy(self.ref.at[at], self.far[0].at[at], self.sem).start()
 
+    def flush(self):
+        pltpu.make_async_copy(self.ref, self.far[0], self.sem).start()
+
     def drain(self):
         pltpu.make_async_copy(self.ref, self.far[0], self.sem).wait()
 
@@ -552,11 +615,46 @@
 class Stage:
     def __init__(self, rows, width):
         self.rows, self.width = rows, width
-        self.begin = self.prepare = self.partial = self.finish = None
+        self.begin = self.prepare = self.finish = None
         self.ends = []
 
 
-def line_chain(stages, need):
+class Chore:
+    def __init__(self, build, stage, left, right, flipped=False):
+        self.stage, self.left, self.right, self.flipped = stage, left, right, flipped
+        columns = left.shape[0] if flipped else left.shape[1]
+        self.units = columns // BLOCK
+        self.product = build.temp((columns, right.shape[1]), jnp.bfloat16)
+        self.task = ShareTask(self.product)
+        self.task.late = True
+
+    def unit(self, number):
+        at = span(number, BLOCK)
+        right = self.right.ref[...].astype(jnp.bfloat16)
+        if self.flipped:
+            product = plain_product(self.left.ref[at, :], right)
+        else:
+            product = lax.dot_general(
+                self.left.ref[:, at], right, (((0,), (0,)), ((), ())), preferred_element_type=jnp.float32
+            )
+        self.product.ref[at, :] = product.astype(jnp.bfloat16)
+
+    def run(self, piece):
+        @pl.when(piece < self.units)
+        def _():
+            self.unit(piece)
+
+        @pl.when(piece == self.units)
+        def _():
+            self.task.ins = [self.product.ref]
+            self.task.begin()
+
+        @pl.when(piece == self.units + 5)
+        def _():
+            self.task.middle()
+
+
+def line_chain(stages, need, part, middle, chores):
     place = lax.axis_index(LINE)
     rows = stages[0].rows
     pieces = chunking(rows)
@@ -597,12 +695,16 @@
 
         lax.fori_loop(first, last, one, 0)
 
+    def chore(stage, piece):
+        for one in chores:
+            if stages[one.stage] is stage:
+                one.run(piece)
+
     @pl.when(is_end)
     def _():
         def give(stage, piece):
-            at = span(piece, step)
-            stage.room[0][at, :] = stage.partial(at).astype(jnp.bfloat16)
             inwards(stage, piece).start()
+            chore(stage, piece)
 
         def take(stage, piece):
             outwards(stage, piece).wait_recv()
@@ -615,9 +717,13 @@
                 low, high = block * per_block, (block + 1) * per_block
                 if index:
                     loop(low, high, lambda piece: take(stages[index - 1], piece))
-                if stage.prepare is not None:
-                    stage.prepare(block)
+                stage.room[0][span(block, per_block * step), :] = stage.prepare(block).astype(jnp.bfloat16)
                 loop(low, high, lambda piece: give(stage, piece))
+                if index == 0:
+
+                    @pl.when(block == 1)
+                    def _():
+                        middle()
 
             loop(0, pieces // per_block, block_step)
         loop(0, pieces, lambda piece: take(stages[-1], piece))
@@ -627,18 +733,22 @@
     @pl.when(jnp.logical_not(is_end))
     def _():
         def add(stage, piece):
-            if stage.prepare is not None:
-
-                @pl.when(lax.rem(piece, per_block) == 0)
-                def _():
-                    stage.prepare(lax.div(piece, per_block))
+            @pl.when(lax.rem(piece, per_block) == 0)
+            def _():
+                part[...] = stage.prepare(lax.div(piece, per_block))
 
             at = span(piece, step)
             send, recv = stage.room[:2]
-            part = stage.partial(at)
             inwards(stage, piece).wait_recv()
-            send[at, :] = (part + recv[at, :].astype(jnp.float32)).astype(jnp.bfloat16)
+            own = part[span(lax.rem(piece, per_block), step), :]
+            send[at, :] = (own + recv[at, :].astype(jnp.float32)).astype(jnp.bfloat16)
             crossing(stage, piece).start()
+            chore(stage, piece)
+            if stage is stages[0]:
+
+                @pl.when(piece == 2 * per_block - 1)
+                def _():
+                    middle()
 
         def settle(stage, piece):
             at = span(piece, step)
@@ -697,7 +807,7 @@
             if held.stage == stage:
                 held.copy_in().wait()
 
-    def run(ins, outs, scratch, meet, ride):
+    def run(ins, outs, scratch, meet, ride, middle):
         ins, outs = list(ins), list(outs)
         sems = scratch[-1]
         for index, held in enumerate(build.helds):
@@ -708,7 +818,7 @@
         build.bound = scratch[n_held:-1]
         for held in reads:
             held.start_in()
-        body(need, meet, ride)
+        body(need, meet, ride, middle)
 
     def end():
         for held in build.helds:
@@ -718,45 +828,48 @@
     return call(run, operands, outs, scratch, kinds, collective_id, tasks, in_vmem=False, end=end)
 
 
-def run_chain(build, stages, collective_id, tasks, kinds=(LINE_ONLY,)):
+def run_chain(build, stages, collective_id, tasks, kinds=(LINE_ONLY,), chores=()):
     slots = []
     for stage in stages:
         pieces = chunking(stage.rows)
         room = [pltpu.VMEM((stage.rows, stage.width), jnp.bfloat16)] * 4
         room += [pltpu.SemaphoreType.DMA((pieces,))] * 6
         slots.append([build.extra(scratch) for scratch in room])
-
-    def body(need, meet, ride):
+    part = build.extra(pltpu.VMEM((min(BLOCK, stages[0].rows), stages[0].width), jnp.float32))
+
+    def body(need, meet, ride, middle):
         for stage, places in zip(stages, slots):
             stage.room = [build.bound[place] for place in places]
         meet()
         ride()
-        line_chain(stages, need)
-
+        line_chain(stages, need, build.bound[part], middle, chores)
+
+    tasks = list(tasks) + [one.task for one in chores]
     return run_build(build, body, kinds, collective_id, tasks)
 
 
 def residual_norm(build, index, stage, base, gain, shift, mode):
     shape = (stage.rows, stage.width)
-    result = build.out(shape, jnp.float32)
+    result = build.temp(shape, jnp.float32) if mode == NORM else None
     normed = build.out(shape, jnp.bfloat16) if mode != END else None
-    low = build.out(shape, jnp.bfloat16) if mode != NORM else None
+    low = build.out(shape, jnp.bfloat16)
     if mode != END:
         gain, shift = build.arg(gain[None], index), build.arg(shift[None], index)
 
     def finish(at, piece):
         value = base.ref[at, :].astype(jnp.float32) + stage.room[3][at, :].astype(jnp.float32)
-        result.write(at, value)
-        if low is not None:
-            rounded = value.astype(jnp.bfloat16)
-            low.write(at, rounded)
+        rounded = value.astype(jnp.bfloat16)
+        low.write(at, rounded)
+        if mode == NORM:
+            result.write(at, value)
+        if mode == NEXT:
             value = rounded.astype(jnp.float32)
-        if normed is not None:
+        if mode != END:
             standard, _ = norm_parts(value)
             normed.write(at, (standard * gain.ref[...] + shift.ref[...]).astype(jnp.bfloat16))
 
     stage.finish = finish
-    return result, normed, low
+    return result, normed
 
 
 def self_out_stage(build, index, layer, attended_t, weight, base):
@@ -768,8 +881,10 @@
     def begin():
         left.ref[...] = flipped.ref[...].T
 
-    stage.begin = begin
-    stage.partial = lambda at: plain_product(left.ref[at, :], matrix.ref[...])
+    def prepare(number):
+        return plain_product(left.ref[span(number, min(BLOCK, rows)), :], matrix.ref[...])
+
+    stage.begin, stage.prepare = begin, prepare
     return stage
 
 
@@ -806,10 +921,11 @@
             total = jnp.sum(e, axis=0, keepdims=True)
             value = plain_product(values_t.ref[cols, :], e.astype(jnp.bfloat16))
             mixed.append((value * (1.0 / total)).astype(jnp.bfloat16))
-        left.write(at, jnp.concatenate(mixed, axis=0).T)
+        mixed = jnp.concatenate(mixed, axis=0).T
+        left.write(at, mixed)
+        return plain_product(mixed, out_of.ref[...])
 
     stage.begin, stage.prepare = begin, prepare
-    stage.partial = lambda at: plain_product(left.ref[at, :], out_of.ref[...])
     return stage
 
 
@@ -818,39 +934,41 @@
     stage = Stage(rows, width)
     hidden, block = into[0].shape[1], min(BLOCK, rows)
     into, out_of = build.pick(into, layer, index), build.pick(out_of, layer, index)
-    before = build.out((rows, hidden), jnp.float32)
+    before = build.out((rows, hidden), jnp.bfloat16)
     left = build.out((rows, hidden), jnp.bfloat16)
 
     def prepare(number):
         at = span(number, block)
         u = plain_product(normed.ref[at, :], into.ref[...])
-        before.write(at, u)
-        left.write(at, (0.5 * u * (1.0 + lax.erf(u * inv_sqrt_two))).astype(jnp.bfloat16))
+        before.write(at, u.astype(jnp.bfloat16))
+        active = (0.5 * u * (1.0 + lax.erf(u * inv_sqrt_two))).astype(jnp.bfloat16)
+        left.write(at, active)
+        return plain_product(active, out_of.ref[...])
 
     stage.prepare = prepare
-    stage.partial = lambda at: plain_product(left.ref[at, :], out_of.ref[...])
     return stage
 
 
-def norm_backward(build, index, stage, value, gain, upstream, kept, spare=None):
+def norm_backward(build, index, stage, value, gain, upstream, feeds, spare=None):
     shape = (stage.rows, stage.width)
     pieces = chunking(stage.rows)
     vector = (1, stage.width)
     by_section = BY_SECTION if value.ndim == 3 else None
     value, gain = build.arg(value, index, by_section), build.arg(gain[None], index)
-    result = (build.out if kept else build.temp)(shape, jnp.float32)
+    result = build.temp(shape, jnp.float32) if feeds else None
     low = build.out(shape, jnp.bfloat16)
     gain_grad, shift_grad = build.out(vector, jnp.float32), build.out(vector, jnp.float32)
     parts = build.extra(pltpu.VMEM((2, pieces, 1, stage.width), jnp.float32))
     if spare is not None:
         spare = build.arg(spare, index)
-        other = build.out(shape, jnp.bfloat16)
+        both = build.out((2,) + shape, jnp.bfloat16)
         sems = build.extra(pltpu.SemaphoreType.DMA((2, pieces)))
 
     def over(at, piece, source):
         target = {SECTION: 1 - lax.axis_index(SECTION)}
         pair = build.bound[sems]
-        return remote(source.ref.at[at], other.ref.at[at], pair.at[0, piece], pair.at[1, piece], target)
+        landing = both.ref.at[lax.axis_index(SECTION), at]
+        return remote(source.ref.at[at], landing, pair.at[0, piece], pair.at[1, piece], target)
 
     def finish(at, piece):
         grad = stage.room[3][at, :].astype(jnp.float32)
@@ -862,7 +980,8 @@
             - standard * jnp.mean(scaled * standard, axis=-1, keepdims=True)
         )
         total = through + upstream.ref[at, :].astype(jnp.float32)
-        result.write(at, total)
+        if feeds:
+            result.write(at, total)
         low.write(at, total.astype(jnp.bfloat16))
         build.bound[parts][0, piece] = jnp.sum(grad * standard, axis=0, keepdims=True)
         build.bound[parts][1, piece] = jnp.sum(grad, axis=0, keepdims=True)
@@ -871,10 +990,12 @@
 
             @pl.when(section == 0)
             def _():
+                both.ref[0, at, :] = low.ref[at, :]
                 over(at, piece, spare).start()
 
             @pl.when(section == 1)
             def _():
+                both.ref[1, at, :] = spare.ref[at, :]
                 over(at, piece, low).start()
 
     def end():
@@ -885,12 +1006,11 @@
             step = stage.rows // pieces
 
             def one(piece, carry):
-                at = span(piece, step)
-                over(at, piece, low).wait()
-                pltpu.make_async_copy(other.ref.at[at], other.far[0].at[at], other.sem).start()
+                over(span(piece, step), piece, low).wait()
                 return carry
 
             lax.fori_loop(0, pieces, one, 0)
+            both.flush()
 
     stage.finish = finish
     stage.ends.append(end)
@@ -908,12 +1028,13 @@
     def prepare(number):
         at = span(number, block)
         grad = nt_product(grad_out.ref[at, :].astype(jnp.bfloat16), out_of.ref[...])
-        u = before.ref[at, :]
+        u = before.ref[at, :].astype(jnp.float32)
         slope = 0.5 * (1.0 + lax.erf(u * inv_sqrt_two)) + u * jnp.exp(-0.5 * u * u) * inv_sqrt_tau
-        left.write(at, (grad * slope).astype(jnp.bfloat16))
-
-    stage.prepare = prepare
-    stage.partial = lambda at: nt_product(left.ref[at, :], into.ref[...])
+        grad = (grad * slope).astype(jnp.bfloat16)
+        left.write(at, grad)
+        return nt_product(grad, into.ref[...])
+
+    stage.prepare, stage.left = prepare, left
     return stage
 
 
@@ -953,13 +1074,14 @@
             query_grads.append((plain_product(keys_t.ref[cols, :], ds) * scale).astype(jnp.bfloat16))
             sums.ref[:, cols] += plain_product(ds, query[:, cols]) * scale
             sums.ref[:, more] += plain_product(p.astype(jnp.bfloat16), grad[:, cols])
-        left.write(at, jnp.concatenate(query_grads, axis=0).T)
+        query_grads = jnp.concatenate(query_grads, axis=0).T
+        left.write(at, query_grads)
+        return nt_product(query_grads, into.ref[...])
 
     def end():
         state_grads.write(slice(0, states.shape[0]), sums.ref[...].astype(jnp.bfloat16))
 
     stage.begin, stage.prepare = begin, prepare
-    stage.partial = lambda at: nt_product(left.ref[at, :], into.ref[...])
     stage.ends.append(end)
     return stage
 
@@ -973,8 +1095,11 @@
     def begin():
         left.ref[...] = flipped.ref[...].T
 
-    stage.begin = begin
-    stage.partial = lambda at: plain_product(left.ref[at, :], matrix.ref[...])
+    def prepare(number):
+        return plain_product(left.ref[span(number, min(BLOCK, rows)), :], matrix.ref[...])
+
+    stage.begin, stage.prepare = begin, prepare
+    stage.left = left
     return stage
 
 
@@ -985,9 +1110,9 @@
     build = Build()
     base = build.arg(entering, 0, BY_SECTION if entering.ndim == 3 else None)
     first = self_out_stage(build, 0, layer, attended_t, output, base)
-    middle, second_normed, _ = residual_norm(build, 0, first, base, gains[2], gains[3], NORM)
+    middle, second_normed = residual_norm(build, 0, first, base, gains[2], gains[3], NORM)
     second = cross_stage(build, 1, layer, second_normed, states, seg, query, cross)
-    latter, third_normed, _ = residual_norm(build, 1, second, middle, gains[4], gains[5], NORM)
+    latter, third_normed = residual_norm(build, 1, second, middle, gains[4], gains[5], NORM)
     stages = [first, second]
     if more:
         stages.append(feed_stage(build, 2, layer, third_normed, *more))
@@ -1004,25 +1129,50 @@
 
 
 def backward_chain(
-    layer, upstream, before, latter, queries, states, seg, middle, gains, weights, collective_id, tasks
+    layer,
+    upstream,
+    before,
+    hidden,
+    third_normed,
+    latter,
+    queries,
+    states,
+    seg,
+    middle,
+    gains,
+    weights,
+    collective_id,
+    tasks,
 ):
     _, query, cross, expand, reduce = weights
     build = Build()
     arriving = build.arg(upstream, 0, BY_SECTION if upstream.ndim == 3 else None)
     first = feed_back_stage(build, 0, layer, arriving, before, reduce, expand)
-    grad_latter, grad_cross = norm_backward(build, 0, first, latter, gains[4], arriving, False)
+    grad_latter, grad_cross = norm_backward(build, 0, first, latter, gains[4], arriving, True)
     second = cross_back_stage(build, 1, layer, grad_cross, queries, states, seg, cross, query)
-    norm_backward(build, 1, second, middle, gains[2], grad_latter, True)
-    return run_chain(build, [first, second], collective_id, tasks)
-
-
-def last_chain(layer, grads_t, entering, gain, upstream, weight, spare, collective_id, tasks):
+    norm_backward(build, 1, second, middle, gains[2], grad_latter, False)
+    chores = [
+        Chore(build, 0, build.arg(hidden, 0), arriving),
+        Chore(build, 1, build.arg(third_normed, 1), first.left),
+    ]
+    return run_chain(build, [first, second], collective_id, tasks, chores=chores)
+
+
+def last_chain(layer, grads_t, entering, gain, upstream, weight, spare, products, collective_id, tasks):
     build = Build()
-    upstream = build.arg(upstream, 0)
+    residual = build.arg(upstream, 0)
     stage = self_in_stage(build, 0, layer, grads_t, weight, upstream.shape[1])
-    norm_backward(build, 0, stage, entering, gain, upstream, True, spare)
+    norm_backward(build, 0, stage, entering, gain, residual, False, spare)
+    chores = []
+    for left, right in products:
+        flipped = left.shape[0] != upstream.shape[0]
+        if right is None:
+            right = stage.left
+        else:
+            right = residual if right is upstream else build.arg(right, 0)
+        chores.append(Chore(build, 0, build.arg(left, 0), right, flipped))
     kinds = (LINE_ONLY,) if spare is None else (LINE_ONLY, SECTION)
-    return run_chain(build, [stage], collective_id, tasks, kinds)
+    return run_chain(build, [stage], collective_id, tasks, kinds, chores)
 
 
 def masked_scores(keys, query_t, begins, start):
@@ -1054,7 +1204,7 @@
     mixed_t = build.temp((frames, HEAD, rows), jnp.bfloat16)
     sems = [build.extra(pltpu.SemaphoreType.DMA((2, frames - 1))) for _ in range(2)]
 
-    def body(need, meet, ride):
+    def body(need, meet, ride, middle):
         me = lax.axis_index(FRAME)
         partners = frame_partners()
         block = min(2 * BLOCK, rows)
@@ -1120,7 +1270,7 @@
     grads_t = build.temp((frames, width, rows), jnp.bfloat16)
     sems = [build.extra(pltpu.SemaphoreType.DMA((2, frames - 1))) for _ in range(2)]
 
-    def body(need, meet, ride):
+    def body(need, meet, ride, middle):
         me = lax.axis_index(FRAME)
         partners = frame_partners()
         block = min(2 * BLOCK, rows)
@@ -1150,6 +1300,7 @@
         for copy in arriving:
             copy.wait()
         columns.ref[3] = grad_t.ref[...].T
+        middle()
         for target in reversed(range(frames)):
             for start in reversed(range(target * rows, (target + 1) * rows, block)):
                 reach = start + block
@@ -1345,7 +1496,7 @@
         vectors[0][0],
         vectors[0][1],
     ).astype(jnp.bfloat16)
-    saved, results = [], []
+    saved = []
     for layer in range(2):
         gains, first = vectors[layer], layer == 0
         tasks = []
@@ -1359,7 +1510,7 @@
         if first:
             weights = list(zip((output_weight, cross_query, cross_output), carried))
             states = carried[3].reshape(2, -1, 2 * columns)
-            (middle, second_normed, queries, cross_att, latter, third_normed), carried = forward_chain(
+            (second_normed, middle, queries, cross_att, third_normed, latter), carried = forward_chain(
                 layer,
                 attended_t,
                 entering,
@@ -1371,15 +1522,15 @@
                 [WeightTask(expand_weight), WeightTask(reduce_weight)],
             )
             weights += list(zip((expand_weight, reduce_weight), carried))
-            (before, hidden, result, next_normed, result_low), _ = feed_chain(
+            (before, hidden, next_normed, result_low), _ = feed_chain(
                 layer, third_normed, latter, weights, vectors[1], 5
             )
         else:
             outs, _ = forward_chain(
                 layer, attended_t, entering, states[layer], seg, gains, weights, 6, []
             )
-            (middle, second_normed, queries, cross_att, latter, third_normed) = outs[:6]
-            before, hidden, result, result_low = outs[6:]
+            second_normed, middle, queries, cross_att, third_normed, latter = outs[:6]
+            before, hidden, result_low = outs[6:]
         saved.append(
             (
                 entering,
@@ -1396,12 +1547,11 @@
                 hidden,
             )
         )
-        results.append(result)
         if first:
             normed, entering = next_normed, result_low
 
     upstream = cotangent
-    in_grads, in_lows, vector_grads, shares = [None] * 2, [None] * 2, [None] * 2, [{}, {}]
+    in_lows, vector_grads, shares = [None] * 2, [None] * 2, [{}, {}]
     totals = {}
 
     def low_product(left, right):
@@ -1410,11 +1560,6 @@
     def crossing(*names):
         return [CrossTask(shares[0][name], shares[1][name], True) for name in names]
 
-    def shared(layer, names, arrays):
-        for name, array in zip(names, arrays):
-            shares[layer][name] = array
-
-    held_back = {}
     for layer in (1, 0):
         last = layer == 0
         gains = vectors[layer]
@@ -1432,16 +1577,7 @@
             before,
             hidden,
         ) = saved[layer]
-        if last:
-            grad_out = in_lows[1]
-        else:
-            grad_out = lax.dynamic_index_in_dim(cotangent, section, 0, keepdims=False)
-            grad_out = grad_out.astype(jnp.bfloat16)
-        tasks = [ShareTask(low_product(hidden, grad_out))]
-        if last:
-            tasks += [ShareTask(grad) for grad in held_back.values()]
-        else:
-            tasks.append(CrossTask(saved[1][0], result_low, False))
+        tasks = [] if last else [BothTask(saved[1][0], result_low)]
         (
             grad_pre,
             grad_cross,
@@ -1449,7 +1585,6 @@
             third_shift_grad,
             grad_queries,
             grad_states,
-            grad_middle,
             grad_self,
             second_gain_grad,
             second_shift_grad,
@@ -1457,6 +1592,8 @@
             layer,
             upstream,
             before,
+            hidden,
+            third_normed,
             latter,
             queries,
             states[layer],
@@ -1467,55 +1604,35 @@
             8 + layer,
             tasks,
         )
-        shares[layer]["reduce"] = carried[0]
-        if last:
-            shared(1, held_back, carried[1:])
-        else:
-            other_result = carried[1]
-
-        expand_grad = low_product(third_normed, grad_pre)
-        tasks = [ShareTask(grad_states)]
-        if last:
-            tasks += [ShareTask(expand_grad)] + crossing("reduce")
+        shares[layer]["reduce"], shares[layer]["expand"] = carried[-2:]
+        if not last:
+            layer_outputs = carried[0]
+
+        tasks = [ShareTask(grad_states)] + (crossing("reduce", "expand") if last else [])
         (grad_heads_t,), carried = self_backward(
             heads_t, grad_self, weights[0], begins, layer, 10 + layer, tasks
         )
         shares[layer]["states"] = carried[0]
         if last:
-            shares[0]["expand"], totals["reduce"] = carried[1:]
-
-        grads = {
-            "cross_output": low_product(cross_att, grad_cross),
-            "cross_query": low_product(second_normed, grad_queries),
-            "output": matmul(attended_t, grad_self).astype(jnp.bfloat16),
-            "heads": lax.dot_general(
-                normed, grad_heads_t, (((0,), (1,)), ((), ())), preferred_element_type=jnp.float32
-            ).astype(jnp.bfloat16),
-        }
+            totals["reduce"], totals["expand"] = carried[1:]
+
+        tasks = [CrossTask(shares[0]["states"], shares[1]["states"], False)] if last else []
+        (in_lows[layer], first_gain_grad, first_shift_grad, *both_grads), carried = last_chain(
+            layer,
+            grad_heads_t,
+            entering,
+            gains[0],
+            grad_self,
+            heads_pair,
+            in_lows[1] if last else None,
+            [(cross_att, grad_cross), (attended_t, grad_self), (second_normed, grad_queries), (normed, None)],
+            12 + layer,
+            tasks,
+        )
+        names = ("cross_output", "output", "cross_query", "heads")
+        shares[layer].update(zip(names, carried[-4:]))
         if last:
-            tasks = [ShareTask(grad) for grad in grads.values()] + crossing("expand")
-            tasks.append(CrossTask(shares[0]["states"], shares[1]["states"], False))
-        else:
-            held_back = grads
-            tasks = [ShareTask(expand_grad)]
-        (in_grads[layer], in_lows[layer], first_gain_grad, first_shift_grad, *other_grad), carried = (
-            last_chain(
-                layer,
-                grad_heads_t,
-                entering,
-                gains[0],
-                grad_middle,
-                heads_pair,
-                in_lows[1] if last else None,
-                12 + layer,
-                tasks,
-            )
-        )
-        if last:
-            shared(0, grads, carried)
-            totals["expand"], other_states = carried[len(grads) :]
-        else:
-            shares[1]["expand"] = carried[0]
+            other_states = carried[0]
         vector_grads[layer] = sum_rows(
             [
                 first_gain_grad,
@@ -1533,7 +1650,6 @@
     text_rows = sum_rows([by_section(own_states, other_states), by_section(other_states, own_states)])
     key_part, value_part = text_rows[:, :columns], text_rows[:, columns:]
     text_part = matmul_nt(key_part, cross_key) + matmul_nt(value_part, cross_value)
-    names = ("heads", "output", "cross_query", "cross_output")
     _, (text_grad, vector_total, cross_grads, *carried) = call(
         None,
         [],
@@ -1557,11 +1673,6 @@
         totals["heads"].reshape(-1, heads, 3, HEAD)[:, :, i].reshape(-1, columns) for i in range(3)
     )
     cross_grads = cross_grads.astype(jnp.float32)
-
-    def both_micros(pair, other):
-        own = by_section(*pair)
-        other = other.astype(own.dtype)
-        return jnp.where(at_zero, jnp.stack([own, other]), jnp.stack([other, own]))
 
     ordered = (
         vector_total[0],
@@ -1581,8 +1692,7 @@
         totals["expand"],
         totals["reduce"],
     )
-    layer_outputs = both_micros(results, other_result)
-    input_grads = both_micros(in_grads, other_grad[0])
+    layer_outputs, input_grads = (a.astype(jnp.float32) for a in (layer_outputs, both_grads[0]))
     return (layer_outputs[None], input_grads[None], text_grad) + tuple(g[None] for g in ordered)
 
 

time: 699 us -> 608 us (0.87)
  Pallas kernels: 604 us -> 562 us
  matrix products: 33.3 us -> 3.23 us
  other arithmetic: 24.7 us -> 12.9 us
    pallas_call x13, Pallas kernels: 604 us -> 562 us  [call(): pl.pallas_call(kernel, out_shape=all_outs, in_specs=in_specs, out_specs=o...]
    dot_general x9 -> x1, matrix products: 23.5 us -> 1.45 us  [matmul_tn(): lax.dot_general(left_side, right_side, (((0,), (0,)), ((), ())), preferre...]
    another operation x5 -> x1, other arithmetic: 7.3 us -> 0.18 us  [the longest x4 7.12 us: both_micros(): return jnp.where(at_zero, jnp.stack([own, other]), jnp.stack([other, own]))]
where the time goes in v4:
time: 608 us; the launch traced here: 599 us
  Pallas kernels  562 us (92%)
  local copies, waits for them, and re-layouts  19.2 us (3%)
  other arithmetic  12.9 us (2%)
    pallas_call x13, Pallas kernels, call(): pl.pallas_call(kernel, out_shape=all_outs, in_specs=in_specs, out_specs=o...  562 us

profile of v4, /device:TPU:0, one launch (start us, length us, event | category | flops | bytes accessed | tf_op | source)
XLA Modules:
  0.0 598.7 jit_solution(13548660472088830620)
XLA Ops:
  0.7 0.0 copy-start
  0.7 1.3 copy.52
  2.0 1.2 copy.53
  3.3 0.2 copy.54
  3.5 0.2 pad_maximum_fusion
  3.7 0.0 copy-start.16
  3.7 0.0 copy-start.17
  3.7 0.0 copy-start.18
  3.7 0.0 copy-start.19
  3.7 0.0 copy-start.20
  3.7 0.0 copy-start.21
  3.7 0.0 copy-start.1
  3.8 1.3 copy.55
  5.1 0.1 concatenate.17
  5.1 0.6 pad.4.refs_1_.refs_2_
  5.7 25.3 %shard_map.339 = (bf16[768,1024]{1,0:T(8,128)(2,1)}, f32[8,1024]{1,0:T(8,128)}) custom-call(bf16[768,1024]{1,0:T(8,128)(2,1)} %bitcast.88, f32[8,1024]{1,0:T(8,128)} %pad.4.refs_1_.refs_2_, f32[8,1024]{1,0:T(8,128)} %pad.4.refs_1_.refs_2_), custom_call_target="tpu_custom_call" | custom-call | tf_op jit(solution)/shard_map/pallas_call | solution.py:517
  31.0 0.8 broadcast_select_fusion.3
  31.8 0.6 fusion.25
  32.4 0.0 copy-start.32
  32.5 0.2 convert_reduce_fusion
  32.7 0.4 fusion.3
  33.1 1.4 fusion.6.refs_0_.refs_12_
  34.6 0.2 reduce-window.8
  34.8 0.7 convert_reduce_fusion.1
  35.5 0.2 convolution_convert_fusion.1
  35.7 0.2 convolution_convert_fusion.2
  36.0 0.7 pad_maximum_fusion.3.refs_7_
  36.6 28.2 %shard_map.340 = (bf16[192,2048]{1,0:T(8,128)(2,1)}, bf16[256,512]{1,0:T(8,128)(2,1)}, bf16[256,1024]{1,0:T(8,128)(2,1)}, bf16[1024,256]{1,0:T(8,128)(2,1)}, bf1...) custom-call(bf16[512,1024]{1,0:T(8,128)(2,1)} %fusion.6.refs_0_.refs_12_, s32[1,2048]{1,0:T(1,128)} %bitcast.138, ...), custom_call_target="tpu_custom_call" | custom-call | tf_op jit(solution)/shard_map/pallas_call | solution.py:517
  64.9 1.9 fusion.23
  66.7 0.7 dynamic-slice.3
  67.4 65.0 %shard_map.341 = (bf16[512,1024]{1,0:T(8,128)(2,1)}, bf16[512,1024]{1,0:T(8,128)(2,1)}, bf16[512,256]{1,0:T(8,128)(2,1)}, bf16[512,256]{1,0:T(8,128)(2,1)}, bf16...) custom-call(bf16[2,512,1024]{2,1,0:T(8,128)(2,1)} %refs_4_.1, ...), custom_call_target="tpu_custom_call" | custom-call | tf_op jit(solution)/shard_map/pallas_call | solution.py:517
  132.4 38.0 %shard_map.342 = (bf16[512,1024]{1,0:T(8,128)(2,1)}, bf16[512,1024]{1,0:T(8,128)(2,1)}, bf16[512,1024]{1,0:T(8,128)(2,1)}, bf16[512,1024]{1,0:T(8,128)(2,1)}) custom-call(bf16[512,1024]{1,0:T(8,128)(2,1)} %get-tuple-element.106.refs_0_.refs_18_, bf16[512,1024]{1,0:T(8,128)(2,1)} %get-tuple-element.107.refs_1_.refs_6_, bf16[1024,1024]{1,0:T(8,128)(2,1)} %bitcast.94, ...), custom_call_target="tpu_custom_call" | custom-call | tf_op jit(solution)/shard_map/pallas_call | solution.py:517
  170.4 21.7 %shard_map.343 = (bf16[192,2048]{1,0:T(8,128)(2,1)}, bf16[256,512]{1,0:T(8,128)(2,1)}) custom-call(bf16[512,1024]{1,0:T(8,128)(2,1)} %get-tuple-element.111.refs_0_.refs_11_, s32[1,2048]{1,0:T(1,128)} %bitcast.139, bf16[768,1024]{1,0:T(8,128)(2,1)} %bitcast.90, bf16[768,1024]{1,0:T(8,128)(2,1)} %get-tuple-element.100.refs_3_), custom_call_target="tpu_custom_call" | custom-call | tf_op jit(solution)/shard_map/pallas_call | solution.py:517
  192.1 81.2 %shard_map.344 = (bf16[512,1024]{1,0:T(8,128)(2,1)}, bf16[512,1024]{1,0:T(8,128)(2,1)}, bf16[512,256]{1,0:T(8,128)(2,1)}, bf16[512,256]{1,0:T(8,128)(2,1)}, bf16...) custom-call(bf16[512,1024]{1,0:T(8,128)(2,1)} %get-tuple-element.110, ...), custom_call_target="tpu_custom_call" | custom-call | tf_op jit(solution)/shard_map/pallas_call | solution.py:517
  273.3 66.0 %shard_map.345 = (bf16[512,1024]{1,0:T(8,128)(2,1)}, bf16[512,1024]{1,0:T(8,128)(2,1)}, f32[1,1024]{1,0:T(1,128)}, f32[1,1024]{1,0:T(1,128)}, bf16[512,256]{1,0:...) custom-call(f32[2,512,1024]{2,1,0:T(8,128)} %refs_0_.3, ...), custom_call_target="tpu_custom_call" | custom-call | tf_op jit(solution)/shard_map/pallas_call | solution.py:517
  339.4 30.2 %shard_map.346 = (bf16[768,512]{1,0:T(8,128)(2,1)}, bf16[64,512]{1,0:T(8,128)(2,1)}) custom-call(bf16[192,2048]{1,0:T(8,128)(2,1)} %get-tuple-element.122.refs_0_, s32[1,2048]{1,0:T(1,128)} %bitcast.140, bf16[512,1024]{1,0:T(8,128)(2,1)} %get-tuple-element.121.refs_2_.refs_0_, bf16[256,1024]{1,0:T(8,128)(2,1)} %bitcast.116, ...), custom_call_target="tpu_custom_call" | custom-call | tf_op jit(solution)/shard_map/pallas_call | solution.py:517
  369.6 38.8 %shard_map.347 = (bf16[512,1024]{1,0:T(8,128)(2,1)}, f32[1,1024]{1,0:T(1,128)}, f32[1,1024]{1,0:T(1,128)}, bf16[64,1024]{1,0:T(8,128)(2,1)}, bf16[64,1024]{1,0:T...) custom-call(bf16[512,1024]{1,0:T(8,128)(2,1)} %get-tuple-element.121.refs_2_.refs_0_, ...), custom_call_target="tpu_custom_call" | custom-call | tf_op jit(solution)/shard_map/pallas_call | solution.py:517
  408.4 64.9 %shard_map.348 = (bf16[512,1024]{1,0:T(8,128)(2,1)}, bf16[512,1024]{1,0:T(8,128)(2,1)}, f32[1,1024]{1,0:T(1,128)}, f32[1,1024]{1,0:T(1,128)}, bf16[512,256]{1,0:...) custom-call(bf16[512,1024]{1,0:T(8,128)(2,1)} %get-tuple-element.129, ...), custom_call_target="tpu_custom_call" | custom-call | tf_op jit(solution)/shard_map/pallas_call | solution.py:517
  473.4 28.5 %shard_map.349 = (bf16[768,512]{1,0:T(8,128)(2,1)}, bf16[64,512]{1,0:T(8,128)(2,1)}, f32[256,1024]{1,0:T(8,128)}, f32[256,1024]{1,0:T(8,128)}) custom-call(bf16[192,2048]{1,0:T(8,128)(2,1)} %get-tuple-element.135.refs_0_, s32[1,2048]{1,0:T(1,128)} %bitcast.141, bf16[512,1024]{1,0:T(8,128)(2,1)} %get-tuple-element.134.refs_2_.refs_0_, ...), custom_call_target="tpu_custom_call" | custom-call | tf_op jit(solution)/shard_map/pallas_call | solution.py:517
  502.0 44.2 %shard_map.350 = (bf16[512,1024]{1,0:T(8,128)(2,1)}, f32[1,1024]{1,0:T(1,128)}, f32[1,1024]{1,0:T(1,128)}, bf16[2,512,1024]{2,1,0:T(8,128)(2,1)}, bf16[64,512]{1...) custom-call(bf16[512,1024]{1,0:T(8,128)(2,1)} %get-tuple-element.134, ...), custom_call_target="tpu_custom_call" | custom-call | tf_op jit(solution)/shard_map/pallas_call | solution.py:517
  546.2 0.9 broadcast_select_fusion
  547.1 1.5 fusion.7.refs_2_
  548.6 0.7 concatenate.20
  549.4 0.1 concatenate.21
  549.4 0.6 pad_maximum_fusion.4.refs_1_
  550.1 0.3 fusion.12
  550.4 1.0 fusion.8.refs_0_
  551.4 29.8 %shard_map.351 = (bf16[128,1024]{1,0:T(8,128)(2,1)}, f32[8,1024]{1,0:T(8,128)}, bf16[256,512]{1,0:T(8,128)(2,1)}, f32[64,1024]{1,0:T(8,128)}, f32[64,1024]{1,0:T...) custom-call(bf16[128,1024]{1,0:T(8,128)(2,1)} %fusion.8.refs_0_, f32[2,8,1024]{2,1,0:T(8,128)} %pad_maximum_fusion.4.refs_1_, ...), custom_call_target="tpu_custom_call" | custom-call | tf_op jit(solution)/shard_map/pallas_call | solution.py:517
  581.2 1.4 copy.57
  582.6 0.1 fusion.22
  582.7 0.8 copy.58
  583.5 0.8 copy.59
  584.3 0.8 copy.60
  585.2 1.0 convert_element_type.37
  586.2 0.8 slice_bitcast_fusion
  587.0 0.8 convert.13
  587.8 1.6 fusion.24
  589.4 2.5 bitcast_convert_fusion
  591.9 2.5 bitcast_convert_fusion.1
  594.4 0.7 copy.67
  595.1 0.7 copy.68
  595.8 0.7 copy.69
  596.5 1.0 copy.70
  597.5 1.0 copy.71
  (61 shorter events, 0.1 us)
Async XLA Ops:
  0.7 35.1 %copy-start = (bf16[1,1024,256]{2,1,0:T(8,128)(2,1)S(1)}, bf16[1,1024,256]{2,1,0:T(8,128)(2,1)}, u32[]{:S(2)}) copy-start(bf16[1,1024,256]{2,1,0:T(8,128)(2,1)} %param.33) | copy-start | bytes 1572868
  0.7 2.6 copy-start.8
  3.7 1.4 copy-start.16
  3.7 1.3 copy-start.17
  3.7 1.3 copy-start.18
  3.7 1.3 copy-start.19
  3.7 1.3 copy-start.20
  3.7 1.3 copy-start.21
  3.7 28.7 %copy-start.1 = (bf16[2,512,1024]{2,1,0:T(8,128)(2,1)S(1)}, bf16[2,512,1024]{2,1,0:T(8,128)(2,1)}, u32[]{:S(2)}) copy-start(bf16[2,512,1024]{2,1,0:T(8,128)(2,1)} %refs_4_.1) | copy-start | bytes 6291460
  32.4 2.1 copy-start.15
  32.4 2.1 copy-start.32
  32.5 3.0 copy-start.2
  32.5 3.0 copy-start.5
  501.9 44.4 %copy-start.9 = (bf16[64,512]{1,0:T(8,128)(2,1)S(1)}, bf16[64,512]{1,0:T(8,128)(2,1)}, u32[]{:S(2)}) copy-start(bf16[64,512]{1,0:T(8,128)(2,1)} %get-tuple-element.147.refs_14_) | copy-start | bytes 196612
  501.9 44.4 %copy-start.10 = (bf16[64,512]{1,0:T(8,128)(2,1)S(1)}, bf16[64,512]{1,0:T(8,128)(2,1)}, u32[]{:S(2)}) copy-start(bf16[64,512]{1,0:T(8,128)(2,1)} %get-tuple-element.146.refs_13_) | copy-start | bytes 196612
  501.9 46.7 %copy-start.28 = (f32[1,1024]{1,0:T(1,128)S(1)}, f32[1,1024]{1,0:T(1,128)}, u32[]{:S(2)}) copy-start(f32[1,1024]{1,0:T(1,128)} %get-tuple-element.154) | copy-start | bytes 12292
  501.9 46.7 %copy-start.29 = (f32[1,1024]{1,0:T(1,128)S(1)}, f32[1,1024]{1,0:T(1,128)}, u32[]{:S(2)}) copy-start(f32[1,1024]{1,0:T(1,128)} %get-tuple-element.155) | copy-start | bytes 12292
  501.9 46.7 %copy-start.30 = (f32[1,1024]{1,0:T(1,128)S(1)}, f32[1,1024]{1,0:T(1,128)}, u32[]{:S(2)}) copy-start(f32[1,1024]{1,0:T(1,128)} %get-tuple-element.152) | copy-start | bytes 12292
  501.9 46.7 %copy-start.31 = (f32[1,1024]{1,0:T(1,128)S(1)}, f32[1,1024]{1,0:T(1,128)}, u32[]{:S(2)}) copy-start(f32[1,1024]{1,0:T(1,128)} %get-tuple-element.153) | copy-start | bytes 12292
  501.9 47.4 %copy-start.22 = (f32[1,1024]{1,0:T(1,128)S(1)}, f32[1,1024]{1,0:T(1,128)}, u32[]{:S(2)}) copy-start(f32[1,1024]{1,0:T(1,128)} %get-tuple-element.160) | copy-start | bytes 12292
  501.9 47.4 %copy-start.23 = (f32[1,1024]{1,0:T(1,128)S(1)}, f32[1,1024]{1,0:T(1,128)}, u32[]{:S(2)}) copy-start(f32[1,1024]{1,0:T(1,128)} %get-tuple-element.161) | copy-start | bytes 12292
  501.9 47.4 %copy-start.24 = (f32[1,1024]{1,0:T(1,128)S(1)}, f32[1,1024]{1,0:T(1,128)}, u32[]{:S(2)}) copy-start(f32[1,1024]{1,0:T(1,128)} %get-tuple-element.158) | copy-start | bytes 12292
  502.0 47.4 %copy-start.25 = (f32[1,1024]{1,0:T(1,128)S(1)}, f32[1,1024]{1,0:T(1,128)}, u32[]{:S(2)}) copy-start(f32[1,1024]{1,0:T(1,128)} %get-tuple-element.159) | copy-start | bytes 12292
  502.0 47.4 %copy-start.26 = (f32[1,1024]{1,0:T(1,128)S(1)}, f32[1,1024]{1,0:T(1,128)}, u32[]{:S(2)}) copy-start(f32[1,1024]{1,0:T(1,128)} %get-tuple-element.156) | copy-start | bytes 12292
  502.0 47.4 %copy-start.27 = (f32[1,1024]{1,0:T(1,128)S(1)}, f32[1,1024]{1,0:T(1,128)}, u32[]{:S(2)}) copy-start(f32[1,1024]{1,0:T(1,128)} %get-tuple-element.157) | copy-start | bytes 12292
  582.6 6.8 %copy-start.4 = (bf16[2,512,1024]{2,1,0:T(8,128)(2,1)S(1)}, bf16[2,512,1024]{2,1,0:T(8,128)(2,1)}, u32[]{:S(2)}) copy-start(bf16[2,512,1024]{2,1,0:T(8,128)(2,1)} %get-tuple-element.148) | copy-start | bytes 6291460
  583.5 3.5 copy-start.11
  589.4 2.5 copy-start.3
  591.9 2.5 copy-start.14
  591.9 3.2 copy-start.13
  591.9 3.9 copy-start.12
  591.9 4.6 copy-start.7
  594.4 3.1 copy-start.6

commit v5 on v4

--- a/solution.py
+++ b/solution.py
@@ -17,7 +17,7 @@
 BUSY = pl.CostEstimate(flops=30_000_000_000, bytes_accessed=8_000_000, transcendentals=0)
 LAG = 3
 BLOCK = 128
-VMEM_BYTES = 56 * 1024 * 1024
+VMEM_BYTES = 60 * 1024 * 1024
 EPS = 1e-05
 SECTION, LINE, FRAME = "section", "head", "frame"
 BOTH, LINE_ONLY, BY_SECTION = "both", "line", "one"
@@ -31,6 +31,7 @@
     scratch = ()
     greets = ()
     late = False
+    hooked = 0
 
     def middle(self):
         pass
@@ -63,37 +64,115 @@
     out_in_vmem = False
     greets = (SECTION, FRAME)
 
+    def __init__(self, weight, layer=None, quarter=None):
+        self.layer = layer
+        self.operands = (weight,) if quarter is None else (weight, quarter)
+        self.outs = (jax.ShapeDtypeStruct(weight.shape, weight.dtype),)
+        self.scratch = (pltpu.SemaphoreType.DMA((10,)),)
+        if layer is not None:
+            self.scratch += (pltpu.VMEM((2,) + weight.shape, weight.dtype),)
+        self.quarter = weight.shape[0] // 4
+
+    @property
+    def ref(self):
+        other = jnp.where(lax.axis_index(SECTION) == self.layer, 0, 1)
+        return self.room[1].at[other]
+
+    def arrived(self, at):
+        return self.out[0].at[at] if self.layer is None else self.room[1].at[1, at]
+
+    def over(self):
+        sems, at = self.room[0], span(lax.axis_index(FRAME), self.quarter)
+        target = {SECTION: 1 - lax.axis_index(SECTION)}
+        return remote(self.ins[0].at[at], self.arrived(at), sems.at[0], sems.at[1], target)
+
+    def along(self):
+        sems, at = self.room[0], span(lax.axis_index(FRAME), self.quarter)
+        target = {FRAME: frame_partners()[1]}
+        source = self.ins[1] if len(self.ins) > 1 else self.arrived(at)
+        return remote(source, self.arrived(at), sems.at[2], sems.at[3], target)
+
+    def settle(self):
+        at = span(lax.axis_index(FRAME), self.quarter)
+        return pltpu.make_async_copy(self.ins[1], self.arrived(at), self.room[0].at[0])
+
+    def within(self):
+        sems, partners = self.room[0], frame_partners()
+        copies = []
+        for k, whose in enumerate((lax.axis_index(FRAME), partners[1])):
+            at = span(whose, self.quarter)
+            copies.append(
+                remote(
+                    self.arrived(at),
+                    self.arrived(at),
+                    sems.at[4 + 2 * k],
+                    sems.at[5 + 2 * k],
+                    {FRAME: partners[0]},
+                )
+            )
+        return copies
+
+    def begin(self):
+        if len(self.ins) > 1:
+            self.settle().start()
+            self.along().start()
+        else:
+            self.over().start()
+        if self.layer is not None:
+            pltpu.make_async_copy(self.ins[0], self.room[1].at[0], self.room[0].at[8]).start()
+
+    def first_hop(self):
+        self.over().wait_recv()
+        self.along().start()
+
+    def second_hop(self):
+        if len(self.ins) > 1:
+            self.settle().wait()
+        self.along().wait_recv()
+        for copy in self.within():
+            copy.start()
+
+    def arrive(self):
+        for copy in self.within():
+            copy.wait_recv()
+        if self.layer is not None:
+            sems = self.room[0]
+            pltpu.make_async_copy(self.ins[0], self.room[1].at[0], sems.at[8]).wait()
+            pltpu.make_async_copy(self.room[1].at[1], self.out[0], sems.at[9]).start()
+
+    def sent(self):
+        over = [] if len(self.ins) > 1 else [self.over()]
+        for copy in over + [self.along()] + self.within():
+            copy.wait_send()
+        if self.layer is not None:
+            pltpu.make_async_copy(self.room[1].at[1], self.out[0], self.room[0].at[9]).wait()
+
+    def steps(self):
+        if self.layer is not None:
+            return [self.sent]
+        return [self.first_hop, self.second_hop][self.hooked :] + [self.arrive, self.sent]
+
+
+class QuarterTask(Task):
+    out_in_vmem = False
+    greets = (SECTION,)
+
     def __init__(self, weight):
+        self.quarter = weight.shape[0] // 4
         self.operands = (weight,)
-        self.outs = (jax.ShapeDtypeStruct(weight.shape, weight.dtype),)
-        self.scratch = (pltpu.SemaphoreType.DMA((4,)),)
-        self.half = weight.shape[0] // 2
-
-    def copies(self):
-        (sems,) = self.room
-        core = lax.rem(lax.axis_index(FRAME), 2)
-        rows = span(core, self.half)
-        other_section = {SECTION: 1 - lax.axis_index(SECTION)}
-        other_core = {FRAME: frame_partners()[0]}
-        over = remote(self.ins[0].at[rows], self.out[0].at[rows], sems.at[0], sems.at[1], other_section)
-        on = remote(self.out[0].at[rows], self.out[0].at[rows], sems.at[2], sems.at[3], other_core)
-        return over, on
+        self.outs = (jax.ShapeDtypeStruct((self.quarter, weight.shape[1]), weight.dtype),)
+        self.scratch = (pltpu.SemaphoreType.DMA((2,)),)
+
+    def over(self):
+        sems, at = self.room[0], span(lax.axis_index(FRAME), self.quarter)
+        target = {SECTION: 1 - lax.axis_index(SECTION)}
+        return remote(self.ins[0].at[at], self.out[0], sems.at[0], sems.at[1], target)
 
     def begin(self):
-        self.copies()[0].start()
+        self.over().start()
 
     def steps(self):
-        over, on = self.copies()
-
-        def pass_on():
-            over.wait_recv()
-            on.start()
-
-        def end():
-            over.wait_send()
-            on.wait()
-
-        return [pass_on, end]
+        return [lambda: self.over().wait()]
 
 
 class ShareTask(Task):
@@ -102,20 +181,21 @@
     def __init__(self, grad):
         rows, width = grad.shape
         self.share = rows // 4
-        self.operands = (grad,) if isinstance(grad, jax.Array) else ()
+        self.far = isinstance(grad, jax.Array)
+        self.operands = (grad,) if self.far else ()
         piece = (self.share, width)
         self.outs = (jax.ShapeDtypeStruct(piece, jnp.bfloat16),)
         self.scratch = (
             pltpu.VMEM((2,) + piece, jnp.bfloat16),
             pltpu.VMEM((2,) + piece, jnp.bfloat16),
-            pltpu.VMEM((2,) + piece, jnp.bfloat16),
             pltpu.SemaphoreType.DMA((3,)),
             pltpu.SemaphoreType.DMA((3,)),
-            pltpu.SemaphoreType.DMA((2,)),
         )
+        if self.far:
+            self.scratch += (pltpu.VMEM((2,) + piece, jnp.bfloat16), pltpu.SemaphoreType.DMA((2,)))
 
     def within(self):
-        own, landing, _, send_sems, recv_sems, here = self.room
+        landing, _, send_sems, recv_sems, *here = self.room
         me = lax.axis_index(FRAME)
         other = frame_partners()[0]
         side = lax.div(me, 2)
@@ -132,19 +212,25 @@
                     {FRAME: other},
                 )
             )
-            copies.append(
-                pltpu.make_async_copy(self.ins[0].at[span(kept, self.share)], own.at[k], here.at[k])
-            )
+            if self.far:
+                own, sems = here
+                source = self.ins[0].at[span(kept, self.share)]
+                copies.append(pltpu.make_async_copy(source, own.at[k], sems.at[k]))
         return copies
 
     def over(self):
-        crossing, send_sems, recv_sems = self.room[2:5]
+        crossing, send_sems, recv_sems = self.room[1:4]
         target = {FRAME: frame_partners()[1]}
         return remote(crossing.at[0], crossing.at[1], send_sems.at[2], recv_sems.at[2], target)
 
     def chip_sum(self, k):
-        own, landing = self.room[:2]
-        return own[k].astype(jnp.float32) + landing[k].astype(jnp.float32)
+        me = lax.axis_index(FRAME)
+        if self.far:
+            own = self.room[4][k]
+        else:
+            side = lax.div(me, 2) if k else 1 - lax.div(me, 2)
+            own = self.ins[0][span(2 * side + lax.rem(me, 2), self.share), :]
+        return own.astype(jnp.float32) + self.room[0][k].astype(jnp.float32)
 
     def begin(self):
         for copy in self.within():
@@ -153,13 +239,13 @@
     def middle(self):
         for copy in self.within():
             copy.wait()
-        self.room[2][0] = self.chip_sum(0).astype(jnp.bfloat16)
+        self.room[1][0] = self.chip_sum(0).astype(jnp.bfloat16)
         self.over().start()
 
     def steps(self):
         def end():
             self.over().wait()
-            total = self.chip_sum(1) + self.room[2][1].astype(jnp.float32)
+            total = self.chip_sum(1) + self.room[1][1].astype(jnp.float32)
             self.out[0][...] = total.astype(jnp.bfloat16)
 
         return [end]
@@ -240,46 +326,58 @@
                     jnp.float32
                 )
 
-        return [end]
+        return [lambda: None, lambda: None, end]
 
 
 class TextTask(Task):
     out_in_vmem = False
-    greets = (SECTION, FRAME, BOTH)
+    greets = (SECTION, FRAME)
 
     def __init__(self, states):
         micros, rows, width = states.shape
         self.operands = (states,)
         self.outs = (jax.ShapeDtypeStruct((2, 4, rows, width), states.dtype),)
-        self.scratch = (pltpu.SemaphoreType.DMA((8,)), pltpu.SemaphoreType.DMA((8,)))
-
-    def copies(self):
-        send_sems, recv_sems = self.room
-        section, me = lax.axis_index(SECTION), lax.axis_index(FRAME)
-        landing = self.out[0].at[section, me]
-        copies = []
-        for far in (0, 1):
-            micro = section if far == 0 else 1 - section
-            for k, frame in enumerate((me,) + frame_partners()):
-                slot = far * 4 + k
-                source = self.ins[0].at[micro]
-                if slot == 0:
-                    copies.append(pltpu.make_async_copy(source, landing, send_sems.at[0]))
-                    continue
-                target = {SECTION: micro, FRAME: frame}
-                copies.append(remote(source, landing, send_sems.at[slot], recv_sems.at[slot], target))
-        return copies
+        self.scratch = (pltpu.SemaphoreType.DMA((3,)),) + (pltpu.SemaphoreType.DMA((2, 3)),) * 2
+
+    def place(self, layer):
+        return self.out[0].at[layer, lax.axis_index(FRAME)]
+
+    def over(self):
+        sems, section = self.room[0], lax.axis_index(SECTION)
+        source = self.ins[0].at[1 - section]
+        return remote(source, self.place(section), sems.at[0], sems.at[1], {SECTION: 1 - section})
+
+    def stay(self):
+        section = lax.axis_index(SECTION)
+        return pltpu.make_async_copy(self.ins[0].at[section], self.place(section), self.room[0].at[2])
+
+    def spread(self, far):
+        section = lax.axis_index(SECTION)
+        layer = 1 - section if far else section
+        source = self.place(layer) if far else self.ins[0].at[section]
+        pair = self.room[1 + far]
+        return [
+            remote(source, self.place(layer), pair.at[0, k], pair.at[1, k], {FRAME: other})
+            for k, other in enumerate(frame_partners())
+        ]
 
     def begin(self):
-        for copy in self.copies():
+        for copy in [self.over(), self.stay()] + self.spread(0):
             copy.start()
 
     def steps(self):
-        def end():
-            for copy in self.copies():
+        def first():
+            self.over().wait_recv()
+            for copy in self.spread(1):
+                copy.start()
+
+        def second():
+            self.over().wait_send()
+            self.stay().wait()
+            for copy in self.spread(0) + self.spread(1):
                 copy.wait()
 
-        return [end]
+        return [first, second]
 
 
 class TotalTask(Task):
@@ -438,8 +536,7 @@
     for target in targets:
         pl.semaphore_signal(barrier, 1, device_id=target, device_id_type=MESH_IDS)
     if LINE_ONLY not in kinds or LINE in kinds:
-        pl.semaphore_wait(barrier, len(targets))
-        return
+        return lambda: pl.semaphore_wait(barrier, len(targets))
 
     for way in (-1, 1):
         other = head + way
@@ -450,13 +547,16 @@
 
     is_end = (head == 0) | (head == 3)
 
-    @pl.when(is_end)
-    def _():
-        pl.semaphore_wait(barrier, len(targets) + 1)
-
-    @pl.when(jnp.logical_not(is_end))
-    def _():
-        pl.semaphore_wait(barrier, len(targets) + 2)
+    def wait():
+        @pl.when(is_end)
+        def _():
+            pl.semaphore_wait(barrier, len(targets) + 1)
+
+        @pl.when(jnp.logical_not(is_end))
+        def _():
+            pl.semaphore_wait(barrier, len(targets) + 2)
+
+    return wait
 
 
 def call(body, operands, outs, scratch, kinds, collective_id, tasks=(), in_vmem=True, end=None):
@@ -487,8 +587,7 @@
         for task, parts in zip(tasks, bound[1:]):
             task.bind(*parts)
 
-        def meet():
-            greet(kinds)
+        meet = greet(kinds)
 
         def ride():
             for task in tasks:
@@ -620,8 +719,9 @@
 
 
 class Chore:
-    def __init__(self, build, stage, left, right, flipped=False):
-        self.stage, self.left, self.right, self.flipped = stage, left, right, flipped
+    def __init__(self, build, stage, piece, each, left, right, flipped=False):
+        self.start, self.each = (stage, piece), each
+        self.left, self.right, self.flipped = left, right, flipped
         columns = left.shape[0] if flipped else left.shape[1]
         self.units = columns // BLOCK
         self.product = build.temp((columns, right.shape[1]), jnp.bfloat16)
@@ -639,22 +739,33 @@
             )
         self.product.ref[at, :] = product.astype(jnp.bfloat16)
 
-    def run(self, piece):
-        @pl.when(piece < self.units)
-        def _():
-            self.unit(piece)
-
-        @pl.when(piece == self.units)
-        def _():
+    def run(self, stage, pieces, piece):
+        shift = (stage - self.start[0]) * pieces - self.start[1]
+        steps = -(-self.units // self.each)
+
+        def at_step(first, last, what):
+            if shift >= last or shift + pieces <= first:
+                return
+            now = piece + shift
+
+            @pl.when((now >= first) & (now < last))
+            def _():
+                what(now)
+
+        def make(now):
+            for more in range(self.each):
+                self.unit(now * self.each + more)
+
+        def begin(now):
             self.task.ins = [self.product.ref]
             self.task.begin()
 
-        @pl.when(piece == self.units + 5)
-        def _():
-            self.task.middle()
-
-
-def line_chain(stages, need, part, middle, chores):
+        at_step(0, steps, make)
+        at_step(steps, steps + 1, begin)
+        at_step(steps + 5, steps + 6, lambda now: self.task.middle())
+
+
+def line_chain(stages, need, part, set_out, middle, chores, hooks):
     place = lax.axis_index(LINE)
     rows = stages[0].rows
     pieces = chunking(rows)
@@ -667,21 +778,30 @@
     peer = {LINE: 3 - place}
 
     def inwards(stage, piece):
-        send, recv, _, _, send_sems, recv_sems = stage.room[:6]
+        send, held, _, send_sems, recv_sems = stage.room[:5]
         at = span(piece, step)
-        return remote(send.at[at], recv.at[at], send_sems.at[piece], recv_sems.at[piece], inner)
+        return remote(send.at[at], held.at[at], send_sems.at[piece], recv_sems.at[piece], inner)
 
     def crossing(stage, piece):
         send, _, across = stage.room[:3]
-        send_sems, recv_sems = stage.room[6:8]
+        send_sems, recv_sems = stage.room[5:7]
         at = span(piece, step)
         return remote(send.at[at], across.at[at], send_sems.at[piece], recv_sems.at[piece], peer)
 
     def outwards(stage, piece):
-        held = stage.room[3]
-        send_sems, recv_sems = stage.room[8:]
+        held = stage.room[1]
+        send_sems, recv_sems = stage.room[7:]
         at = span(piece, step)
         return remote(held.at[at], held.at[at], send_sems.at[piece], recv_sems.at[piece], outer)
+
+    def hook(stage, piece, at_end):
+        for run, *spots in hooks:
+            index, when = spots[0 if at_end else 1]
+            if stages[index] is stage:
+
+                @pl.when(piece == when)
+                def _():
+                    run()
 
     def open_stage(index):
         need(index)
@@ -697,14 +817,14 @@
 
     def chore(stage, piece):
         for one in chores:
-            if stages[one.stage] is stage:
-                one.run(piece)
+            one.run(stages.index(stage), pieces, piece)
 
     @pl.when(is_end)
     def _():
         def give(stage, piece):
             inwards(stage, piece).start()
             chore(stage, piece)
+            hook(stage, piece, True)
 
         def take(stage, piece):
             outwards(stage, piece).wait_recv()
@@ -718,6 +838,8 @@
                 if index:
                     loop(low, high, lambda piece: take(stages[index - 1], piece))
                 stage.room[0][span(block, per_block * step), :] = stage.prepare(block).astype(jnp.bfloat16)
+                if index == 0:
+                    pl.when(block == 0)(set_out)
                 loop(low, high, lambda piece: give(stage, piece))
                 if index == 0:
 
@@ -737,13 +859,16 @@
             def _():
                 part[...] = stage.prepare(lax.div(piece, per_block))
 
+            if stage is stages[0]:
+                pl.when(piece == 0)(set_out)
             at = span(piece, step)
-            send, recv = stage.room[:2]
+            send, held = stage.room[:2]
             inwards(stage, piece).wait_recv()
             own = part[span(lax.rem(piece, per_block), step), :]
-            send[at, :] = (own + recv[at, :].astype(jnp.float32)).astype(jnp.bfloat16)
+            send[at, :] = (own + held[at, :].astype(jnp.float32)).astype(jnp.bfloat16)
             crossing(stage, piece).start()
             chore(stage, piece)
+            hook(stage, piece, False)
             if stage is stages[0]:
 
                 @pl.when(piece == 2 * per_block - 1)
@@ -752,7 +877,7 @@
 
         def settle(stage, piece):
             at = span(piece, step)
-            send, _, across, held = stage.room[:4]
+            send, held, across = stage.room[:3]
             crossing(stage, piece).wait_recv()
             total = send[at, :].astype(jnp.float32) + across[at, :].astype(jnp.float32)
             held[at, :] = total.astype(jnp.bfloat16)
@@ -828,11 +953,11 @@
     return call(run, operands, outs, scratch, kinds, collective_id, tasks, in_vmem=False, end=end)
 
 
-def run_chain(build, stages, collective_id, tasks, kinds=(LINE_ONLY,), chores=()):
+def run_chain(build, stages, collective_id, tasks, kinds=(LINE_ONLY,), chores=(), hooks=()):
     slots = []
     for stage in stages:
         pieces = chunking(stage.rows)
-        room = [pltpu.VMEM((stage.rows, stage.width), jnp.bfloat16)] * 4
+        room = [pltpu.VMEM((stage.rows, stage.width), jnp.bfloat16)] * 3
         room += [pltpu.SemaphoreType.DMA((pieces,))] * 6
         slots.append([build.extra(scratch) for scratch in room])
     part = build.extra(pltpu.VMEM((min(BLOCK, stages[0].rows), stages[0].width), jnp.float32))
@@ -840,9 +965,11 @@
     def body(need, meet, ride, middle):
         for stage, places in zip(stages, slots):
             stage.room = [build.bound[place] for place in places]
-        meet()
-        ride()
-        line_chain(stages, need, build.bound[part], middle, chores)
+        def set_out():
+            meet()
+            ride()
+
+        line_chain(stages, need, build.bound[part], set_out, middle, chores, hooks)
 
     tasks = list(tasks) + [one.task for one in chores]
     return run_build(build, body, kinds, collective_id, tasks)
@@ -857,7 +984,7 @@
         gain, shift = build.arg(gain[None], index), build.arg(shift[None], index)
 
     def finish(at, piece):
-        value = base.ref[at, :].astype(jnp.float32) + stage.room[3][at, :].astype(jnp.float32)
+        value = base.ref[at, :].astype(jnp.float32) + stage.room[1][at, :].astype(jnp.float32)
         rounded = value.astype(jnp.bfloat16)
         low.write(at, rounded)
         if mode == NORM:
@@ -896,9 +1023,10 @@
 def cross_stage(build, index, layer, normed, states, seg, into, out_of):
     rows, width = normed.shape
     stage = Stage(rows, width)
-    columns, block = into[0].shape[1], min(BLOCK, rows)
     states, seg = build.arg(states, index), build.arg(seg, index)
-    into, out_of = build.pick(into, layer, index), build.pick(out_of, layer, index)
+    columns, block = states.shape[1] // 2, min(BLOCK, rows)
+    if not isinstance(into, WeightTask):
+        into, out_of = build.pick(into, layer, index), build.pick(out_of, layer, index)
     queries = build.out((rows, columns), jnp.bfloat16)
     left = build.out((rows, columns), jnp.bfloat16)
     values_t = build.temp((columns, states.shape[0]), jnp.bfloat16)
@@ -932,8 +1060,12 @@
 def feed_stage(build, index, layer, normed, into, out_of):
     rows, width = normed.shape
     stage = Stage(rows, width)
-    hidden, block = into[0].shape[1], min(BLOCK, rows)
-    into, out_of = build.pick(into, layer, index), build.pick(out_of, layer, index)
+    block = min(BLOCK, rows)
+    if isinstance(into, WeightTask):
+        hidden = into.operands[0].shape[1]
+    else:
+        hidden = into[0].shape[1]
+        into, out_of = build.pick(into, layer, index), build.pick(out_of, layer, index)
     before = build.out((rows, hidden), jnp.bfloat16)
     left = build.out((rows, hidden), jnp.bfloat16)
 
@@ -971,7 +1103,7 @@
         return remote(source.ref.at[at], landing, pair.at[0, piece], pair.at[1, piece], target)
 
     def finish(at, piece):
-        grad = stage.room[3][at, :].astype(jnp.float32)
+        grad = stage.room[1][at, :].astype(jnp.float32)
         standard, inverse = norm_parts(value.ref[at, :].astype(jnp.float32))
         scaled = grad * gain.ref[...]
         through = inverse * (
@@ -1086,17 +1218,28 @@
     return stage
 
 
-def self_in_stage(build, index, layer, grads_t, weight, width):
+def self_in_stage(build, index, layer, grads_t, weights, width):
     columns, rows = grads_t.shape
     stage = Stage(rows, width)
-    flipped, matrix = build.arg(grads_t, index), build.pick(weight, layer, index)
+    part = columns // 3
+    flipped = build.arg(grads_t, index)
+    matrices = [build.pick(weight, layer, index) for weight in weights]
     left = build.temp((rows, columns), jnp.bfloat16)
 
     def begin():
-        left.ref[...] = flipped.ref[...].T
+        for number in range(3):
+            heads = [
+                flipped.ref[(3 * head + number) * HEAD : (3 * head + number + 1) * HEAD, :]
+                for head in range(part // HEAD)
+            ]
+            left.ref[:, number * part : (number + 1) * part] = jnp.concatenate(heads, axis=0).T
 
     def prepare(number):
-        return plain_product(left.ref[span(number, min(BLOCK, rows)), :], matrix.ref[...])
+        at = span(number, min(BLOCK, rows))
+        total = jnp.zeros((min(BLOCK, rows), width), jnp.float32)
+        for number, matrix in enumerate(matrices):
+            total = total + nt_product(left.ref[at, number * part : (number + 1) * part], matrix.ref[...])
+        return total
 
     stage.begin, stage.prepare = begin, prepare
     stage.left = left
@@ -1104,65 +1247,63 @@
 
 
 def forward_chain(
-    layer, attended_t, entering, states, seg, gains, weights, collective_id, tasks
+    layer, attended_t, entering, states, seg, gains, after, weights, collective_id, tasks, late
 ):
-    output, query, cross, *more = weights
+    output, query, cross, expand, reduce = weights
     build = Build()
     base = build.arg(entering, 0, BY_SECTION if entering.ndim == 3 else None)
     first = self_out_stage(build, 0, layer, attended_t, output, base)
     middle, second_normed = residual_norm(build, 0, first, base, gains[2], gains[3], NORM)
     second = cross_stage(build, 1, layer, second_normed, states, seg, query, cross)
     latter, third_normed = residual_norm(build, 1, second, middle, gains[4], gains[5], NORM)
-    stages = [first, second]
-    if more:
-        stages.append(feed_stage(build, 2, layer, third_normed, *more))
-        residual_norm(build, 2, stages[2], latter, None, None, END)
-    return run_chain(build, stages, collective_id, tasks)
-
-
-def feed_chain(layer, normed, latter, weights, after, collective_id):
-    build = Build()
-    normed, latter = build.arg(normed, 0), build.arg(latter, 0)
-    stage = feed_stage(build, 0, layer, normed, *weights[3:])
-    residual_norm(build, 0, stage, latter, after[0], after[1], NEXT)
-    return run_chain(build, [stage], collective_id, [])
-
-
-def backward_chain(
-    layer,
-    upstream,
-    before,
-    hidden,
-    third_normed,
-    latter,
-    queries,
-    states,
-    seg,
-    middle,
-    gains,
-    weights,
-    collective_id,
-    tasks,
-):
+    third = feed_stage(build, 2, layer, third_normed, expand, reduce)
+    mode = END if after is None else NEXT
+    residual_norm(build, 2, third, latter, *((None, None) if after is None else after[:2]), mode)
+    hooks = []
+    if isinstance(expand, WeightTask):
+        hooks = [
+            (expand.second_hop, (1, 4), (0, 15)),
+            (reduce.first_hop, (1, 0), (0, 10)),
+            (reduce.second_hop, (1, 15), (1, 8)),
+        ]
+        for one in late:
+            hooks += [(one.first_hop, (2, 0), (1, 8)), (one.second_hop, (2, 10), (2, 4))]
+        start_second = second.begin
+
+        def begin_second():
+            query.second_hop()
+            cross.second_hop()
+            query.arrive()
+            cross.arrive()
+            start_second()
+
+        def begin_third():
+            expand.arrive()
+            reduce.arrive()
+
+        second.begin, third.begin = begin_second, begin_third
+    return run_chain(build, [first, second, third], collective_id, tasks, hooks=hooks)
+
+
+def add_backward(build, index, layer, arriving, saved, states, seg, gains, weights):
     _, query, cross, expand, reduce = weights
-    build = Build()
-    arriving = build.arg(upstream, 0, BY_SECTION if upstream.ndim == 3 else None)
-    first = feed_back_stage(build, 0, layer, arriving, before, reduce, expand)
-    grad_latter, grad_cross = norm_backward(build, 0, first, latter, gains[4], arriving, True)
-    second = cross_back_stage(build, 1, layer, grad_cross, queries, states, seg, cross, query)
-    norm_backward(build, 1, second, middle, gains[2], grad_latter, False)
+    middle, latter, third_normed, queries, before, hidden = saved
+    first = feed_back_stage(build, index, layer, arriving, before, reduce, expand)
+    grad_latter, grad_cross = norm_backward(build, index, first, latter, gains[4], arriving, True)
+    second = cross_back_stage(build, index + 1, layer, grad_cross, queries, states, seg, cross, query)
+    norm_backward(build, index + 1, second, middle, gains[2], grad_latter, False)
+    first_piece, each = (12, 2) if index else (0, 1)
     chores = [
-        Chore(build, 0, build.arg(hidden, 0), arriving),
-        Chore(build, 1, build.arg(third_normed, 1), first.left),
+        Chore(build, index, first_piece, each, build.arg(hidden, index), arriving),
+        Chore(build, index + 1, 0, each, build.arg(third_normed, index + 1), first.left),
     ]
-    return run_chain(build, [first, second], collective_id, tasks, chores=chores)
-
-
-def last_chain(layer, grads_t, entering, gain, upstream, weight, spare, products, collective_id, tasks):
-    build = Build()
+    return [first, second], chores
+
+
+def add_last(build, layer, grads_t, entering, gain, upstream, weights, spare, products):
     residual = build.arg(upstream, 0)
-    stage = self_in_stage(build, 0, layer, grads_t, weight, upstream.shape[1])
-    norm_backward(build, 0, stage, entering, gain, residual, False, spare)
+    stage = self_in_stage(build, 0, layer, grads_t, weights, upstream.shape[1])
+    _, low = norm_backward(build, 0, stage, entering, gain, residual, False, spare)
     chores = []
     for left, right in products:
         flipped = left.shape[0] != upstream.shape[0]
@@ -1170,9 +1311,28 @@
             right = stage.left
         else:
             right = residual if right is upstream else build.arg(right, 0)
-        chores.append(Chore(build, 0, build.arg(left, 0), right, flipped))
-    kinds = (LINE_ONLY,) if spare is None else (LINE_ONLY, SECTION)
-    return run_chain(build, [stage], collective_id, tasks, kinds, chores)
+        chores.append(Chore(build, 0, 0, 1, build.arg(left, 0), right, flipped))
+    return stage, low, chores
+
+
+def backward_chain(layer, upstream, saved, states, seg, gains, weights, collective_id, tasks):
+    build = Build()
+    arriving = build.arg(upstream, 0, BY_SECTION)
+    stages, chores = add_backward(build, 0, layer, arriving, saved, states, seg, gains, weights)
+    return run_chain(build, stages, collective_id, tasks, chores=chores)
+
+
+def last_chain(layer, *rest, spare, products, collective_id, tasks):
+    build = Build()
+    stage, _, chores = add_last(build, layer, *rest, spare, products)
+    return run_chain(build, [stage], collective_id, tasks, (LINE_ONLY, SECTION), chores)
+
+
+def between_chain(layer, last, products, backward, collective_id, tasks):
+    build = Build()
+    stage, low, chores = add_last(build, layer, *last, None, products)
+    stages, more = add_backward(build, 1, layer - 1, low, *backward)
+    return run_chain(build, [stage] + stages, collective_id, tasks, chores=chores + more)
 
 
 def masked_scores(keys, query_t, begins, start):
@@ -1192,45 +1352,96 @@
     ]
 
 
-def self_forward(normed, weight, begins, layer, collective_id, tasks):
-    rows, frames, width = normed.shape[0], 4, 3 * HEAD
+def turned_parts(normed, matrices, own, at):
+    for part, matrix in enumerate(matrices):
+        turned = plain_product(normed, matrix.ref[...]).astype(jnp.bfloat16).T
+        for head in range(4):
+            rows = slice(part * HEAD, (part + 1) * HEAD)
+            own.ref[at + (head, rows)] = turned[head * HEAD : (head + 1) * HEAD, :]
+
+
+def self_forward(normed, weights, begins, layer, collective_id, tasks, early):
+    first = int(normed.ndim == 3)
+    rows, frames, width = normed.shape[-2], 4, 3 * HEAD
     all_rows = rows * frames
     build = Build()
-    normed, begins, weight = build.arg(normed, 0), build.arg(begins, 1), build.pick(weight, layer, 0)
+    normed, begins = build.arg(normed, 0), build.arg(begins, 1)
+    if first:
+        matrices = [build.arg(weight, 0) for weight in weights]
+    else:
+        matrices = [build.pick(weight, layer, 0) for weight in weights]
     heads_t = build.out((width, all_rows), jnp.bfloat16)
     out = build.out((frames * HEAD, rows), jnp.bfloat16)
-    own = build.temp((frames, width, rows), jnp.bfloat16)
+    own = build.temp((1 + first, frames, width, rows), jnp.bfloat16)
     keys = build.temp((all_rows, HEAD), jnp.bfloat16)
     mixed_t = build.temp((frames, HEAD, rows), jnp.bfloat16)
     sems = [build.extra(pltpu.SemaphoreType.DMA((2, frames - 1))) for _ in range(2)]
+    over_sems = build.extra(pltpu.SemaphoreType.DMA((2, frames)))
 
     def body(need, meet, ride, middle):
-        me = lax.axis_index(FRAME)
+        me, section = lax.axis_index(FRAME), lax.axis_index(SECTION)
         partners = frame_partners()
         block = min(2 * BLOCK, rows)
-        arriving = to_frames(
-            lambda g: own.ref.at[g], lambda f: heads_t.ref.at[:, span(f, rows)], build.bound[sems[0]]
-        )
+        landing = heads_t.ref.at[:, span(me, rows)]
+        arriving = to_frames(lambda g: own.ref.at[0, g], lambda f: landing, build.bound[sems[0]])
         leaving = to_frames(
             lambda g: mixed_t.ref.at[g], lambda f: out.ref.at[span(f, HEAD), :], build.bound[sems[1]]
         )
-
-        def project(other):
-            return nt_product(weight.ref[span(other, width), :], normed.ref[...]).astype(jnp.bfloat16)
-
-        meet()
+        pair = build.bound[over_sems]
+        over = [
+            remote(own.ref.at[first, g], landing, pair.at[0, k], pair.at[1, k], {SECTION: 1, FRAME: g})
+            for k, g in enumerate((me,) + partners)
+        ]
+
         need(0)
-        for k in (2, 1, 0):
-            own.ref[partners[k]] = project(partners[k])
-            arriving[k].start()
+        if first:
+
+            @pl.when(section == 0)
+            def _():
+                turned_parts(normed.ref[1], matrices, own, (1,))
+                meet()
+                for copy in over:
+                    copy.start()
+                turned_parts(normed.ref[0], matrices, own, (0,))
+                for copy in arriving[::-1]:
+                    copy.start()
+                heads_t.ref[:, span(me, rows)] = own.ref[0, me]
+
+            @pl.when(section == 1)
+            def _():
+                meet()
+
+        else:
+            turned_parts(normed.ref[...], matrices, own, (0,))
+            meet()
+            for copy in arriving[::-1]:
+                copy.start()
+            heads_t.ref[:, span(me, rows)] = own.ref[0, me]
         ride()
-        heads_t.ref[:, span(me, rows)] = project(me)
         need(1)
-        for copy in arriving:
-            copy.wait()
-        pltpu.make_async_copy(heads_t.ref, heads_t.far[0], heads_t.sem).start()
+        if first:
+
+            @pl.when(section == 0)
+            def _():
+                for copy in arriving + over:
+                    copy.wait_send()
+                for copy in arriving:
+                    copy.wait_recv()
+
+            @pl.when(section == 1)
+            def _():
+                for copy in over:
+                    copy.wait_recv()
+
+        else:
+            for copy in arriving:
+                copy.wait()
+        heads_t.flush()
         keys.ref[...] = heads_t.ref[HEAD : 2 * HEAD, :].T
         for target in range(frames):
+            if target == frames - 1:
+                for task in early:
+                    task.first_hop()
             for start in range(target * rows, (target + 1) * rows, block):
                 reach = start + block
                 scores = masked_scores(
@@ -1251,9 +1462,10 @@
         out.ref[span(me, HEAD), :] = mixed_t.ref[me]
         for copy in leaving:
             copy.wait()
-        pltpu.make_async_copy(out.ref, out.far[0], out.sem).start()
-
-    return run_build(build, body, (FRAME,), collective_id, tasks)
+        out.flush()
+
+    kinds = (FRAME, SECTION, BOTH) if first else (FRAME,)
+    return run_build(build, body, kinds, collective_id, tasks)
 
 
 def self_backward(heads_t, grad_low, weight, begins, layer, collective_id, tasks):
@@ -1285,11 +1497,14 @@
         def project(other):
             return nt_product(weight.ref[span(other, HEAD), :], grad_low.ref[...]).astype(jnp.bfloat16)
 
+        need(0)
+        own.ref[partners[2]] = project(partners[2])
+        own.ref[partners[1]] = project(partners[1])
         meet()
-        need(0)
-        for k in (2, 1, 0):
-            own.ref[partners[k]] = project(partners[k])
-            arriving[k].start()
+        arriving[2].start()
+        arriving[1].start()
+        own.ref[partners[0]] = project(partners[0])
+        arriving[0].start()
         ride()
         grad_t.ref[:, span(me, rows)] = project(me)
         key_sum.ref[...] = jnp.zeros(key_sum.shape, jnp.float32)
@@ -1335,7 +1550,7 @@
         out.ref[span(me, width), :] = grads_t.ref[me]
         for copy in leaving:
             copy.wait()
-        pltpu.make_async_copy(out.ref, out.far[0], out.sem).start()
+        out.flush()
 
     return run_build(build, body, (FRAME,), collective_id, tasks)
 
@@ -1464,20 +1679,13 @@
         reduce_weight,
     ) = (w[0] for w in matrix_args)
     columns = query_weight.shape[1]
-    heads = columns // HEAD
 
     def by_section(first, second):
         return jnp.where(at_zero, first, second)
 
     own_vectors = jnp.pad(jnp.concatenate(vector_args, axis=0), ((0, 2), (0, 0)))
-    heads_weight = jnp.stack(
-        [w.T.reshape(heads, HEAD, model_width) for w in (query_weight, key_weight, value_weight)], axis=1
-    ).reshape(3 * columns, model_width)
-    _, (other_heads, other_vectors) = call(
-        None, [], [], [], (), 1, [WeightTask(heads_weight), CrossTask(own_vectors, own_vectors, False)]
-    )
-    vectors = [by_section(own_vectors, other_vectors), by_section(other_vectors, own_vectors)]
-    heads_pair = (heads_weight, other_heads)
+    self_weights = (query_weight, key_weight, value_weight)
+    normed = layer_norm(inputs.astype(jnp.float32), own_vectors[0], own_vectors[1]).astype(jnp.bfloat16)
     text_local = text.reshape(-1, model_width)
     text_states = jnp.concatenate(
         [matmul(text_local, cross_key), matmul(text_local, cross_value)], axis=1
@@ -1491,46 +1699,59 @@
     seg = lax.dynamic_slice_in_dim(seg, frame_index * rows_dev, rows_dev, 1)
 
     entering = inputs
-    normed = layer_norm(
-        lax.dynamic_index_in_dim(inputs, section, 0, keepdims=False).astype(jnp.float32),
-        vectors[0][0],
-        vectors[0][1],
-    ).astype(jnp.bfloat16)
     saved = []
     for layer in range(2):
-        gains, first = vectors[layer], layer == 0
+        first = layer == 0
         tasks = []
         if first:
-            tasks = [WeightTask(w) for w in (output_weight, cross_query, cross_output)]
-            tasks.append(TextTask(text_states))
+            early = [WeightTask(output_weight)]
+            early[0].hooked = 1
+            tasks = early + [CrossTask(own_vectors, own_vectors, False), TextTask(text_states)]
+            tasks += [QuarterTask(w) for w in (cross_query, cross_output, expand_weight)]
         (heads_t, attended_t), carried = self_forward(
-            normed, heads_pair, begins, layer, 2 + layer, tasks
+            normed,
+            self_weights if first else self_pairs,
+            begins,
+            layer,
+            2 + layer,
+            tasks,
+            early if first else [],
         )
+        if first:
+            vectors = [by_section(own_vectors, carried[1]), by_section(carried[1], own_vectors)]
+            normed = layer_norm(
+                lax.dynamic_index_in_dim(inputs, section, 0, keepdims=False).astype(jnp.float32),
+                vectors[0][0],
+                vectors[0][1],
+            ).astype(jnp.bfloat16)
+        gains = vectors[layer]
         tasks = []
         if first:
-            weights = list(zip((output_weight, cross_query, cross_output), carried))
-            states = carried[3].reshape(2, -1, 2 * columns)
-            (second_normed, middle, queries, cross_att, third_normed, latter), carried = forward_chain(
-                layer,
-                attended_t,
-                entering,
-                states[layer],
-                seg,
-                gains,
-                weights,
-                4,
-                [WeightTask(expand_weight), WeightTask(reduce_weight)],
-            )
-            weights += list(zip((expand_weight, reduce_weight), carried))
-            (before, hidden, next_normed, result_low), _ = feed_chain(
-                layer, third_normed, latter, weights, vectors[1], 5
-            )
-        else:
-            outs, _ = forward_chain(
-                layer, attended_t, entering, states[layer], seg, gains, weights, 6, []
-            )
-            second_normed, middle, queries, cross_att, third_normed, latter = outs[:6]
-            before, hidden, result_low = outs[6:]
+            states = carried[2].reshape(2, -1, 2 * columns)
+            others = (cross_query, cross_output, expand_weight, reduce_weight)
+            coming = [WeightTask(w, 0, q) for w, q in zip(others, carried[3:] + [None])]
+            late = [WeightTask(w) for w in self_weights]
+            for task in late:
+                task.hooked = 2
+            weights = [(output_weight, carried[0])]
+            tasks = coming + late
+        outs, carried = forward_chain(
+            layer,
+            attended_t,
+            entering,
+            states[layer],
+            seg,
+            gains,
+            vectors[1] if first else None,
+            weights + coming if first else weights,
+            4 + layer,
+            tasks,
+            late if first else [],
+        )
+        second_normed, middle, queries, cross_att, third_normed, latter, before, hidden = outs[:8]
+        if first:
+            weights += list(zip(others, carried))
+            self_pairs = list(zip(self_weights, carried[4:]))
         saved.append(
             (
                 entering,
@@ -1548,10 +1769,11 @@
             )
         )
         if first:
-            normed, entering = next_normed, result_low
-
-    upstream = cotangent
-    in_lows, vector_grads, shares = [None] * 2, [None] * 2, [{}, {}]
+            normed, entering = outs[8:]
+        else:
+            (result_low,) = outs[8:]
+
+    vector_grads, shares = [None] * 2, [{}, {}]
     totals = {}
 
     def low_product(left, right):
@@ -1560,91 +1782,82 @@
     def crossing(*names):
         return [CrossTask(shares[0][name], shares[1][name], True) for name in names]
 
-    for layer in (1, 0):
-        last = layer == 0
-        gains = vectors[layer]
-        (
-            entering,
-            normed,
-            heads_t,
-            attended_t,
-            middle,
-            second_normed,
-            latter,
-            third_normed,
-            queries,
-            cross_att,
-            before,
-            hidden,
-        ) = saved[layer]
-        tasks = [] if last else [BothTask(saved[1][0], result_low)]
-        (
-            grad_pre,
-            grad_cross,
-            third_gain_grad,
-            third_shift_grad,
-            grad_queries,
-            grad_states,
-            grad_self,
-            second_gain_grad,
-            second_shift_grad,
-        ), carried = backward_chain(
-            layer,
-            upstream,
-            before,
-            hidden,
-            third_normed,
-            latter,
-            queries,
-            states[layer],
-            seg,
-            middle,
-            gains,
-            weights,
-            8 + layer,
-            tasks,
-        )
-        shares[layer]["reduce"], shares[layer]["expand"] = carried[-2:]
-        if not last:
-            layer_outputs = carried[0]
-
-        tasks = [ShareTask(grad_states)] + (crossing("reduce", "expand") if last else [])
-        (grad_heads_t,), carried = self_backward(
-            heads_t, grad_self, weights[0], begins, layer, 10 + layer, tasks
-        )
-        shares[layer]["states"] = carried[0]
-        if last:
-            totals["reduce"], totals["expand"] = carried[1:]
-
-        tasks = [CrossTask(shares[0]["states"], shares[1]["states"], False)] if last else []
-        (in_lows[layer], first_gain_grad, first_shift_grad, *both_grads), carried = last_chain(
-            layer,
-            grad_heads_t,
-            entering,
-            gains[0],
-            grad_self,
-            heads_pair,
-            in_lows[1] if last else None,
-            [(cross_att, grad_cross), (attended_t, grad_self), (second_normed, grad_queries), (normed, None)],
-            12 + layer,
-            tasks,
-        )
-        names = ("cross_output", "output", "cross_query", "heads")
-        shares[layer].update(zip(names, carried[-4:]))
-        if last:
-            other_states = carried[0]
-        vector_grads[layer] = sum_rows(
-            [
-                first_gain_grad,
-                first_shift_grad,
-                second_gain_grad,
-                second_shift_grad,
-                third_gain_grad,
-                third_shift_grad,
-                jnp.zeros((2, model_width), jnp.float32),
-            ]
-        )
-        upstream = in_lows[layer]
+    def unpack(outs):
+        names = ("grad_pre", "grad_cross", "gain5", "shift5", "queries", "states", "grad_self", "gain3", "shift3")
+        return dict(zip(names, outs))
+
+    def for_backward(layer):
+        return saved[layer][4], *saved[layer][6:9], *saved[layer][10:]
+
+    def products(layer, outs):
+        attended_t, second_normed, cross_att = saved[layer][3], saved[layer][5], saved[layer][9]
+        return [
+            (cross_att, outs["grad_cross"]),
+            (attended_t, outs["grad_self"]),
+            (second_normed, outs["queries"]),
+            (saved[layer][1], None),
+        ]
+
+    def vector_rows(outs, first):
+        rows = first + [outs[name] for name in ("gain3", "shift3", "gain5", "shift5")]
+        return sum_rows(rows + [jnp.zeros((2, model_width), jnp.float32)])
+
+    names = ("cross_output", "output", "cross_query", "heads")
+    outs, carried = backward_chain(
+        1,
+        cotangent,
+        for_backward(1),
+        states[1],
+        seg,
+        vectors[1],
+        weights,
+        8,
+        [BothTask(saved[1][0], result_low)],
+    )
+    later = unpack(outs)
+    layer_outputs, shares[1]["reduce"], shares[1]["expand"] = carried
+    (grad_heads_t,), (shares[1]["states"],) = self_backward(
+        saved[1][2], later["grad_self"], weights[0], begins, 1, 9, [ShareTask(later["states"])]
+    )
+    outs, carried = between_chain(
+        1,
+        (grad_heads_t, saved[1][0], vectors[1][0], later["grad_self"], self_pairs),
+        products(1, later),
+        (for_backward(0), states[0], seg, vectors[0], weights),
+        10,
+        [],
+    )
+    later_low, first_vectors = outs[0], list(outs[1:3])
+    vector_grads[1] = vector_rows(later, first_vectors)
+    sooner = unpack(outs[3:])
+    shares[1].update(zip(names, carried))
+    shares[0]["reduce"], shares[0]["expand"] = carried[4:]
+    (grad_heads_t,), carried = self_backward(
+        saved[0][2],
+        sooner["grad_self"],
+        weights[0],
+        begins,
+        0,
+        11,
+        [ShareTask(sooner["states"])] + crossing("reduce", "expand"),
+    )
+    shares[0]["states"], totals["reduce"], totals["expand"] = carried
+    outs, carried = last_chain(
+        0,
+        grad_heads_t,
+        saved[0][0],
+        vectors[0][0],
+        sooner["grad_self"],
+        self_pairs,
+        spare=later_low,
+        products=products(0, sooner),
+        collective_id=12,
+        tasks=[CrossTask(shares[0]["states"], shares[1]["states"], False)],
+    )
+    both_grads = outs[3]
+    vector_grads[0] = vector_rows(sooner, list(outs[1:3]))
+    other_states = carried[0]
+    shares[0].update(zip(names, carried[1:]))
 
     own_states = by_section(shares[0]["states"], shares[1]["states"])
     text_rows = sum_rows([by_section(own_states, other_states), by_section(other_states, own_states)])
@@ -1669,9 +1882,7 @@
     vector_total = lax.dynamic_slice_in_dim(
         vector_total, frame_index * (model_width // 4), model_width // 4, 1
     )
-    grad_query, grad_key, grad_value = (
-        totals["heads"].reshape(-1, heads, 3, HEAD)[:, :, i].reshape(-1, columns) for i in range(3)
-    )
+    grad_query, grad_key, grad_value = jnp.split(totals["heads"], 3, axis=1)
     cross_grads = cross_grads.astype(jnp.float32)
 
     ordered = (
@@ -1692,7 +1903,7 @@
         totals["expand"],
         totals["reduce"],
     )
-    layer_outputs, input_grads = (a.astype(jnp.float32) for a in (layer_outputs, both_grads[0]))
+    layer_outputs, input_grads = (a.astype(jnp.float32) for a in (layer_outputs, both_grads))
     return (layer_outputs[None], input_grads[None], text_grad) + tuple(g[None] for g in ordered)
 
 

time: 608 us -> 565 us (0.929)
  Pallas kernels: 562 us -> 521 us
  local copies, waits for them, and re-layouts: 19.2 us -> 12.9 us
    pallas_call x13 -> x10, Pallas kernels: 562 us -> 521 us  [call(): pl.pallas_call(kernel, out_shape=all_outs, in_specs=in_specs, out_specs=o...]
where the time goes in v5:
time: 565 us; the launch traced here: 556 us
  Pallas kernels  521 us (92%)
  other arithmetic  17.7 us (3%)
  local copies, waits for them, and re-layouts  12.9 us (2%)
    pallas_call x10, Pallas kernels, call(): pl.pallas_call(kernel, out_shape=all_outs, in_specs=in_specs, out_specs=o...  521 us

profile of v5, /device:TPU:0, one launch (start us, length us, event | category | flops | bytes accessed | tf_op | source)
XLA Modules:
  0.0 556.4 jit_solution(15607704108134451384)
XLA Ops:
  0.7 0.0 copy-start
  0.7 0.0 copy-start.1
  0.7 0.8 fusion.24
  1.5 0.2 reduce-window.8
  1.7 0.7 convert_reduce_fusion.2
  2.4 2.0 convert_reduce_fusion
  4.4 0.7 fusion.2
  5.1 0.0 copy-done.17
  5.1 0.0 copy-start.3
  5.2 0.0 copy-start.6
  5.2 0.0 copy-start.19
  5.2 0.0 copy-start.20
  5.2 0.0 copy-start.21
  5.2 0.0 copy-start.22
  5.2 2.1 fusion.5.refs_0_
  7.4 0.2 convolution_convert_fusion.1
  7.6 0.2 convolution_convert_fusion.2
  7.8 0.7 pad_maximum_fusion.2.refs_8_
  8.5 0.0 copy-done.19
  8.5 0.0 copy-done.21
  8.5 0.1 concatenate.17
  8.6 0.6 pad.4.refs_6_.refs_7_
  9.2 43.8 %shard_map.339 = (bf16[192,2048]{1,0:T(8,128)(2,1)}, bf16[256,512]{1,0:T(8,128)(2,1)}, bf16[256,1024]{1,0:T(8,128)(2,1)}, f32[8,1024]{1,0:T(8,128)}, bf16[2,4,64...) custom-call(bf16[2,512,1024]{2,1,0:T(8,128)(2,1)} %fusion.5.refs_0_, ...), custom_call_target="tpu_custom_call" | custom-call | tf_op jit(solution)/shard_map/pallas_call | solution.py:616
  53.0 0.8 broadcast_select_fusion.3
  53.7 0.6 fusion.30
  54.4 1.9 fusion.28
  56.2 0.6 dynamic-slice.3
  56.8 87.3 %shard_map.340 = (bf16[512,1024]{1,0:T(8,128)(2,1)}, bf16[512,1024]{1,0:T(8,128)(2,1)}, bf16[512,256]{1,0:T(8,128)(2,1)}, bf16[512,256]{1,0:T(8,128)(2,1)}, bf16...) custom-call(bf16[2,512,1024]{2,1,0:T(8,128)(2,1)} %refs_8_.1, ...), custom_call_target="tpu_custom_call" | custom-call | tf_op jit(solution)/shard_map/pallas_call | solution.py:616
  144.2 24.0 %shard_map.341 = (bf16[192,2048]{1,0:T(8,128)(2,1)}, bf16[256,512]{1,0:T(8,128)(2,1)}) custom-call(bf16[512,1024]{1,0:T(8,128)(2,1)} %get-tuple-element.112.refs_0_.refs_15_, s32[1,2048]{1,0:T(1,128)} %bitcast.132, bf16[1024,256]{1,0:T(8,128)(2,1)} %bitcast.105, bf16[1024,256]{1,0:T(8,128)(2,1)} %get-tuple-element.113.refs_3_, bf16[1024,256]{1,0:T(8,128)(2,1)} %bitcast.110, ...), custom_call_target="tpu_custom_call" | custom-call | tf_op jit(solution)/shard_map/pallas_call | solution.py:616
  168.2 82.2 %shard_map.342 = (bf16[512,1024]{1,0:T(8,128)(2,1)}, bf16[512,1024]{1,0:T(8,128)(2,1)}, bf16[512,256]{1,0:T(8,128)(2,1)}, bf16[512,256]{1,0:T(8,128)(2,1)}, bf16...) custom-call(bf16[512,1024]{1,0:T(8,128)(2,1)} %get-tuple-element.111, ...), custom_call_target="tpu_custom_call" | custom-call | tf_op jit(solution)/shard_map/pallas_call | solution.py:616
  250.4 64.7 %shard_map.343 = (bf16[512,1024]{1,0:T(8,128)(2,1)}, bf16[512,1024]{1,0:T(8,128)(2,1)}, f32[1,1024]{1,0:T(1,128)}, f32[1,1024]{1,0:T(1,128)}, bf16[512,256]{1,0:...) custom-call(f32[2,512,1024]{2,1,0:T(8,128)} %refs_0_.3, ...), custom_call_target="tpu_custom_call" | custom-call | tf_op jit(solution)/shard_map/pallas_call | solution.py:616
  315.0 28.6 %shard_map.344 = (bf16[768,512]{1,0:T(8,128)(2,1)}, bf16[64,512]{1,0:T(8,128)(2,1)}) custom-call(bf16[192,2048]{1,0:T(8,128)(2,1)} %get-tuple-element.130.refs_0_, s32[1,2048]{1,0:T(1,128)} %bitcast.133, bf16[512,1024]{1,0:T(8,128)(2,1)} %get-tuple-element.129.refs_2_.refs_0_, bf16[256,1024]{1,0:T(8,128)(2,1)} %bitcast.101, ...), custom_call_target="tpu_custom_call" | custom-call | tf_op jit(solution)/shard_map/pallas_call | solution.py:616
  343.6 88.4 %shard_map.345 = (bf16[512,1024]{1,0:T(8,128)(2,1)}, f32[1,1024]{1,0:T(1,128)}, f32[1,1024]{1,0:T(1,128)}, bf16[512,1024]{1,0:T(8,128)(2,1)}, bf16[512,1024]{1,0...) custom-call(bf16[512,1024]{1,0:T(8,128)(2,1)} %get-tuple-element.129, ...), custom_call_target="tpu_custom_call" | custom-call | tf_op jit(solution)/shard_map/pallas_call | solution.py:616
  432.1 0.0 copy-start.2
  432.1 29.1 %shard_map.346 = (bf16[768,512]{1,0:T(8,128)(2,1)}, bf16[64,512]{1,0:T(8,128)(2,1)}, f32[256,1024]{1,0:T(8,128)}, f32[256,1024]{1,0:T(8,128)}) custom-call(bf16[192,2048]{1,0:T(8,128)(2,1)} %get-tuple-element.144.refs_0_, s32[1,2048]{1,0:T(1,128)} %bitcast.134, bf16[512,1024]{1,0:T(8,128)(2,1)} %get-tuple-element.143.refs_2_.refs_0_, ...), custom_call_target="tpu_custom_call" | custom-call | tf_op jit(solution)/shard_map/pallas_call | solution.py:616
  461.2 0.2 convert_reduce_fusion.1
  461.4 0.4 fusion.9
  461.8 0.0 copy-done.16
  461.8 1.4 fusion.12.refs_16_
  463.3 45.4 %shard_map.347 = (bf16[512,1024]{1,0:T(8,128)(2,1)}, f32[1,1024]{1,0:T(1,128)}, f32[1,1024]{1,0:T(1,128)}, bf16[2,512,1024]{2,1,0:T(8,128)(2,1)}, bf16[64,512]{1...) custom-call(bf16[512,1024]{1,0:T(8,128)(2,1)} %get-tuple-element.143, ...), custom_call_target="tpu_custom_call" | custom-call | tf_op jit(solution)/shard_map/pallas_call | solution.py:616
  508.7 0.9 broadcast_select_fusion
  509.6 1.5 fusion.13.refs_2_
  511.1 0.0 copy-done.30
  511.1 0.0 copy-done.31
  511.1 0.0 copy-done.32
  511.1 0.8 concatenate.20
  511.9 0.1 concatenate.21
  511.9 0.6 pad_maximum_fusion.3.refs_1_
  512.6 0.3 fusion.18
  512.9 1.0 fusion.14.refs_0_
  513.9 27.9 %shard_map.348 = (bf16[128,1024]{1,0:T(8,128)(2,1)}, f32[8,1024]{1,0:T(8,128)}, bf16[256,512]{1,0:T(8,128)(2,1)}, f32[64,1024]{1,0:T(8,128)}, f32[64,1024]{1,0:T...) custom-call(bf16[128,1024]{1,0:T(8,128)(2,1)} %fusion.14.refs_0_, f32[2,8,1024]{2,1,0:T(8,128)} %pad_maximum_fusion.3.refs_1_, ...), custom_call_target="tpu_custom_call" | custom-call | tf_op jit(solution)/shard_map/pallas_call | solution.py:616
  541.8 1.1 convert_element_type.45
  543.0 0.8 slice_bitcast_fusion
  543.8 0.0 copy-done.9
  543.8 0.9 slice_bitcast_fusion.2
  544.7 0.8 convert.13
  545.5 1.6 fusion.29
  547.1 2.5 bitcast_convert_fusion
  549.6 2.5 bitcast_convert_fusion.1
  552.1 0.7 copy.47
  552.8 0.7 copy.48
  553.5 0.7 copy.49
  554.2 1.0 copy.50
  555.2 1.0 copy.51
  (54 shorter events, 0.1 us)
Async XLA Ops:
  0.7 6.9 %copy-start = (bf16[1,1024,256]{2,1,0:T(8,128)(2,1)S(1)}, bf16[1,1024,256]{2,1,0:T(8,128)(2,1)}, u32[]{:S(2)}) copy-start(bf16[1,1024,256]{2,1,0:T(8,128)(2,1)} %param.33) | copy-start | bytes 1572868
  0.7 3.7 copy-start.1
  2.4 2.7 copy-start.17
  2.4 2.7 copy-start.18
  5.1 2.2 copy-start.3
  5.2 2.2 copy-start.6
  5.2 3.4 copy-start.19
  5.2 3.3 copy-start.20
  5.2 3.3 copy-start.21
  5.2 3.3 copy-start.22
  54.4 407.4 %copy-start.16 = (f32[1,1024]{1,0:T(1,128)}, f32[1,1024]{1,0:T(1,128)S(1)}, u32[]{:S(2)}) copy-start(f32[1,1024]{1,0:T(1,128)S(1)} %get-tuple-element.209.refs_9_) | copy-start | bytes 12292
  432.1 29.1 %copy-start.2 = (bf16[2,512,1024]{2,1,0:T(8,128)(2,1)S(1)}, bf16[2,512,1024]{2,1,0:T(8,128)(2,1)}, u32[]{:S(2)}) copy-start(bf16[2,512,1024]{2,1,0:T(8,128)(2,1)} %refs_8_.1) | copy-start | bytes 6291460
  463.3 45.5 %copy-start.10 = (bf16[64,512]{1,0:T(8,128)(2,1)S(1)}, bf16[64,512]{1,0:T(8,128)(2,1)}, u32[]{:S(2)}) copy-start(bf16[64,512]{1,0:T(8,128)(2,1)} %get-tuple-element.157.refs_18_) | copy-start | bytes 196612
  463.3 45.5 %copy-start.11 = (bf16[64,512]{1,0:T(8,128)(2,1)S(1)}, bf16[64,512]{1,0:T(8,128)(2,1)}, u32[]{:S(2)}) copy-start(bf16[64,512]{1,0:T(8,128)(2,1)} %get-tuple-element.156.refs_17_) | copy-start | bytes 196612
  463.3 47.8 %copy-start.29 = (f32[1,1024]{1,0:T(1,128)S(1)}, f32[1,1024]{1,0:T(1,128)}, u32[]{:S(2)}) copy-start(f32[1,1024]{1,0:T(1,128)} %get-tuple-element.164) | copy-start | bytes 12292
  463.3 47.8 %copy-start.30 = (f32[1,1024]{1,0:T(1,128)S(1)}, f32[1,1024]{1,0:T(1,128)}, u32[]{:S(2)}) copy-start(f32[1,1024]{1,0:T(1,128)} %get-tuple-element.165) | copy-start | bytes 12292
  463.3 47.8 %copy-start.31 = (f32[1,1024]{1,0:T(1,128)S(1)}, f32[1,1024]{1,0:T(1,128)}, u32[]{:S(2)}) copy-start(f32[1,1024]{1,0:T(1,128)} %get-tuple-element.162) | copy-start | bytes 12292
  463.3 47.8 %copy-start.32 = (f32[1,1024]{1,0:T(1,128)S(1)}, f32[1,1024]{1,0:T(1,128)}, u32[]{:S(2)}) copy-start(f32[1,1024]{1,0:T(1,128)} %get-tuple-element.163) | copy-start | bytes 12292
  463.3 48.5 %copy-start.23 = (f32[1,1024]{1,0:T(1,128)S(1)}, f32[1,1024]{1,0:T(1,128)}, u32[]{:S(2)}) copy-start(f32[1,1024]{1,0:T(1,128)} %get-tuple-element.170) | copy-start | bytes 12292
  463.3 48.5 %copy-start.24 = (f32[1,1024]{1,0:T(1,128)S(1)}, f32[1,1024]{1,0:T(1,128)}, u32[]{:S(2)}) copy-start(f32[1,1024]{1,0:T(1,128)} %get-tuple-element.171) | copy-start | bytes 12292
  463.3 48.5 %copy-start.25 = (f32[1,1024]{1,0:T(1,128)S(1)}, f32[1,1024]{1,0:T(1,128)}, u32[]{:S(2)}) copy-start(f32[1,1024]{1,0:T(1,128)} %get-tuple-element.168) | copy-start | bytes 12292
  463.3 48.5 %copy-start.26 = (f32[1,1024]{1,0:T(1,128)S(1)}, f32[1,1024]{1,0:T(1,128)}, u32[]{:S(2)}) copy-start(f32[1,1024]{1,0:T(1,128)} %get-tuple-element.169) | copy-start | bytes 12292
  463.3 48.5 %copy-start.27 = (f32[1,1024]{1,0:T(1,128)S(1)}, f32[1,1024]{1,0:T(1,128)}, u32[]{:S(2)}) copy-start(f32[1,1024]{1,0:T(1,128)} %get-tuple-element.166) | copy-start | bytes 12292
  463.3 48.5 %copy-start.28 = (f32[1,1024]{1,0:T(1,128)S(1)}, f32[1,1024]{1,0:T(1,128)}, u32[]{:S(2)}) copy-start(f32[1,1024]{1,0:T(1,128)} %get-tuple-element.167) | copy-start | bytes 12292
  541.8 2.0 copy-start.9
  541.8 2.9 copy-start.12
  541.8 5.3 copy-start.5
  547.1 2.5 copy-start.4
  549.6 2.5 copy-start.15
  549.6 3.2 copy-start.14
  549.6 3.9 copy-start.13
  549.6 4.6 copy-start.8
  552.1 3.1 copy-start.7

commit v6 on v5

--- a/solution.py
+++ b/solution.py
@@ -38,6 +38,7 @@
 
     def bind(self, ins, outs, scratch):
         self.ins, self.out, self.room = ins, outs, scratch
+        self.far_ins = ins
 
 
 def remote(source, landing, send_sem, recv_sem, target):
@@ -213,7 +214,7 @@
                 )
             )
             if self.far:
-                own, sems = here
+                own, sems = here[:2]
                 source = self.ins[0].at[span(kept, self.share)]
                 copies.append(pltpu.make_async_copy(source, own.at[k], sems.at[k]))
         return copies
@@ -249,6 +250,112 @@
             self.out[0][...] = total.astype(jnp.bfloat16)
 
         return [end]
+
+
+class ShareCrossTask(ShareTask):
+    greets = (FRAME, SECTION)
+    late = True
+
+    def __init__(self, grad, later):
+        super().__init__(grad)
+        self.operands = (later,)
+        self.base = len(self.scratch)
+        self.outs = (jax.ShapeDtypeStruct(later.shape, jnp.float32),)
+        self.scratch += (pltpu.VMEM((3,) + later.shape, jnp.bfloat16), pltpu.SemaphoreType.DMA((3,)))
+
+    def crossing(self, which):
+        parts, sems = self.room[self.base :]
+        target = {SECTION: 1 - lax.axis_index(SECTION)}
+        later = self.far_ins[0]
+        over = remote(parts.at[0] if which else later, parts.at[1], sems.at[0], sems.at[1], target)
+        return over, pltpu.make_async_copy(later, parts.at[2], sems.at[2])
+
+    def steps(self):
+        parts = self.room[self.base]
+        section = lax.axis_index(SECTION)
+
+        def send():
+            self.over().wait()
+            total = self.chip_sum(1) + self.room[1][1].astype(jnp.float32)
+            parts[0] = total.astype(jnp.bfloat16)
+            for which in (0, 1):
+
+                @pl.when(section == which)
+                def _():
+                    over, stay = self.crossing(which)
+                    over.start()
+                    if which:
+                        stay.start()
+
+        def end():
+            over, stay = self.crossing(1)
+            over.wait()
+            came = parts[1].astype(jnp.float32)
+
+            @pl.when(section == 0)
+            def _():
+                self.out[0][...] = parts[0].astype(jnp.float32) + came
+
+            @pl.when(section == 1)
+            def _():
+                stay.wait()
+                self.out[0][...] = parts[2].astype(jnp.float32) + came
+
+        return [send, lambda: None, lambda: None, end]
+
+
+class StatesTask(ShareTask):
+    greets = (FRAME, SECTION)
+    out_in_vmem = True
+
+    def __init__(self, grad, later):
+        super().__init__(grad)
+        self.operands = (grad, later)
+        self.base = len(self.scratch)
+        self.outs = ()
+        shape = (2,) + later.shape
+        self.scratch += (pltpu.VMEM(shape, jnp.bfloat16), pltpu.VMEM(later.shape, jnp.bfloat16))
+        self.scratch += (pltpu.SemaphoreType.DMA((3,)),)
+
+    @property
+    def both(self):
+        return self.room[self.base]
+
+    def crossing(self, which):
+        both, total, sems = self.room[self.base :]
+        later, place = self.ins[1], both.at[which]
+        over = remote(total if which else later, place, sems.at[0], sems.at[1], {SECTION: 1 - which})
+        return over, pltpu.make_async_copy(later, place, sems.at[2])
+
+    def cross(self):
+        self.over().wait()
+        both, total, _ = self.room[self.base :]
+        total[...] = (self.chip_sum(1) + self.room[1][1].astype(jnp.float32)).astype(jnp.bfloat16)
+        section = lax.axis_index(SECTION)
+        for which in (0, 1):
+
+            @pl.when(section == which)
+            def _():
+                over, stay = self.crossing(which)
+                over.start()
+                if which:
+                    stay.start()
+                else:
+                    both[0] = total[...]
+
+    def arrive(self):
+        section = lax.axis_index(SECTION)
+        for which in (0, 1):
+
+            @pl.when(section == which)
+            def _():
+                over, stay = self.crossing(which)
+                over.wait()
+                if which:
+                    stay.wait()
+
+    def steps(self):
+        return []
 
 
 class BothTask(Task):
@@ -332,10 +439,10 @@
 class TextTask(Task):
     out_in_vmem = False
     greets = (SECTION, FRAME)
+    late = True
 
     def __init__(self, states):
         micros, rows, width = states.shape
-        self.operands = (states,)
         self.outs = (jax.ShapeDtypeStruct((2, 4, rows, width), states.dtype),)
         self.scratch = (pltpu.SemaphoreType.DMA((3,)),) + (pltpu.SemaphoreType.DMA((2, 3)),) * 2
 
@@ -383,10 +490,11 @@
 class TotalTask(Task):
     greets = (SECTION, LINE)
 
+    late = True
+
     def __init__(self, part):
         rows, width = part.shape
         self.share = rows // 4
-        self.operands = (part,)
         self.outs = (jax.ShapeDtypeStruct((rows, width), jnp.bfloat16),)
         piece = (self.share, width)
         self.scratch = (
@@ -436,17 +544,18 @@
         for copy in self.spread():
             copy.start()
 
+    def sum_first(self):
+        landing, sums = self.room[:2]
+        for copy in self.spread():
+            copy.wait()
+        total = landing[0].astype(jnp.float32)
+        for by in (1, 2, 3):
+            total = total + landing[by].astype(jnp.float32)
+        sums[0] = total.astype(jnp.bfloat16)
+        self.over().start()
+
     def steps(self):
-        landing, sums = self.room[:2]
-
-        def first():
-            for copy in self.spread():
-                copy.wait()
-            total = landing[0].astype(jnp.float32)
-            for by in (1, 2, 3):
-                total = total + landing[by].astype(jnp.float32)
-            sums[0] = total.astype(jnp.bfloat16)
-            self.over().start()
+        sums = self.room[1]
 
         def second():
             self.over().wait()
@@ -459,14 +568,14 @@
             for copy in self.gather():
                 copy.wait()
 
-        return [first, second, third]
+        return [second, third]
 
 
 class VectorTask(Task):
     greets = (SECTION, FRAME)
+    late = True
 
     def __init__(self, grads):
-        self.operands = (grads,)
         shape = grads.shape[1:]
         self.outs = (jax.ShapeDtypeStruct(shape, jnp.float32),)
         self.scratch = (
@@ -687,7 +796,7 @@
 
 class Build:
     def __init__(self):
-        self.helds, self.rooms, self.extras = [], [], []
+        self.helds, self.extras, self.starts, self.finals = [], [], [], []
 
     def add(self, held):
         self.helds.append(held)
@@ -714,18 +823,18 @@
 class Stage:
     def __init__(self, rows, width):
         self.rows, self.width = rows, width
-        self.begin = self.prepare = self.finish = None
+        self.begin = self.prepare = self.finish = self.after = None
         self.ends = []
 
 
 class Chore:
-    def __init__(self, build, stage, piece, each, left, right, flipped=False):
-        self.start, self.each = (stage, piece), each
+    def __init__(self, build, stage, piece, each, left, right, flipped=False, later=None, wait=5):
+        self.start, self.each, self.wait = (stage, piece), each, wait
         self.left, self.right, self.flipped = left, right, flipped
         columns = left.shape[0] if flipped else left.shape[1]
         self.units = columns // BLOCK
         self.product = build.temp((columns, right.shape[1]), jnp.bfloat16)
-        self.task = ShareTask(self.product)
+        self.task = ShareTask(self.product) if later is None else ShareCrossTask(self.product, later)
         self.task.late = True
 
     def unit(self, number):
@@ -762,7 +871,7 @@
 
         at_step(0, steps, make)
         at_step(steps, steps + 1, begin)
-        at_step(steps + 5, steps + 6, lambda now: self.task.middle())
+        at_step(steps + self.wait, steps + self.wait + 1, lambda now: self.task.middle())
 
 
 def line_chain(stages, need, part, set_out, middle, chores, hooks):
@@ -803,6 +912,14 @@
                 def _():
                     run()
 
+    def finish(stage, piece):
+        stage.finish(span(piece, step), piece)
+        if stage.after is not None:
+
+            @pl.when(lax.rem(piece, per_block) == per_block - 1)
+            def _():
+                stage.after(lax.div(piece, per_block))
+
     def open_stage(index):
         need(index)
         if stages[index].begin is not None:
@@ -821,14 +938,13 @@
 
     @pl.when(is_end)
     def _():
-        def give(stage, piece):
-            inwards(stage, piece).start()
+        def beside(stage, piece):
             chore(stage, piece)
             hook(stage, piece, True)
 
         def take(stage, piece):
             outwards(stage, piece).wait_recv()
-            stage.finish(span(piece, step), piece)
+            finish(stage, piece)
 
         for index, stage in enumerate(stages):
             open_stage(index)
@@ -840,7 +956,8 @@
                 stage.room[0][span(block, per_block * step), :] = stage.prepare(block).astype(jnp.bfloat16)
                 if index == 0:
                     pl.when(block == 0)(set_out)
-                loop(low, high, lambda piece: give(stage, piece))
+                loop(low, high, lambda piece: inwards(stage, piece).start())
+                loop(low, high, lambda piece: beside(stage, piece))
                 if index == 0:
 
                     @pl.when(block == 1)
@@ -882,7 +999,7 @@
             total = send[at, :].astype(jnp.float32) + across[at, :].astype(jnp.float32)
             held[at, :] = total.astype(jnp.bfloat16)
             outwards(stage, piece).start()
-            stage.finish(at, piece)
+            finish(stage, piece)
 
         for index, stage in enumerate(stages):
             open_stage(index)
@@ -943,9 +1060,13 @@
         build.bound = scratch[n_held:-1]
         for held in reads:
             held.start_in()
+        for start in build.starts:
+            start()
         body(need, meet, ride, middle)
 
     def end():
+        for final in build.finals:
+            final()
         for held in build.helds:
             if held.kept:
                 held.drain()
@@ -953,7 +1074,9 @@
     return call(run, operands, outs, scratch, kinds, collective_id, tasks, in_vmem=False, end=end)
 
 
-def run_chain(build, stages, collective_id, tasks, kinds=(LINE_ONLY,), chores=(), hooks=()):
+def run_chain(
+    build, stages, collective_id, tasks, kinds=(LINE_ONLY,), chores=(), hooks=(), then=None, first=None, ahead=0, last=()
+):
     slots = []
     for stage in stages:
         pieces = chunking(stage.rows)
@@ -969,19 +1092,32 @@
             meet()
             ride()
 
-        line_chain(stages, need, build.bound[part], set_out, middle, chores, hooks)
-
-    tasks = list(tasks) + [one.task for one in chores]
+        def nothing():
+            pass
+
+        go_on = middle
+        if first is not None:
+            first(need, meet, ride, middle)
+            set_out = go_on = nothing
+        line_chain(
+            stages, lambda index: need(index + ahead), build.bound[part], set_out, go_on, chores, hooks
+        )
+        if then is not None:
+            then(need)
+
+    tasks = list(tasks) + [one.task for one in chores] + list(last)
     return run_build(build, body, kinds, collective_id, tasks)
 
 
-def residual_norm(build, index, stage, base, gain, shift, mode):
+def scaled_rows(standard, gains, row):
+    return (standard * gains.ref[row : row + 1] + gains.ref[row + 1 : row + 2]).astype(jnp.bfloat16)
+
+
+def residual_norm(build, stage, base, gains, row, mode):
     shape = (stage.rows, stage.width)
     result = build.temp(shape, jnp.float32) if mode == NORM else None
     normed = build.out(shape, jnp.bfloat16) if mode != END else None
     low = build.out(shape, jnp.bfloat16)
-    if mode != END:
-        gain, shift = build.arg(gain[None], index), build.arg(shift[None], index)
 
     def finish(at, piece):
         value = base.ref[at, :].astype(jnp.float32) + stage.room[1][at, :].astype(jnp.float32)
@@ -993,10 +1129,27 @@
             value = rounded.astype(jnp.float32)
         if mode != END:
             standard, _ = norm_parts(value)
-            normed.write(at, (standard * gain.ref[...] + shift.ref[...]).astype(jnp.bfloat16))
+            normed.write(at, scaled_rows(standard, gains, row))
 
     stage.finish = finish
     return result, normed
+
+
+def gain_rows(build, vectors, layer, index):
+    if isinstance(vectors, tuple):
+        return build.pick(vectors, layer, index)
+    return build.arg(vectors, index)
+
+
+def vector_rows(build, width):
+    grads = build.out((8, width), jnp.float32)
+
+    def clear():
+        grads.ref[...] = jnp.zeros(grads.shape, jnp.float32)
+
+    build.starts.append(clear)
+    build.finals.append(grads.flush)
+    return grads
 
 
 def self_out_stage(build, index, layer, attended_t, weight, base):
@@ -1081,15 +1234,12 @@
     return stage
 
 
-def norm_backward(build, index, stage, value, gain, upstream, feeds, spare=None):
+def norm_backward(build, index, stage, value, gains, row, grads, upstream, feeds, spare=None):
     shape = (stage.rows, stage.width)
     pieces = chunking(stage.rows)
-    vector = (1, stage.width)
-    by_section = BY_SECTION if value.ndim == 3 else None
-    value, gain = build.arg(value, index, by_section), build.arg(gain[None], index)
+    value = build.arg(value, index, BY_SECTION if value.ndim == 3 else None)
     result = build.temp(shape, jnp.float32) if feeds else None
     low = build.out(shape, jnp.bfloat16)
-    gain_grad, shift_grad = build.out(vector, jnp.float32), build.out(vector, jnp.float32)
     parts = build.extra(pltpu.VMEM((2, pieces, 1, stage.width), jnp.float32))
     if spare is not None:
         spare = build.arg(spare, index)
@@ -1105,7 +1255,7 @@
     def finish(at, piece):
         grad = stage.room[1][at, :].astype(jnp.float32)
         standard, inverse = norm_parts(value.ref[at, :].astype(jnp.float32))
-        scaled = grad * gain.ref[...]
+        scaled = grad * gains.ref[row : row + 1]
         through = inverse * (
             scaled
             - jnp.mean(scaled, axis=-1, keepdims=True)
@@ -1131,20 +1281,20 @@
                 over(at, piece, low).start()
 
     def end():
-        whole = slice(0, 1)
-        gain_grad.write(whole, jnp.sum(build.bound[parts][0], axis=0))
-        shift_grad.write(whole, jnp.sum(build.bound[parts][1], axis=0))
-        if spare is not None:
-            step = stage.rows // pieces
-
-            def one(piece, carry):
-                over(span(piece, step), piece, low).wait()
-                return carry
-
-            lax.fori_loop(0, pieces, one, 0)
-            both.flush()
-
-    stage.finish = finish
+        grads.ref[row : row + 1] = jnp.sum(build.bound[parts][0], axis=0)
+        grads.ref[row + 1 : row + 2] = jnp.sum(build.bound[parts][1], axis=0)
+
+    def settle():
+        def one(piece, carry):
+            over(span(piece, stage.rows // pieces), piece, low).wait()
+            return carry
+
+        lax.fori_loop(0, pieces, one, 0)
+        both.flush()
+
+    if spare is not None:
+        build.finals.append(settle)
+    stage.finish, stage.value = finish, value
     stage.ends.append(end)
     return result, low
 
@@ -1213,7 +1363,7 @@
     def end():
         state_grads.write(slice(0, states.shape[0]), sums.ref[...].astype(jnp.bfloat16))
 
-    stage.begin, stage.prepare = begin, prepare
+    stage.begin, stage.prepare, stage.state_grads = begin, prepare, state_grads
     stage.ends.append(end)
     return stage
 
@@ -1222,7 +1372,7 @@
     columns, rows = grads_t.shape
     stage = Stage(rows, width)
     part = columns // 3
-    flipped = build.arg(grads_t, index)
+    flipped = grads_t if isinstance(grads_t, Held) else build.arg(grads_t, index)
     matrices = [build.pick(weight, layer, index) for weight in weights]
     left = build.temp((rows, columns), jnp.bfloat16)
 
@@ -1247,27 +1397,29 @@
 
 
 def forward_chain(
-    layer, attended_t, entering, states, seg, gains, after, weights, collective_id, tasks, late
+    layer, attended_t, entering, states, seg, vectors, weights, collective_id, tasks=(), late=None, begins=None
 ):
     output, query, cross, expand, reduce = weights
     build = Build()
+    gains = build.pick(vectors, layer, 0)
     base = build.arg(entering, 0, BY_SECTION if entering.ndim == 3 else None)
     first = self_out_stage(build, 0, layer, attended_t, output, base)
-    middle, second_normed = residual_norm(build, 0, first, base, gains[2], gains[3], NORM)
+    middle, second_normed = residual_norm(build, first, base, gains, 2, NORM)
     second = cross_stage(build, 1, layer, second_normed, states, seg, query, cross)
-    latter, third_normed = residual_norm(build, 1, second, middle, gains[4], gains[5], NORM)
+    latter, third_normed = residual_norm(build, second, middle, gains, 4, NORM)
     third = feed_stage(build, 2, layer, third_normed, expand, reduce)
-    mode = END if after is None else NEXT
-    residual_norm(build, 2, third, latter, *((None, None) if after is None else after[:2]), mode)
-    hooks = []
+    after = None if late is None else build.pick(vectors, 1 - layer, 2)
+    _, next_normed = residual_norm(build, third, latter, after, 0, END if late is None else NEXT)
+    hooks, then, kinds = [], None, (LINE_ONLY,)
     if isinstance(expand, WeightTask):
         hooks = [
-            (expand.second_hop, (1, 4), (0, 15)),
-            (reduce.first_hop, (1, 0), (0, 10)),
-            (reduce.second_hop, (1, 15), (1, 8)),
+            (expand.first_hop, (1, 0), (0, 9)),
+            (reduce.first_hop, (1, 5), (1, 0)),
+            (expand.second_hop, (1, 9), (1, 2)),
+            (reduce.second_hop, (1, 15), (1, 9)),
         ]
         for one in late:
-            hooks += [(one.first_hop, (2, 0), (1, 8)), (one.second_hop, (2, 10), (2, 4))]
+            hooks += [(one.first_hop, (2, 0), (1, 8)), (one.second_hop, (2, 8), (2, 0))]
         start_second = second.begin
 
         def begin_second():
@@ -1282,57 +1434,204 @@
             reduce.arrive()
 
         second.begin, third.begin = begin_second, begin_third
-    return run_chain(build, [first, second, third], collective_id, tasks, hooks=hooks)
-
-
-def add_backward(build, index, layer, arriving, saved, states, seg, gains, weights):
+        attention = Attention(build, third.rows, begins, 2)
+        sender = BlockSender(build, third.rows, 3 * HEAD, attention.heads_t)
+
+        def project(block):
+            @pl.when(block == 0)
+            def _():
+                for one in late:
+                    one.arrive()
+
+            lanes = span(block, BLOCK)
+            turned_parts(next_normed.ref[lanes, :], late, sender.own, (), lanes)
+            sender.send(block)
+
+        def then(need):
+            sender.wait()
+            attention.run()
+
+        third.after = project
+        kinds = (LINE_ONLY, FRAME)
+    return run_chain(build, [first, second, third], collective_id, tasks, kinds, hooks=hooks, then=then)
+
+
+def add_backward(build, index, layer, arriving, saved, states, seg, vectors, weights):
     _, query, cross, expand, reduce = weights
     middle, latter, third_normed, queries, before, hidden = saved
+    gains, grads = gain_rows(build, vectors, layer, index), vector_rows(build, arriving.shape[1])
     first = feed_back_stage(build, index, layer, arriving, before, reduce, expand)
-    grad_latter, grad_cross = norm_backward(build, index, first, latter, gains[4], arriving, True)
+    grad_latter, grad_cross = norm_backward(build, index, first, latter, gains, 4, grads, arriving, True)
     second = cross_back_stage(build, index + 1, layer, grad_cross, queries, states, seg, cross, query)
-    norm_backward(build, index + 1, second, middle, gains[2], grad_latter, False)
-    first_piece, each = (12, 2) if index else (0, 1)
+    _, grad_self = norm_backward(
+        build, index + 1, second, middle, gains, 2, grads, grad_latter, False
+    )
+    first_piece, each, wait = (12, 4, 3) if index else (0, 1, 5)
     chores = [
-        Chore(build, index, first_piece, each, build.arg(hidden, index), arriving),
-        Chore(build, index + 1, 0, each, build.arg(third_normed, index + 1), first.left),
+        Chore(build, index, first_piece, each, build.arg(hidden, index), arriving, wait=wait),
+        Chore(build, index + 1, 0, each, build.arg(third_normed, index + 1), first.left, wait=wait),
     ]
-    return [first, second], chores
-
-
-def add_last(build, layer, grads_t, entering, gain, upstream, weights, spare, products):
-    residual = build.arg(upstream, 0)
-    stage = self_in_stage(build, 0, layer, grads_t, weights, upstream.shape[1])
-    _, low = norm_backward(build, 0, stage, entering, gain, residual, False, spare)
+    return [first, second], chores, grad_self, second.state_grads
+
+
+def add_last(
+    build, index, layer, grads_t, entering, vectors, grads, residual, weights, spare, products, later=None
+):
+    stage = self_in_stage(build, index, layer, grads_t, weights, residual.shape[1])
+    stage.gains = gain_rows(build, vectors, layer, index)
+    _, low = norm_backward(build, index, stage, entering, stage.gains, 0, grads, residual, False, spare)
     chores = []
-    for left, right in products:
-        flipped = left.shape[0] != upstream.shape[0]
+    for number, (left, right) in enumerate(products):
+        flipped = left is not None and left.shape[0] != residual.shape[0]
         if right is None:
             right = stage.left
+        elif right is not residual:
+            right = build.arg(right, index)
+        more = None if later is None else later[number]
+        if left is None:
+            stage.normed = build.temp(residual.shape, jnp.bfloat16)
+            chores.append(Chore(build, 0, 3, 1, stage.normed, right, False, more, 4))
         else:
-            right = residual if right is upstream else build.arg(right, 0)
-        chores.append(Chore(build, 0, 0, 1, build.arg(left, 0), right, flipped))
+            chores.append(Chore(build, 0, 0, 1, build.arg(left, index), right, flipped, more))
     return stage, low, chores
 
 
-def backward_chain(layer, upstream, saved, states, seg, gains, weights, collective_id, tasks):
+def backward_chain(layer, upstream, saved, states, seg, vectors, weights, heads_t, begins, collective_id, tasks):
     build = Build()
     arriving = build.arg(upstream, 0, BY_SECTION)
-    stages, chores = add_backward(build, 0, layer, arriving, saved, states, seg, gains, weights)
-    return run_chain(build, stages, collective_id, tasks, chores=chores)
-
-
-def last_chain(layer, *rest, spare, products, collective_id, tasks):
+    stages, chores, grad_self, grad_states = add_backward(
+        build, 0, layer, arriving, saved, states, seg, vectors, weights
+    )
+    output = build.pick(weights[0], layer, 1)
+    attention = AttentionBack(build, stages[1].rows, heads_t, begins, 1)
+    sender = BlockSender(build, stages[1].rows, HEAD, attention.grad_t)
+    share = ShareTask(grad_states)
+    share.late = True
+
+    def project(block):
+        lanes = span(block, BLOCK)
+        turned_grads(grad_self.ref[lanes, :], output, sender.own, lanes)
+        sender.send(block)
+
+    def then(need):
+        share.ins = [grad_states.ref]
+        share.begin()
+        attention.begin()
+        sender.wait()
+        attention.run(share.middle)
+
+    stages[1].after = project
+    kinds = (LINE_ONLY, FRAME)
+    return run_chain(build, stages, collective_id, tasks + [share], kinds, chores, then=then)
+
+
+def between_chain(layer, grads_t, entering, vectors, upstream, weights, products, backward, collective_id, tasks):
     build = Build()
-    stage, _, chores = add_last(build, layer, *rest, spare, products)
-    return run_chain(build, [stage], collective_id, tasks, (LINE_ONLY, SECTION), chores)
-
-
-def between_chain(layer, last, products, backward, collective_id, tasks):
+    residual = build.arg(upstream, 0)
+    products = [(left, residual if right is upstream else right) for left, right in products]
+    grads = vector_rows(build, residual.shape[1])
+    stage, low, chores = add_last(
+        build, 0, layer, grads_t, entering, vectors, grads, residual, weights, None, products
+    )
+    stages, more, _, _ = add_backward(build, 1, layer - 1, low, *backward)
+    return run_chain(build, [stage] + stages, collective_id, tasks, chores=chores + more)
+
+
+def last_kernel(
+    heads_t,
+    grad_self,
+    output,
+    begins,
+    inputs,
+    vectors,
+    weights,
+    spare,
+    products,
+    later,
+    states,
+    text_local,
+    text_weights,
+    vector_grads,
+    collective_id,
+    tasks,
+):
+    rows, width = grad_self.shape
     build = Build()
-    stage, low, chores = add_last(build, layer, *last, None, products)
-    stages, more = add_backward(build, 1, layer - 1, low, *backward)
-    return run_chain(build, [stage] + stages, collective_id, tasks, chores=chores + more)
+    attention = AttentionBack(build, rows, heads_t, begins, 1)
+    grad_low, output = build.arg(grad_self, 0), build.pick(output, 0, 0)
+    own = build.temp((4, HEAD, rows), jnp.bfloat16)
+    sems = build.extra(pltpu.SemaphoreType.DMA((2, 3)))
+    products = [(left, grad_low if right is grad_self else right) for left, right in products]
+    vector_grads = [build.arg(grads, 2) for grads in vector_grads]
+    stage, _, chores = add_last(
+        build, 2, 0, attention.out, inputs, vectors, vector_grads[1], grad_low, weights, spare, products, later
+    )
+    text_local = build.arg(text_local, 2)
+    text_weights = [build.arg(weight, 2) for weight in text_weights]
+    columns = text_weights[0].shape[1]
+    text_rows = build.temp((text_local.shape[0], 2 * columns), jnp.bfloat16)
+    text_part = build.temp(text_local.shape, jnp.bfloat16)
+    both_grads = build.temp((2, 8, width), jnp.float32)
+    chores.append(Chore(build, 0, 10, 2, text_local, text_rows, wait=1))
+    from_states, from_vectors, from_text = StatesTask(*states), VectorTask(both_grads), TotalTask(text_part)
+
+    def make_normed():
+        def one(number, carry):
+            at = span(number, BLOCK)
+            standard, _ = norm_parts(stage.value.ref[at, :].astype(jnp.float32))
+            stage.normed.ref[at, :] = scaled_rows(standard, stage.gains, 0)
+            return carry
+
+        lax.fori_loop(0, rows // BLOCK, one, 0)
+
+    def text_step():
+        from_states.arrive()
+        text_rows.ref[...] = jnp.concatenate([from_states.both[0], from_states.both[1]], axis=0)
+        total = nt_product(text_rows.ref[:, :columns], text_weights[0].ref[...])
+        total = total + nt_product(text_rows.ref[:, columns:], text_weights[1].ref[...])
+        text_part.ref[...] = total.astype(jnp.bfloat16)
+        from_text.ins = [text_part.ref]
+        from_text.begin()
+
+    def first(need, meet, ride, middle):
+        me, grad_t = lax.axis_index(FRAME), attention.grad_t
+        landing = grad_t.ref.at[:, span(me, rows)]
+        arriving = to_frames(lambda g: own.ref.at[g], lambda f: landing, build.bound[sems])
+        need(0)
+        turned_grads(grad_low.ref[...], output, own, slice(0, rows))
+        meet()
+        for copy in arriving[::-1]:
+            copy.start()
+        ride()
+        grad_t.ref[:, span(me, rows)] = own.ref[me]
+        need(1)
+        attention.begin()
+        for copy in arriving:
+            copy.wait()
+        attention.run(middle)
+        from_states.cross()
+
+    def then(need):
+        from_text.sum_first()
+        both_grads.ref[0] = vector_grads[1].ref[...]
+        both_grads.ref[1] = vector_grads[0].ref[...]
+        from_vectors.ins = [both_grads.ref]
+        from_vectors.begin()
+
+    tasks = [from_states] + list(tasks)
+    return run_chain(
+        build,
+        [stage],
+        collective_id,
+        tasks,
+        (LINE_ONLY, SECTION),
+        chores,
+        [(make_normed, (0, 2), (0, 2)), (text_step, (0, 9), (0, 9))],
+        then,
+        first,
+        2,
+        [from_vectors, from_text],
+    )
 
 
 def masked_scores(keys, query_t, begins, start):
@@ -1352,100 +1651,46 @@
     ]
 
 
-def turned_parts(normed, matrices, own, at):
+def turned_parts(normed, matrices, own, at, lanes):
     for part, matrix in enumerate(matrices):
         turned = plain_product(normed, matrix.ref[...]).astype(jnp.bfloat16).T
         for head in range(4):
             rows = slice(part * HEAD, (part + 1) * HEAD)
-            own.ref[at + (head, rows)] = turned[head * HEAD : (head + 1) * HEAD, :]
-
-
-def self_forward(normed, weights, begins, layer, collective_id, tasks, early):
-    first = int(normed.ndim == 3)
-    rows, frames, width = normed.shape[-2], 4, 3 * HEAD
-    all_rows = rows * frames
-    build = Build()
-    normed, begins = build.arg(normed, 0), build.arg(begins, 1)
-    if first:
-        matrices = [build.arg(weight, 0) for weight in weights]
-    else:
-        matrices = [build.pick(weight, layer, 0) for weight in weights]
-    heads_t = build.out((width, all_rows), jnp.bfloat16)
-    out = build.out((frames * HEAD, rows), jnp.bfloat16)
-    own = build.temp((1 + first, frames, width, rows), jnp.bfloat16)
-    keys = build.temp((all_rows, HEAD), jnp.bfloat16)
-    mixed_t = build.temp((frames, HEAD, rows), jnp.bfloat16)
-    sems = [build.extra(pltpu.SemaphoreType.DMA((2, frames - 1))) for _ in range(2)]
-    over_sems = build.extra(pltpu.SemaphoreType.DMA((2, frames)))
-
-    def body(need, meet, ride, middle):
-        me, section = lax.axis_index(FRAME), lax.axis_index(SECTION)
-        partners = frame_partners()
+            own.ref[at + (head, rows, lanes)] = turned[head * HEAD : (head + 1) * HEAD, :]
+
+
+class Attention:
+    def __init__(self, build, rows, begins, stage):
+        frames, width = 4, 3 * HEAD
+        self.rows = rows
+        self.begins = build.arg(begins, stage)
+        self.heads_t = build.out((width, rows * frames), jnp.bfloat16)
+        self.out = build.out((frames * HEAD, rows), jnp.bfloat16)
+        self.keys = build.temp((rows * frames, HEAD), jnp.bfloat16)
+        self.mixed_t = build.temp((frames, HEAD, rows), jnp.bfloat16)
+        self.sems = build.extra(pltpu.SemaphoreType.DMA((2, frames - 1)))
+        self.build = build
+
+    def run(self, early=()):
+        me, partners, rows = lax.axis_index(FRAME), frame_partners(), self.rows
+        heads_t, keys, mixed_t, out = self.heads_t, self.keys, self.mixed_t, self.out
         block = min(2 * BLOCK, rows)
-        landing = heads_t.ref.at[:, span(me, rows)]
-        arriving = to_frames(lambda g: own.ref.at[0, g], lambda f: landing, build.bound[sems[0]])
         leaving = to_frames(
-            lambda g: mixed_t.ref.at[g], lambda f: out.ref.at[span(f, HEAD), :], build.bound[sems[1]]
+            lambda g: mixed_t.ref.at[g], lambda f: out.ref.at[span(f, HEAD), :], self.build.bound[self.sems]
         )
-        pair = build.bound[over_sems]
-        over = [
-            remote(own.ref.at[first, g], landing, pair.at[0, k], pair.at[1, k], {SECTION: 1, FRAME: g})
-            for k, g in enumerate((me,) + partners)
-        ]
-
-        need(0)
-        if first:
-
-            @pl.when(section == 0)
-            def _():
-                turned_parts(normed.ref[1], matrices, own, (1,))
-                meet()
-                for copy in over:
-                    copy.start()
-                turned_parts(normed.ref[0], matrices, own, (0,))
-                for copy in arriving[::-1]:
-                    copy.start()
-                heads_t.ref[:, span(me, rows)] = own.ref[0, me]
-
-            @pl.when(section == 1)
-            def _():
-                meet()
-
-        else:
-            turned_parts(normed.ref[...], matrices, own, (0,))
-            meet()
-            for copy in arriving[::-1]:
-                copy.start()
-            heads_t.ref[:, span(me, rows)] = own.ref[0, me]
-        ride()
-        need(1)
-        if first:
-
-            @pl.when(section == 0)
-            def _():
-                for copy in arriving + over:
-                    copy.wait_send()
-                for copy in arriving:
-                    copy.wait_recv()
-
-            @pl.when(section == 1)
-            def _():
-                for copy in over:
-                    copy.wait_recv()
-
-        else:
-            for copy in arriving:
-                copy.wait()
         heads_t.flush()
         keys.ref[...] = heads_t.ref[HEAD : 2 * HEAD, :].T
-        for target in range(frames):
-            if target == frames - 1:
+        for target in range(4):
+            if target == 3:
                 for task in early:
                     task.first_hop()
             for start in range(target * rows, (target + 1) * rows, block):
                 reach = start + block
                 scores = masked_scores(
-                    keys.ref[:reach, :], heads_t.ref[:HEAD, start:reach], begins.ref[:, start:reach], start
+                    keys.ref[:reach, :],
+                    heads_t.ref[:HEAD, start:reach],
+                    self.begins.ref[:, start:reach],
+                    start,
                 )
                 e = jnp.exp(scores - jnp.max(scores, axis=0, keepdims=True))
                 total = jnp.sum(e, axis=0, keepdims=True)
@@ -1464,59 +1709,154 @@
             copy.wait()
         out.flush()
 
-    kinds = (FRAME, SECTION, BOTH) if first else (FRAME,)
-    return run_build(build, body, kinds, collective_id, tasks)
-
-
-def self_backward(heads_t, grad_low, weight, begins, layer, collective_id, tasks):
-    rows, frames, width = grad_low.shape[0], 4, 3 * HEAD
-    all_rows = rows * frames
+
+class BlockSender:
+    def __init__(self, build, rows, height, landing):
+        self.rows, self.landing = rows, landing
+        self.blocks = rows // BLOCK
+        self.own = build.temp((4, height, rows), jnp.bfloat16)
+        self.sems = build.extra(pltpu.SemaphoreType.DMA((2, 3, self.blocks)))
+        self.build = build
+
+    def copies(self, block):
+        lanes, me = span(block, BLOCK), lax.axis_index(FRAME)
+        place = self.landing.ref.at[:, span(me * self.blocks + block, BLOCK)]
+        sems = self.build.bound[self.sems]
+        return [
+            remote(
+                self.own.ref.at[other, :, lanes], place, sems.at[0, k, block], sems.at[1, k, block], {FRAME: other}
+            )
+            for k, other in enumerate(frame_partners())
+        ]
+
+    def send(self, block):
+        me = lax.axis_index(FRAME)
+        for copy in self.copies(block)[::-1]:
+            copy.start()
+        lanes = span(block, BLOCK)
+        self.landing.ref[:, span(me * self.blocks + block, BLOCK)] = self.own.ref[me, :, lanes]
+
+    def wait(self):
+        def one(block, carry):
+            for copy in self.copies(block):
+                copy.wait()
+            return carry
+
+        lax.fori_loop(0, self.blocks, one, 0)
+
+
+def first_attention(inputs, vectors, weights, begins, text, text_weights, collective_id, tasks, early):
+    micros, rows, model = inputs.shape
+    frames, width = 4, 3 * HEAD
     build = Build()
-    heads_t, begins = build.arg(heads_t, 1), build.arg(begins, 1)
-    grad_low, weight = build.arg(grad_low, 0), build.pick(weight, layer, 0)
-    out = build.out((frames * width, rows), jnp.bfloat16)
-    own = build.temp((frames, HEAD, rows), jnp.bfloat16)
-    grad_t = build.temp((HEAD, all_rows), jnp.bfloat16)
-    columns = build.temp((4, all_rows, HEAD), jnp.bfloat16)
-    key_sum, value_sum = (build.temp((all_rows, HEAD), jnp.float32) for _ in range(2))
-    grads_t = build.temp((frames, width, rows), jnp.bfloat16)
-    sems = [build.extra(pltpu.SemaphoreType.DMA((2, frames - 1))) for _ in range(2)]
+    inputs, vectors = build.arg(inputs, 0), build.arg(vectors, 0)
+    matrices = [build.arg(weight, 0) for weight in weights]
+    attention = Attention(build, rows, begins, 1)
+    text, text_weights = build.arg(text, 1), [build.arg(weight, 1) for weight in text_weights]
+    heads_t = attention.heads_t
+    normed = build.temp((rows, model), jnp.bfloat16)
+    own = build.temp((2, frames, width, rows), jnp.bfloat16)
+    columns = text_weights[0].shape[1]
+    states = build.temp((micros, text.shape[0] // micros, 2 * columns), jnp.bfloat16)
+    sems = build.extra(pltpu.SemaphoreType.DMA((2, frames - 1)))
+    over_sems = build.extra(pltpu.SemaphoreType.DMA((2, frames)))
+    from_text = TextTask(states)
+
+    def project(micro):
+        def one(number, carry):
+            at = span(number, BLOCK)
+            standard, _ = norm_parts(inputs.ref[micro, at, :].astype(jnp.float32))
+            normed.ref[at, :] = scaled_rows(standard, vectors, 0)
+            return carry
+
+        lax.fori_loop(0, rows // BLOCK, one, 0)
+        turned_parts(normed.ref[...], matrices, own, (micro,), slice(0, rows))
 
     def body(need, meet, ride, middle):
-        me = lax.axis_index(FRAME)
-        partners = frame_partners()
-        block = min(2 * BLOCK, rows)
-        scale = HEAD ** (-0.5)
-        arriving = to_frames(
-            lambda g: own.ref.at[g], lambda f: grad_t.ref.at[:, span(f, rows)], build.bound[sems[0]]
-        )
-        leaving = to_frames(
-            lambda g: grads_t.ref.at[g], lambda f: out.ref.at[span(f, width), :], build.bound[sems[1]]
-        )
-
-        def project(other):
-            return nt_product(weight.ref[span(other, HEAD), :], grad_low.ref[...]).astype(jnp.bfloat16)
-
+        me, section = lax.axis_index(FRAME), lax.axis_index(SECTION)
+        landing = heads_t.ref.at[:, span(me, rows)]
+        arriving = to_frames(lambda g: own.ref.at[0, g], lambda f: landing, build.bound[sems])
+        pair = build.bound[over_sems]
+        over = [
+            remote(own.ref.at[1, g], landing, pair.at[0, k], pair.at[1, k], {SECTION: 1, FRAME: g})
+            for k, g in enumerate((me,) + frame_partners())
+        ]
         need(0)
-        own.ref[partners[2]] = project(partners[2])
-        own.ref[partners[1]] = project(partners[1])
-        meet()
-        arriving[2].start()
-        arriving[1].start()
-        own.ref[partners[0]] = project(partners[0])
-        arriving[0].start()
+
+        @pl.when(section == 0)
+        def _():
+            project(1)
+            meet()
+            for copy in over:
+                copy.start()
+            project(0)
+            for copy in arriving[::-1]:
+                copy.start()
+            heads_t.ref[:, span(me, rows)] = own.ref[0, me]
+
+        @pl.when(section == 1)
+        def _():
+            meet()
+
+        need(1)
+        for part, weight in enumerate(text_weights):
+            made = plain_product(text.ref[...], weight.ref[...]).astype(jnp.bfloat16)
+            for micro in range(micros):
+                some = slice(micro * states.shape[1], (micro + 1) * states.shape[1])
+                states.ref[micro, :, part * columns : (part + 1) * columns] = made[some, :]
+        from_text.ins = [states.ref]
+        from_text.begin()
         ride()
-        grad_t.ref[:, span(me, rows)] = project(me)
+
+        @pl.when(section == 0)
+        def _():
+            for copy in arriving + over:
+                copy.wait_send()
+            for copy in arriving:
+                copy.wait_recv()
+
+        @pl.when(section == 1)
+        def _():
+            for copy in over:
+                copy.wait_recv()
+
+        attention.run(early)
+
+    return run_build(build, body, (FRAME, SECTION, BOTH), collective_id, tasks + [from_text])
+
+
+class AttentionBack:
+    def __init__(self, build, rows, heads_t, begins, stage):
+        frames, width = 4, 3 * HEAD
+        all_rows = rows * frames
+        self.build, self.rows = build, rows
+        self.heads_t, self.begins = build.arg(heads_t, stage), build.arg(begins, stage)
+        self.out = build.out((frames * width, rows), jnp.bfloat16)
+        self.grad_t = build.temp((HEAD, all_rows), jnp.bfloat16)
+        self.columns = build.temp((4, all_rows, HEAD), jnp.bfloat16)
+        self.key_sum, self.value_sum = (build.temp((all_rows, HEAD), jnp.float32) for _ in range(2))
+        self.grads_t = build.temp((frames, width, rows), jnp.bfloat16)
+        self.sems = build.extra(pltpu.SemaphoreType.DMA((2, frames - 1)))
+
+    def begin(self):
+        key_sum, value_sum = self.key_sum, self.value_sum
         key_sum.ref[...] = jnp.zeros(key_sum.shape, jnp.float32)
         value_sum.ref[...] = jnp.zeros(key_sum.shape, jnp.float32)
-        need(1)
         for part in range(3):
-            columns.ref[part] = heads_t.ref[part * HEAD : (part + 1) * HEAD, :].T
-        for copy in arriving:
-            copy.wait()
+            self.columns.ref[part] = self.heads_t.ref[part * HEAD : (part + 1) * HEAD, :].T
+
+    def run(self, middle):
+        rows, width, scale = self.rows, 3 * HEAD, HEAD ** (-0.5)
+        me, partners = lax.axis_index(FRAME), frame_partners()
+        heads_t, begins, grad_t, columns = self.heads_t, self.begins, self.grad_t, self.columns
+        key_sum, value_sum, grads_t, out = self.key_sum, self.value_sum, self.grads_t, self.out
+        block = min(2 * BLOCK, rows)
+        leaving = to_frames(
+            lambda g: grads_t.ref.at[g], lambda f: out.ref.at[span(f, width), :], self.build.bound[self.sems]
+        )
         columns.ref[3] = grad_t.ref[...].T
         middle()
-        for target in reversed(range(frames)):
+        for target in reversed(range(4)):
             for start in reversed(range(target * rows, (target + 1) * rows, block)):
                 reach = start + block
                 scores = masked_scores(
@@ -1552,7 +1892,11 @@
             copy.wait()
         out.flush()
 
-    return run_build(build, body, (FRAME,), collective_id, tasks)
+
+def turned_grads(grad, weight, own, lanes):
+    turned = nt_product(weight.ref[...], grad).astype(jnp.bfloat16)
+    for head in range(4):
+        own.ref[head, :, lanes] = turned[head * HEAD : (head + 1) * HEAD, :]
 
 
 def matmul(left_side, right_side):
@@ -1654,10 +1998,6 @@
         grad_keys.reshape(key_rows.shape),
         grad_values.reshape(value_rows.shape),
     )
-
-
-def sum_rows(rows):
-    return jnp.concatenate(rows, axis=0)
 
 
 def on_four_frames(inputs, lengths, text, cotangent, vector_args, matrix_args):
@@ -1685,12 +2025,7 @@
 
     own_vectors = jnp.pad(jnp.concatenate(vector_args, axis=0), ((0, 2), (0, 0)))
     self_weights = (query_weight, key_weight, value_weight)
-    normed = layer_norm(inputs.astype(jnp.float32), own_vectors[0], own_vectors[1]).astype(jnp.bfloat16)
     text_local = text.reshape(-1, model_width)
-    text_states = jnp.concatenate(
-        [matmul(text_local, cross_key), matmul(text_local, cross_value)], axis=1
-    ).astype(jnp.bfloat16)
-    text_states = text_states.reshape(micro_count, -1, 2 * columns)
 
     item_ends = jnp.cumsum(lax.dynamic_index_in_dim(lengths, section, 0, keepdims=False))
     passed = jnp.arange(rows_all, dtype=jnp.int32)[None, :] >= item_ends[:, None]
@@ -1698,92 +2033,73 @@
     seg = jnp.sum(passed.astype(jnp.int32), axis=0, keepdims=True)
     seg = lax.dynamic_slice_in_dim(seg, frame_index * rows_dev, rows_dev, 1)
 
-    entering = inputs
-    saved = []
-    for layer in range(2):
-        first = layer == 0
-        tasks = []
-        if first:
-            early = [WeightTask(output_weight)]
-            early[0].hooked = 1
-            tasks = early + [CrossTask(own_vectors, own_vectors, False), TextTask(text_states)]
-            tasks += [QuarterTask(w) for w in (cross_query, cross_output, expand_weight)]
-        (heads_t, attended_t), carried = self_forward(
+    early = WeightTask(output_weight)
+    early.hooked = 1
+    others = (cross_query, cross_output, expand_weight, reduce_weight)
+    (heads_t, attended_t), carried = first_attention(
+        inputs,
+        own_vectors,
+        self_weights,
+        begins,
+        text_local,
+        (cross_key, cross_value),
+        1,
+        [early, CrossTask(own_vectors, own_vectors, False)] + [QuarterTask(w) for w in others[:2]],
+        [early],
+    )
+    vectors = (own_vectors, carried[1])
+    selected = [by_section(*vectors), by_section(*vectors[::-1])]
+    states = carried[4].reshape(2, -1, 2 * columns)
+    coming = [WeightTask(w, 0, quarter) for w, quarter in zip(others, carried[2:4] + [None] * 2)]
+    late = [WeightTask(w, 1) for w in self_weights]
+    weights = [(output_weight, carried[0])]
+    outs, carried = forward_chain(
+        0,
+        attended_t,
+        inputs,
+        states[0],
+        seg,
+        vectors,
+        weights + coming,
+        2,
+        coming + late,
+        late,
+        begins,
+    )
+    weights += list(zip(others, carried))
+    self_pairs = list(zip(self_weights, carried[4:]))
+    def keep(entering, normed, heads_t, attended_t, outs):
+        second_normed, middle, queries, cross_att, third_normed, latter, before, hidden = outs[:8]
+        return (
+            entering,
             normed,
-            self_weights if first else self_pairs,
-            begins,
-            layer,
-            2 + layer,
-            tasks,
-            early if first else [],
+            heads_t,
+            attended_t,
+            middle,
+            second_normed,
+            latter,
+            third_normed,
+            queries,
+            cross_att,
+            before,
+            hidden,
         )
-        if first:
-            vectors = [by_section(own_vectors, carried[1]), by_section(carried[1], own_vectors)]
-            normed = layer_norm(
-                lax.dynamic_index_in_dim(inputs, section, 0, keepdims=False).astype(jnp.float32),
-                vectors[0][0],
-                vectors[0][1],
-            ).astype(jnp.bfloat16)
-        gains = vectors[layer]
-        tasks = []
-        if first:
-            states = carried[2].reshape(2, -1, 2 * columns)
-            others = (cross_query, cross_output, expand_weight, reduce_weight)
-            coming = [WeightTask(w, 0, q) for w, q in zip(others, carried[3:] + [None])]
-            late = [WeightTask(w) for w in self_weights]
-            for task in late:
-                task.hooked = 2
-            weights = [(output_weight, carried[0])]
-            tasks = coming + late
-        outs, carried = forward_chain(
-            layer,
-            attended_t,
-            entering,
-            states[layer],
-            seg,
-            gains,
-            vectors[1] if first else None,
-            weights + coming if first else weights,
-            4 + layer,
-            tasks,
-            late if first else [],
-        )
-        second_normed, middle, queries, cross_att, third_normed, latter, before, hidden = outs[:8]
-        if first:
-            weights += list(zip(others, carried))
-            self_pairs = list(zip(self_weights, carried[4:]))
-        saved.append(
-            (
-                entering,
-                normed,
-                heads_t,
-                attended_t,
-                middle,
-                second_normed,
-                latter,
-                third_normed,
-                queries,
-                cross_att,
-                before,
-                hidden,
-            )
-        )
-        if first:
-            normed, entering = outs[8:]
-        else:
-            (result_low,) = outs[8:]
-
-    vector_grads, shares = [None] * 2, [{}, {}]
-    totals = {}
-
-    def low_product(left, right):
-        return matmul_tn(left, right).astype(jnp.bfloat16)
+
+    saved = [keep(inputs, None, heads_t, attended_t, outs)]
+    normed, entering, heads_t, attended_t = outs[8:]
+    outs, _ = forward_chain(
+        1, attended_t, entering, states[1], seg, vectors, weights, 3
+    )
+    saved.append(keep(entering, normed, heads_t, attended_t, outs))
+    result_low = outs[8]
+
+    shares = [{}, {}]
 
     def crossing(*names):
         return [CrossTask(shares[0][name], shares[1][name], True) for name in names]
 
     def unpack(outs):
-        names = ("grad_pre", "grad_cross", "gain5", "shift5", "queries", "states", "grad_self", "gain3", "shift3")
+        names = ("vectors", "grad_pre", "grad_cross", "queries", "states", "grad_self")
         return dict(zip(names, outs))
 
     def for_backward(layer):
@@ -1798,10 +2114,6 @@
             (saved[layer][1], None),
         ]
 
-    def vector_rows(outs, first):
-        rows = first + [outs[name] for name in ("gain3", "shift3", "gain5", "shift5")]
-        return sum_rows(rows + [jnp.zeros((2, model_width), jnp.float32)])
-
     names = ("cross_output", "output", "cross_query", "heads")
     outs, carried = backward_chain(
         1,
@@ -1809,102 +2121,154 @@
         for_backward(1),
         states[1],
         seg,
-        vectors[1],
+        vectors,
         weights,
+        saved[1][2],
+        begins,
         8,
         [BothTask(saved[1][0], result_low)],
     )
-    later = unpack(outs)
-    layer_outputs, shares[1]["reduce"], shares[1]["expand"] = carried
-    (grad_heads_t,), (shares[1]["states"],) = self_backward(
-        saved[1][2], later["grad_self"], weights[0], begins, 1, 9, [ShareTask(later["states"])]
-    )
+    later, grad_heads_t = unpack(outs), outs[6]
+    layer_outputs, shares[1]["states"], shares[1]["reduce"], shares[1]["expand"] = carried
     outs, carried = between_chain(
         1,
-        (grad_heads_t, saved[1][0], vectors[1][0], later["grad_self"], self_pairs),
+        grad_heads_t,
+        saved[1][0],
+        selected[1],
+        later["grad_self"],
+        self_pairs,
         products(1, later),
-        (for_backward(0), states[0], seg, vectors[0], weights),
+        (for_backward(0), states[0], seg, selected[0], weights),
         10,
         [],
     )
-    later_low, first_vectors = outs[0], list(outs[1:3])
-    vector_grads[1] = vector_rows(later, first_vectors)
-    sooner = unpack(outs[3:])
+    last_vectors, later_low = outs[:2]
+    sooner = unpack(outs[2:])
     shares[1].update(zip(names, carried))
     shares[0]["reduce"], shares[0]["expand"] = carried[4:]
-    (grad_heads_t,), carried = self_backward(
+    outs, carried = last_kernel(
         saved[0][2],
         sooner["grad_self"],
         weights[0],
         begins,
-        0,
+        inputs,
+        vectors,
+        self_pairs,
+        later_low,
+        products(0, sooner),
+        [shares[1][name] for name in names],
+        (sooner["states"], shares[1]["states"]),
+        text_local,
+        (cross_key, cross_value),
+        (later["vectors"] + last_vectors, sooner["vectors"]),
         11,
-        [ShareTask(sooner["states"])] + crossing("reduce", "expand"),
-    )
-    shares[0]["states"], totals["reduce"], totals["expand"] = carried
-    outs, carried = last_chain(
-        0,
-        grad_heads_t,
-        saved[0][0],
-        vectors[0][0],
-        sooner["grad_self"],
-        self_pairs,
-        spare=later_low,
-        products=products(0, sooner),
-        collective_id=12,
-        tasks=[CrossTask(shares[0]["states"], shares[1]["states"], False)],
-    )
-    both_grads = outs[3]
-    vector_grads[0] = vector_rows(sooner, list(outs[1:3]))
-    other_states = carried[0]
-    shares[0].update(zip(names, carried[1:]))
-
-    own_states = by_section(shares[0]["states"], shares[1]["states"])
-    text_rows = sum_rows([by_section(own_states, other_states), by_section(other_states, own_states)])
-    key_part, value_part = text_rows[:, :columns], text_rows[:, columns:]
-    text_part = matmul_nt(key_part, cross_key) + matmul_nt(value_part, cross_value)
-    _, (text_grad, vector_total, cross_grads, *carried) = call(
-        None,
-        [],
-        [],
-        [],
-        (),
-        18,
-        [
-            TotalTask(text_part.astype(jnp.bfloat16)),
-            VectorTask(jnp.stack(vector_grads)),
-            ShareTask(low_product(text_local, text_rows)),
+        crossing("reduce", "expand"),
+    )
+    both_grads = outs[-1]
+    totals = dict(zip(("reduce", "expand") + names + ("text",), carried))
+    cross_grads, (vector_total, text_grad) = totals["text"], carried[7:]
+    kernel_outs = widen(
+        [layer_outputs, both_grads, text_grad, cross_grads],
+        [totals[name] for name in ("reduce", "expand", "cross_output", "output", "cross_query", "heads")],
+        vector_total,
+    )
+    layer_outputs, input_grads, text_grad, cross_key_grad, cross_value_grad = kernel_outs[:5]
+    reduce_grad, expand_grad, cross_output_grad, output_grad, cross_query_grad = kernel_outs[5:10]
+    query_grad, key_grad, value_grad = kernel_outs[10:13]
+    rows = kernel_outs[13:]
+    ordered = (
+        rows[0],
+        rows[1],
+        query_grad,
+        key_grad,
+        value_grad,
+        output_grad,
+        rows[2],
+        rows[3],
+        cross_query_grad,
+        cross_key_grad,
+        cross_value_grad,
+        cross_output_grad,
+        rows[4],
+        rows[5],
+        expand_grad,
+        reduce_grad,
+    )
+    vector_places = (0, 1, 6, 7, 12, 13)
+    ordered = tuple(
+        g if place in vector_places else g[None] for place, g in enumerate(ordered)
+    )
+    return (layer_outputs[None], input_grads[None], text_grad.reshape(text.shape)) + ordered
+
+
+def widen(lows, wides, vectors):
+    *lows, pair = lows
+    *wides, triple = wides
+    wide = jnp.float32
+    half, third = pair.shape[1] // 2, triple.shape[1] // 3
+    quarter = vectors.shape[1] // 4
+    outs = [jax.ShapeDtypeStruct(low.shape, wide) for low in lows]
+    outs += [jax.ShapeDtypeStruct((pair.shape[0], half), wide)] * 2
+    outs += [jax.ShapeDtypeStruct(one.shape, wide) for one in wides]
+    outs += [jax.ShapeDtypeStruct((triple.shape[0], third), wide)] * 3
+    outs += [jax.ShapeDtypeStruct((1, quarter), wide)] * 6
+    widened = [*lows, pair]
+    n_in, n_out, n_low = len(widened) + len(wides) + 2, len(outs), len(widened)
+
+    def kernel(*refs):
+        ins, outs = refs[:n_in], refs[n_in : n_in + n_out]
+        narrow = refs[n_in + n_out : n_in + n_out + n_low]
+        broad = refs[n_in + n_out + n_low : n_in + n_out + 2 * n_low]
+        *held, rows, in_sems, out_sems = refs[n_in + n_out + 2 * n_low :]
+        lane = span(lax.axis_index(FRAME), quarter)
+        started = []
+
+        def copy(source, landing):
+            one = pltpu.make_async_copy(source, landing, out_sems.at[len(started)])
+            one.start()
+            started.append(one)
+
+        loads = [pltpu.make_async_copy(ins[i], narrow[i], in_sems.at[i]) for i in range(n_low)]
+        copied = [
+            pltpu.make_async_copy(source, room, in_sems.at[n_low + i])
+            for i, (source, room) in enumerate(zip(ins[n_low:], held + [rows]))
         ]
-        + crossing(*names),
-    )
-    totals.update(zip(names, carried))
-    text_grad = text_grad.astype(jnp.float32).reshape(text.shape)
-    vector_total = lax.dynamic_slice_in_dim(
-        vector_total, frame_index * (model_width // 4), model_width // 4, 1
-    )
-    grad_query, grad_key, grad_value = jnp.split(totals["heads"], 3, axis=1)
-    cross_grads = cross_grads.astype(jnp.float32)
-
-    ordered = (
-        vector_total[0],
-        vector_total[1],
-        grad_query,
-        grad_key,
-        grad_value,
-        totals["output"],
-        vector_total[2],
-        vector_total[3],
-        totals["cross_query"],
-        cross_grads[:, :columns],
-        cross_grads[:, columns:],
-        totals["cross_output"],
-        vector_total[4],
-        vector_total[5],
-        totals["expand"],
-        totals["reduce"],
-    )
-    layer_outputs, input_grads = (a.astype(jnp.float32) for a in (layer_outputs, both_grads))
-    return (layer_outputs[None], input_grads[None], text_grad) + tuple(g[None] for g in ordered)
+        for load in copied + loads:
+            load.start()
+        for i in range(len(wides)):
+            copied[i].wait()
+            copy(held[i], outs[n_low + 1 + i])
+        place = n_low + 1 + len(wides)
+        copied[-2].wait()
+        for part in range(3):
+            copy(held[-1].at[:, part * third : (part + 1) * third], outs[place + part])
+        copied[-1].wait()
+        for row in range(6):
+            copy(rows.at[row : row + 1, lane], outs[place + 3 + row])
+        for i in range(n_low):
+            loads[i].wait()
+            broad[i][...] = narrow[i][...].astype(wide)
+            if i + 1 < n_low:
+                copy(broad[i], outs[i])
+            else:
+                copy(broad[i].at[:, :half], outs[i])
+                copy(broad[i].at[:, half:], outs[i + 1])
+        for one in started:
+            one.wait()
+
+    anywhere = pl.BlockSpec(memory_space=pl.ANY)
+    scratch = [pltpu.VMEM(low.shape, jnp.bfloat16) for low in widened]
+    scratch += [pltpu.VMEM(low.shape, wide) for low in widened]
+    scratch += [pltpu.VMEM(one.shape, wide) for one in (*wides, triple, vectors)]
+    scratch += [pltpu.SemaphoreType.DMA((n_in,)), pltpu.SemaphoreType.DMA((n_out,))]
+    return pl.pallas_call(
+        kernel,
+        out_shape=outs,
+        in_specs=[anywhere] * n_in,
+        out_specs=[anywhere] * n_out,
+        scratch_shapes=scratch,
+        compiler_params=pltpu.CompilerParams(vmem_limit_bytes=VMEM_BYTES),
+    )(*widened, *wides, triple, vectors)
 
 
 def self_attention(query, key_rows, value_rows, masks):

time: 565 us -> 520 us (0.920)
  Pallas kernels: 521 us -> 503 us
  other arithmetic: 17.7 us -> 2.91 us
  local copies, waits for them, and re-layouts: 12.9 us -> 4.63 us
    pallas_call x10 -> x6, Pallas kernels: 521 us -> 495 us  [call(): pl.pallas_call(kernel, out_shape=all_outs, in_specs=in_specs, out_specs=o...]
    pallas_call x0 -> x1, Pallas kernels: none -> 8.11 us  [widen(): pl.pallas_call(kernel, out_shape=outs, in_specs=[anywhere] * n_in, out_sp...]
where the time goes in v6:
time: 520 us; the launch traced here: 512 us
  Pallas kernels  503 us (97%)
    pallas_call x6, Pallas kernels, call(): pl.pallas_call(kernel, out_shape=all_outs, in_specs=in_specs, out_specs=o...  495 us

profile of v6, /device:TPU:0, one launch (start us, length us, event | category | flops | bytes accessed | tf_op | source)
XLA Modules:
  0.0 511.6 jit_solution(15811998651080043328)
XLA Ops:
  0.7 0.0 copy-start
  0.7 0.7 copy-done
  1.3 0.2 reduce-window.8
  1.5 0.7 convert_reduce_fusion
  2.2 0.8 concatenate.3
  3.1 0.6 pad.4.refs_1_.refs_10_.refs_11_.refs_0_.refs_8_.refs_13_
  3.7 38.3 %shard_map.339 = (bf16[192,2048]{1,0:T(8,128)(2,1)}, bf16[256,512]{1,0:T(8,128)(2,1)}, bf16[256,1024]{1,0:T(8,128)(2,1)}, f32[8,1024]{1,0:T(8,128)}, bf16[256,25...) custom-call(bf16[2,512,1024]{2,1,0:T(8,128)(2,1)} %refs_15_.1, ...), custom_call_target="tpu_custom_call" | custom-call | tf_op jit(solution)/shard_map/pallas_call | solution.py:725
  42.0 1.9 fusion
  43.8 0.7 dynamic-slice.3
  44.5 101.7 %shard_map.340 = (bf16[512,1024]{1,0:T(8,128)(2,1)}, bf16[512,1024]{1,0:T(8,128)(2,1)}, bf16[512,256]{1,0:T(8,128)(2,1)}, bf16[512,256]{1,0:T(8,128)(2,1)}, bf16...) custom-call(f32[8,1024]{1,0:T(8,128)} %pad.4.refs_1_.refs_10_.refs_1, ...), custom_call_target="tpu_custom_call" | custom-call | tf_op jit(solution)/shard_map/pallas_call | solution.py:725
  146.1 82.0 %shard_map.341 = (bf16[512,1024]{1,0:T(8,128)(2,1)}, bf16[512,1024]{1,0:T(8,128)(2,1)}, bf16[512,256]{1,0:T(8,128)(2,1)}, bf16[512,256]{1,0:T(8,128)(2,1)}, bf16...) custom-call(f32[8,1024]{1,0:T(8,128)} %pad.4.refs_1_.refs_10_.refs_1, ...), custom_call_target="tpu_custom_call" | custom-call | tf_op jit(solution)/shard_map/pallas_call | solution.py:725
  228.1 0.0 copy-start.2
  228.1 90.0 %shard_map.342 = (f32[8,1024]{1,0:T(8,128)}, bf16[512,1024]{1,0:T(8,128)(2,1)}, bf16[512,1024]{1,0:T(8,128)(2,1)}, bf16[512,256]{1,0:T(8,128)(2,1)}, bf16[256,51...) custom-call(f32[2,512,1024]{2,1,0:T(8,128)} %refs_0_.3, ...), custom_call_target="tpu_custom_call" | custom-call | tf_op jit(solution)/shard_map/pallas_call | solution.py:725
  318.1 0.0 copy-done.2
  318.1 0.6 broadcast_select_fusion
  318.8 0.0 copy-start.3
  318.8 89.0 %shard_map.343 = (f32[8,1024]{1,0:T(8,128)}, bf16[512,1024]{1,0:T(8,128)(2,1)}, f32[8,1024]{1,0:T(8,128)}, bf16[512,1024]{1,0:T(8,128)(2,1)}, bf16[512,1024]{1,0...) custom-call(bf16[512,1024]{1,0:T(8,128)(2,1)} %get-tuple-element.127, ...), custom_call_target="tpu_custom_call" | custom-call | tf_op jit(solution)/shard_map/pallas_call | solution.py:725
  407.8 0.0 copy-done.3
  407.8 1.4 add.14.refs_5_
  409.2 94.0 %shard_map.344 = (bf16[768,512]{1,0:T(8,128)(2,1)}, bf16[512,1024]{1,0:T(8,128)(2,1)}, bf16[2,512,1024]{2,1,0:T(8,128)(2,1)}, f32[256,1024]{1,0:T(8,128)}, f32[2...) custom-call(bf16[192,2048]{1,0:T(8,128)(2,1)} %get-tuple-element.126, ...), custom_call_target="tpu_custom_call" | custom-call | tf_op jit(solution)/shard_map/pallas_call | solution.py:725
  503.2 0.0 copy-start.1
  503.2 8.1 %shard_map.345 = (f32[2,512,1024]{2,1,0:T(8,128)}, f32[2,512,1024]{2,1,0:T(8,128)}, f32[128,1024]{1,0:T(8,128)}, f32[256,256]{1,0:T(8,128)}, f32[256,256]{1,0:T(...) custom-call(bf16[2,512,1024]{2,1,0:T(8,128)(2,1)} %get-tuple-element, ...), custom_call_target="tpu_custom_call" | custom-call | tf_op jit(solution)/shard_map/pallas_call | solution.py:2264
  511.3 0.0 copy-done.1
  (1 shorter events, 0.0 us)
Async XLA Ops:
  0.7 0.7 copy-start
  228.1 90.0 %copy-start.2 = (f32[8,1024]{1,0:T(8,128)S(1)}, f32[8,1024]{1,0:T(8,128)}, u32[]{:S(2)}) copy-start(f32[8,1024]{1,0:T(8,128)} %get-tuple-element.105.refs_1_.refs_9_.refs_2_.refs_14_) | copy-start | bytes 98308
  318.8 89.0 %copy-start.3 = (f32[8,1024]{1,0:T(8,128)S(1)}, f32[8,1024]{1,0:T(8,128)}, u32[]{:S(2)}) copy-start(f32[8,1024]{1,0:T(8,128)} %get-tuple-element.144) | copy-start | bytes 98308
  503.2 8.1 %copy-start.1 = (s32[2,4]{1,0:T(2,128)S(1)}, s32[2,4]{1,0:T(2,128)}, u32[]{:S(2)}) copy-start(s32[2,4]{1,0:T(2,128)} %param.21) | copy-start | bytes 100

commit v7 on v6

--- a/solution.py
+++ b/solution.py
@@ -270,22 +270,24 @@
         over = remote(parts.at[0] if which else later, parts.at[1], sems.at[0], sems.at[1], target)
         return over, pltpu.make_async_copy(later, parts.at[2], sems.at[2])
 
+    def send(self):
+        parts = self.room[self.base]
+        section = lax.axis_index(SECTION)
+        self.over().wait()
+        total = self.chip_sum(1) + self.room[1][1].astype(jnp.float32)
+        parts[0] = total.astype(jnp.bfloat16)
+        for which in (0, 1):
+
+            @pl.when(section == which)
+            def _():
+                over, stay = self.crossing(which)
+                over.start()
+                if which:
+                    stay.start()
+
     def steps(self):
         parts = self.room[self.base]
         section = lax.axis_index(SECTION)
-
-        def send():
-            self.over().wait()
-            total = self.chip_sum(1) + self.room[1][1].astype(jnp.float32)
-            parts[0] = total.astype(jnp.bfloat16)
-            for which in (0, 1):
-
-                @pl.when(section == which)
-                def _():
-                    over, stay = self.crossing(which)
-                    over.start()
-                    if which:
-                        stay.start()
 
         def end():
             over, stay = self.crossing(1)
@@ -301,7 +303,8 @@
                 stay.wait()
                 self.out[0][...] = parts[2].astype(jnp.float32) + came
 
-        return [send, lambda: None, lambda: None, end]
+        first = (lambda: None) if self.hooked else self.send
+        return [first, lambda: None, lambda: None, end]
 
 
 class StatesTask(ShareTask):
@@ -836,6 +839,15 @@
         self.product = build.temp((columns, right.shape[1]), jnp.bfloat16)
         self.task = ShareTask(self.product) if later is None else ShareCrossTask(self.product, later)
         self.task.late = True
+
+    def make_all(self):
+        def one(number, carry):
+            self.unit(number)
+            return carry
+
+        lax.fori_loop(0, self.units, one, 0)
+        self.task.ins = [self.product.ref]
+        self.task.begin()
 
     def unit(self, number):
         at = span(number, BLOCK)
@@ -1563,8 +1575,14 @@
     sems = build.extra(pltpu.SemaphoreType.DMA((2, 3)))
     products = [(left, grad_low if right is grad_self else right) for left, right in products]
     vector_grads = [build.arg(grads, 2) for grads in vector_grads]
+    early = []
+    for (left, right), share in zip(products[:3], later):
+        flipped = left.shape[0] != rows
+        right = right if right is grad_low else build.arg(right, 1)
+        early.append(Chore(build, 0, 0, 1, build.arg(left, 1), right, flipped, share))
+        early[-1].task.hooked = 1
     stage, _, chores = add_last(
-        build, 2, 0, attention.out, inputs, vectors, vector_grads[1], grad_low, weights, spare, products, later
+        build, 2, 0, attention.out, inputs, vectors, vector_grads[1], grad_low, weights, spare, products[3:], later[3:]
     )
     text_local = build.arg(text_local, 2)
     text_weights = [build.arg(weight, 2) for weight in text_weights]
@@ -1605,11 +1623,21 @@
         ride()
         grad_t.ref[:, span(me, rows)] = own.ref[me]
         need(1)
+        for one in early:
+            one.make_all()
         attention.begin()
         for copy in arriving:
             copy.wait()
-        attention.run(middle)
+
+        def along():
+            middle()
+            for one in early:
+                one.task.middle()
+
+        attention.run(along)
         from_states.cross()
+        for one in early:
+            one.task.send()
 
     def then(need):
         from_text.sum_first()
@@ -1618,7 +1646,7 @@
         from_vectors.ins = [both_grads.ref]
         from_vectors.begin()
 
-    tasks = [from_states] + list(tasks)
+    tasks = [from_states] + list(tasks) + [one.task for one in early]
     return run_chain(
         build,
         [stage],
@@ -2023,7 +2051,7 @@
     def by_section(first, second):
         return jnp.where(at_zero, first, second)
 
-    own_vectors = jnp.pad(jnp.concatenate(vector_args, axis=0), ((0, 2), (0, 0)))
+    own_vectors = jnp.concatenate([*vector_args, jnp.zeros((2, model_width), jnp.float32)], axis=0)
     self_weights = (query_weight, key_weight, value_weight)
     text_local = text.reshape(-1, model_width)
 

time: 520 us -> 513 us (0.987)
  Pallas kernels: 503 us -> 496 us
    pallas_call x6, Pallas kernels: 495 us -> 487 us  [call(): pl.pallas_call(kernel, out_shape=all_outs, in_specs=in_specs, out_specs=o...]
where the time goes in v7:
time: 513 us; the launch traced here: 504 us
  Pallas kernels  496 us (97%)
    pallas_call x6, Pallas kernels, call(): pl.pallas_call(kernel, out_shape=all_outs, in_specs=in_specs, out_specs=o...  487 us

profile of v7, /device:TPU:0, one launch (start us, length us, event | category | flops | bytes accessed | tf_op | source)
XLA Modules:
  0.0 504.1 jit_solution(8425406625015422578)
XLA Ops:
  0.7 0.0 copy-start
  0.7 0.7 copy-done
  1.3 0.2 reduce-window.8
  1.5 0.7 convert_reduce_fusion
  2.3 1.4 concatenate.3.refs_1_.refs_10_.refs_11_.refs_0_.refs_8_.refs_18_
  3.7 38.3 %shard_map.339 = (bf16[192,2048]{1,0:T(8,128)(2,1)}, bf16[256,512]{1,0:T(8,128)(2,1)}, bf16[256,1024]{1,0:T(8,128)(2,1)}, f32[8,1024]{1,0:T(8,128)}, bf16[256,25...) custom-call(bf16[2,512,1024]{2,1,0:T(8,128)(2,1)} %refs_20_.1, ...), custom_call_target="tpu_custom_call" | custom-call | tf_op jit(solution)/shard_map/pallas_call | solution.py:728
  42.0 1.9 fusion
  43.8 0.7 dynamic-slice.3
  44.5 101.6 %shard_map.340 = (bf16[512,1024]{1,0:T(8,128)(2,1)}, bf16[512,1024]{1,0:T(8,128)(2,1)}, bf16[512,256]{1,0:T(8,128)(2,1)}, bf16[512,256]{1,0:T(8,128)(2,1)}, bf16...) custom-call(f32[8,1024]{1,0:T(8,128)} %concatenate.3.refs_1_.refs_10, ...), custom_call_target="tpu_custom_call" | custom-call | tf_op jit(solution)/shard_map/pallas_call | solution.py:728
  146.1 82.0 %shard_map.341 = (bf16[512,1024]{1,0:T(8,128)(2,1)}, bf16[512,1024]{1,0:T(8,128)(2,1)}, bf16[512,256]{1,0:T(8,128)(2,1)}, bf16[512,256]{1,0:T(8,128)(2,1)}, bf16...) custom-call(f32[8,1024]{1,0:T(8,128)} %concatenate.3.refs_1_.refs_10, ...), custom_call_target="tpu_custom_call" | custom-call | tf_op jit(solution)/shard_map/pallas_call | solution.py:728
  228.1 0.0 copy-start.2
  228.1 0.0 copy-start.3
  228.1 90.0 %shard_map.342 = (f32[8,1024]{1,0:T(8,128)}, bf16[512,1024]{1,0:T(8,128)(2,1)}, bf16[512,1024]{1,0:T(8,128)(2,1)}, bf16[512,256]{1,0:T(8,128)(2,1)}, bf16[256,51...) custom-call(f32[2,512,1024]{2,1,0:T(8,128)} %refs_0_.3, ...), custom_call_target="tpu_custom_call" | custom-call | tf_op jit(solution)/shard_map/pallas_call | solution.py:728
  318.2 0.0 copy-done.2
  318.2 0.0 copy-done.3
  318.2 0.6 broadcast_select_fusion
  318.8 0.0 copy-start.4
  318.8 89.2 %shard_map.343 = (f32[8,1024]{1,0:T(8,128)}, bf16[512,1024]{1,0:T(8,128)(2,1)}, f32[8,1024]{1,0:T(8,128)}, bf16[512,1024]{1,0:T(8,128)(2,1)}, bf16[512,1024]{1,0...) custom-call(bf16[512,1024]{1,0:T(8,128)(2,1)} %get-tuple-element.127, ...), custom_call_target="tpu_custom_call" | custom-call | tf_op jit(solution)/shard_map/pallas_call | solution.py:728
  408.1 0.0 copy-done.4
  408.1 1.4 add.12.refs_5_
  409.4 86.3 %shard_map.344 = (bf16[768,512]{1,0:T(8,128)(2,1)}, bf16[512,1024]{1,0:T(8,128)(2,1)}, bf16[2,512,1024]{2,1,0:T(8,128)(2,1)}, f32[256,1024]{1,0:T(8,128)}, f32[2...) custom-call(bf16[192,2048]{1,0:T(8,128)(2,1)} %get-tuple-element.126, ...), custom_call_target="tpu_custom_call" | custom-call | tf_op jit(solution)/shard_map/pallas_call | solution.py:728
  495.7 0.0 copy-start.1
  495.7 8.1 %shard_map.345 = (f32[2,512,1024]{2,1,0:T(8,128)}, f32[2,512,1024]{2,1,0:T(8,128)}, f32[128,1024]{1,0:T(8,128)}, f32[256,256]{1,0:T(8,128)}, f32[256,256]{1,0:T(...) custom-call(bf16[2,512,1024]{2,1,0:T(8,128)(2,1)} %get-tuple-element, ...), custom_call_target="tpu_custom_call" | custom-call | tf_op jit(solution)/shard_map/pallas_call | solution.py:2292
  503.9 0.0 copy-done.1
  (2 shorter events, 0.0 us)
Async XLA Ops:
  0.7 0.7 copy-start
  228.1 90.1 %copy-start.2 = (f32[8,1024]{1,0:T(8,128)S(1)}, f32[8,1024]{1,0:T(8,128)}, u32[]{:S(2)}) copy-start(f32[8,1024]{1,0:T(8,128)} %concatenate.3.refs_1_.refs_10_.refs_11_.refs_0_.refs_8_.refs_18_) | copy-start | bytes 98308
  228.1 90.1 %copy-start.3 = (f32[8,1024]{1,0:T(8,128)S(1)}, f32[8,1024]{1,0:T(8,128)}, u32[]{:S(2)}) copy-start(f32[8,1024]{1,0:T(8,128)} %get-tuple-element.105.refs_1_.refs_9_.refs_2_.refs_19_) | copy-start | bytes 98308
  318.8 89.3 %copy-start.4 = (f32[8,1024]{1,0:T(8,128)S(1)}, f32[8,1024]{1,0:T(8,128)}, u32[]{:S(2)}) copy-start(f32[8,1024]{1,0:T(8,128)} %get-tuple-element.144) | copy-start | bytes 98308
  495.7 8.1 %copy-start.1 = (s32[2,4]{1,0:T(2,128)S(1)}, s32[2,4]{1,0:T(2,128)}, u32[]{:S(2)}) copy-start(s32[2,4]{1,0:T(2,128)} %param.21) | copy-start | bytes 100

commit v8 on v7

--- a/solution.py
+++ b/solution.py
@@ -1782,42 +1782,61 @@
     attention = Attention(build, rows, begins, 1)
     text, text_weights = build.arg(text, 1), [build.arg(weight, 1) for weight in text_weights]
     heads_t = attention.heads_t
-    normed = build.temp((rows, model), jnp.bfloat16)
     own = build.temp((2, frames, width, rows), jnp.bfloat16)
     columns = text_weights[0].shape[1]
     states = build.temp((micros, text.shape[0] // micros, 2 * columns), jnp.bfloat16)
     sems = build.extra(pltpu.SemaphoreType.DMA((2, frames - 1)))
-    over_sems = build.extra(pltpu.SemaphoreType.DMA((2, frames)))
+    blocks = rows // BLOCK
+    over_sems = build.extra(pltpu.SemaphoreType.DMA((2, frames, blocks)))
     from_text = TextTask(states)
 
-    def project(micro):
+    def project(micro, then):
         def one(number, carry):
             at = span(number, BLOCK)
             standard, _ = norm_parts(inputs.ref[micro, at, :].astype(jnp.float32))
-            normed.ref[at, :] = scaled_rows(standard, vectors, 0)
+            turned_parts(scaled_rows(standard, vectors, 0), matrices, own, (micro,), at)
+            then(number)
             return carry
 
-        lax.fori_loop(0, rows // BLOCK, one, 0)
-        turned_parts(normed.ref[...], matrices, own, (micro,), slice(0, rows))
+        lax.fori_loop(0, blocks, one, 0)
 
     def body(need, meet, ride, middle):
         me, section = lax.axis_index(FRAME), lax.axis_index(SECTION)
         landing = heads_t.ref.at[:, span(me, rows)]
         arriving = to_frames(lambda g: own.ref.at[0, g], lambda f: landing, build.bound[sems])
         pair = build.bound[over_sems]
-        over = [
-            remote(own.ref.at[1, g], landing, pair.at[0, k], pair.at[1, k], {SECTION: 1, FRAME: g})
-            for k, g in enumerate((me,) + frame_partners())
-        ]
+        def over(block):
+            place = heads_t.ref.at[:, span(me * blocks + block, BLOCK)]
+            return [
+                remote(
+                    own.ref.at[1, g, :, span(block, BLOCK)],
+                    place,
+                    pair.at[0, k, block],
+                    pair.at[1, k, block],
+                    {SECTION: 1, FRAME: g},
+                )
+                for k, g in enumerate((me,) + frame_partners())
+            ]
+
+        def each(what):
+            def one(block, carry):
+                for copy in over(block):
+                    what(copy)
+                return carry
+
+            lax.fori_loop(0, blocks, one, 0)
+
+        def send(block):
+            pl.when(block == 0)(meet)
+            for copy in over(block):
+                copy.start()
+
         need(0)
 
         @pl.when(section == 0)
         def _():
-            project(1)
-            meet()
-            for copy in over:
-                copy.start()
-            project(0)
+            project(1, send)
+            project(0, lambda block: None)
             for copy in arriving[::-1]:
                 copy.start()
             heads_t.ref[:, span(me, rows)] = own.ref[0, me]
@@ -1838,15 +1857,13 @@
 
         @pl.when(section == 0)
         def _():
-            for copy in arriving + over:
-                copy.wait_send()
             for copy in arriving:
-                copy.wait_recv()
+                copy.wait()
+            each(lambda copy: copy.wait_send())
 
         @pl.when(section == 1)
         def _():
-            for copy in over:
-                copy.wait_recv()
+            each(lambda copy: copy.wait_recv())
 
         attention.run(early)
 

time: 513 us -> 511 us (level)
  no operation moved by 1% of the time
where the time goes in v8:
time: 511 us; the launch traced here: 503 us
  Pallas kernels  494 us (97%)
    pallas_call x6, Pallas kernels, call(): pl.pallas_call(kernel, out_shape=all_outs, in_specs=in_specs, out_specs=o...  486 us

profile of v8, /device:TPU:0, one launch (start us, length us, event | category | flops | bytes accessed | tf_op | source)
XLA Modules:
  0.0 503.1 jit_solution(6265024956970829934)
XLA Ops:
  0.7 0.0 copy-start
  0.7 0.7 copy-done
  1.3 0.2 reduce-window.8
  1.5 0.7 convert_reduce_fusion
  2.3 1.4 concatenate.3.refs_1_.refs_10_.refs_11_.refs_0_.refs_8_.refs_18_
  3.7 37.7 %shard_map.339 = (bf16[192,2048]{1,0:T(8,128)(2,1)}, bf16[256,512]{1,0:T(8,128)(2,1)}, bf16[256,1024]{1,0:T(8,128)(2,1)}, f32[8,1024]{1,0:T(8,128)}, bf16[256,25...) custom-call(bf16[2,512,1024]{2,1,0:T(8,128)(2,1)} %refs_20_.1, ...), custom_call_target="tpu_custom_call" | custom-call | tf_op jit(solution)/shard_map/pallas_call | solution.py:728
  41.4 1.9 fusion
  43.3 0.7 dynamic-slice.3
  43.9 101.1 %shard_map.340 = (bf16[512,1024]{1,0:T(8,128)(2,1)}, bf16[512,1024]{1,0:T(8,128)(2,1)}, bf16[512,256]{1,0:T(8,128)(2,1)}, bf16[512,256]{1,0:T(8,128)(2,1)}, bf16...) custom-call(f32[8,1024]{1,0:T(8,128)} %concatenate.3.refs_1_.refs_10, ...), custom_call_target="tpu_custom_call" | custom-call | tf_op jit(solution)/shard_map/pallas_call | solution.py:728
  145.0 82.0 %shard_map.341 = (bf16[512,1024]{1,0:T(8,128)(2,1)}, bf16[512,1024]{1,0:T(8,128)(2,1)}, bf16[512,256]{1,0:T(8,128)(2,1)}, bf16[512,256]{1,0:T(8,128)(2,1)}, bf16...) custom-call(f32[8,1024]{1,0:T(8,128)} %concatenate.3.refs_1_.refs_10, ...), custom_call_target="tpu_custom_call" | custom-call | tf_op jit(solution)/shard_map/pallas_call | solution.py:728
  227.0 0.0 copy-start.2
  227.0 0.0 copy-start.3
  227.0 90.0 %shard_map.342 = (f32[8,1024]{1,0:T(8,128)}, bf16[512,1024]{1,0:T(8,128)(2,1)}, bf16[512,1024]{1,0:T(8,128)(2,1)}, bf16[512,256]{1,0:T(8,128)(2,1)}, bf16[256,51...) custom-call(f32[2,512,1024]{2,1,0:T(8,128)} %refs_0_.3, ...), custom_call_target="tpu_custom_call" | custom-call | tf_op jit(solution)/shard_map/pallas_call | solution.py:728
  317.0 0.0 copy-done.2
  317.0 0.0 copy-done.3
  317.0 0.6 broadcast_select_fusion
  317.7 0.0 copy-start.4
  317.7 89.2 %shard_map.343 = (f32[8,1024]{1,0:T(8,128)}, bf16[512,1024]{1,0:T(8,128)(2,1)}, f32[8,1024]{1,0:T(8,128)}, bf16[512,1024]{1,0:T(8,128)(2,1)}, bf16[512,1024]{1,0...) custom-call(bf16[512,1024]{1,0:T(8,128)(2,1)} %get-tuple-element.127, ...), custom_call_target="tpu_custom_call" | custom-call | tf_op jit(solution)/shard_map/pallas_call | solution.py:728
  406.9 0.0 copy-done.4
  406.9 1.4 add.12.refs_5_
  408.3 86.4 %shard_map.344 = (bf16[768,512]{1,0:T(8,128)(2,1)}, bf16[512,1024]{1,0:T(8,128)(2,1)}, bf16[2,512,1024]{2,1,0:T(8,128)(2,1)}, f32[256,1024]{1,0:T(8,128)}, f32[2...) custom-call(bf16[192,2048]{1,0:T(8,128)(2,1)} %get-tuple-element.126, ...), custom_call_target="tpu_custom_call" | custom-call | tf_op jit(solution)/shard_map/pallas_call | solution.py:728
  494.7 0.0 copy-start.1
  494.7 8.1 %shard_map.345 = (f32[2,512,1024]{2,1,0:T(8,128)}, f32[2,512,1024]{2,1,0:T(8,128)}, f32[128,1024]{1,0:T(8,128)}, f32[256,256]{1,0:T(8,128)}, f32[256,256]{1,0:T(...) custom-call(bf16[2,512,1024]{2,1,0:T(8,128)(2,1)} %get-tuple-element, ...), custom_call_target="tpu_custom_call" | custom-call | tf_op jit(solution)/shard_map/pallas_call | solution.py:2309
  502.8 0.0 copy-done.1
  (2 shorter events, 0.0 us)
Async XLA Ops:
  0.7 0.7 copy-start
  227.0 90.0 %copy-start.2 = (f32[8,1024]{1,0:T(8,128)S(1)}, f32[8,1024]{1,0:T(8,128)}, u32[]{:S(2)}) copy-start(f32[8,1024]{1,0:T(8,128)} %concatenate.3.refs_1_.refs_10_.refs_11_.refs_0_.refs_8_.refs_18_) | copy-start | bytes 98308
  227.0 90.0 %copy-start.3 = (f32[8,1024]{1,0:T(8,128)S(1)}, f32[8,1024]{1,0:T(8,128)}, u32[]{:S(2)}) copy-start(f32[8,1024]{1,0:T(8,128)} %get-tuple-element.105.refs_1_.refs_9_.refs_2_.refs_19_) | copy-start | bytes 98308
  317.7 89.2 %copy-start.4 = (f32[8,1024]{1,0:T(8,128)S(1)}, f32[8,1024]{1,0:T(8,128)}, u32[]{:S(2)}) copy-start(f32[8,1024]{1,0:T(8,128)} %get-tuple-element.144) | copy-start | bytes 98308
  494.7 8.1 %copy-start.1 = (s32[2,4]{1,0:T(2,128)S(1)}, s32[2,4]{1,0:T(2,128)}, u32[]{:S(2)}) copy-start(s32[2,4]{1,0:T(2,128)} %param.21) | copy-start | bytes 100
